TPU v7x, 512 devices: a whole 4x8x8 slice. The times are simulated.
512 devices in a mesh: pp: 8 (over z), sp: 64 (over y, x, core).
Axes of the slice: x: 4, y: 8, z: 8, core: 2. Of those that a mesh axis runs over, the one named last changes fastest.
Arguments:
- queries: bfloat16 [8, 8192, 4096], P('pp', 'sp'), may hold values from -8 to 8
- keys: bfloat16 [8, 8192, 512], P('pp', 'sp'), may hold values from -8 to 8
- values: bfloat16 [8, 8192, 512], P('pp', 'sp'), may hold values from -6 to 6
- doc_ids: int32 [8, 8192], P('pp', 'sp'), may hold values from 0 to 7, never falling along the last dimension, each value on 1 to 2048 neighbouring positions
Outputs:
- handed: bfloat16 [8, 8192, 4096], P('pp', 'sp')
Inputs may be any that keep to these rules, and one draw needn't show every extreme that they name: `doc_ids`: ids never fall along a micro-batch, each document has 1 to 2048 tokens, and one has exactly 2048.
All inputs are finite; a program needn't handle non-finite values.
Results may differ from a plain program's by a relative error of at most 0.008.
Values may be sent and summed in bfloat16 or wider, within the bound.
No kernel may reach another device: no remote copies, remote signals or barrier semaphores. Data moves between devices by JAX's collectives and lax.ppermute only.
A program may use at most 64 MiB of HBM per device.

v0:
```python
import jax
import jax.numpy as jnp
from jax import lax
from jax.sharding import PartitionSpec as P

HQ = 32
HK = 4
HEAD = 128


def shifted(block, axis, distance):
    devices = range(lax.axis_size(axis))
    route = [(i - distance, i) for i in devices if i - distance in devices]
    return lax.ppermute(block, axis, route)


def shifted_2(block, axis, distance):
    devices = range(lax.axis_size(axis))
    route = [((i - distance) % len(devices), i) for i in devices]
    return lax.ppermute(block, axis, route)


def fold_shard(state, kv_pair, key_ids, back, context):
    queries4, qpos, qids, index, tokens = context
    running, totals, accum = state
    scale = 1.0 / HEAD**0.5
    key_part = kv_pair[0].reshape(tokens, HK, HEAD)
    val_part = kv_pair[1].reshape(tokens, HK, HEAD)
    scores = (
        jnp.einsum("tkgd,skd->kgts", queries4, key_part, preferred_element_type=jnp.float32) * scale
    )
    source = index - back
    kpos = source * tokens + jnp.arange(tokens, dtype=jnp.int32)
    allowed = (key_ids[None, :] == qids[:, None]) & (kpos[None, :] <= qpos[:, None]) & (source >= 0)
    masked = jnp.where(allowed, scores, -jnp.inf)
    newmax = jnp.maximum(running, jnp.max(masked, axis=-1))
    safemax = jnp.where(jnp.isfinite(newmax), newmax, 0.0)
    weight = jnp.where(allowed, jnp.exp(scores - safemax[..., None]), 0.0)
    factor = jnp.exp(running - safemax)
    totals = totals * factor + jnp.sum(weight, axis=-1)
    accum = accum * factor[..., None] + jnp.einsum(
        "kgts,skd->kgtd", weight.astype(jnp.bfloat16), val_part, preferred_element_type=jnp.float32
    )
    return (newmax, totals, accum)


def shards(queries, keys, values, doc_ids):
    tokens = queries.shape[1]
    group = HQ // HK
    look = min(16, lax.axis_size("sp") // 2)
    index = lax.axis_index("sp")
    queries4 = queries[0].reshape(tokens, HK, group, HEAD)
    qpos = index * tokens + jnp.arange(tokens, dtype=jnp.int32)
    qids = doc_ids[0]
    context = (queries4, qpos, qids, index, tokens)
    kv_own = jnp.stack([keys[0], values[0]], axis=0)
    state = (
        jnp.full((HK, group, tokens), -jnp.inf, jnp.float32),
        jnp.zeros((HK, group, tokens), jnp.float32),
        jnp.zeros((HK, group, tokens, HEAD), jnp.float32),
    )
    state = fold_shard(state, kv_own, qids, 0, context)

    def cycle_step(back, carry):
        held, held_ids, inner = carry
        held, held_ids = shifted((held, held_ids), "sp", 1)
        inner = fold_shard(inner, held, held_ids, back, context)
        return (held, held_ids, inner)

    final = lax.fori_loop(1, look + 1, cycle_step, (kv_own, qids, state))
    state = final[2]
    running, totals, accum = state
    result = accum / totals[..., None]
    attended = result.transpose(2, 0, 1, 3).reshape(1, tokens, HQ * HEAD).astype(jnp.bfloat16)
    return shifted_2(attended, "pp", 1)


def solution(mesh):
    return jax.shard_map(
        shards,
        mesh=mesh,
        in_specs=(P("pp", "sp", None), P("pp", "sp", None), P("pp", "sp", None), P("pp", "sp")),
        out_specs=P("pp", "sp", None),
        check_vma=False,
    )
```

profile of v0, /device:TPU:31, one launch (start us, length us, event | category | flops | bytes accessed | tf_op | source)
XLA Modules:
  0.0 302.7 jit_solution(2036885005389781682)
XLA Ops:
  9.8 257.5 %while.22 = (s32[]{:T(128)}, bf16[2,128,512]{1,2,0:T(8,128)(2,1)}, s32[128]{0:T(128)S(1)}, f32[4,8,128]{2,1,0:T(8,128)S(1)}, f32[4,8,128]{2,1,0:T(8,128)S(1)}, /...) while((s32[]{:T(128)}, bf16[2,128,512]{1,2,0:T(8,128)(2,1)}, ...), condition=%wide.region_5.6_spmd.clone, body=%wide.region_2.5_spmd.clone.sunk | while | flops 275341568 | bytes 14244087 | solution.py:70
  9.8 4.9 %collective-permute-start.1 = (s32[128]{0:T(128)S(1)}, s32[128]{0:T(128)S(1)}, u32[]{:S(2)}, u32[]{:S(2)}) collective-permute-start(s32[128]{0:T(128)S(1)} %get-tuple-element.340), channel_id=1, source_target_pairs={{0,1},{1,2},{2,3},{3,4},{4,5},{5,6},{6,7},{7,8},{8,9},{9,10},{10,1... | collective-permute-start | bytes 1544 | tf_op jit(solution)/shard_map/while/body/eval_jaxpr/ppermute | solution.py:14
  14.7 1.9 collective-permute-start
  16.8 3.5 %collective-permute-done = bf16[2,128,512]{1,2,0:T(8,128)(2,1)S(1)} collective-permute-done((bf16[2,128,512]{1,2,0:T(8,128)(2,1)}, bf16[2,128,512]{1,2,0:T(8,128)(2,1)S(1)}, u32[]{:S(2)}, u32[]{:S(2)}) %collective-permute-start) | collective-permute-done | bytes 262176 | tf_op jit(solution)/shard_map/while/body/eval_jaxpr/ppermute | solution.py:14
  23.4 7.6 %collective-permute-start.1 = (s32[128]{0:T(128)S(1)}, s32[128]{0:T(128)S(1)}, u32[]{:S(2)}, u32[]{:S(2)}) collective-permute-start(s32[128]{0:T(128)S(1)} %get-tuple-element.340), channel_id=1, source_target_pairs={{0,1},{1,2},{2,3},{3,4},{4,5},{5,6},{6,7},{7,8},{8,9},{9,10},{10,1... | collective-permute-start | bytes 1544 | tf_op jit(solution)/shard_map/while/body/eval_jaxpr/ppermute | solution.py:14
  31.0 1.9 collective-permute-start
  33.1 3.5 %collective-permute-done = bf16[2,128,512]{1,2,0:T(8,128)(2,1)S(1)} collective-permute-done((bf16[2,128,512]{1,2,0:T(8,128)(2,1)}, bf16[2,128,512]{1,2,0:T(8,128)(2,1)S(1)}, u32[]{:S(2)}, u32[]{:S(2)}) %collective-permute-start) | collective-permute-done | bytes 262176 | tf_op jit(solution)/shard_map/while/body/eval_jaxpr/ppermute | solution.py:14
  39.7 7.6 %collective-permute-start.1 = (s32[128]{0:T(128)S(1)}, s32[128]{0:T(128)S(1)}, u32[]{:S(2)}, u32[]{:S(2)}) collective-permute-start(s32[128]{0:T(128)S(1)} %get-tuple-element.340), channel_id=1, source_target_pairs={{0,1},{1,2},{2,3},{3,4},{4,5},{5,6},{6,7},{7,8},{8,9},{9,10},{10,1... | collective-permute-start | bytes 1544 | tf_op jit(solution)/shard_map/while/body/eval_jaxpr/ppermute | solution.py:14
  47.3 1.9 collective-permute-start
  49.3 3.5 %collective-permute-done = bf16[2,128,512]{1,2,0:T(8,128)(2,1)S(1)} collective-permute-done((bf16[2,128,512]{1,2,0:T(8,128)(2,1)}, bf16[2,128,512]{1,2,0:T(8,128)(2,1)S(1)}, u32[]{:S(2)}, u32[]{:S(2)}) %collective-permute-start) | collective-permute-done | bytes 262176 | tf_op jit(solution)/shard_map/while/body/eval_jaxpr/ppermute | solution.py:14
  55.9 7.6 %collective-permute-start.1 = (s32[128]{0:T(128)S(1)}, s32[128]{0:T(128)S(1)}, u32[]{:S(2)}, u32[]{:S(2)}) collective-permute-start(s32[128]{0:T(128)S(1)} %get-tuple-element.340), channel_id=1, source_target_pairs={{0,1},{1,2},{2,3},{3,4},{4,5},{5,6},{6,7},{7,8},{8,9},{9,10},{10,1... | collective-permute-start | bytes 1544 | tf_op jit(solution)/shard_map/while/body/eval_jaxpr/ppermute | solution.py:14
  63.5 1.9 collective-permute-start
  65.6 3.5 %collective-permute-done = bf16[2,128,512]{1,2,0:T(8,128)(2,1)S(1)} collective-permute-done((bf16[2,128,512]{1,2,0:T(8,128)(2,1)}, bf16[2,128,512]{1,2,0:T(8,128)(2,1)S(1)}, u32[]{:S(2)}, u32[]{:S(2)}) %collective-permute-start) | collective-permute-done | bytes 262176 | tf_op jit(solution)/shard_map/while/body/eval_jaxpr/ppermute | solution.py:14
  72.2 7.6 %collective-permute-start.1 = (s32[128]{0:T(128)S(1)}, s32[128]{0:T(128)S(1)}, u32[]{:S(2)}, u32[]{:S(2)}) collective-permute-start(s32[128]{0:T(128)S(1)} %get-tuple-element.340), channel_id=1, source_target_pairs={{0,1},{1,2},{2,3},{3,4},{4,5},{5,6},{6,7},{7,8},{8,9},{9,10},{10,1... | collective-permute-start | bytes 1544 | tf_op jit(solution)/shard_map/while/body/eval_jaxpr/ppermute | solution.py:14
  79.8 1.9 collective-permute-start
  81.9 3.5 %collective-permute-done = bf16[2,128,512]{1,2,0:T(8,128)(2,1)S(1)} collective-permute-done((bf16[2,128,512]{1,2,0:T(8,128)(2,1)}, bf16[2,128,512]{1,2,0:T(8,128)(2,1)S(1)}, u32[]{:S(2)}, u32[]{:S(2)}) %collective-permute-start) | collective-permute-done | bytes 262176 | tf_op jit(solution)/shard_map/while/body/eval_jaxpr/ppermute | solution.py:14
  88.4 7.6 %collective-permute-start.1 = (s32[128]{0:T(128)S(1)}, s32[128]{0:T(128)S(1)}, u32[]{:S(2)}, u32[]{:S(2)}) collective-permute-start(s32[128]{0:T(128)S(1)} %get-tuple-element.340), channel_id=1, source_target_pairs={{0,1},{1,2},{2,3},{3,4},{4,5},{5,6},{6,7},{7,8},{8,9},{9,10},{10,1... | collective-permute-start | bytes 1544 | tf_op jit(solution)/shard_map/while/body/eval_jaxpr/ppermute | solution.py:14
  96.0 1.9 collective-permute-start
  98.1 3.5 %collective-permute-done = bf16[2,128,512]{1,2,0:T(8,128)(2,1)S(1)} collective-permute-done((bf16[2,128,512]{1,2,0:T(8,128)(2,1)}, bf16[2,128,512]{1,2,0:T(8,128)(2,1)S(1)}, u32[]{:S(2)}, u32[]{:S(2)}) %collective-permute-start) | collective-permute-done | bytes 262176 | tf_op jit(solution)/shard_map/while/body/eval_jaxpr/ppermute | solution.py:14
  104.7 7.6 %collective-permute-start.1 = (s32[128]{0:T(128)S(1)}, s32[128]{0:T(128)S(1)}, u32[]{:S(2)}, u32[]{:S(2)}) collective-permute-start(s32[128]{0:T(128)S(1)} %get-tuple-element.340), channel_id=1, source_target_pairs={{0,1},{1,2},{2,3},{3,4},{4,5},{5,6},{6,7},{7,8},{8,9},{9,10},{10,1... | collective-permute-start | bytes 1544 | tf_op jit(solution)/shard_map/while/body/eval_jaxpr/ppermute | solution.py:14
  112.3 1.9 collective-permute-start
  114.4 3.5 %collective-permute-done = bf16[2,128,512]{1,2,0:T(8,128)(2,1)S(1)} collective-permute-done((bf16[2,128,512]{1,2,0:T(8,128)(2,1)}, bf16[2,128,512]{1,2,0:T(8,128)(2,1)S(1)}, u32[]{:S(2)}, u32[]{:S(2)}) %collective-permute-start) | collective-permute-done | bytes 262176 | tf_op jit(solution)/shard_map/while/body/eval_jaxpr/ppermute | solution.py:14
  121.0 7.6 %collective-permute-start.1 = (s32[128]{0:T(128)S(1)}, s32[128]{0:T(128)S(1)}, u32[]{:S(2)}, u32[]{:S(2)}) collective-permute-start(s32[128]{0:T(128)S(1)} %get-tuple-element.340), channel_id=1, source_target_pairs={{0,1},{1,2},{2,3},{3,4},{4,5},{5,6},{6,7},{7,8},{8,9},{9,10},{10,1... | collective-permute-start | bytes 1544 | tf_op jit(solution)/shard_map/while/body/eval_jaxpr/ppermute | solution.py:14
  128.6 1.9 collective-permute-start
  130.6 3.5 %collective-permute-done = bf16[2,128,512]{1,2,0:T(8,128)(2,1)S(1)} collective-permute-done((bf16[2,128,512]{1,2,0:T(8,128)(2,1)}, bf16[2,128,512]{1,2,0:T(8,128)(2,1)S(1)}, u32[]{:S(2)}, u32[]{:S(2)}) %collective-permute-start) | collective-permute-done | bytes 262176 | tf_op jit(solution)/shard_map/while/body/eval_jaxpr/ppermute | solution.py:14
  137.2 7.6 %collective-permute-start.1 = (s32[128]{0:T(128)S(1)}, s32[128]{0:T(128)S(1)}, u32[]{:S(2)}, u32[]{:S(2)}) collective-permute-start(s32[128]{0:T(128)S(1)} %get-tuple-element.340), channel_id=1, source_target_pairs={{0,1},{1,2},{2,3},{3,4},{4,5},{5,6},{6,7},{7,8},{8,9},{9,10},{10,1... | collective-permute-start | bytes 1544 | tf_op jit(solution)/shard_map/while/body/eval_jaxpr/ppermute | solution.py:14
  144.8 1.9 collective-permute-start
  146.9 3.5 %collective-permute-done = bf16[2,128,512]{1,2,0:T(8,128)(2,1)S(1)} collective-permute-done((bf16[2,128,512]{1,2,0:T(8,128)(2,1)}, bf16[2,128,512]{1,2,0:T(8,128)(2,1)S(1)}, u32[]{:S(2)}, u32[]{:S(2)}) %collective-permute-start) | collective-permute-done | bytes 262176 | tf_op jit(solution)/shard_map/while/body/eval_jaxpr/ppermute | solution.py:14
  153.5 7.6 %collective-permute-start.1 = (s32[128]{0:T(128)S(1)}, s32[128]{0:T(128)S(1)}, u32[]{:S(2)}, u32[]{:S(2)}) collective-permute-start(s32[128]{0:T(128)S(1)} %get-tuple-element.340), channel_id=1, source_target_pairs={{0,1},{1,2},{2,3},{3,4},{4,5},{5,6},{6,7},{7,8},{8,9},{9,10},{10,1... | collective-permute-start | bytes 1544 | tf_op jit(solution)/shard_map/while/body/eval_jaxpr/ppermute | solution.py:14
  161.1 1.9 collective-permute-start
  163.2 3.5 %collective-permute-done = bf16[2,128,512]{1,2,0:T(8,128)(2,1)S(1)} collective-permute-done((bf16[2,128,512]{1,2,0:T(8,128)(2,1)}, bf16[2,128,512]{1,2,0:T(8,128)(2,1)S(1)}, u32[]{:S(2)}, u32[]{:S(2)}) %collective-permute-start) | collective-permute-done | bytes 262176 | tf_op jit(solution)/shard_map/while/body/eval_jaxpr/ppermute | solution.py:14
  169.8 7.6 %collective-permute-start.1 = (s32[128]{0:T(128)S(1)}, s32[128]{0:T(128)S(1)}, u32[]{:S(2)}, u32[]{:S(2)}) collective-permute-start(s32[128]{0:T(128)S(1)} %get-tuple-element.340), channel_id=1, source_target_pairs={{0,1},{1,2},{2,3},{3,4},{4,5},{5,6},{6,7},{7,8},{8,9},{9,10},{10,1... | collective-permute-start | bytes 1544 | tf_op jit(solution)/shard_map/while/body/eval_jaxpr/ppermute | solution.py:14
  177.4 1.9 collective-permute-start
  179.4 3.5 %collective-permute-done = bf16[2,128,512]{1,2,0:T(8,128)(2,1)S(1)} collective-permute-done((bf16[2,128,512]{1,2,0:T(8,128)(2,1)}, bf16[2,128,512]{1,2,0:T(8,128)(2,1)S(1)}, u32[]{:S(2)}, u32[]{:S(2)}) %collective-permute-start) | collective-permute-done | bytes 262176 | tf_op jit(solution)/shard_map/while/body/eval_jaxpr/ppermute | solution.py:14
  186.0 7.6 %collective-permute-start.1 = (s32[128]{0:T(128)S(1)}, s32[128]{0:T(128)S(1)}, u32[]{:S(2)}, u32[]{:S(2)}) collective-permute-start(s32[128]{0:T(128)S(1)} %get-tuple-element.340), channel_id=1, source_target_pairs={{0,1},{1,2},{2,3},{3,4},{4,5},{5,6},{6,7},{7,8},{8,9},{9,10},{10,1... | collective-permute-start | bytes 1544 | tf_op jit(solution)/shard_map/while/body/eval_jaxpr/ppermute | solution.py:14
  193.6 1.9 collective-permute-start
  195.7 3.5 %collective-permute-done = bf16[2,128,512]{1,2,0:T(8,128)(2,1)S(1)} collective-permute-done((bf16[2,128,512]{1,2,0:T(8,128)(2,1)}, bf16[2,128,512]{1,2,0:T(8,128)(2,1)S(1)}, u32[]{:S(2)}, u32[]{:S(2)}) %collective-permute-start) | collective-permute-done | bytes 262176 | tf_op jit(solution)/shard_map/while/body/eval_jaxpr/ppermute | solution.py:14
  202.3 7.6 %collective-permute-start.1 = (s32[128]{0:T(128)S(1)}, s32[128]{0:T(128)S(1)}, u32[]{:S(2)}, u32[]{:S(2)}) collective-permute-start(s32[128]{0:T(128)S(1)} %get-tuple-element.340), channel_id=1, source_target_pairs={{0,1},{1,2},{2,3},{3,4},{4,5},{5,6},{6,7},{7,8},{8,9},{9,10},{10,1... | collective-permute-start | bytes 1544 | tf_op jit(solution)/shard_map/while/body/eval_jaxpr/ppermute | solution.py:14
  209.9 1.9 collective-permute-start
  212.0 3.5 %collective-permute-done = bf16[2,128,512]{1,2,0:T(8,128)(2,1)S(1)} collective-permute-done((bf16[2,128,512]{1,2,0:T(8,128)(2,1)}, bf16[2,128,512]{1,2,0:T(8,128)(2,1)S(1)}, u32[]{:S(2)}, u32[]{:S(2)}) %collective-permute-start) | collective-permute-done | bytes 262176 | tf_op jit(solution)/shard_map/while/body/eval_jaxpr/ppermute | solution.py:14
  218.5 7.6 %collective-permute-start.1 = (s32[128]{0:T(128)S(1)}, s32[128]{0:T(128)S(1)}, u32[]{:S(2)}, u32[]{:S(2)}) collective-permute-start(s32[128]{0:T(128)S(1)} %get-tuple-element.340), channel_id=1, source_target_pairs={{0,1},{1,2},{2,3},{3,4},{4,5},{5,6},{6,7},{7,8},{8,9},{9,10},{10,1... | collective-permute-start | bytes 1544 | tf_op jit(solution)/shard_map/while/body/eval_jaxpr/ppermute | solution.py:14
  228.2 3.5 %collective-permute-done = bf16[2,128,512]{1,2,0:T(8,128)(2,1)S(1)} collective-permute-done((bf16[2,128,512]{1,2,0:T(8,128)(2,1)}, bf16[2,128,512]{1,2,0:T(8,128)(2,1)S(1)}, u32[]{:S(2)}, u32[]{:S(2)}) %collective-permute-start) | collective-permute-done | bytes 262176 | tf_op jit(solution)/shard_map/while/body/eval_jaxpr/ppermute | solution.py:14
  234.8 7.6 %collective-permute-start.1 = (s32[128]{0:T(128)S(1)}, s32[128]{0:T(128)S(1)}, u32[]{:S(2)}, u32[]{:S(2)}) collective-permute-start(s32[128]{0:T(128)S(1)} %get-tuple-element.340), channel_id=1, source_target_pairs={{0,1},{1,2},{2,3},{3,4},{4,5},{5,6},{6,7},{7,8},{8,9},{9,10},{10,1... | collective-permute-start | bytes 1544 | tf_op jit(solution)/shard_map/while/body/eval_jaxpr/ppermute | solution.py:14
  244.5 3.5 %collective-permute-done = bf16[2,128,512]{1,2,0:T(8,128)(2,1)S(1)} collective-permute-done((bf16[2,128,512]{1,2,0:T(8,128)(2,1)}, bf16[2,128,512]{1,2,0:T(8,128)(2,1)S(1)}, u32[]{:S(2)}, u32[]{:S(2)}) %collective-permute-start) | collective-permute-done | bytes 262176 | tf_op jit(solution)/shard_map/while/body/eval_jaxpr/ppermute | solution.py:14
  251.1 7.6 %collective-permute-start.1 = (s32[128]{0:T(128)S(1)}, s32[128]{0:T(128)S(1)}, u32[]{:S(2)}, u32[]{:S(2)}) collective-permute-start(s32[128]{0:T(128)S(1)} %get-tuple-element.340), channel_id=1, source_target_pairs={{0,1},{1,2},{2,3},{3,4},{4,5},{5,6},{6,7},{7,8},{8,9},{9,10},{10,1... | collective-permute-start | bytes 1544 | tf_op jit(solution)/shard_map/while/body/eval_jaxpr/ppermute | solution.py:14
  260.7 3.5 %collective-permute-done = bf16[2,128,512]{1,2,0:T(8,128)(2,1)S(1)} collective-permute-done((bf16[2,128,512]{1,2,0:T(8,128)(2,1)}, bf16[2,128,512]{1,2,0:T(8,128)(2,1)S(1)}, u32[]{:S(2)}, u32[]{:S(2)}) %collective-permute-start) | collective-permute-done | bytes 262176 | tf_op jit(solution)/shard_map/while/body/eval_jaxpr/ppermute | solution.py:14
  269.2 4.0 %collective-permute-start.2 = (bf16[1,128,4096]{2,1,0:T(8,128)(2,1)S(1)}, bf16[1,128,4096]{2,1,0:T(8,128)(2,1)S(1)}, u32[]{:S(2)}, u32[]{:S(2)}) collective-permute-start(bf16[1,128,4096]{2,1,0:T(8,128)(2,1)S(1)} %convert_element_type.30), channel_id=1, source_target_pairs={{448,0},{0,64},{64,128},{128,192},{192,256},{256,320},{320,384},{3... | collective-permute-start | bytes 3145736 | tf_op jit(solution)/shard_map/ppermute | solution.py:20
  273.2 28.5 %collective-permute-done.2 = bf16[1,128,4096]{2,1,0:T(8,128)(2,1)S(1)} collective-permute-done((bf16[1,128,4096]{2,1,0:T(8,128)(2,1)S(1)}, bf16[1,128,4096]{2,1,0:T(8,128)(2,1)S(1)}, u32[]{:S(2)}, u32[]{:S(2)}) %collective-permute-start.2) | collective-permute-done | bytes 1048608 | tf_op jit(solution)/shard_map/ppermute | solution.py:20
  (216 shorter events, 69.4 us)
Async XLA Ops:
  4.6 2.3 copy-start
  9.8 6.9 %collective-permute-start.1 = (s32[128]{0:T(128)S(1)}, s32[128]{0:T(128)S(1)}, u32[]{:S(2)}, u32[]{:S(2)}) collective-permute-start(s32[128]{0:T(128)S(1)} %get-tuple-element.340), channel_id=1, source_target_pairs={{0,1},{1,2},{2,3},{3,4},{4,5},{5,6},{6,7},{7,8},{8,9},{9,10},{10,1... | collective-permute-start | bytes 1544 | tf_op jit(solution)/shard_map/while/body/eval_jaxpr/ppermute | solution.py:14
  14.7 5.5 %collective-permute-start = (bf16[2,128,512]{1,2,0:T(8,128)(2,1)}, bf16[2,128,512]{1,2,0:T(8,128)(2,1)S(1)}, u32[]{:S(2)}, u32[]{:S(2)}) collective-permute-start(bf16[2,128,512]{1,2,0:T(8,128)(2,1)} %get-tuple-element.339), channel_id=1, source_target_pairs={{0,1},{1,2},{2,3},{3,4},{4,5},{5,6},{6,7},{7,8},{8,9},{9,10},{10,1... | collective-permute-start | bytes 786440 | tf_op jit(solution)/shard_map/while/body/eval_jaxpr/ppermute | solution.py:14
  23.4 9.6 %collective-permute-start.1 = (s32[128]{0:T(128)S(1)}, s32[128]{0:T(128)S(1)}, u32[]{:S(2)}, u32[]{:S(2)}) collective-permute-start(s32[128]{0:T(128)S(1)} %get-tuple-element.340), channel_id=1, source_target_pairs={{0,1},{1,2},{2,3},{3,4},{4,5},{5,6},{6,7},{7,8},{8,9},{9,10},{10,1... | collective-permute-start | bytes 1544 | tf_op jit(solution)/shard_map/while/body/eval_jaxpr/ppermute | solution.py:14
  31.0 5.5 %collective-permute-start = (bf16[2,128,512]{1,2,0:T(8,128)(2,1)}, bf16[2,128,512]{1,2,0:T(8,128)(2,1)S(1)}, u32[]{:S(2)}, u32[]{:S(2)}) collective-permute-start(bf16[2,128,512]{1,2,0:T(8,128)(2,1)} %get-tuple-element.339), channel_id=1, source_target_pairs={{0,1},{1,2},{2,3},{3,4},{4,5},{5,6},{6,7},{7,8},{8,9},{9,10},{10,1... | collective-permute-start | bytes 786440 | tf_op jit(solution)/shard_map/while/body/eval_jaxpr/ppermute | solution.py:14
  39.7 9.6 %collective-permute-start.1 = (s32[128]{0:T(128)S(1)}, s32[128]{0:T(128)S(1)}, u32[]{:S(2)}, u32[]{:S(2)}) collective-permute-start(s32[128]{0:T(128)S(1)} %get-tuple-element.340), channel_id=1, source_target_pairs={{0,1},{1,2},{2,3},{3,4},{4,5},{5,6},{6,7},{7,8},{8,9},{9,10},{10,1... | collective-permute-start | bytes 1544 | tf_op jit(solution)/shard_map/while/body/eval_jaxpr/ppermute | solution.py:14
  47.3 5.5 %collective-permute-start = (bf16[2,128,512]{1,2,0:T(8,128)(2,1)}, bf16[2,128,512]{1,2,0:T(8,128)(2,1)S(1)}, u32[]{:S(2)}, u32[]{:S(2)}) collective-permute-start(bf16[2,128,512]{1,2,0:T(8,128)(2,1)} %get-tuple-element.339), channel_id=1, source_target_pairs={{0,1},{1,2},{2,3},{3,4},{4,5},{5,6},{6,7},{7,8},{8,9},{9,10},{10,1... | collective-permute-start | bytes 786440 | tf_op jit(solution)/shard_map/while/body/eval_jaxpr/ppermute | solution.py:14
  55.9 9.6 %collective-permute-start.1 = (s32[128]{0:T(128)S(1)}, s32[128]{0:T(128)S(1)}, u32[]{:S(2)}, u32[]{:S(2)}) collective-permute-start(s32[128]{0:T(128)S(1)} %get-tuple-element.340), channel_id=1, source_target_pairs={{0,1},{1,2},{2,3},{3,4},{4,5},{5,6},{6,7},{7,8},{8,9},{9,10},{10,1... | collective-permute-start | bytes 1544 | tf_op jit(solution)/shard_map/while/body/eval_jaxpr/ppermute | solution.py:14
  63.5 5.5 %collective-permute-start = (bf16[2,128,512]{1,2,0:T(8,128)(2,1)}, bf16[2,128,512]{1,2,0:T(8,128)(2,1)S(1)}, u32[]{:S(2)}, u32[]{:S(2)}) collective-permute-start(bf16[2,128,512]{1,2,0:T(8,128)(2,1)} %get-tuple-element.339), channel_id=1, source_target_pairs={{0,1},{1,2},{2,3},{3,4},{4,5},{5,6},{6,7},{7,8},{8,9},{9,10},{10,1... | collective-permute-start | bytes 786440 | tf_op jit(solution)/shard_map/while/body/eval_jaxpr/ppermute | solution.py:14
  72.2 9.6 %collective-permute-start.1 = (s32[128]{0:T(128)S(1)}, s32[128]{0:T(128)S(1)}, u32[]{:S(2)}, u32[]{:S(2)}) collective-permute-start(s32[128]{0:T(128)S(1)} %get-tuple-element.340), channel_id=1, source_target_pairs={{0,1},{1,2},{2,3},{3,4},{4,5},{5,6},{6,7},{7,8},{8,9},{9,10},{10,1... | collective-permute-start | bytes 1544 | tf_op jit(solution)/shard_map/while/body/eval_jaxpr/ppermute | solution.py:14
  79.8 5.5 %collective-permute-start = (bf16[2,128,512]{1,2,0:T(8,128)(2,1)}, bf16[2,128,512]{1,2,0:T(8,128)(2,1)S(1)}, u32[]{:S(2)}, u32[]{:S(2)}) collective-permute-start(bf16[2,128,512]{1,2,0:T(8,128)(2,1)} %get-tuple-element.339), channel_id=1, source_target_pairs={{0,1},{1,2},{2,3},{3,4},{4,5},{5,6},{6,7},{7,8},{8,9},{9,10},{10,1... | collective-permute-start | bytes 786440 | tf_op jit(solution)/shard_map/while/body/eval_jaxpr/ppermute | solution.py:14
  88.4 9.6 %collective-permute-start.1 = (s32[128]{0:T(128)S(1)}, s32[128]{0:T(128)S(1)}, u32[]{:S(2)}, u32[]{:S(2)}) collective-permute-start(s32[128]{0:T(128)S(1)} %get-tuple-element.340), channel_id=1, source_target_pairs={{0,1},{1,2},{2,3},{3,4},{4,5},{5,6},{6,7},{7,8},{8,9},{9,10},{10,1... | collective-permute-start | bytes 1544 | tf_op jit(solution)/shard_map/while/body/eval_jaxpr/ppermute | solution.py:14
  96.0 5.5 %collective-permute-start = (bf16[2,128,512]{1,2,0:T(8,128)(2,1)}, bf16[2,128,512]{1,2,0:T(8,128)(2,1)S(1)}, u32[]{:S(2)}, u32[]{:S(2)}) collective-permute-start(bf16[2,128,512]{1,2,0:T(8,128)(2,1)} %get-tuple-element.339), channel_id=1, source_target_pairs={{0,1},{1,2},{2,3},{3,4},{4,5},{5,6},{6,7},{7,8},{8,9},{9,10},{10,1... | collective-permute-start | bytes 786440 | tf_op jit(solution)/shard_map/while/body/eval_jaxpr/ppermute | solution.py:14
  104.7 9.6 %collective-permute-start.1 = (s32[128]{0:T(128)S(1)}, s32[128]{0:T(128)S(1)}, u32[]{:S(2)}, u32[]{:S(2)}) collective-permute-start(s32[128]{0:T(128)S(1)} %get-tuple-element.340), channel_id=1, source_target_pairs={{0,1},{1,2},{2,3},{3,4},{4,5},{5,6},{6,7},{7,8},{8,9},{9,10},{10,1... | collective-permute-start | bytes 1544 | tf_op jit(solution)/shard_map/while/body/eval_jaxpr/ppermute | solution.py:14
  112.3 5.5 %collective-permute-start = (bf16[2,128,512]{1,2,0:T(8,128)(2,1)}, bf16[2,128,512]{1,2,0:T(8,128)(2,1)S(1)}, u32[]{:S(2)}, u32[]{:S(2)}) collective-permute-start(bf16[2,128,512]{1,2,0:T(8,128)(2,1)} %get-tuple-element.339), channel_id=1, source_target_pairs={{0,1},{1,2},{2,3},{3,4},{4,5},{5,6},{6,7},{7,8},{8,9},{9,10},{10,1... | collective-permute-start | bytes 786440 | tf_op jit(solution)/shard_map/while/body/eval_jaxpr/ppermute | solution.py:14
  121.0 9.5 %collective-permute-start.1 = (s32[128]{0:T(128)S(1)}, s32[128]{0:T(128)S(1)}, u32[]{:S(2)}, u32[]{:S(2)}) collective-permute-start(s32[128]{0:T(128)S(1)} %get-tuple-element.340), channel_id=1, source_target_pairs={{0,1},{1,2},{2,3},{3,4},{4,5},{5,6},{6,7},{7,8},{8,9},{9,10},{10,1... | collective-permute-start | bytes 1544 | tf_op jit(solution)/shard_map/while/body/eval_jaxpr/ppermute | solution.py:14
  128.6 5.5 %collective-permute-start = (bf16[2,128,512]{1,2,0:T(8,128)(2,1)}, bf16[2,128,512]{1,2,0:T(8,128)(2,1)S(1)}, u32[]{:S(2)}, u32[]{:S(2)}) collective-permute-start(bf16[2,128,512]{1,2,0:T(8,128)(2,1)} %get-tuple-element.339), channel_id=1, source_target_pairs={{0,1},{1,2},{2,3},{3,4},{4,5},{5,6},{6,7},{7,8},{8,9},{9,10},{10,1... | collective-permute-start | bytes 786440 | tf_op jit(solution)/shard_map/while/body/eval_jaxpr/ppermute | solution.py:14
  137.2 9.6 %collective-permute-start.1 = (s32[128]{0:T(128)S(1)}, s32[128]{0:T(128)S(1)}, u32[]{:S(2)}, u32[]{:S(2)}) collective-permute-start(s32[128]{0:T(128)S(1)} %get-tuple-element.340), channel_id=1, source_target_pairs={{0,1},{1,2},{2,3},{3,4},{4,5},{5,6},{6,7},{7,8},{8,9},{9,10},{10,1... | collective-permute-start | bytes 1544 | tf_op jit(solution)/shard_map/while/body/eval_jaxpr/ppermute | solution.py:14
  144.8 5.5 %collective-permute-start = (bf16[2,128,512]{1,2,0:T(8,128)(2,1)}, bf16[2,128,512]{1,2,0:T(8,128)(2,1)S(1)}, u32[]{:S(2)}, u32[]{:S(2)}) collective-permute-start(bf16[2,128,512]{1,2,0:T(8,128)(2,1)} %get-tuple-element.339), channel_id=1, source_target_pairs={{0,1},{1,2},{2,3},{3,4},{4,5},{5,6},{6,7},{7,8},{8,9},{9,10},{10,1... | collective-permute-start | bytes 786440 | tf_op jit(solution)/shard_map/while/body/eval_jaxpr/ppermute | solution.py:14
  153.5 9.5 %collective-permute-start.1 = (s32[128]{0:T(128)S(1)}, s32[128]{0:T(128)S(1)}, u32[]{:S(2)}, u32[]{:S(2)}) collective-permute-start(s32[128]{0:T(128)S(1)} %get-tuple-element.340), channel_id=1, source_target_pairs={{0,1},{1,2},{2,3},{3,4},{4,5},{5,6},{6,7},{7,8},{8,9},{9,10},{10,1... | collective-permute-start | bytes 1544 | tf_op jit(solution)/shard_map/while/body/eval_jaxpr/ppermute | solution.py:14
  161.1 5.5 %collective-permute-start = (bf16[2,128,512]{1,2,0:T(8,128)(2,1)}, bf16[2,128,512]{1,2,0:T(8,128)(2,1)S(1)}, u32[]{:S(2)}, u32[]{:S(2)}) collective-permute-start(bf16[2,128,512]{1,2,0:T(8,128)(2,1)} %get-tuple-element.339), channel_id=1, source_target_pairs={{0,1},{1,2},{2,3},{3,4},{4,5},{5,6},{6,7},{7,8},{8,9},{9,10},{10,1... | collective-permute-start | bytes 786440 | tf_op jit(solution)/shard_map/while/body/eval_jaxpr/ppermute | solution.py:14
  169.8 9.6 %collective-permute-start.1 = (s32[128]{0:T(128)S(1)}, s32[128]{0:T(128)S(1)}, u32[]{:S(2)}, u32[]{:S(2)}) collective-permute-start(s32[128]{0:T(128)S(1)} %get-tuple-element.340), channel_id=1, source_target_pairs={{0,1},{1,2},{2,3},{3,4},{4,5},{5,6},{6,7},{7,8},{8,9},{9,10},{10,1... | collective-permute-start | bytes 1544 | tf_op jit(solution)/shard_map/while/body/eval_jaxpr/ppermute | solution.py:14
  177.4 5.5 %collective-permute-start = (bf16[2,128,512]{1,2,0:T(8,128)(2,1)}, bf16[2,128,512]{1,2,0:T(8,128)(2,1)S(1)}, u32[]{:S(2)}, u32[]{:S(2)}) collective-permute-start(bf16[2,128,512]{1,2,0:T(8,128)(2,1)} %get-tuple-element.339), channel_id=1, source_target_pairs={{0,1},{1,2},{2,3},{3,4},{4,5},{5,6},{6,7},{7,8},{8,9},{9,10},{10,1... | collective-permute-start | bytes 786440 | tf_op jit(solution)/shard_map/while/body/eval_jaxpr/ppermute | solution.py:14
  186.0 9.5 %collective-permute-start.1 = (s32[128]{0:T(128)S(1)}, s32[128]{0:T(128)S(1)}, u32[]{:S(2)}, u32[]{:S(2)}) collective-permute-start(s32[128]{0:T(128)S(1)} %get-tuple-element.340), channel_id=1, source_target_pairs={{0,1},{1,2},{2,3},{3,4},{4,5},{5,6},{6,7},{7,8},{8,9},{9,10},{10,1... | collective-permute-start | bytes 1544 | tf_op jit(solution)/shard_map/while/body/eval_jaxpr/ppermute | solution.py:14
  193.6 5.5 %collective-permute-start = (bf16[2,128,512]{1,2,0:T(8,128)(2,1)}, bf16[2,128,512]{1,2,0:T(8,128)(2,1)S(1)}, u32[]{:S(2)}, u32[]{:S(2)}) collective-permute-start(bf16[2,128,512]{1,2,0:T(8,128)(2,1)} %get-tuple-element.339), channel_id=1, source_target_pairs={{0,1},{1,2},{2,3},{3,4},{4,5},{5,6},{6,7},{7,8},{8,9},{9,10},{10,1... | collective-permute-start | bytes 786440 | tf_op jit(solution)/shard_map/while/body/eval_jaxpr/ppermute | solution.py:14
  202.3 9.6 %collective-permute-start.1 = (s32[128]{0:T(128)S(1)}, s32[128]{0:T(128)S(1)}, u32[]{:S(2)}, u32[]{:S(2)}) collective-permute-start(s32[128]{0:T(128)S(1)} %get-tuple-element.340), channel_id=1, source_target_pairs={{0,1},{1,2},{2,3},{3,4},{4,5},{5,6},{6,7},{7,8},{8,9},{9,10},{10,1... | collective-permute-start | bytes 1544 | tf_op jit(solution)/shard_map/while/body/eval_jaxpr/ppermute | solution.py:14
  209.9 5.5 %collective-permute-start = (bf16[2,128,512]{1,2,0:T(8,128)(2,1)}, bf16[2,128,512]{1,2,0:T(8,128)(2,1)S(1)}, u32[]{:S(2)}, u32[]{:S(2)}) collective-permute-start(bf16[2,128,512]{1,2,0:T(8,128)(2,1)} %get-tuple-element.339), channel_id=1, source_target_pairs={{0,1},{1,2},{2,3},{3,4},{4,5},{5,6},{6,7},{7,8},{8,9},{9,10},{10,1... | collective-permute-start | bytes 786440 | tf_op jit(solution)/shard_map/while/body/eval_jaxpr/ppermute | solution.py:14
  218.5 9.5 %collective-permute-start.1 = (s32[128]{0:T(128)S(1)}, s32[128]{0:T(128)S(1)}, u32[]{:S(2)}, u32[]{:S(2)}) collective-permute-start(s32[128]{0:T(128)S(1)} %get-tuple-element.340), channel_id=1, source_target_pairs={{0,1},{1,2},{2,3},{3,4},{4,5},{5,6},{6,7},{7,8},{8,9},{9,10},{10,1... | collective-permute-start | bytes 1544 | tf_op jit(solution)/shard_map/while/body/eval_jaxpr/ppermute | solution.py:14
  226.1 5.5 %collective-permute-start = (bf16[2,128,512]{1,2,0:T(8,128)(2,1)}, bf16[2,128,512]{1,2,0:T(8,128)(2,1)S(1)}, u32[]{:S(2)}, u32[]{:S(2)}) collective-permute-start(bf16[2,128,512]{1,2,0:T(8,128)(2,1)} %get-tuple-element.339), channel_id=1, source_target_pairs={{0,1},{1,2},{2,3},{3,4},{4,5},{5,6},{6,7},{7,8},{8,9},{9,10},{10,1... | collective-permute-start | bytes 786440 | tf_op jit(solution)/shard_map/while/body/eval_jaxpr/ppermute | solution.py:14
  234.8 9.6 %collective-permute-start.1 = (s32[128]{0:T(128)S(1)}, s32[128]{0:T(128)S(1)}, u32[]{:S(2)}, u32[]{:S(2)}) collective-permute-start(s32[128]{0:T(128)S(1)} %get-tuple-element.340), channel_id=1, source_target_pairs={{0,1},{1,2},{2,3},{3,4},{4,5},{5,6},{6,7},{7,8},{8,9},{9,10},{10,1... | collective-permute-start | bytes 1544 | tf_op jit(solution)/shard_map/while/body/eval_jaxpr/ppermute | solution.py:14
  242.4 5.5 %collective-permute-start = (bf16[2,128,512]{1,2,0:T(8,128)(2,1)}, bf16[2,128,512]{1,2,0:T(8,128)(2,1)S(1)}, u32[]{:S(2)}, u32[]{:S(2)}) collective-permute-start(bf16[2,128,512]{1,2,0:T(8,128)(2,1)} %get-tuple-element.339), channel_id=1, source_target_pairs={{0,1},{1,2},{2,3},{3,4},{4,5},{5,6},{6,7},{7,8},{8,9},{9,10},{10,1... | collective-permute-start | bytes 786440 | tf_op jit(solution)/shard_map/while/body/eval_jaxpr/ppermute | solution.py:14
  251.1 9.5 %collective-permute-start.1 = (s32[128]{0:T(128)S(1)}, s32[128]{0:T(128)S(1)}, u32[]{:S(2)}, u32[]{:S(2)}) collective-permute-start(s32[128]{0:T(128)S(1)} %get-tuple-element.340), channel_id=1, source_target_pairs={{0,1},{1,2},{2,3},{3,4},{4,5},{5,6},{6,7},{7,8},{8,9},{9,10},{10,1... | collective-permute-start | bytes 1544 | tf_op jit(solution)/shard_map/while/body/eval_jaxpr/ppermute | solution.py:14
  258.7 5.5 %collective-permute-start = (bf16[2,128,512]{1,2,0:T(8,128)(2,1)}, bf16[2,128,512]{1,2,0:T(8,128)(2,1)S(1)}, u32[]{:S(2)}, u32[]{:S(2)}) collective-permute-start(bf16[2,128,512]{1,2,0:T(8,128)(2,1)} %get-tuple-element.339), channel_id=1, source_target_pairs={{0,1},{1,2},{2,3},{3,4},{4,5},{5,6},{6,7},{7,8},{8,9},{9,10},{10,1... | collective-permute-start | bytes 786440 | tf_op jit(solution)/shard_map/while/body/eval_jaxpr/ppermute | solution.py:14
  269.2 32.5 %collective-permute-start.2 = (bf16[1,128,4096]{2,1,0:T(8,128)(2,1)S(1)}, bf16[1,128,4096]{2,1,0:T(8,128)(2,1)S(1)}, u32[]{:S(2)}, u32[]{:S(2)}) collective-permute-start(bf16[1,128,4096]{2,1,0:T(8,128)(2,1)S(1)} %convert_element_type.30), channel_id=1, source_target_pairs={{448,0},{0,64},{64,128},{128,192},{192,256},{256,320},{320,384},{3... | collective-permute-start | bytes 3145736 | tf_op jit(solution)/shard_map/ppermute | solution.py:20
where the time goes:
time: 304 us; the launch traced here: 303 us
  starting transfers between devices  153 us (50%)
  waiting for transfers between devices  83.8 us (28%)
  matrix products  31.4 us (10%)
  local copies, waits for them, and re-layouts  20.7 us (7%)
  other arithmetic  11.5 us (4%)
    ppermute x32, starting transfers between devices, shifted(): return lax.ppermute(block, axis, route)  149 us
    ppermute x32, waiting for transfers between devices, shifted(): return lax.ppermute(block, axis, route)  55.4 us
    ppermute x1, waiting for transfers between devices, shifted_2(): return lax.ppermute(block, axis, route)  28.5 us
    dot_general x17, matrix products, fold_shard(): jnp.einsum('kgts,skd->kgtd', weight.astype(jnp.bfloat16), val_part, prefe...  22.8 us
    while x48, local copies, waits for them, and re-layouts  11.4 us
    dot_general x17, matrix products, fold_shard(): jnp.einsum('tkgd,skd->kgts', queries4, key_part, preferred_element_type=j...  8.56 us
    reduce_sum x17, other arithmetic, fold_shard(): totals = totals * factor + jnp.sum(weight, axis=-1)  7.93 us
  transfers between devices with their start and end apart: 33, of which 17 were waited for; matrix products, arithmetic and copies ran while one was open for 1% of the time, Pallas kernels for 0%

commit v1 on v0

v1 whole, which is shorter than its diff:
```python
import jax
import jax.numpy as jnp
from jax import lax
from jax.experimental import pallas as pl
from jax.experimental.pallas import tpu as pltpu
from jax.sharding import PartitionSpec as P

HQ = 32
HK = 4
HEAD = 128
GROUP = HQ // HK
BLOCK = 128
ROWS = BLOCK + 16
CHIPS = 32
WINDOW = 9
SCALE = 1.4426950408889634 / HEAD**0.5
FAR = -131072.0
NT = (((1,), (1,)), ((), ()))


def attend(chip, core, qs_ref, qf_ref, blocks, os_ref, of_ref, kaug, vaug):
    lane = lax.broadcasted_iota(jnp.int32, (BLOCK, HEAD), 1)
    row = lax.broadcasted_iota(jnp.int32, (BLOCK, HEAD), 0)
    below = jnp.zeros((1, HEAD), jnp.int32)
    ids = []
    for ref, back in blocks:
        for half in range(2):
            one = ref[half, BLOCK : BLOCK + 16, :HEAD][0:1].astype(jnp.float32)
            ids.append(jnp.where(chip >= back, one, -1.0))
    ids = jnp.concatenate(ids, axis=0)
    lane1 = lax.broadcasted_iota(jnp.int32, (1, HEAD), 1)
    for doc in range(1, 8):
        count = jnp.sum((ids < doc).astype(jnp.float32), axis=(0, 1), keepdims=True)
        below = jnp.where(lane1 == doc, count.astype(jnp.int32), below)
    ahead = jnp.sum((ids < 0).astype(jnp.float32), axis=(0, 1), keepdims=True).astype(jnp.int32)
    whole = 2 * WINDOW * BLOCK
    first = jnp.where(lane1 == 0, ahead, jnp.where(lane1 == 8, 0, jnp.where(lane1 > 8, whole, below)))
    last = pltpu.roll(below, HEAD - 1, 1)
    last = jnp.where(lane1 == 7, whole, jnp.where(lane1 == 8, ahead, jnp.where(lane1 > 8, whole, last)))
    one = jnp.ones((BLOCK, HEAD), jnp.bfloat16)
    for slot, (ref, back) in enumerate(blocks):
        for half in range(2):
            at = (2 * slot + half) * BLOCK
            place = (WINDOW - 1 - back) * 2 * BLOCK + (core ^ half) * BLOCK + row
            inside = (place >= first) & (place < last)
            hot = jnp.where(inside, 1.0, 0.0).astype(jnp.bfloat16)
            for kv in range(2):
                kaug[kv, at : at + BLOCK, :HEAD] = ref[half, :BLOCK, kv * HEAD : (kv + 1) * HEAD]
                kaug[kv, at : at + BLOCK, HEAD:] = hot
                vaug[kv, at : at + BLOCK, :HEAD] = ref[half, :BLOCK, (2 + kv) * HEAD : (3 + kv) * HEAD]
                vaug[kv, at : at + BLOCK, HEAD:] = one
    for q_ref, o_ref, half in ((qf_ref, of_ref, 1), (qs_ref, os_ref, 0)):
        place = (WINDOW - 1) * 2 * BLOCK + (core ^ half) * BLOCK + row
        inside = (place >= first) & (place < last)
        away = jnp.where(inside | (lane > 8), 0.0, FAR).astype(jnp.bfloat16)
        away = jnp.concatenate([away, away], axis=0)
        tall = lax.broadcasted_iota(jnp.int32, (2 * BLOCK, 2 * BLOCK), 0)
        wide = lax.broadcasted_iota(jnp.int32, (2 * BLOCK, 2 * BLOCK), 1)
        qat = (core ^ half) * BLOCK + (tall & (BLOCK - 1))
        kat = (core ^ (wide >> 7)) * BLOCK + (wide & (BLOCK - 1))
        future = kat > qat
        for kv in range(2):
            for pair in range(GROUP // 2):
                at = (kv * GROUP + 2 * pair) * HEAD
                q2 = jnp.concatenate([q_ref[:, at : at + HEAD], q_ref[:, at + HEAD : at + 2 * HEAD]], axis=0)
                q2 = jnp.concatenate([q2, away], axis=1)
                score = lax.dot_general(q2, kaug[kv], NT, preferred_element_type=jnp.float32)
                own = jnp.where(future, FAR, score[:, : 2 * BLOCK])
                score = jnp.concatenate([own, score[:, 2 * BLOCK :]], axis=1)
                top = jnp.max(score, axis=1, keepdims=True)
                weight = jnp.exp2((score - top) * SCALE).astype(jnp.bfloat16)
                both = jnp.dot(weight, vaug[kv], preferred_element_type=jnp.float32)
                result = (both[:, :HEAD] / both[:, HEAD:]).astype(jnp.bfloat16)
                o_ref[:, at : at + HEAD] = result[:BLOCK]
                o_ref[:, at + HEAD : at + 2 * HEAD] = result[BLOCK:]


def kernel(where_ref, qs, qf, b0, b4, b8, x1, x2, x3, os_ref, of_ref, kaug, vaug):
    chip, core = where_ref[0], where_ref[1]
    blocks = [(b0, 0), (b4, 4), (b8, 8)]
    for step, ref in ((1, x1), (2, x2), (3, x3)):
        blocks.append((ref.at[0], jnp.where(core == 0, step, 8 - step)))
        blocks.append((ref.at[1], jnp.where(core == 0, 4 + step, 4 - step)))
    attend(chip, core, qs, qf, blocks, os_ref, of_ref, kaug, vaug)


def attention(place, qs, qf, b0, b4, b8, x1, x2, x3):
    vmem = pl.BlockSpec(memory_space=pltpu.VMEM)
    keys = 2 * WINDOW * BLOCK
    rows = 2 * BLOCK * HQ // 2
    return pl.pallas_call(
        kernel,
        out_shape=[jax.ShapeDtypeStruct(qs.shape, jnp.bfloat16)] * 2,
        in_specs=[pl.BlockSpec(memory_space=pltpu.SMEM)] + [vmem] * 8,
        out_specs=[vmem] * 2,
        scratch_shapes=[pltpu.VMEM((2, keys, 2 * HEAD), jnp.bfloat16)] * 2,
        compiler_params=pltpu.CompilerParams(vmem_limit_bytes=48 * 1024 * 1024),
        cost_estimate=pl.CostEstimate(
            flops=8 * rows * keys * HEAD, bytes_accessed=6 << 20, transcendentals=rows * keys
        ),
    )(place, qs, qf, b0, b4, b8, x1, x2, x3)


def at(y, x, core):
    return ((y % 8) * 4 + x) * 2 + core


def shards(queries, keys, values, doc_ids):
    index = lax.axis_index("sp")
    chip, core = index // 2, index % 2
    first = core == 0

    def section(block, flip):
        pairs = [(p * 64 + s, (p + 1) % 8 * 64 + (s ^ flip)) for p in range(8) for s in range(64)]
        return lax.ppermute(block, ("pp", "sp"), pairs)

    def along_y(block):
        return lax.ppermute(block, "sp", [(s, (s + 8) % 64) for s in range(64)])

    def along_x(block):
        return lax.ppermute(block, "sp", [(s, (s + (2 if s % 2 == 0 else -2)) % 64) for s in range(64)])

    def swap(block):
        return lax.ppermute(block, "sp", [(s, s ^ 1) for s in range(64)])

    ids = jnp.pad(doc_ids[0].astype(jnp.bfloat16)[None], ((0, 15), (0, 384)))

    def part(j):
        cols = slice(j * 256, (j + 1) * 256)
        return jnp.concatenate([jnp.concatenate([keys[0][:, cols], values[0][:, cols]], axis=1), ids], axis=0)

    half0, half1 = part(0), part(1)
    same = section(jnp.where(first, half0, half1), 0)
    flip = section(jnp.where(first, half1, half0), 1)
    b0 = jnp.stack([same, flip])
    q = queries[0]
    qs = section(jnp.where(first, q[:, :2048], q[:, 2048:]), 0)
    qf = section(jnp.where(first, q[:, 2048:], q[:, :2048]), 1)
    b4 = along_y(b0)
    b8 = along_y(b4)
    x1 = along_x(jnp.stack([jnp.where(first, b0, b8), b4]))
    x2 = along_x(x1)
    x3 = along_x(x2)
    place = jnp.stack([chip, core]).astype(jnp.int32)
    os_, of_ = attention(place, qs, qf, b0, b4, b8, x1, x2, x3)
    got = swap(of_)
    out = jnp.where(first, jnp.concatenate([os_, got], axis=1), jnp.concatenate([got, os_], axis=1))
    return out[None]


def solution(mesh):
    return jax.shard_map(
        shards,
        mesh=mesh,
        in_specs=(P("pp", "sp", None), P("pp", "sp", None), P("pp", "sp", None), P("pp", "sp")),
        out_specs=P("pp", "sp", None),
        check_vma=False,
    )
```

time: 304 us -> 126 us (0.41)
  the two profiles are of different devices: /device:TPU:31 before, /device:TPU:1 now
where the time goes in v1:
time: 126 us; the launch traced here: 124 us
  waiting for transfers between devices  67.6 us (54%)
  starting transfers between devices  39.3 us (31%)
  Pallas kernels  13.1 us (10%)
  other arithmetic  3.16 us (3%)
    ppermute x4, waiting for transfers between devices, section(): return lax.ppermute(block, ('pp', 'sp'), pairs)  33 us
    ppermute x2, waiting for transfers between devices, along_y(): return lax.ppermute(block, 'sp', [(s, (s + 8) % 64) for s in range(64)])  18.7 us
    ppermute x3, starting transfers between devices, along_x(): lax.ppermute(block, 'sp', [(s, (s + (2 if s % 2 == 0 else -2)) % 64) for...  17.6 us
    ppermute x4, starting transfers between devices, section(): return lax.ppermute(block, ('pp', 'sp'), pairs)  14.5 us
    ppermute x3, waiting for transfers between devices, along_x(): lax.ppermute(block, 'sp', [(s, (s + (2 if s % 2 == 0 else -2)) % 64) for...  14 us
    pallas_call x1, Pallas kernels, attention(): pl.pallas_call(kernel, out_shape=[jax.ShapeDtypeStruct(qs.shape, jnp.bflo...  13.1 us
    ppermute x2, starting transfers between devices, along_y(): return lax.ppermute(block, 'sp', [(s, (s + 8) % 64) for s in range(64)])  5.25 us
  transfers between devices with their start and end apart: 10, of which 9 were waited for; matrix products, arithmetic and copies ran while one was open for 1% of the time, Pallas kernels for 0%

profile of v1, /device:TPU:1, one launch (start us, length us, event | category | flops | bytes accessed | tf_op | source)
XLA Modules:
  0.0 124.3 jit_solution(9624759400778377424)
XLA Ops:
  0.0 0.7 convert_element_type.6
  0.7 1.0 fusion.3
  1.7 4.8 %collective-permute-start.2 = (bf16[144,512]{1,0:T(8,128)(2,1)S(1)}, bf16[144,512]{1,0:T(8,128)(2,1)S(1)}, u32[]{:S(2)}, u32[]{:S(2)}) collective-permute-start(bf16[144,512]{1,0:T(8,128)(2,1)S(1)} %get-tuple-element.11), channel_id=1, source_target_pairs={{0,64},{1,65},{2,66},{3,67},{4,68},{5,69},{6,70},{7,71},{8,72},{9,... | collective-permute-start | bytes 442376 | tf_op jit(solution)/shard_map/ppermute | solution.py:115
  6.5 4.8 %collective-permute-start.3 = (bf16[144,512]{1,0:T(8,128)(2,1)S(1)}, bf16[144,512]{1,0:T(8,128)(2,1)S(1)}, u32[]{:S(2)}, u32[]{:S(2)}) collective-permute-start(bf16[144,512]{1,0:T(8,128)(2,1)S(1)} %get-tuple-element.12), channel_id=1, source_target_pairs={{0,65},{1,64},{2,67},{3,66},{4,69},{5,68},{6,71},{7,70},{8,73},{9,... | collective-permute-start | bytes 442376 | tf_op jit(solution)/shard_map/ppermute | solution.py:115
  11.4 5.4 %collective-permute-done.2 = bf16[144,512]{1,0:T(8,128)(2,1)S(1)} collective-permute-done((bf16[144,512]{1,0:T(8,128)(2,1)S(1)}, bf16[144,512]{1,0:T(8,128)(2,1)S(1)}, u32[]{:S(2)}, u32[]{:S(2)}) %collective-permute-start.2) | collective-permute-done | bytes 147488 | tf_op jit(solution)/shard_map/ppermute | solution.py:115
  16.7 3.7 %collective-permute-done.3 = bf16[144,512]{1,0:T(8,128)(2,1)S(1)} collective-permute-done((bf16[144,512]{1,0:T(8,128)(2,1)S(1)}, bf16[144,512]{1,0:T(8,128)(2,1)S(1)}, u32[]{:S(2)}, u32[]{:S(2)}) %collective-permute-start.3) | collective-permute-done | bytes 147488 | tf_op jit(solution)/shard_map/ppermute | solution.py:115
  20.5 0.0 copy-start
  20.5 3.3 %collective-permute-start.4 = (bf16[2,144,512]{2,1,0:T(8,128)(2,1)S(1)}, bf16[2,144,512]{2,1,0:T(8,128)(2,1)S(1)}, u32[]{:S(2)}, u32[]{:S(2)}) collective-permute-start(bf16[2,144,512]{2,1,0:T(8,128)(2,1)S(1)} %pad_maximum_fusion.1.b0), channel_id=1, source_target_pairs={{0,8},{1,9},{2,10},{3,11},{4,12},{5,13},{6,14},{7,15},{8,16},{9,17... | collective-permute-start | bytes 884744 | tf_op jit(solution)/shard_map/ppermute | solution.py:118
  23.8 9.4 %collective-permute-done.4.b4 = bf16[2,144,512]{2,1,0:T(8,128)(2,1)S(1)} collective-permute-done((bf16[2,144,512]{2,1,0:T(8,128)(2,1)S(1)}, bf16[2,144,512]{2,1,0:T(8,128)(2,1)S(1)}, u32[]{:S(2)}, u32[]{:S(2)}) %collective-permute-start.4) | collective-permute-done | bytes 294944 | tf_op jit(solution)/shard_map/ppermute | solution.py:118
  33.2 1.9 %collective-permute-start.5 = (bf16[2,144,512]{2,1,0:T(8,128)(2,1)S(1)}, bf16[2,144,512]{2,1,0:T(8,128)(2,1)S(1)}, u32[]{:S(2)}, u32[]{:S(2)}) collective-permute-start(bf16[2,144,512]{2,1,0:T(8,128)(2,1)S(1)} %collective-permute-done.4.b4), channel_id=1, source_target_pairs={{0,8},{1,9},{2,10},{3,11},{4,12},{5,13},{6,14},{7,15},{8,16},{9,17... | collective-permute-start | bytes 884744 | tf_op jit(solution)/shard_map/ppermute | solution.py:118
  35.1 9.3 %collective-permute-done.5.b8 = bf16[2,144,512]{2,1,0:T(8,128)(2,1)S(1)} collective-permute-done((bf16[2,144,512]{2,1,0:T(8,128)(2,1)S(1)}, bf16[2,144,512]{2,1,0:T(8,128)(2,1)S(1)}, u32[]{:S(2)}, u32[]{:S(2)}) %collective-permute-start.5) | collective-permute-done | bytes 294944 | tf_op jit(solution)/shard_map/ppermute | solution.py:118
  44.5 0.1 pad_maximum_fusion
  44.6 3.7 %collective-permute-start.6 = (bf16[2,2,144,512]{3,2,1,0:T(8,128)(2,1)S(1)}, bf16[2,2,144,512]{3,2,1,0:T(8,128)(2,1)S(1)}, u32[]{:S(2)}, u32[]{:S(2)}) collective-permute-start(bf16[2,2,144,512]{3,2,1,0:T(8,128)(2,1)S(1)} %pad_maximum_fusion), channel_id=1, source_target_pairs={{0,2},{1,63},{2,4},{3,1},{4,6},{5,3},{6,8},{7,5},{8,10},{9,7},{10,... | collective-permute-start | bytes 1769480 | tf_op jit(solution)/shard_map/ppermute | solution.py:121
  48.3 7.2 %collective-permute-done.6.x1 = bf16[2,2,144,512]{3,2,1,0:T(8,128)(2,1)S(1)} collective-permute-done((bf16[2,2,144,512]{3,2,1,0:T(8,128)(2,1)S(1)}, bf16[2,2,144,512]{3,2,1,0:T(8,128)(2,1)S(1)}, u32[]{:S(2)}, u32[]{:S(2)}) %collective-permute-start.6) | collective-permute-done | bytes 589856 | tf_op jit(solution)/shard_map/ppermute | solution.py:121
  55.5 6.8 %collective-permute-start.7 = (bf16[2,2,144,512]{3,2,1,0:T(8,128)(2,1)S(1)}, bf16[2,2,144,512]{3,2,1,0:T(8,128)(2,1)S(1)}, u32[]{:S(2)}, u32[]{:S(2)}) collective-permute-start(bf16[2,2,144,512]{3,2,1,0:T(8,128)(2,1)S(1)} %collective-permute-done.6.x1), channel_id=1, source_target_pairs={{0,2},{1,63},{2,4},{3,1},{4,6},{5,3},{6,8},{7,5},{8,10},{9,7},{10,... | collective-permute-start | bytes 1769480 | tf_op jit(solution)/shard_map/ppermute | solution.py:121
  62.3 6.8 %collective-permute-done.7.x2 = bf16[2,2,144,512]{3,2,1,0:T(8,128)(2,1)S(1)} collective-permute-done((bf16[2,2,144,512]{3,2,1,0:T(8,128)(2,1)S(1)}, bf16[2,2,144,512]{3,2,1,0:T(8,128)(2,1)S(1)}, u32[]{:S(2)}, u32[]{:S(2)}) %collective-permute-start.7) | collective-permute-done | bytes 589856 | tf_op jit(solution)/shard_map/ppermute | solution.py:121
  69.1 7.1 %collective-permute-start.8 = (bf16[2,2,144,512]{3,2,1,0:T(8,128)(2,1)S(1)}, bf16[2,2,144,512]{3,2,1,0:T(8,128)(2,1)S(1)}, u32[]{:S(2)}, u32[]{:S(2)}) collective-permute-start(bf16[2,2,144,512]{3,2,1,0:T(8,128)(2,1)S(1)} %collective-permute-done.7.x2), channel_id=1, source_target_pairs={{0,2},{1,63},{2,4},{3,1},{4,6},{5,3},{6,8},{7,5},{8,10},{9,7},{10,... | collective-permute-start | bytes 1769480 | tf_op jit(solution)/shard_map/ppermute | solution.py:121
  76.2 0.0 copy-done
  76.2 1.0 broadcast_select_fusion
  77.3 1.9 %collective-permute-start.1 = (bf16[128,2048]{1,0:T(8,128)(2,1)}, bf16[128,2048]{1,0:T(8,128)(2,1)S(1)}, u32[]{:S(2)}, u32[]{:S(2)}) collective-permute-start(bf16[128,2048]{1,0:T(8,128)(2,1)} %get-tuple-element.9), channel_id=1, source_target_pairs={{0,65},{1,64},{2,67},{3,66},{4,69},{5,68},{6,71},{7,70},{8,73},{9,... | collective-permute-start | bytes 1572872 | tf_op jit(solution)/shard_map/ppermute | solution.py:115
  79.2 3.0 %collective-permute-start = (bf16[128,2048]{1,0:T(8,128)(2,1)}, bf16[128,2048]{1,0:T(8,128)(2,1)}, u32[]{:S(2)}, u32[]{:S(2)}) collective-permute-start(bf16[128,2048]{1,0:T(8,128)(2,1)} %get-tuple-element.10), channel_id=1, source_target_pairs={{0,64},{1,65},{2,66},{3,67},{4,68},{5,69},{6,70},{7,71},{8,72},{9,... | collective-permute-start | bytes 1572872 | tf_op jit(solution)/shard_map/ppermute | solution.py:115
  82.2 0.1 pad_add_fusion.where_ref
  82.2 11.8 %collective-permute-done.1.qf = bf16[128,2048]{1,0:T(8,128)(2,1)S(1)} collective-permute-done((bf16[128,2048]{1,0:T(8,128)(2,1)}, bf16[128,2048]{1,0:T(8,128)(2,1)S(1)}, u32[]{:S(2)}, u32[]{:S(2)}) %collective-permute-start.1) | collective-permute-done | bytes 524320 | tf_op jit(solution)/shard_map/ppermute | solution.py:115
  94.0 12.1 %collective-permute-done.qs = bf16[128,2048]{1,0:T(8,128)(2,1)} collective-permute-done((bf16[128,2048]{1,0:T(8,128)(2,1)}, bf16[128,2048]{1,0:T(8,128)(2,1)}, u32[]{:S(2)}, u32[]{:S(2)}) %collective-permute-start) | collective-permute-done | bytes 524320 | tf_op jit(solution)/shard_map/ppermute | solution.py:115
  106.1 0.0 collective-permute-done.8.x3
  106.1 13.1 %shard_map.46 = (bf16[128,2048]{1,0:T(8,128)(2,1)S(1)}, bf16[128,2048]{1,0:T(8,128)(2,1)S(1)}) custom-call(s32[2]{0:T(128)S(1)} %pad_add_fusion.where_ref, bf16[128,2048]{1,0:T(8,128)(2,1)} %collective-permute-done.qs, bf16[128,2048]{1,0:T(8,128)(2,1)S(1)} %collective-permute-done.1.qf, bf16[2,144,512]{2,1,0:T(8,128)(2,1)S(1)} %pad_maximum_fusion.1.b0, ...), custom_call_target="tpu_custom_call" | custom-call | flops 9663676416 | bytes 6291456 | tf_op jit(solution)/shard_map/pallas_call | solution.py:91
  119.2 1.9 %collective-permute-start.9 = (bf16[128,2048]{1,0:T(8,128)(2,1)S(1)}, bf16[128,2048]{1,0:T(8,128)(2,1)S(1)}, u32[]{:S(2)}, u32[]{:S(2)}) collective-permute-start(bf16[128,2048]{1,0:T(8,128)(2,1)S(1)} %get-tuple-element.8), channel_id=1, source_target_pairs={{0,1},{1,0},{2,3},{3,2},{4,5},{5,4},{6,7},{7,6},{8,9},{9,8},{10,11... | collective-permute-start | bytes 1572872 | tf_op jit(solution)/shard_map/ppermute | solution.py:124
  121.2 1.9 %collective-permute-done.9 = bf16[128,2048]{1,0:T(8,128)(2,1)S(1)} collective-permute-done((bf16[128,2048]{1,0:T(8,128)(2,1)S(1)}, bf16[128,2048]{1,0:T(8,128)(2,1)S(1)}, u32[]{:S(2)}, u32[]{:S(2)}) %collective-permute-start.9) | collective-permute-done | bytes 524320 | tf_op jit(solution)/shard_map/ppermute | solution.py:124
  123.1 1.2 maximum_select_fusion
  (3 shorter events, 0.1 us)
Async XLA Ops:
  1.7 15.1 %collective-permute-start.2 = (bf16[144,512]{1,0:T(8,128)(2,1)S(1)}, bf16[144,512]{1,0:T(8,128)(2,1)S(1)}, u32[]{:S(2)}, u32[]{:S(2)}) collective-permute-start(bf16[144,512]{1,0:T(8,128)(2,1)S(1)} %get-tuple-element.11), channel_id=1, source_target_pairs={{0,64},{1,65},{2,66},{3,67},{4,68},{5,69},{6,70},{7,71},{8,72},{9,... | collective-permute-start | bytes 442376 | tf_op jit(solution)/shard_map/ppermute | solution.py:115
  6.5 13.9 %collective-permute-start.3 = (bf16[144,512]{1,0:T(8,128)(2,1)S(1)}, bf16[144,512]{1,0:T(8,128)(2,1)S(1)}, u32[]{:S(2)}, u32[]{:S(2)}) collective-permute-start(bf16[144,512]{1,0:T(8,128)(2,1)S(1)} %get-tuple-element.12), channel_id=1, source_target_pairs={{0,65},{1,64},{2,67},{3,66},{4,69},{5,68},{6,71},{7,70},{8,73},{9,... | collective-permute-start | bytes 442376 | tf_op jit(solution)/shard_map/ppermute | solution.py:115
  20.5 55.7 %copy-start = (bf16[1,128,4096]{2,1,0:T(8,128)(2,1)S(1)}, bf16[1,128,4096]{2,1,0:T(8,128)(2,1)}, u32[]{:S(2)}) copy-start(bf16[1,128,4096]{2,1,0:T(8,128)(2,1)} %param.4) | copy-start | bytes 3145732
  20.5 12.8 %collective-permute-start.4 = (bf16[2,144,512]{2,1,0:T(8,128)(2,1)S(1)}, bf16[2,144,512]{2,1,0:T(8,128)(2,1)S(1)}, u32[]{:S(2)}, u32[]{:S(2)}) collective-permute-start(bf16[2,144,512]{2,1,0:T(8,128)(2,1)S(1)} %pad_maximum_fusion.1.b0), channel_id=1, source_target_pairs={{0,8},{1,9},{2,10},{3,11},{4,12},{5,13},{6,14},{7,15},{8,16},{9,17... | collective-permute-start | bytes 884744 | tf_op jit(solution)/shard_map/ppermute | solution.py:118
  33.2 11.2 %collective-permute-start.5 = (bf16[2,144,512]{2,1,0:T(8,128)(2,1)S(1)}, bf16[2,144,512]{2,1,0:T(8,128)(2,1)S(1)}, u32[]{:S(2)}, u32[]{:S(2)}) collective-permute-start(bf16[2,144,512]{2,1,0:T(8,128)(2,1)S(1)} %collective-permute-done.4.b4), channel_id=1, source_target_pairs={{0,8},{1,9},{2,10},{3,11},{4,12},{5,13},{6,14},{7,15},{8,16},{9,17... | collective-permute-start | bytes 884744 | tf_op jit(solution)/shard_map/ppermute | solution.py:118
  44.6 10.9 %collective-permute-start.6 = (bf16[2,2,144,512]{3,2,1,0:T(8,128)(2,1)S(1)}, bf16[2,2,144,512]{3,2,1,0:T(8,128)(2,1)S(1)}, u32[]{:S(2)}, u32[]{:S(2)}) collective-permute-start(bf16[2,2,144,512]{3,2,1,0:T(8,128)(2,1)S(1)} %pad_maximum_fusion), channel_id=1, source_target_pairs={{0,2},{1,63},{2,4},{3,1},{4,6},{5,3},{6,8},{7,5},{8,10},{9,7},{10,... | collective-permute-start | bytes 1769480 | tf_op jit(solution)/shard_map/ppermute | solution.py:121
  55.5 13.6 %collective-permute-start.7 = (bf16[2,2,144,512]{3,2,1,0:T(8,128)(2,1)S(1)}, bf16[2,2,144,512]{3,2,1,0:T(8,128)(2,1)S(1)}, u32[]{:S(2)}, u32[]{:S(2)}) collective-permute-start(bf16[2,2,144,512]{3,2,1,0:T(8,128)(2,1)S(1)} %collective-permute-done.6.x1), channel_id=1, source_target_pairs={{0,2},{1,63},{2,4},{3,1},{4,6},{5,3},{6,8},{7,5},{8,10},{9,7},{10,... | collective-permute-start | bytes 1769480 | tf_op jit(solution)/shard_map/ppermute | solution.py:121
  69.1 37.0 %collective-permute-start.8 = (bf16[2,2,144,512]{3,2,1,0:T(8,128)(2,1)S(1)}, bf16[2,2,144,512]{3,2,1,0:T(8,128)(2,1)S(1)}, u32[]{:S(2)}, u32[]{:S(2)}) collective-permute-start(bf16[2,2,144,512]{3,2,1,0:T(8,128)(2,1)S(1)} %collective-permute-done.7.x2), channel_id=1, source_target_pairs={{0,2},{1,63},{2,4},{3,1},{4,6},{5,3},{6,8},{7,5},{8,10},{9,7},{10,... | collective-permute-start | bytes 1769480 | tf_op jit(solution)/shard_map/ppermute | solution.py:121
  77.3 16.8 %collective-permute-start.1 = (bf16[128,2048]{1,0:T(8,128)(2,1)}, bf16[128,2048]{1,0:T(8,128)(2,1)S(1)}, u32[]{:S(2)}, u32[]{:S(2)}) collective-permute-start(bf16[128,2048]{1,0:T(8,128)(2,1)} %get-tuple-element.9), channel_id=1, source_target_pairs={{0,65},{1,64},{2,67},{3,66},{4,69},{5,68},{6,71},{7,70},{8,73},{9,... | collective-permute-start | bytes 1572872 | tf_op jit(solution)/shard_map/ppermute | solution.py:115
  79.2 27.0 %collective-permute-start = (bf16[128,2048]{1,0:T(8,128)(2,1)}, bf16[128,2048]{1,0:T(8,128)(2,1)}, u32[]{:S(2)}, u32[]{:S(2)}) collective-permute-start(bf16[128,2048]{1,0:T(8,128)(2,1)} %get-tuple-element.10), channel_id=1, source_target_pairs={{0,64},{1,65},{2,66},{3,67},{4,68},{5,69},{6,70},{7,71},{8,72},{9,... | collective-permute-start | bytes 1572872 | tf_op jit(solution)/shard_map/ppermute | solution.py:115
  119.2 3.8 %collective-permute-start.9 = (bf16[128,2048]{1,0:T(8,128)(2,1)S(1)}, bf16[128,2048]{1,0:T(8,128)(2,1)S(1)}, u32[]{:S(2)}, u32[]{:S(2)}) collective-permute-start(bf16[128,2048]{1,0:T(8,128)(2,1)S(1)} %get-tuple-element.8), channel_id=1, source_target_pairs={{0,1},{1,0},{2,3},{3,2},{4,5},{5,4},{6,7},{7,6},{8,9},{9,8},{10,11... | collective-permute-start | bytes 1572872 | tf_op jit(solution)/shard_map/ppermute | solution.py:124

commit v2 on v1

v2 whole, which is shorter than its diff:
```python
import functools

import jax
import jax.numpy as jnp
from jax import lax
from jax.experimental import pallas as pl
from jax.experimental.pallas import tpu as pltpu
from jax.sharding import PartitionSpec as P

HQ = 32
HK = 4
HEAD = 128
GROUP = HQ // HK
BLOCK = 128
ROWS = BLOCK + 16
SCALE = 1.4426950408889634 / HEAD**0.5
FAR = -131072.0
NT = (((1,), (1,)), ((), ()))


def marks(refs):
    ids = [ref[half, BLOCK : BLOCK + 16, :HEAD][0:1].astype(jnp.float32) for ref in refs for half in range(2)]
    ids = jnp.concatenate(ids, axis=0)
    lane = lax.broadcasted_iota(jnp.int32, ids.shape, 1)
    first = jnp.zeros(ids.shape, jnp.int32)
    last = jnp.zeros(ids.shape, jnp.int32)
    for doc in range(8):
        count = jnp.sum((ids <= doc).astype(jnp.float32), axis=1, keepdims=True).astype(jnp.int32)
        last = jnp.where(lane == doc, count, last)
        first = jnp.where(lane == doc + 1, count, first)
    first = jnp.where(lane > 7, BLOCK, first)
    return first, last


def piece(half, own, carried, last, n_blocks, core_ref, q_ref, *refs):
    b0 = refs[0]
    blocks = []
    for ref in refs[1 - own : n_blocks]:
        blocks.extend([ref] if len(ref.shape) == 3 else [ref.at[0], ref.at[1]])
    refs = refs[n_blocks:]
    old, refs = (refs[:3], refs[3:]) if carried else (None, refs)
    new, (kaug, vaug) = refs[:-2], refs[-2:]
    core = core_ref[0]
    row = lax.broadcasted_iota(jnp.int32, (BLOCK, HEAD), 0)
    lane = lax.broadcasted_iota(jnp.int32, (BLOCK, HEAD), 1)
    first, end = marks([b0] + blocks)
    one = jnp.ones((BLOCK, HEAD), jnp.bfloat16)
    for slot, ref in enumerate(blocks):
        for part in range(2):
            at = (2 * slot + part) * BLOCK
            mark = 2 * slot + part + 2
            inside = (row >= first[mark : mark + 1]) & (row < end[mark : mark + 1])
            hot = jnp.where(inside, 1.0, 0.0).astype(jnp.bfloat16)
            for kv in range(2):
                kaug[kv, at : at + BLOCK, :HEAD] = ref[part, :BLOCK, kv * HEAD : (kv + 1) * HEAD]
                kaug[kv, at : at + BLOCK, HEAD:] = hot
                vaug[kv, at : at + BLOCK, :HEAD] = ref[part, :BLOCK, (2 + kv) * HEAD : (3 + kv) * HEAD]
                vaug[kv, at : at + BLOCK, HEAD:] = one
    inside = (row >= first[half : half + 1]) & (row < end[half : half + 1])
    away = jnp.where(inside | (lane > 7), 0.0, FAR).astype(jnp.bfloat16)
    away = jnp.concatenate([away, away], axis=0)
    if own:
        tall = lax.broadcasted_iota(jnp.int32, (2 * BLOCK, 2 * BLOCK), 0)
        wide = lax.broadcasted_iota(jnp.int32, (2 * BLOCK, 2 * BLOCK), 1)
        qat = (core ^ half) * BLOCK + (tall & (BLOCK - 1))
        kat = (core ^ (wide >> 7)) * BLOCK + (wide & (BLOCK - 1))
        future = kat > qat
    for kv in range(2):
        for pair in range(GROUP // 2):
            head = kv * GROUP + 2 * pair
            at = head * HEAD
            rows = slice(head * BLOCK, (head + 2) * BLOCK)
            q2 = jnp.concatenate([q_ref[:, at : at + HEAD], q_ref[:, at + HEAD : at + 2 * HEAD]], axis=0)
            q2 = jnp.concatenate([q2, away], axis=1)
            score = lax.dot_general(q2, kaug[kv], NT, preferred_element_type=jnp.float32)
            if own:
                mine = jnp.where(future, FAR, score[:, : 2 * BLOCK])
                score = mine if len(blocks) == 1 else jnp.concatenate([mine, score[:, 2 * BLOCK :]], axis=1)
            top = jnp.max(score, axis=1, keepdims=True)
            if carried:
                before = old[0][rows, :]
                top = jnp.maximum(top, before[:, :1])
            weight = jnp.exp2((score - top) * SCALE).astype(jnp.bfloat16)
            both = jnp.dot(weight, vaug[kv], preferred_element_type=jnp.float32)
            total, accum = both[:, HEAD:], both[:, :HEAD]
            if carried:
                factor = jnp.exp2((before - top) * SCALE)
                total = total + old[1][rows, :] * factor
                accum = accum + old[2][rows, :] * factor
            if last:
                result = (accum / total).astype(jnp.bfloat16)
                new[0][:, at : at + HEAD] = result[:BLOCK]
                new[0][:, at + HEAD : at + 2 * HEAD] = result[BLOCK:]
            else:
                new[0][rows, :] = jnp.broadcast_to(top, (2 * BLOCK, HEAD))
                new[1][rows, :] = total
                new[2][rows, :] = accum


def attend(core, half, q, b0, blocks, own=False, state=(), last=False):
    vmem = pl.BlockSpec(memory_space=pltpu.VMEM)
    count = own + sum(1 if block.ndim == 3 else 2 for block in blocks)
    keys = 2 * BLOCK * count
    rows = BLOCK * HQ // 2
    if last:
        out_shape = jax.ShapeDtypeStruct(q.shape, jnp.bfloat16)
    else:
        out_shape = [jax.ShapeDtypeStruct((rows, HEAD), jnp.float32)] * 3
    return pl.pallas_call(
        functools.partial(piece, half, own, bool(state), last, 1 + len(blocks)),
        out_shape=out_shape,
        in_specs=[pl.BlockSpec(memory_space=pltpu.SMEM)] + [vmem] * (2 + len(blocks) + len(state)),
        out_specs=vmem if last else [vmem] * 3,
        scratch_shapes=[pltpu.VMEM((2, keys, 2 * HEAD), jnp.bfloat16)] * 2,
        compiler_params=pltpu.CompilerParams(vmem_limit_bytes=32 * 1024 * 1024),
        cost_estimate=pl.CostEstimate(
            flops=8 * rows * keys * HEAD, bytes_accessed=4 << 20, transcendentals=rows * keys
        ),
    )(core, q, b0, *blocks, *state)


def shards(queries, keys, values, doc_ids):
    core = lax.axis_index("sp") % 2
    first = core == 0

    def section(block, flip, dy=0):
        pairs = [(p * 64 + s, (p + 1) % 8 * 64 + ((s + 8 * dy) % 64 ^ flip)) for p in range(8) for s in range(64)]
        return lax.ppermute(block, ("pp", "sp"), pairs)

    def along_y(block):
        return lax.ppermute(block, "sp", [(s, (s + 8) % 64) for s in range(64)])

    def along_x(block, step0, step1):
        return lax.ppermute(block, "sp", [(s, (s + 2 * (step1 if s % 2 else step0)) % 64) for s in range(64)])

    def swap(block):
        return lax.ppermute(block, "sp", [(s, s ^ 1) for s in range(64)])

    ids = jnp.pad(doc_ids[0].astype(jnp.bfloat16)[None], ((0, 15), (0, 384)))

    def part(j):
        cols = slice(j * 256, (j + 1) * 256)
        return jnp.concatenate([jnp.concatenate([keys[0][:, cols], values[0][:, cols]], axis=1), ids], axis=0)

    half0, half1 = part(0), part(1)
    mine, other = jnp.where(first, half0, half1), jnp.where(first, half1, half0)
    q = queries[0]
    b0 = jnp.stack([section(mine, 0), section(other, 1)])
    b4 = jnp.stack([section(mine, 0, 1), section(other, 1, 1)])
    b0, b4, q = lax.optimization_barrier((b0, b4, q))
    qf = section(jnp.where(first, q[:, 2048:], q[:, :2048]), 1)
    b8 = along_y(b4)
    p1 = along_x(jnp.where(first, b0, b4), 1, -1)
    p2 = along_x(jnp.where(first, b4, b0), -1, 1)
    qf, b8, p1, p2, q, b0, b4 = lax.optimization_barrier((qf, b8, p1, p2, q, b0, b4))
    qs = section(jnp.where(first, q[:, :2048], q[:, 2048:]), 0)
    p3 = along_x(jnp.stack([jnp.where(first, b4, b8), p1]), 1, -1)
    p4 = along_x(jnp.where(first, b8, b4), -1, 1)
    place = core[None].astype(jnp.int32)
    state = attend(place, 1, qf, b0, [b4, b8, p1, p2], own=True)
    qs, p3, p4, qf, b0, b4, b8, p1, p2, *state = lax.optimization_barrier((qs, p3, p4, qf, b0, b4, b8, p1, p2, *state))
    p5 = along_x(p3[0], 1, -1)
    state2 = attend(place, 0, qs, b0, [b4, b8, p1, p2, p3, p4], own=True)
    p5, qs, qf, b0, p3, p4, *state2 = lax.optimization_barrier((p5, qs, qf, b0, p3, p4, *state2))
    of_ = attend(place, 1, qf, b0, [p3, p4, p5], state=state, last=True)
    got = swap(of_)
    os_ = attend(place, 0, qs, b0, [p5], state=state2, last=True)
    out = jnp.where(first, jnp.concatenate([os_, got], axis=1), jnp.concatenate([got, os_], axis=1))
    return out[None]


def solution(mesh):
    return jax.shard_map(
        shards,
        mesh=mesh,
        in_specs=(P("pp", "sp", None), P("pp", "sp", None), P("pp", "sp", None), P("pp", "sp")),
        out_specs=P("pp", "sp", None),
        check_vma=False,
    )
```

time: 126 us -> 91.8 us (0.73)
  waiting for transfers between devices: 67.6 us -> 22.3 us
  starting transfers between devices: 39.3 us -> 48.4 us
  Pallas kernels: 13.1 us -> 17.1 us
    ppermute x4 -> x6, waiting for transfers between devices: 33 us -> 9.22 us  [section(): return lax.ppermute(block, ('pp', 'sp'), pairs)]
    ppermute x2 -> x1, waiting for transfers between devices: 18.7 us -> 0.01 us  [along_y(): return lax.ppermute(block, 'sp', [(s, (s + 8) % 64) for s in range(64)])]
    ppermute x4 -> x6, starting transfers between devices: 14.5 us -> 24.5 us  [section(): return lax.ppermute(block, ('pp', 'sp'), pairs)]
    pallas_call x1 -> x4, Pallas kernels: 13.1 us -> 17.1 us  [attend(): pl.pallas_call(functools.partial(piece, half, own, bool(state), last, 1 +...]
    ppermute x2 -> x1, starting transfers between devices: 5.25 us -> 2.38 us  [along_y(): return lax.ppermute(block, 'sp', [(s, (s + 8) % 64) for s in range(64)])]
    ppermute x1, starting transfers between devices: 1.92 us -> 3.84 us  [swap(): return lax.ppermute(block, 'sp', [(s, s ^ 1) for s in range(64)])]
    ppermute x1, waiting for transfers between devices: 1.88 us -> 0.01 us  [swap(): return lax.ppermute(block, 'sp', [(s, s ^ 1) for s in range(64)])]
    ppermute x3 -> x5, waiting for transfers between devices: 14 us -> 13.1 us  [along_x(): lax.ppermute(block, 'sp', [(s, (s + 2 * (step1 if s % 2 else step0)) % 64...]
  transfers between devices with their start and end apart: 10 -> 13, of which waited for: 9 -> 6; matrix products, arithmetic and copies ran while one was open for 1% -> 0% of each run, Pallas kernels for 0% -> 15%
where the time goes in v2:
time: 91.8 us; the launch traced here: 91.3 us
  starting transfers between devices  48.4 us (53%)
  waiting for transfers between devices  22.3 us (24%)
  Pallas kernels  17.1 us (19%)
  other arithmetic  2.24 us (2%)
  local copies, waits for them, and re-layouts  1.06 us (1%)
    ppermute x6, starting transfers between devices, section(): return lax.ppermute(block, ('pp', 'sp'), pairs)  24.5 us
    ppermute x5, starting transfers between devices, along_x(): lax.ppermute(block, 'sp', [(s, (s + 2 * (step1 if s % 2 else step0)) % 64...  17.7 us
    pallas_call x4, Pallas kernels, attend(): pl.pallas_call(functools.partial(piece, half, own, bool(state), last, 1 +...  17.1 us
    ppermute x5, waiting for transfers between devices, along_x(): lax.ppermute(block, 'sp', [(s, (s + 2 * (step1 if s % 2 else step0)) % 64...  13.1 us
    ppermute x6, waiting for transfers between devices, section(): return lax.ppermute(block, ('pp', 'sp'), pairs)  9.22 us
    ppermute x1, starting transfers between devices, swap(): return lax.ppermute(block, 'sp', [(s, s ^ 1) for s in range(64)])  3.84 us
    ppermute x1, starting transfers between devices, along_y(): return lax.ppermute(block, 'sp', [(s, (s + 8) % 64) for s in range(64)])  2.38 us
  transfers between devices with their start and end apart: 13, of which 6 were waited for; matrix products, arithmetic and copies ran while one was open for 0% of the time, Pallas kernels for 15%

profile of v2, /device:TPU:1, one launch (start us, length us, event | category | flops | bytes accessed | tf_op | source)
XLA Modules:
  0.0 91.3 jit_solution(17840403401939094545)
XLA Ops:
  0.0 0.7 convert_element_type.6
  0.7 0.0 copy-start
  0.7 1.0 %fusion.3 = (bf16[128,256]{1,0:T(8,128)(2,1)S(1)}, bf16[128,256]{1,0:T(8,128)(2,1)S(1)}, bf16[128,256]{1,0:T(8,128)(2,1)S(1)}, bf16[128,256]{1,0:T(8,128)(2,1)S(1)}) fusion(bf16[128,512]{1,0:T(8,128)(2,1)} %bitcast.24, bf16[128,512]{1,0:T(8,128)(2,1)} %bitcast.25), kind=kLoop, calls=%fused_computation.17 | loop fusion | bytes 524288 | tf_op jit(solution)/shard_map/slice | solution.py:143
  1.8 5.8 %collective-permute-start.2 = (bf16[144,512]{1,0:T(8,128)(2,1)S(1)}, bf16[144,512]{1,0:T(8,128)(2,1)S(1)}, u32[]{:S(2)}, u32[]{:S(2)}) collective-permute-start(bf16[144,512]{1,0:T(8,128)(2,1)S(1)} %get-tuple-element.83), channel_id=1, source_target_pairs={{0,72},{1,73},{2,74},{3,75},{4,76},{5,77},{6,78},{7,79},{8,80},{9,... | collective-permute-start | bytes 442376 | tf_op jit(solution)/shard_map/ppermute | solution.py:128
  7.6 5.9 %collective-permute-start.3 = (bf16[144,512]{1,0:T(8,128)(2,1)S(1)}, bf16[144,512]{1,0:T(8,128)(2,1)S(1)}, u32[]{:S(2)}, u32[]{:S(2)}) collective-permute-start(bf16[144,512]{1,0:T(8,128)(2,1)S(1)} %get-tuple-element.84), channel_id=1, source_target_pairs={{0,73},{1,72},{2,75},{3,74},{4,77},{5,76},{6,79},{7,78},{8,81},{9,... | collective-permute-start | bytes 442376 | tf_op jit(solution)/shard_map/ppermute | solution.py:128
  13.5 4.0 %collective-permute-start = (bf16[144,512]{1,0:T(8,128)(2,1)S(1)}, bf16[144,512]{1,0:T(8,128)(2,1)S(1)}, u32[]{:S(2)}, u32[]{:S(2)}) collective-permute-start(bf16[144,512]{1,0:T(8,128)(2,1)S(1)} %get-tuple-element.83), channel_id=1, source_target_pairs={{0,64},{1,65},{2,66},{3,67},{4,68},{5,69},{6,70},{7,71},{8,72},{9,... | collective-permute-start | bytes 442376 | tf_op jit(solution)/shard_map/ppermute | solution.py:128
  17.5 4.9 %collective-permute-start.1 = (bf16[144,512]{1,0:T(8,128)(2,1)S(1)}, bf16[144,512]{1,0:T(8,128)(2,1)S(1)}, u32[]{:S(2)}, u32[]{:S(2)}) collective-permute-start(bf16[144,512]{1,0:T(8,128)(2,1)S(1)} %get-tuple-element.84), channel_id=1, source_target_pairs={{0,65},{1,64},{2,67},{3,66},{4,69},{5,68},{6,71},{7,70},{8,73},{9,... | collective-permute-start | bytes 442376 | tf_op jit(solution)/shard_map/ppermute | solution.py:128
  22.4 0.0 collective-permute-done.2
  22.4 1.1 %collective-permute-done.3 = bf16[144,512]{1,0:T(8,128)(2,1)S(1)} collective-permute-done((bf16[144,512]{1,0:T(8,128)(2,1)S(1)}, bf16[144,512]{1,0:T(8,128)(2,1)S(1)}, u32[]{:S(2)}, u32[]{:S(2)}) %collective-permute-start.3) | collective-permute-done | bytes 147488 | tf_op jit(solution)/shard_map/ppermute | solution.py:128
  23.6 3.3 %collective-permute-done = bf16[144,512]{1,0:T(8,128)(2,1)S(1)} collective-permute-done((bf16[144,512]{1,0:T(8,128)(2,1)S(1)}, bf16[144,512]{1,0:T(8,128)(2,1)S(1)}, u32[]{:S(2)}, u32[]{:S(2)}) %collective-permute-start) | collective-permute-done | bytes 147488 | tf_op jit(solution)/shard_map/ppermute | solution.py:128
  26.9 3.2 %collective-permute-done.1 = bf16[144,512]{1,0:T(8,128)(2,1)S(1)} collective-permute-done((bf16[144,512]{1,0:T(8,128)(2,1)S(1)}, bf16[144,512]{1,0:T(8,128)(2,1)S(1)}, u32[]{:S(2)}, u32[]{:S(2)}) %collective-permute-start.1) | collective-permute-done | bytes 147488 | tf_op jit(solution)/shard_map/ppermute | solution.py:128
  30.1 0.0 copy-done
  30.1 0.1 slice_select_fusion.1
  30.1 1.9 %collective-permute-start.4 = (bf16[128,2048]{1,0:T(8,128)(2,1)S(1)}, bf16[128,2048]{1,0:T(8,128)(2,1)S(1)}, u32[]{:S(2)}, u32[]{:S(2)}) collective-permute-start(bf16[128,2048]{1,0:T(8,128)(2,1)S(1)} %slice_select_fusion.1), channel_id=1, source_target_pairs={{0,65},{1,64},{2,67},{3,66},{4,69},{5,68},{6,71},{7,70},{8,73},{9,... | collective-permute-start | bytes 1572872 | tf_op jit(solution)/shard_map/ppermute | solution.py:128
  32.1 5.1 %collective-permute-start.6 = (bf16[2,144,512]{2,1,0:T(8,128)(2,1)S(1)}, bf16[2,144,512]{2,1,0:T(8,128)(2,1)S(1)}, u32[]{:S(2)}, u32[]{:S(2)}) collective-permute-start(bf16[2,144,512]{2,1,0:T(8,128)(2,1)S(1)} %get-tuple-element.82), channel_id=1, source_target_pairs={{0,2},{1,63},{2,4},{3,1},{4,6},{5,3},{6,8},{7,5},{8,10},{9,7},{10,... | collective-permute-start | bytes 884744 | tf_op jit(solution)/shard_map/ppermute | solution.py:134
  37.2 1.9 %collective-permute-start.7 = (bf16[2,144,512]{2,1,0:T(8,128)(2,1)S(1)}, bf16[2,144,512]{2,1,0:T(8,128)(2,1)S(1)}, u32[]{:S(2)}, u32[]{:S(2)}) collective-permute-start(bf16[2,144,512]{2,1,0:T(8,128)(2,1)S(1)} %get-tuple-element.81), channel_id=1, source_target_pairs={{0,62},{1,3},{2,0},{3,5},{4,2},{5,7},{6,4},{7,9},{8,6},{9,11},{10,... | collective-permute-start | bytes 884744 | tf_op jit(solution)/shard_map/ppermute | solution.py:134
  39.2 2.4 %collective-permute-start.5 = (bf16[2,144,512]{2,1,0:T(8,128)(2,1)S(1)}, bf16[2,144,512]{2,1,0:T(8,128)(2,1)S(1)}, u32[]{:S(2)}, u32[]{:S(2)}) collective-permute-start(bf16[2,144,512]{2,1,0:T(8,128)(2,1)S(1)} %pad_maximum_fusion.2.refs_1_), channel_id=1, source_target_pairs={{0,8},{1,9},{2,10},{3,11},{4,12},{5,13},{6,14},{7,15},{8,16},{9,17... | collective-permute-start | bytes 884744 | tf_op jit(solution)/shard_map/ppermute | solution.py:131
  41.6 0.0 collective-permute-done.6.refs_3_
  41.6 7.9 %collective-permute-done.7.refs_4_ = bf16[2,144,512]{2,1,0:T(8,128)(2,1)S(1)} collective-permute-done((bf16[2,144,512]{2,1,0:T(8,128)(2,1)S(1)}, bf16[2,144,512]{2,1,0:T(8,128)(2,1)S(1)}, u32[]{:S(2)}, u32[]{:S(2)}) %collective-permute-start.7) | collective-permute-done | bytes 294944 | tf_op jit(solution)/shard_map/ppermute | solution.py:134
  49.4 0.0 collective-permute-done.5.refs_2_
  49.4 0.0 collective-permute-done.4.q_ref
  49.5 0.1 pad_maximum_fusion
  49.5 6.7 %collective-permute-start.9 = (bf16[2,2,144,512]{3,2,1,0:T(8,128)(2,1)S(1)}, bf16[2,2,144,512]{3,2,1,0:T(8,128)(2,1)S(1)}, u32[]{:S(2)}, u32[]{:S(2)}) collective-permute-start(bf16[2,2,144,512]{3,2,1,0:T(8,128)(2,1)S(1)} %pad_maximum_fusion), channel_id=1, source_target_pairs={{0,2},{1,63},{2,4},{3,1},{4,6},{5,3},{6,8},{7,5},{8,10},{9,7},{10,... | collective-permute-start | bytes 1769480 | tf_op jit(solution)/shard_map/ppermute | solution.py:134
  56.2 0.1 slice_select_fusion
  56.3 1.9 %collective-permute-start.8 = (bf16[128,2048]{1,0:T(8,128)(2,1)S(1)}, bf16[128,2048]{1,0:T(8,128)(2,1)S(1)}, u32[]{:S(2)}, u32[]{:S(2)}) collective-permute-start(bf16[128,2048]{1,0:T(8,128)(2,1)S(1)} %slice_select_fusion), channel_id=1, source_target_pairs={{0,64},{1,65},{2,66},{3,67},{4,68},{5,69},{6,70},{7,71},{8,72},{9,... | collective-permute-start | bytes 1572872 | tf_op jit(solution)/shard_map/ppermute | solution.py:128
  58.2 1.9 %collective-permute-start.10 = (bf16[2,144,512]{2,1,0:T(8,128)(2,1)S(1)}, bf16[2,144,512]{2,1,0:T(8,128)(2,1)S(1)}, u32[]{:S(2)}, u32[]{:S(2)}) collective-permute-start(bf16[2,144,512]{2,1,0:T(8,128)(2,1)S(1)} %get-tuple-element.79), channel_id=1, source_target_pairs={{0,62},{1,3},{2,0},{3,5},{4,2},{5,7},{6,4},{7,9},{8,6},{9,11},{10,... | collective-permute-start | bytes 884744 | tf_op jit(solution)/shard_map/ppermute | solution.py:134
  60.2 4.0 %shard_map.46 = (f32[2048,128]{1,0:T(8,128)S(1)}, f32[2048,128]{1,0:T(8,128)S(1)}, f32[2048,128]{1,0:T(8,128)S(1)}) custom-call(s32[1]{0:T(128)} %bitcast.core_ref, bf16[128,2048]{1,0:T(8,128)(2,1)S(1)} %collective-permute-done.4.q_ref, bf16[2,144,512]{2,1,0:T(8,128)(2,1)S(1)} %pad_maximum_fusion.1.refs_0_, ...), custom_call_target="tpu_custom_call" | custom-call | flops 2684354560 | bytes 4194304 | tf_op jit(solution)/shard_map/pallas_call | solution.py:109
  64.2 5.2 %collective-permute-done.10.refs_6_.refs_2_ = bf16[2,144,512]{2,1,0:T(8,128)(2,1)S(1)} collective-permute-done((bf16[2,144,512]{2,1,0:T(8,128)(2,1)S(1)}, bf16[2,144,512]{2,1,0:T(8,128)(2,1)S(1)}, u32[]{:S(2)}, u32[]{:S(2)}) %collective-permute-start.10) | collective-permute-done | bytes 294944 | tf_op jit(solution)/shard_map/ppermute | solution.py:134
  69.4 1.6 %collective-permute-done.8.q_ref = bf16[128,2048]{1,0:T(8,128)(2,1)S(1)} collective-permute-done((bf16[128,2048]{1,0:T(8,128)(2,1)S(1)}, bf16[128,2048]{1,0:T(8,128)(2,1)S(1)}, u32[]{:S(2)}, u32[]{:S(2)}) %collective-permute-start.8) | collective-permute-done | bytes 524320 | tf_op jit(solution)/shard_map/ppermute | solution.py:128
  71.0 0.0 collective-permute-done.9.refs_5_.refs_1_
  71.0 2.1 %collective-permute-start.11 = (bf16[2,144,512]{2,1,0:T(8,128)(2,1)S(1)}, bf16[2,144,512]{2,1,0:T(8,128)(2,1)S(1)}, u32[]{:S(2)}, u32[]{:S(2)}) collective-permute-start(bf16[2,144,512]{2,1,0:T(8,128)(2,1)S(1)} %slice_bitcast_fusion), channel_id=1, source_target_pairs={{0,2},{1,63},{2,4},{3,1},{4,6},{5,3},{6,8},{7,5},{8,10},{9,7},{10,... | collective-permute-start | bytes 884744 | tf_op jit(solution)/shard_map/ppermute | solution.py:134
  73.1 6.4 %shard_map.47 = (f32[2048,128]{1,0:T(8,128)S(1)}, f32[2048,128]{1,0:T(8,128)S(1)}, f32[2048,128]{1,0:T(8,128)S(1)}) custom-call(s32[1]{0:T(128)} %bitcast.core_ref, bf16[128,2048]{1,0:T(8,128)(2,1)S(1)} %collective-permute-done.8.q_ref, bf16[2,144,512]{2,1,0:T(8,128)(2,1)S(1)} %pad_maximum_fusion.1.refs_0_, ...), custom_call_target="tpu_custom_call" | custom-call | flops 4294967296 | bytes 4194304 | tf_op jit(solution)/shard_map/pallas_call | solution.py:109
  79.6 0.0 collective-permute-done.11.refs_1_.refs_3_
  79.6 3.8 %shard_map.49 = bf16[128,2048]{1,0:T(8,128)(2,1)S(1)} custom-call(s32[1]{0:T(128)} %bitcast.core_ref, bf16[128,2048]{1,0:T(8,128)(2,1)S(1)} %collective-permute-done.4.q_ref, bf16[2,144,512]{2,1,0:T(8,128)(2,1)S(1)} %pad_maximum_fusion.1.refs_0_, bf16[2,2,144,512]{3,2,1,0:T(8,128)(2,1)S(1)} %collective-permute-done.9.refs_5_.refs_1_, ...), custom_call_target="tpu_custom_call" | custom-call | flops 2147483648 | bytes 4194304 | tf_op jit(solution)/shard_map/pallas_call | solution.py:109
  83.3 3.8 %collective-permute-start.12 = (bf16[128,2048]{1,0:T(8,128)(2,1)S(1)}, bf16[128,2048]{1,0:T(8,128)(2,1)S(1)}, u32[]{:S(2)}, u32[]{:S(2)}) collective-permute-start(bf16[128,2048]{1,0:T(8,128)(2,1)S(1)} %shard_map.49), channel_id=1, source_target_pairs={{0,1},{1,0},{2,3},{3,2},{4,5},{5,4},{6,7},{7,6},{8,9},{9,8},{10,11... | collective-permute-start | bytes 1572872 | tf_op jit(solution)/shard_map/ppermute | solution.py:137
  87.2 2.9 %shard_map.48 = bf16[128,2048]{1,0:T(8,128)(2,1)S(1)} custom-call(s32[1]{0:T(128)} %bitcast.core_ref, bf16[128,2048]{1,0:T(8,128)(2,1)S(1)} %collective-permute-done.8.q_ref, bf16[2,144,512]{2,1,0:T(8,128)(2,1)S(1)} %pad_maximum_fusion.1.refs_0_, bf16[2,144,512]{2,1,0:T(8,128)(2,1)S(1)} %collective-permute-done.11.refs_1_.refs_3_, ...), custom_call_target="tpu_custom_call" | custom-call | flops 536870912 | bytes 4194304 | tf_op jit(solution)/shard_map/pallas_call | solution.py:109
  90.1 0.0 collective-permute-done.12
  90.1 1.2 %maximum_select_fusion = bf16[1,128,4096]{2,1,0:T(8,128)(2,1)} fusion(bf16[1,128,2048]{2,1,0:T(8,128)(2,1)S(1)} %bitcast.19, bf16[1,128,2048]{2,1,0:T(8,128)(2,1)S(1)} %bitcast.15, pred[]{:T(512)S(6)} %eq.5), kind=kLoop, calls=%fused_computation | loop fusion | flops 4718592 | bytes 2097153 | tf_op jit(solution)/shard_map/jit(_where)/select_n | solution.py:168
  (6 shorter events, 0.2 us)
Async XLA Ops:
  0.7 29.4 %copy-start = (bf16[1,128,4096]{2,1,0:T(8,128)(2,1)S(1)}, bf16[1,128,4096]{2,1,0:T(8,128)(2,1)}, u32[]{:S(2)}) copy-start(bf16[1,128,4096]{2,1,0:T(8,128)(2,1)} %param.4) | copy-start | bytes 3145732
  1.8 20.7 %collective-permute-start.2 = (bf16[144,512]{1,0:T(8,128)(2,1)S(1)}, bf16[144,512]{1,0:T(8,128)(2,1)S(1)}, u32[]{:S(2)}, u32[]{:S(2)}) collective-permute-start(bf16[144,512]{1,0:T(8,128)(2,1)S(1)} %get-tuple-element.83), channel_id=1, source_target_pairs={{0,72},{1,73},{2,74},{3,75},{4,76},{5,77},{6,78},{7,79},{8,80},{9,... | collective-permute-start | bytes 442376 | tf_op jit(solution)/shard_map/ppermute | solution.py:128
  7.6 15.9 %collective-permute-start.3 = (bf16[144,512]{1,0:T(8,128)(2,1)S(1)}, bf16[144,512]{1,0:T(8,128)(2,1)S(1)}, u32[]{:S(2)}, u32[]{:S(2)}) collective-permute-start(bf16[144,512]{1,0:T(8,128)(2,1)S(1)} %get-tuple-element.84), channel_id=1, source_target_pairs={{0,73},{1,72},{2,75},{3,74},{4,77},{5,76},{6,79},{7,78},{8,81},{9,... | collective-permute-start | bytes 442376 | tf_op jit(solution)/shard_map/ppermute | solution.py:128
  13.5 13.4 %collective-permute-start = (bf16[144,512]{1,0:T(8,128)(2,1)S(1)}, bf16[144,512]{1,0:T(8,128)(2,1)S(1)}, u32[]{:S(2)}, u32[]{:S(2)}) collective-permute-start(bf16[144,512]{1,0:T(8,128)(2,1)S(1)} %get-tuple-element.83), channel_id=1, source_target_pairs={{0,64},{1,65},{2,66},{3,67},{4,68},{5,69},{6,70},{7,71},{8,72},{9,... | collective-permute-start | bytes 442376 | tf_op jit(solution)/shard_map/ppermute | solution.py:128
  17.5 12.6 %collective-permute-start.1 = (bf16[144,512]{1,0:T(8,128)(2,1)S(1)}, bf16[144,512]{1,0:T(8,128)(2,1)S(1)}, u32[]{:S(2)}, u32[]{:S(2)}) collective-permute-start(bf16[144,512]{1,0:T(8,128)(2,1)S(1)} %get-tuple-element.84), channel_id=1, source_target_pairs={{0,65},{1,64},{2,67},{3,66},{4,69},{5,68},{6,71},{7,70},{8,73},{9,... | collective-permute-start | bytes 442376 | tf_op jit(solution)/shard_map/ppermute | solution.py:128
  30.1 19.3 %collective-permute-start.4 = (bf16[128,2048]{1,0:T(8,128)(2,1)S(1)}, bf16[128,2048]{1,0:T(8,128)(2,1)S(1)}, u32[]{:S(2)}, u32[]{:S(2)}) collective-permute-start(bf16[128,2048]{1,0:T(8,128)(2,1)S(1)} %slice_select_fusion.1), channel_id=1, source_target_pairs={{0,65},{1,64},{2,67},{3,66},{4,69},{5,68},{6,71},{7,70},{8,73},{9,... | collective-permute-start | bytes 1572872 | tf_op jit(solution)/shard_map/ppermute | solution.py:128
  32.1 9.4 %collective-permute-start.6 = (bf16[2,144,512]{2,1,0:T(8,128)(2,1)S(1)}, bf16[2,144,512]{2,1,0:T(8,128)(2,1)S(1)}, u32[]{:S(2)}, u32[]{:S(2)}) collective-permute-start(bf16[2,144,512]{2,1,0:T(8,128)(2,1)S(1)} %get-tuple-element.82), channel_id=1, source_target_pairs={{0,2},{1,63},{2,4},{3,1},{4,6},{5,3},{6,8},{7,5},{8,10},{9,7},{10,... | collective-permute-start | bytes 884744 | tf_op jit(solution)/shard_map/ppermute | solution.py:134
  37.2 12.2 %collective-permute-start.7 = (bf16[2,144,512]{2,1,0:T(8,128)(2,1)S(1)}, bf16[2,144,512]{2,1,0:T(8,128)(2,1)S(1)}, u32[]{:S(2)}, u32[]{:S(2)}) collective-permute-start(bf16[2,144,512]{2,1,0:T(8,128)(2,1)S(1)} %get-tuple-element.81), channel_id=1, source_target_pairs={{0,62},{1,3},{2,0},{3,5},{4,2},{5,7},{6,4},{7,9},{8,6},{9,11},{10,... | collective-permute-start | bytes 884744 | tf_op jit(solution)/shard_map/ppermute | solution.py:134
  39.2 10.3 %collective-permute-start.5 = (bf16[2,144,512]{2,1,0:T(8,128)(2,1)S(1)}, bf16[2,144,512]{2,1,0:T(8,128)(2,1)S(1)}, u32[]{:S(2)}, u32[]{:S(2)}) collective-permute-start(bf16[2,144,512]{2,1,0:T(8,128)(2,1)S(1)} %pad_maximum_fusion.2.refs_1_), channel_id=1, source_target_pairs={{0,8},{1,9},{2,10},{3,11},{4,12},{5,13},{6,14},{7,15},{8,16},{9,17... | collective-permute-start | bytes 884744 | tf_op jit(solution)/shard_map/ppermute | solution.py:131
  49.5 21.5 %collective-permute-start.9 = (bf16[2,2,144,512]{3,2,1,0:T(8,128)(2,1)S(1)}, bf16[2,2,144,512]{3,2,1,0:T(8,128)(2,1)S(1)}, u32[]{:S(2)}, u32[]{:S(2)}) collective-permute-start(bf16[2,2,144,512]{3,2,1,0:T(8,128)(2,1)S(1)} %pad_maximum_fusion), channel_id=1, source_target_pairs={{0,2},{1,63},{2,4},{3,1},{4,6},{5,3},{6,8},{7,5},{8,10},{9,7},{10,... | collective-permute-start | bytes 1769480 | tf_op jit(solution)/shard_map/ppermute | solution.py:134
  56.3 14.7 %collective-permute-start.8 = (bf16[128,2048]{1,0:T(8,128)(2,1)S(1)}, bf16[128,2048]{1,0:T(8,128)(2,1)S(1)}, u32[]{:S(2)}, u32[]{:S(2)}) collective-permute-start(bf16[128,2048]{1,0:T(8,128)(2,1)S(1)} %slice_select_fusion), channel_id=1, source_target_pairs={{0,64},{1,65},{2,66},{3,67},{4,68},{5,69},{6,70},{7,71},{8,72},{9,... | collective-permute-start | bytes 1572872 | tf_op jit(solution)/shard_map/ppermute | solution.py:128
  58.2 11.1 %collective-permute-start.10 = (bf16[2,144,512]{2,1,0:T(8,128)(2,1)S(1)}, bf16[2,144,512]{2,1,0:T(8,128)(2,1)S(1)}, u32[]{:S(2)}, u32[]{:S(2)}) collective-permute-start(bf16[2,144,512]{2,1,0:T(8,128)(2,1)S(1)} %get-tuple-element.79), channel_id=1, source_target_pairs={{0,62},{1,3},{2,0},{3,5},{4,2},{5,7},{6,4},{7,9},{8,6},{9,11},{10,... | collective-permute-start | bytes 884744 | tf_op jit(solution)/shard_map/ppermute | solution.py:134
  71.0 8.5 %collective-permute-start.11 = (bf16[2,144,512]{2,1,0:T(8,128)(2,1)S(1)}, bf16[2,144,512]{2,1,0:T(8,128)(2,1)S(1)}, u32[]{:S(2)}, u32[]{:S(2)}) collective-permute-start(bf16[2,144,512]{2,1,0:T(8,128)(2,1)S(1)} %slice_bitcast_fusion), channel_id=1, source_target_pairs={{0,2},{1,63},{2,4},{3,1},{4,6},{5,3},{6,8},{7,5},{8,10},{9,7},{10,... | collective-permute-start | bytes 884744 | tf_op jit(solution)/shard_map/ppermute | solution.py:134
  83.3 6.7 %collective-permute-start.12 = (bf16[128,2048]{1,0:T(8,128)(2,1)S(1)}, bf16[128,2048]{1,0:T(8,128)(2,1)S(1)}, u32[]{:S(2)}, u32[]{:S(2)}) collective-permute-start(bf16[128,2048]{1,0:T(8,128)(2,1)S(1)} %shard_map.49), channel_id=1, source_target_pairs={{0,1},{1,0},{2,3},{3,2},{4,5},{5,4},{6,7},{7,6},{8,9},{9,8},{10,11... | collective-permute-start | bytes 1572872 | tf_op jit(solution)/shard_map/ppermute | solution.py:137

commit v3 on v2

--- a/solution.py
+++ b/solution.py
@@ -79,8 +79,9 @@
             top = jnp.max(score, axis=1, keepdims=True)
             if carried:
                 before = old[0][rows, :]
-                top = jnp.maximum(top, before[:, :1])
-            weight = jnp.exp2((score - top) * SCALE).astype(jnp.bfloat16)
+                top = jnp.maximum(jnp.broadcast_to(top, before.shape), before)
+            wide = jnp.concatenate([top] * (2 * len(blocks)), axis=1) if carried else top
+            weight = jnp.exp2((score - wide) * SCALE).astype(jnp.bfloat16)
             both = jnp.dot(weight, vaug[kv], preferred_element_type=jnp.float32)
             total, accum = both[:, HEAD:], both[:, :HEAD]
             if carried:
@@ -152,12 +153,14 @@
     b8 = along_y(b4)
     p1 = along_x(jnp.where(first, b0, b4), 1, -1)
     p2 = along_x(jnp.where(first, b4, b0), -1, 1)
+    b8, qf = lax.optimization_barrier((b8, qf))
     qf, b8, p1, p2, q, b0, b4 = lax.optimization_barrier((qf, b8, p1, p2, q, b0, b4))
     qs = section(jnp.where(first, q[:, :2048], q[:, 2048:]), 0)
     p3 = along_x(jnp.stack([jnp.where(first, b4, b8), p1]), 1, -1)
-    p4 = along_x(jnp.where(first, b8, b4), -1, 1)
+    p4 = along_y(p2)
     place = core[None].astype(jnp.int32)
     state = attend(place, 1, qf, b0, [b4, b8, p1, p2], own=True)
+    qs, qf = lax.optimization_barrier((qs, qf))
     qs, p3, p4, qf, b0, b4, b8, p1, p2, *state = lax.optimization_barrier((qs, p3, p4, qf, b0, b4, b8, p1, p2, *state))
     p5 = along_x(p3[0], 1, -1)
     state2 = attend(place, 0, qs, b0, [b4, b8, p1, p2, p3, p4], own=True)

time: 91.8 us -> 89.7 us (0.977)
  starting transfers between devices: 48.4 us -> 45.4 us
  waiting for transfers between devices: 22.3 us -> 25 us
  Pallas kernels: 17.1 us -> 15.3 us
    ppermute x6, waiting for transfers between devices: 9.22 us -> 19.3 us  [section(): return lax.ppermute(block, ('pp', 'sp'), pairs)]
    ppermute x5 -> x4, waiting for transfers between devices: 13.1 us -> 4.95 us  [along_x(): lax.ppermute(block, 'sp', [(s, (s + 2 * (step1 if s % 2 else step0)) % 64...]
    ppermute x5 -> x4, starting transfers between devices: 17.7 us -> 12.7 us  [along_x(): lax.ppermute(block, 'sp', [(s, (s + 2 * (step1 if s % 2 else step0)) % 64...]
    pallas_call x4, Pallas kernels: 17.1 us -> 15.3 us  [attend(): pl.pallas_call(functools.partial(piece, half, own, bool(state), last, 1 +...]
    ppermute x1 -> x2, starting transfers between devices: 2.38 us -> 3.84 us  [along_y(): return lax.ppermute(block, 'sp', [(s, (s + 8) % 64) for s in range(64)])]
  transfers between devices with their start and end apart: 13 -> 13, of which waited for: 6 -> 8; matrix products, arithmetic and copies ran while one was open for 0% -> 0% of each run, Pallas kernels for 15% -> 13%
where the time goes in v3:
time: 89.7 us; the launch traced here: 89.2 us
  starting transfers between devices  45.4 us (51%)
  waiting for transfers between devices  25 us (28%)
  Pallas kernels  15.3 us (17%)
  other arithmetic  2.23 us (2%)
  local copies, waits for them, and re-layouts  1.06 us (1%)
    ppermute x6, starting transfers between devices, section(): return lax.ppermute(block, ('pp', 'sp'), pairs)  24.5 us
    ppermute x6, waiting for transfers between devices, section(): return lax.ppermute(block, ('pp', 'sp'), pairs)  19.3 us
    pallas_call x4, Pallas kernels, attend(): pl.pallas_call(functools.partial(piece, half, own, bool(state), last, 1 +...  15.3 us
    ppermute x4, starting transfers between devices, along_x(): lax.ppermute(block, 'sp', [(s, (s + 2 * (step1 if s % 2 else step0)) % 64...  12.7 us
    ppermute x4, waiting for transfers between devices, along_x(): lax.ppermute(block, 'sp', [(s, (s + 2 * (step1 if s % 2 else step0)) % 64...  4.95 us
    ppermute x1, starting transfers between devices, swap(): return lax.ppermute(block, 'sp', [(s, s ^ 1) for s in range(64)])  4.39 us
    ppermute x2, starting transfers between devices, along_y(): return lax.ppermute(block, 'sp', [(s, (s + 8) % 64) for s in range(64)])  3.84 us
  transfers between devices with their start and end apart: 13, of which 8 were waited for; matrix products, arithmetic and copies ran while one was open for 0% of the time, Pallas kernels for 13%

profile of v3, /device:TPU:1, one launch (start us, length us, event | category | flops | bytes accessed | tf_op | source)
XLA Modules:
  0.0 89.2 jit_solution(5799911025847329466)
XLA Ops:
  0.0 0.7 convert_element_type.6
  0.7 0.0 copy-start
  0.7 1.0 %fusion.3 = (bf16[128,256]{1,0:T(8,128)(2,1)S(1)}, bf16[128,256]{1,0:T(8,128)(2,1)S(1)}, bf16[128,256]{1,0:T(8,128)(2,1)S(1)}, bf16[128,256]{1,0:T(8,128)(2,1)S(1)}) fusion(bf16[128,512]{1,0:T(8,128)(2,1)} %bitcast.24, bf16[128,512]{1,0:T(8,128)(2,1)} %bitcast.25), kind=kLoop, calls=%fused_computation.16 | loop fusion | bytes 524288 | tf_op jit(solution)/shard_map/slice | solution.py:144
  1.8 5.8 %collective-permute-start.2 = (bf16[144,512]{1,0:T(8,128)(2,1)S(1)}, bf16[144,512]{1,0:T(8,128)(2,1)S(1)}, u32[]{:S(2)}, u32[]{:S(2)}) collective-permute-start(bf16[144,512]{1,0:T(8,128)(2,1)S(1)} %get-tuple-element.89), channel_id=1, source_target_pairs={{0,72},{1,73},{2,74},{3,75},{4,76},{5,77},{6,78},{7,79},{8,80},{9,... | collective-permute-start | bytes 442376 | tf_op jit(solution)/shard_map/ppermute | solution.py:129
  7.6 5.9 %collective-permute-start.3 = (bf16[144,512]{1,0:T(8,128)(2,1)S(1)}, bf16[144,512]{1,0:T(8,128)(2,1)S(1)}, u32[]{:S(2)}, u32[]{:S(2)}) collective-permute-start(bf16[144,512]{1,0:T(8,128)(2,1)S(1)} %get-tuple-element.90), channel_id=1, source_target_pairs={{0,73},{1,72},{2,75},{3,74},{4,77},{5,76},{6,79},{7,78},{8,81},{9,... | collective-permute-start | bytes 442376 | tf_op jit(solution)/shard_map/ppermute | solution.py:129
  13.5 4.0 %collective-permute-start = (bf16[144,512]{1,0:T(8,128)(2,1)S(1)}, bf16[144,512]{1,0:T(8,128)(2,1)S(1)}, u32[]{:S(2)}, u32[]{:S(2)}) collective-permute-start(bf16[144,512]{1,0:T(8,128)(2,1)S(1)} %get-tuple-element.89), channel_id=1, source_target_pairs={{0,64},{1,65},{2,66},{3,67},{4,68},{5,69},{6,70},{7,71},{8,72},{9,... | collective-permute-start | bytes 442376 | tf_op jit(solution)/shard_map/ppermute | solution.py:129
  17.5 4.9 %collective-permute-start.1 = (bf16[144,512]{1,0:T(8,128)(2,1)S(1)}, bf16[144,512]{1,0:T(8,128)(2,1)S(1)}, u32[]{:S(2)}, u32[]{:S(2)}) collective-permute-start(bf16[144,512]{1,0:T(8,128)(2,1)S(1)} %get-tuple-element.90), channel_id=1, source_target_pairs={{0,65},{1,64},{2,67},{3,66},{4,69},{5,68},{6,71},{7,70},{8,73},{9,... | collective-permute-start | bytes 442376 | tf_op jit(solution)/shard_map/ppermute | solution.py:129
  22.4 0.0 collective-permute-done.2
  22.4 1.1 %collective-permute-done.3 = bf16[144,512]{1,0:T(8,128)(2,1)S(1)} collective-permute-done((bf16[144,512]{1,0:T(8,128)(2,1)S(1)}, bf16[144,512]{1,0:T(8,128)(2,1)S(1)}, u32[]{:S(2)}, u32[]{:S(2)}) %collective-permute-start.3) | collective-permute-done | bytes 147488 | tf_op jit(solution)/shard_map/ppermute | solution.py:129
  23.6 3.3 %collective-permute-done = bf16[144,512]{1,0:T(8,128)(2,1)S(1)} collective-permute-done((bf16[144,512]{1,0:T(8,128)(2,1)S(1)}, bf16[144,512]{1,0:T(8,128)(2,1)S(1)}, u32[]{:S(2)}, u32[]{:S(2)}) %collective-permute-start) | collective-permute-done | bytes 147488 | tf_op jit(solution)/shard_map/ppermute | solution.py:129
  26.9 3.2 %collective-permute-done.1 = bf16[144,512]{1,0:T(8,128)(2,1)S(1)} collective-permute-done((bf16[144,512]{1,0:T(8,128)(2,1)S(1)}, bf16[144,512]{1,0:T(8,128)(2,1)S(1)}, u32[]{:S(2)}, u32[]{:S(2)}) %collective-permute-start.1) | collective-permute-done | bytes 147488 | tf_op jit(solution)/shard_map/ppermute | solution.py:129
  30.1 0.0 copy-done
  30.1 0.1 slice_select_fusion.1
  30.1 1.9 %collective-permute-start.5 = (bf16[128,2048]{1,0:T(8,128)(2,1)S(1)}, bf16[128,2048]{1,0:T(8,128)(2,1)S(1)}, u32[]{:S(2)}, u32[]{:S(2)}) collective-permute-start(bf16[128,2048]{1,0:T(8,128)(2,1)S(1)} %slice_select_fusion.1), channel_id=1, source_target_pairs={{0,65},{1,64},{2,67},{3,66},{4,69},{5,68},{6,71},{7,70},{8,73},{9,... | collective-permute-start | bytes 1572872 | tf_op jit(solution)/shard_map/ppermute | solution.py:129
  32.1 1.9 %collective-permute-start.4 = (bf16[2,144,512]{2,1,0:T(8,128)(2,1)S(1)}, bf16[2,144,512]{2,1,0:T(8,128)(2,1)S(1)}, u32[]{:S(2)}, u32[]{:S(2)}) collective-permute-start(bf16[2,144,512]{2,1,0:T(8,128)(2,1)S(1)} %pad_maximum_fusion.2.refs_1_), channel_id=1, source_target_pairs={{0,8},{1,9},{2,10},{3,11},{4,12},{5,13},{6,14},{7,15},{8,16},{9,17... | collective-permute-start | bytes 884744 | tf_op jit(solution)/shard_map/ppermute | solution.py:132
  34.1 6.8 %collective-permute-start.6 = (bf16[2,144,512]{2,1,0:T(8,128)(2,1)S(1)}, bf16[2,144,512]{2,1,0:T(8,128)(2,1)S(1)}, u32[]{:S(2)}, u32[]{:S(2)}) collective-permute-start(bf16[2,144,512]{2,1,0:T(8,128)(2,1)S(1)} %get-tuple-element.88), channel_id=1, source_target_pairs={{0,2},{1,63},{2,4},{3,1},{4,6},{5,3},{6,8},{7,5},{8,10},{9,7},{10,... | collective-permute-start | bytes 884744 | tf_op jit(solution)/shard_map/ppermute | solution.py:135
  40.8 1.9 %collective-permute-start.7 = (bf16[2,144,512]{2,1,0:T(8,128)(2,1)S(1)}, bf16[2,144,512]{2,1,0:T(8,128)(2,1)S(1)}, u32[]{:S(2)}, u32[]{:S(2)}) collective-permute-start(bf16[2,144,512]{2,1,0:T(8,128)(2,1)S(1)} %get-tuple-element.87), channel_id=1, source_target_pairs={{0,62},{1,3},{2,0},{3,5},{4,2},{5,7},{6,4},{7,9},{8,6},{9,11},{10,... | collective-permute-start | bytes 884744 | tf_op jit(solution)/shard_map/ppermute | solution.py:135
  42.8 0.6 collective-permute-done.4.refs_2_
  43.4 4.1 %collective-permute-done.5.q_ref = bf16[128,2048]{1,0:T(8,128)(2,1)S(1)} collective-permute-done((bf16[128,2048]{1,0:T(8,128)(2,1)S(1)}, bf16[128,2048]{1,0:T(8,128)(2,1)S(1)}, u32[]{:S(2)}, u32[]{:S(2)}) %collective-permute-start.5) | collective-permute-done | bytes 524320 | tf_op jit(solution)/shard_map/ppermute | solution.py:129
  47.5 0.0 collective-permute-done.6.refs_3_
  47.5 4.9 %collective-permute-done.7.refs_4_ = bf16[2,144,512]{2,1,0:T(8,128)(2,1)S(1)} collective-permute-done((bf16[2,144,512]{2,1,0:T(8,128)(2,1)S(1)}, bf16[2,144,512]{2,1,0:T(8,128)(2,1)S(1)}, u32[]{:S(2)}, u32[]{:S(2)}) %collective-permute-start.7) | collective-permute-done | bytes 294944 | tf_op jit(solution)/shard_map/ppermute | solution.py:135
  52.5 0.1 pad_maximum_fusion
  52.5 1.9 %collective-permute-start.9 = (bf16[2,2,144,512]{3,2,1,0:T(8,128)(2,1)S(1)}, bf16[2,2,144,512]{3,2,1,0:T(8,128)(2,1)S(1)}, u32[]{:S(2)}, u32[]{:S(2)}) collective-permute-start(bf16[2,2,144,512]{3,2,1,0:T(8,128)(2,1)S(1)} %pad_maximum_fusion), channel_id=1, source_target_pairs={{0,2},{1,63},{2,4},{3,1},{4,6},{5,3},{6,8},{7,5},{8,10},{9,7},{10,... | collective-permute-start | bytes 1769480 | tf_op jit(solution)/shard_map/ppermute | solution.py:135
  54.5 0.1 slice_select_fusion
  54.5 1.9 %collective-permute-start.8 = (bf16[128,2048]{1,0:T(8,128)(2,1)S(1)}, bf16[128,2048]{1,0:T(8,128)(2,1)S(1)}, u32[]{:S(2)}, u32[]{:S(2)}) collective-permute-start(bf16[128,2048]{1,0:T(8,128)(2,1)S(1)} %slice_select_fusion), channel_id=1, source_target_pairs={{0,64},{1,65},{2,66},{3,67},{4,68},{5,69},{6,70},{7,71},{8,72},{9,... | collective-permute-start | bytes 1572872 | tf_op jit(solution)/shard_map/ppermute | solution.py:129
  56.5 1.9 %collective-permute-start.10 = (bf16[2,144,512]{2,1,0:T(8,128)(2,1)S(1)}, bf16[2,144,512]{2,1,0:T(8,128)(2,1)S(1)}, u32[]{:S(2)}, u32[]{:S(2)}) collective-permute-start(bf16[2,144,512]{2,1,0:T(8,128)(2,1)S(1)} %collective-permute-done.7.refs_4_), channel_id=1, source_target_pairs={{0,8},{1,9},{2,10},{3,11},{4,12},{5,13},{6,14},{7,15},{8,16},{9,17... | collective-permute-start | bytes 884744 | tf_op jit(solution)/shard_map/ppermute | solution.py:132
  58.4 4.0 %shard_map.46 = (f32[2048,128]{1,0:T(8,128)S(1)}, f32[2048,128]{1,0:T(8,128)S(1)}, f32[2048,128]{1,0:T(8,128)S(1)}) custom-call(s32[1]{0:T(128)} %bitcast.core_ref, bf16[128,2048]{1,0:T(8,128)(2,1)S(1)} %collective-permute-done.5.q_ref, bf16[2,144,512]{2,1,0:T(8,128)(2,1)S(1)} %pad_maximum_fusion.1.refs_0_, ...), custom_call_target="tpu_custom_call" | custom-call | flops 2684354560 | bytes 4194304 | tf_op jit(solution)/shard_map/pallas_call | solution.py:110
  62.4 7.6 %collective-permute-done.8.q_ref = bf16[128,2048]{1,0:T(8,128)(2,1)S(1)} collective-permute-done((bf16[128,2048]{1,0:T(8,128)(2,1)S(1)}, bf16[128,2048]{1,0:T(8,128)(2,1)S(1)}, u32[]{:S(2)}, u32[]{:S(2)}) %collective-permute-start.8) | collective-permute-done | bytes 524320 | tf_op jit(solution)/shard_map/ppermute | solution.py:129
  70.0 0.0 collective-permute-done.10.refs_6_.refs_2_
  70.0 0.0 collective-permute-done.9.refs_5_.refs_1_
  70.1 2.1 %collective-permute-start.11 = (bf16[2,144,512]{2,1,0:T(8,128)(2,1)S(1)}, bf16[2,144,512]{2,1,0:T(8,128)(2,1)S(1)}, u32[]{:S(2)}, u32[]{:S(2)}) collective-permute-start(bf16[2,144,512]{2,1,0:T(8,128)(2,1)S(1)} %slice_bitcast_fusion), channel_id=1, source_target_pairs={{0,2},{1,63},{2,4},{3,1},{4,6},{5,3},{6,8},{7,5},{8,10},{9,7},{10,... | collective-permute-start | bytes 884744 | tf_op jit(solution)/shard_map/ppermute | solution.py:135
  72.2 6.4 %shard_map.47 = (f32[2048,128]{1,0:T(8,128)S(1)}, f32[2048,128]{1,0:T(8,128)S(1)}, f32[2048,128]{1,0:T(8,128)S(1)}) custom-call(s32[1]{0:T(128)} %bitcast.core_ref, bf16[128,2048]{1,0:T(8,128)(2,1)S(1)} %collective-permute-done.8.q_ref, bf16[2,144,512]{2,1,0:T(8,128)(2,1)S(1)} %pad_maximum_fusion.1.refs_0_, ...), custom_call_target="tpu_custom_call" | custom-call | flops 4294967296 | bytes 4194304 | tf_op jit(solution)/shard_map/pallas_call | solution.py:110
  78.6 0.0 collective-permute-done.11.refs_1_.refs_3_
  78.6 3.5 %shard_map.49 = bf16[128,2048]{1,0:T(8,128)(2,1)S(1)} custom-call(s32[1]{0:T(128)} %bitcast.core_ref, bf16[128,2048]{1,0:T(8,128)(2,1)S(1)} %collective-permute-done.5.q_ref, bf16[2,144,512]{2,1,0:T(8,128)(2,1)S(1)} %pad_maximum_fusion.1.refs_0_, bf16[2,2,144,512]{3,2,1,0:T(8,128)(2,1)S(1)} %collective-permute-done.9.refs_5_.refs_1_, ...), custom_call_target="tpu_custom_call" | custom-call | flops 2147483648 | bytes 4194304 | tf_op jit(solution)/shard_map/pallas_call | solution.py:110
  82.1 4.4 %collective-permute-start.12 = (bf16[128,2048]{1,0:T(8,128)(2,1)S(1)}, bf16[128,2048]{1,0:T(8,128)(2,1)S(1)}, u32[]{:S(2)}, u32[]{:S(2)}) collective-permute-start(bf16[128,2048]{1,0:T(8,128)(2,1)S(1)} %shard_map.49), channel_id=1, source_target_pairs={{0,1},{1,0},{2,3},{3,2},{4,5},{5,4},{6,7},{7,6},{8,9},{9,8},{10,11... | collective-permute-start | bytes 1572872 | tf_op jit(solution)/shard_map/ppermute | solution.py:138
  86.5 1.4 %shard_map.48 = bf16[128,2048]{1,0:T(8,128)(2,1)S(1)} custom-call(s32[1]{0:T(128)} %bitcast.core_ref, bf16[128,2048]{1,0:T(8,128)(2,1)S(1)} %collective-permute-done.8.q_ref, bf16[2,144,512]{2,1,0:T(8,128)(2,1)S(1)} %pad_maximum_fusion.1.refs_0_, bf16[2,144,512]{2,1,0:T(8,128)(2,1)S(1)} %collective-permute-done.11.refs_1_.refs_3_, ...), custom_call_target="tpu_custom_call" | custom-call | flops 536870912 | bytes 4194304 | tf_op jit(solution)/shard_map/pallas_call | solution.py:110
  87.9 0.1 collective-permute-done.12
  88.0 1.2 %maximum_select_fusion = bf16[1,128,4096]{2,1,0:T(8,128)(2,1)} fusion(bf16[1,128,2048]{2,1,0:T(8,128)(2,1)S(1)} %bitcast.19, bf16[1,128,2048]{2,1,0:T(8,128)(2,1)S(1)} %bitcast.15, pred[]{:T(512)S(6)} %eq.5), kind=kLoop, calls=%fused_computation | loop fusion | flops 4718592 | bytes 2097153 | tf_op jit(solution)/shard_map/jit(_where)/select_n | solution.py:171
  (6 shorter events, 0.2 us)
Async XLA Ops:
  0.7 29.4 %copy-start = (bf16[1,128,4096]{2,1,0:T(8,128)(2,1)S(1)}, bf16[1,128,4096]{2,1,0:T(8,128)(2,1)}, u32[]{:S(2)}) copy-start(bf16[1,128,4096]{2,1,0:T(8,128)(2,1)} %param.4) | copy-start | bytes 3145732
  1.8 20.7 %collective-permute-start.2 = (bf16[144,512]{1,0:T(8,128)(2,1)S(1)}, bf16[144,512]{1,0:T(8,128)(2,1)S(1)}, u32[]{:S(2)}, u32[]{:S(2)}) collective-permute-start(bf16[144,512]{1,0:T(8,128)(2,1)S(1)} %get-tuple-element.89), channel_id=1, source_target_pairs={{0,72},{1,73},{2,74},{3,75},{4,76},{5,77},{6,78},{7,79},{8,80},{9,... | collective-permute-start | bytes 442376 | tf_op jit(solution)/shard_map/ppermute | solution.py:129
  7.6 15.9 %collective-permute-start.3 = (bf16[144,512]{1,0:T(8,128)(2,1)S(1)}, bf16[144,512]{1,0:T(8,128)(2,1)S(1)}, u32[]{:S(2)}, u32[]{:S(2)}) collective-permute-start(bf16[144,512]{1,0:T(8,128)(2,1)S(1)} %get-tuple-element.90), channel_id=1, source_target_pairs={{0,73},{1,72},{2,75},{3,74},{4,77},{5,76},{6,79},{7,78},{8,81},{9,... | collective-permute-start | bytes 442376 | tf_op jit(solution)/shard_map/ppermute | solution.py:129
  13.5 13.4 %collective-permute-start = (bf16[144,512]{1,0:T(8,128)(2,1)S(1)}, bf16[144,512]{1,0:T(8,128)(2,1)S(1)}, u32[]{:S(2)}, u32[]{:S(2)}) collective-permute-start(bf16[144,512]{1,0:T(8,128)(2,1)S(1)} %get-tuple-element.89), channel_id=1, source_target_pairs={{0,64},{1,65},{2,66},{3,67},{4,68},{5,69},{6,70},{7,71},{8,72},{9,... | collective-permute-start | bytes 442376 | tf_op jit(solution)/shard_map/ppermute | solution.py:129
  17.5 12.6 %collective-permute-start.1 = (bf16[144,512]{1,0:T(8,128)(2,1)S(1)}, bf16[144,512]{1,0:T(8,128)(2,1)S(1)}, u32[]{:S(2)}, u32[]{:S(2)}) collective-permute-start(bf16[144,512]{1,0:T(8,128)(2,1)S(1)} %get-tuple-element.90), channel_id=1, source_target_pairs={{0,65},{1,64},{2,67},{3,66},{4,69},{5,68},{6,71},{7,70},{8,73},{9,... | collective-permute-start | bytes 442376 | tf_op jit(solution)/shard_map/ppermute | solution.py:129
  30.1 17.3 %collective-permute-start.5 = (bf16[128,2048]{1,0:T(8,128)(2,1)S(1)}, bf16[128,2048]{1,0:T(8,128)(2,1)S(1)}, u32[]{:S(2)}, u32[]{:S(2)}) collective-permute-start(bf16[128,2048]{1,0:T(8,128)(2,1)S(1)} %slice_select_fusion.1), channel_id=1, source_target_pairs={{0,65},{1,64},{2,67},{3,66},{4,69},{5,68},{6,71},{7,70},{8,73},{9,... | collective-permute-start | bytes 1572872 | tf_op jit(solution)/shard_map/ppermute | solution.py:129
  32.1 11.3 %collective-permute-start.4 = (bf16[2,144,512]{2,1,0:T(8,128)(2,1)S(1)}, bf16[2,144,512]{2,1,0:T(8,128)(2,1)S(1)}, u32[]{:S(2)}, u32[]{:S(2)}) collective-permute-start(bf16[2,144,512]{2,1,0:T(8,128)(2,1)S(1)} %pad_maximum_fusion.2.refs_1_), channel_id=1, source_target_pairs={{0,8},{1,9},{2,10},{3,11},{4,12},{5,13},{6,14},{7,15},{8,16},{9,17... | collective-permute-start | bytes 884744 | tf_op jit(solution)/shard_map/ppermute | solution.py:132
  34.1 13.4 %collective-permute-start.6 = (bf16[2,144,512]{2,1,0:T(8,128)(2,1)S(1)}, bf16[2,144,512]{2,1,0:T(8,128)(2,1)S(1)}, u32[]{:S(2)}, u32[]{:S(2)}) collective-permute-start(bf16[2,144,512]{2,1,0:T(8,128)(2,1)S(1)} %get-tuple-element.88), channel_id=1, source_target_pairs={{0,2},{1,63},{2,4},{3,1},{4,6},{5,3},{6,8},{7,5},{8,10},{9,7},{10,... | collective-permute-start | bytes 884744 | tf_op jit(solution)/shard_map/ppermute | solution.py:135
  40.8 11.6 %collective-permute-start.7 = (bf16[2,144,512]{2,1,0:T(8,128)(2,1)S(1)}, bf16[2,144,512]{2,1,0:T(8,128)(2,1)S(1)}, u32[]{:S(2)}, u32[]{:S(2)}) collective-permute-start(bf16[2,144,512]{2,1,0:T(8,128)(2,1)S(1)} %get-tuple-element.87), channel_id=1, source_target_pairs={{0,62},{1,3},{2,0},{3,5},{4,2},{5,7},{6,4},{7,9},{8,6},{9,11},{10,... | collective-permute-start | bytes 884744 | tf_op jit(solution)/shard_map/ppermute | solution.py:135
  52.5 17.5 %collective-permute-start.9 = (bf16[2,2,144,512]{3,2,1,0:T(8,128)(2,1)S(1)}, bf16[2,2,144,512]{3,2,1,0:T(8,128)(2,1)S(1)}, u32[]{:S(2)}, u32[]{:S(2)}) collective-permute-start(bf16[2,2,144,512]{3,2,1,0:T(8,128)(2,1)S(1)} %pad_maximum_fusion), channel_id=1, source_target_pairs={{0,2},{1,63},{2,4},{3,1},{4,6},{5,3},{6,8},{7,5},{8,10},{9,7},{10,... | collective-permute-start | bytes 1769480 | tf_op jit(solution)/shard_map/ppermute | solution.py:135
  54.5 15.5 %collective-permute-start.8 = (bf16[128,2048]{1,0:T(8,128)(2,1)S(1)}, bf16[128,2048]{1,0:T(8,128)(2,1)S(1)}, u32[]{:S(2)}, u32[]{:S(2)}) collective-permute-start(bf16[128,2048]{1,0:T(8,128)(2,1)S(1)} %slice_select_fusion), channel_id=1, source_target_pairs={{0,64},{1,65},{2,66},{3,67},{4,68},{5,69},{6,70},{7,71},{8,72},{9,... | collective-permute-start | bytes 1572872 | tf_op jit(solution)/shard_map/ppermute | solution.py:129
  56.5 13.6 %collective-permute-start.10 = (bf16[2,144,512]{2,1,0:T(8,128)(2,1)S(1)}, bf16[2,144,512]{2,1,0:T(8,128)(2,1)S(1)}, u32[]{:S(2)}, u32[]{:S(2)}) collective-permute-start(bf16[2,144,512]{2,1,0:T(8,128)(2,1)S(1)} %collective-permute-done.7.refs_4_), channel_id=1, source_target_pairs={{0,8},{1,9},{2,10},{3,11},{4,12},{5,13},{6,14},{7,15},{8,16},{9,17... | collective-permute-start | bytes 884744 | tf_op jit(solution)/shard_map/ppermute | solution.py:132
  70.1 8.5 %collective-permute-start.11 = (bf16[2,144,512]{2,1,0:T(8,128)(2,1)S(1)}, bf16[2,144,512]{2,1,0:T(8,128)(2,1)S(1)}, u32[]{:S(2)}, u32[]{:S(2)}) collective-permute-start(bf16[2,144,512]{2,1,0:T(8,128)(2,1)S(1)} %slice_bitcast_fusion), channel_id=1, source_target_pairs={{0,2},{1,63},{2,4},{3,1},{4,6},{5,3},{6,8},{7,5},{8,10},{9,7},{10,... | collective-permute-start | bytes 884744 | tf_op jit(solution)/shard_map/ppermute | solution.py:135
  82.1 5.9 %collective-permute-start.12 = (bf16[128,2048]{1,0:T(8,128)(2,1)S(1)}, bf16[128,2048]{1,0:T(8,128)(2,1)S(1)}, u32[]{:S(2)}, u32[]{:S(2)}) collective-permute-start(bf16[128,2048]{1,0:T(8,128)(2,1)S(1)} %shard_map.49), channel_id=1, source_target_pairs={{0,1},{1,0},{2,3},{3,2},{4,5},{5,4},{6,7},{7,6},{8,9},{9,8},{10,11... | collective-permute-start | bytes 1572872 | tf_op jit(solution)/shard_map/ppermute | solution.py:138

commit v4 on v3

--- a/solution.py
+++ b/solution.py
@@ -121,7 +121,8 @@
 
 
 def shards(queries, keys, values, doc_ids):
-    core = lax.axis_index("sp") % 2
+    place = lax.axis_index("sp")
+    core, column = place % 2, place // 2 % 4
     first = core == 0
 
     def section(block, flip, dy=0):
@@ -131,8 +132,11 @@
     def along_y(block):
         return lax.ppermute(block, "sp", [(s, (s + 8) % 64) for s in range(64)])
 
-    def along_x(block, step0, step1):
-        return lax.ppermute(block, "sp", [(s, (s + 2 * (step1 if s % 2 else step0)) % 64) for s in range(64)])
+    def even_pair(block):
+        return lax.ppermute(block, "sp", [(s, s ^ 2) for s in range(64)])
+
+    def odd_pair(block):
+        return lax.ppermute(block, "sp", [(s, s // 8 * 8 + (s + (2 if s & 2 else -2)) % 8) for s in range(64)])
 
     def swap(block):
         return lax.ppermute(block, "sp", [(s, s ^ 1) for s in range(64)])
@@ -146,28 +150,27 @@
     half0, half1 = part(0), part(1)
     mine, other = jnp.where(first, half0, half1), jnp.where(first, half1, half0)
     q = queries[0]
-    b0 = jnp.stack([section(mine, 0), section(other, 1)])
     b4 = jnp.stack([section(mine, 0, 1), section(other, 1, 1)])
-    b0, b4, q = lax.optimization_barrier((b0, b4, q))
+    b4, q = lax.optimization_barrier((b4, q))
+    b8 = along_y(b4)
+    e1 = even_pair(b4)
+    f1 = odd_pair(b4)
+    b0 = jnp.stack(lax.optimization_barrier((section(mine, 0), section(other, 1))))
     qf = section(jnp.where(first, q[:, 2048:], q[:, :2048]), 1)
-    b8 = along_y(b4)
-    p1 = along_x(jnp.where(first, b0, b4), 1, -1)
-    p2 = along_x(jnp.where(first, b4, b0), -1, 1)
-    b8, qf = lax.optimization_barrier((b8, qf))
-    qf, b8, p1, p2, q, b0, b4 = lax.optimization_barrier((qf, b8, p1, p2, q, b0, b4))
+    b8, e1, f1, b0, b4 = lax.optimization_barrier((b8, e1, f1, b0, b4))
     qs = section(jnp.where(first, q[:, :2048], q[:, 2048:]), 0)
-    p3 = along_x(jnp.stack([jnp.where(first, b4, b8), p1]), 1, -1)
-    p4 = along_y(p2)
-    place = core[None].astype(jnp.int32)
-    state = attend(place, 1, qf, b0, [b4, b8, p1, p2], own=True)
-    qs, qf = lax.optimization_barrier((qs, qf))
-    qs, p3, p4, qf, b0, b4, b8, p1, p2, *state = lax.optimization_barrier((qs, p3, p4, qf, b0, b4, b8, p1, p2, *state))
-    p5 = along_x(p3[0], 1, -1)
-    state2 = attend(place, 0, qs, b0, [b4, b8, p1, p2, p3, p4], own=True)
-    p5, qs, qf, b0, p3, p4, *state2 = lax.optimization_barrier((p5, qs, qf, b0, p3, p4, *state2))
-    of_ = attend(place, 1, qf, b0, [p3, p4, p5], state=state, last=True)
+    f2 = odd_pair(jnp.where(column < 2, b0, b8))
+    e2 = even_pair(jnp.where(column % 2 == 0, b0, b8))
+    at = core[None].astype(jnp.int32)
+    state = attend(at, 1, qf, b0, [b4, b8, e1, f1], own=True)
+    e2, f2, qf, b0, b4, b8, e1, f1, *state = lax.optimization_barrier((e2, f2, qf, b0, b4, b8, e1, f1, *state))
+    e3 = even_pair(f2)
+    f3 = odd_pair(e1)
+    state2 = attend(at, 0, qs, b0, [b4, b8, e1, f1, e2, f2], own=True)
+    e3, f3, qs, qf, b0, e2, f2, *state2 = lax.optimization_barrier((e3, f3, qs, qf, b0, e2, f2, *state2))
+    of_ = attend(at, 1, qf, b0, [e2, f2, e3, f3], state=state, last=True)
     got = swap(of_)
-    os_ = attend(place, 0, qs, b0, [p5], state=state2, last=True)
+    os_ = attend(at, 0, qs, b0, [e3, f3], state=state2, last=True)
     out = jnp.where(first, jnp.concatenate([os_, got], axis=1), jnp.concatenate([got, os_], axis=1))
     return out[None]
 

time: 89.7 us -> 80.8 us (0.901)
  waiting for transfers between devices: 25 us -> 9.97 us
  starting transfers between devices: 45.4 us -> 49.8 us
  other arithmetic: 2.23 us -> 3.96 us
  Pallas kernels: 15.3 us -> 14.2 us
    ppermute x6, waiting for transfers between devices: 19.3 us -> 5.73 us  [section(): return lax.ppermute(block, ('pp', 'sp'), pairs)]
    ppermute x6, starting transfers between devices: 24.5 us -> 28.2 us  [section(): return lax.ppermute(block, ('pp', 'sp'), pairs)]
    ppermute x4 -> x6, starting transfers between devices: 12.7 us -> 16.1 us  [the longest x3 8.85 us: odd_pair(): lax.ppermute(block, 'sp', [(s, s // 8 * 8 + (s + (2 if s & 2 else -2)) %...]
    ppermute x2 -> x1, starting transfers between devices: 3.84 us -> 2.12 us  [along_y(): return lax.ppermute(block, 'sp', [(s, (s + 8) % 64) for s in range(64)])]
    pallas_call x4, Pallas kernels: 15.3 us -> 14.2 us  [attend(): pl.pallas_call(functools.partial(piece, half, own, bool(state), last, 1 +...]
    ppermute x1, starting transfers between devices: 4.39 us -> 3.4 us  [swap(): return lax.ppermute(block, 'sp', [(s, s ^ 1) for s in range(64)])]
    ppermute x4 -> x6, waiting for transfers between devices: 4.95 us -> 4.24 us  [the longest x3 4.23 us: odd_pair(): lax.ppermute(block, 'sp', [(s, s // 8 * 8 + (s + (2 if s & 2 else -2)) %...]
  transfers between devices with their start and end apart: 13 -> 14, of which waited for: 8 -> 5; matrix products, arithmetic and copies ran while one was open for 0% -> 2% of each run, Pallas kernels for 13% -> 14%
where the time goes in v4:
time: 80.8 us; the launch traced here: 79.9 us
  starting transfers between devices  49.8 us (62%)
  Pallas kernels  14.2 us (18%)
  waiting for transfers between devices  9.97 us (12%)
  other arithmetic  3.96 us (5%)
  local copies, waits for them, and re-layouts  1.61 us (2%)
    ppermute x6, starting transfers between devices, section(): return lax.ppermute(block, ('pp', 'sp'), pairs)  28.2 us
    pallas_call x4, Pallas kernels, attend(): pl.pallas_call(functools.partial(piece, half, own, bool(state), last, 1 +...  14.2 us
    ppermute x3, starting transfers between devices, odd_pair(): lax.ppermute(block, 'sp', [(s, s // 8 * 8 + (s + (2 if s & 2 else -2)) %...  8.85 us
    ppermute x3, starting transfers between devices, even_pair(): return lax.ppermute(block, 'sp', [(s, s ^ 2) for s in range(64)])  7.25 us
    ppermute x6, waiting for transfers between devices, section(): return lax.ppermute(block, ('pp', 'sp'), pairs)  5.73 us
    ppermute x3, waiting for transfers between devices, odd_pair(): lax.ppermute(block, 'sp', [(s, s // 8 * 8 + (s + (2 if s & 2 else -2)) %...  4.23 us
    ppermute x1, starting transfers between devices, swap(): return lax.ppermute(block, 'sp', [(s, s ^ 1) for s in range(64)])  3.4 us
    ppermute x1, starting transfers between devices, along_y(): return lax.ppermute(block, 'sp', [(s, (s + 8) % 64) for s in range(64)])  2.12 us
  transfers between devices with their start and end apart: 14, of which 5 were waited for; matrix products, arithmetic and copies ran while one was open for 2% of the time, Pallas kernels for 14%

profile of v4, /device:TPU:1, one launch (start us, length us, event | category | flops | bytes accessed | tf_op | source)
XLA Modules:
  0.0 79.9 jit_solution(6395958709919574174)
XLA Ops:
  0.0 0.0 copy-start
  0.0 0.7 convert_element_type.6
  0.8 1.0 %fusion.3 = (bf16[128,256]{1,0:T(8,128)(2,1)S(1)}, bf16[128,256]{1,0:T(8,128)(2,1)S(1)}, bf16[128,256]{1,0:T(8,128)(2,1)S(1)}, bf16[128,256]{1,0:T(8,128)(2,1)S(1)}) fusion(bf16[128,512]{1,0:T(8,128)(2,1)} %bitcast.16, bf16[128,512]{1,0:T(8,128)(2,1)} %bitcast.17), kind=kLoop, calls=%fused_computation.13 | loop fusion | bytes 524288 | tf_op jit(solution)/shard_map/slice | solution.py:148
  1.8 5.8 %collective-permute-start = (bf16[144,512]{1,0:T(8,128)(2,1)S(1)}, bf16[144,512]{1,0:T(8,128)(2,1)S(1)}, u32[]{:S(2)}, u32[]{:S(2)}) collective-permute-start(bf16[144,512]{1,0:T(8,128)(2,1)S(1)} %get-tuple-element.81), channel_id=1, source_target_pairs={{0,72},{1,73},{2,74},{3,75},{4,76},{5,77},{6,78},{7,79},{8,80},{9,... | collective-permute-start | bytes 442376 | tf_op jit(solution)/shard_map/ppermute | solution.py:130
  7.6 5.9 %collective-permute-start.1 = (bf16[144,512]{1,0:T(8,128)(2,1)S(1)}, bf16[144,512]{1,0:T(8,128)(2,1)S(1)}, u32[]{:S(2)}, u32[]{:S(2)}) collective-permute-start(bf16[144,512]{1,0:T(8,128)(2,1)S(1)} %get-tuple-element.82), channel_id=1, source_target_pairs={{0,73},{1,72},{2,75},{3,74},{4,77},{5,76},{6,79},{7,78},{8,81},{9,... | collective-permute-start | bytes 442376 | tf_op jit(solution)/shard_map/ppermute | solution.py:130
  13.5 4.0 %collective-permute-start.5 = (bf16[144,512]{1,0:T(8,128)(2,1)S(1)}, bf16[144,512]{1,0:T(8,128)(2,1)S(1)}, u32[]{:S(2)}, u32[]{:S(2)}) collective-permute-start(bf16[144,512]{1,0:T(8,128)(2,1)S(1)} %get-tuple-element.81), channel_id=1, source_target_pairs={{0,64},{1,65},{2,66},{3,67},{4,68},{5,69},{6,70},{7,71},{8,72},{9,... | collective-permute-start | bytes 442376 | tf_op jit(solution)/shard_map/ppermute | solution.py:130
  17.5 4.9 %collective-permute-start.6 = (bf16[144,512]{1,0:T(8,128)(2,1)S(1)}, bf16[144,512]{1,0:T(8,128)(2,1)}, u32[]{:S(2)}, u32[]{:S(2)}) collective-permute-start(bf16[144,512]{1,0:T(8,128)(2,1)S(1)} %get-tuple-element.82), channel_id=1, source_target_pairs={{0,65},{1,64},{2,67},{3,66},{4,69},{5,68},{6,71},{7,70},{8,73},{9,... | collective-permute-start | bytes 442376 | tf_op jit(solution)/shard_map/ppermute | solution.py:130
  22.4 0.0 collective-permute-done
  22.4 1.1 %collective-permute-done.1 = bf16[144,512]{1,0:T(8,128)(2,1)S(1)} collective-permute-done((bf16[144,512]{1,0:T(8,128)(2,1)S(1)}, bf16[144,512]{1,0:T(8,128)(2,1)S(1)}, u32[]{:S(2)}, u32[]{:S(2)}) %collective-permute-start.1) | collective-permute-done | bytes 147488 | tf_op jit(solution)/shard_map/ppermute | solution.py:130
  23.6 2.1 %collective-permute-start.2 = (bf16[2,144,512]{2,1,0:T(8,128)(2,1)S(1)}, bf16[2,144,512]{2,1,0:T(8,128)(2,1)S(1)}, u32[]{:S(2)}, u32[]{:S(2)}) collective-permute-start(bf16[2,144,512]{2,1,0:T(8,128)(2,1)S(1)} %pad_maximum_fusion.refs_1_), channel_id=1, source_target_pairs={{0,8},{1,9},{2,10},{3,11},{4,12},{5,13},{6,14},{7,15},{8,16},{9,17... | collective-permute-start | bytes 884744 | tf_op jit(solution)/shard_map/ppermute | solution.py:133
  25.7 3.1 %collective-permute-start.3 = (bf16[2,144,512]{2,1,0:T(8,128)(2,1)S(1)}, bf16[2,144,512]{2,1,0:T(8,128)(2,1)S(1)}, u32[]{:S(2)}, u32[]{:S(2)}) collective-permute-start(bf16[2,144,512]{2,1,0:T(8,128)(2,1)S(1)} %pad_maximum_fusion.refs_1_), channel_id=1, source_target_pairs={{0,2},{1,3},{2,0},{3,1},{4,6},{5,7},{6,4},{7,5},{8,10},{9,11},{10,... | collective-permute-start | bytes 884744 | tf_op jit(solution)/shard_map/ppermute | solution.py:136
  28.8 3.7 %collective-permute-start.4 = (bf16[2,144,512]{2,1,0:T(8,128)(2,1)S(1)}, bf16[2,144,512]{2,1,0:T(8,128)(2,1)S(1)}, u32[]{:S(2)}, u32[]{:S(2)}) collective-permute-start(bf16[2,144,512]{2,1,0:T(8,128)(2,1)S(1)} %pad_maximum_fusion.refs_1_), channel_id=1, source_target_pairs={{0,6},{1,7},{2,4},{3,5},{4,2},{5,3},{6,0},{7,1},{8,14},{9,15},{10,... | collective-permute-start | bytes 884744 | tf_op jit(solution)/shard_map/ppermute | solution.py:139
  32.6 0.0 copy-done
  32.6 0.9 %broadcast_select_fusion = (bf16[128,2048]{1,0:T(8,128)(2,1)S(1)}, bf16[128,2048]{1,0:T(8,128)(2,1)}) fusion(pred[]{:T(512)S(6)} %eq.10, bf16[128,4096]{1,0:T(8,128)(2,1)S(1)} %bitcast.11), kind=kLoop, calls=%fused_computation.1 | loop fusion | flops 524288 | bytes 2097153 | tf_op jit(solution)/shard_map/jit(_where)/select_n | solution.py:161
  33.4 0.0 collective-permute-done.5
  33.4 0.0 copy-start.1
  33.4 0.7 copy-done.1
  34.1 4.5 %collective-permute-start.9 = (bf16[128,2048]{1,0:T(8,128)(2,1)}, bf16[128,2048]{1,0:T(8,128)(2,1)S(1)}, u32[]{:S(2)}, u32[]{:S(2)}) collective-permute-start(bf16[128,2048]{1,0:T(8,128)(2,1)} %get-tuple-element.78), channel_id=1, source_target_pairs={{0,65},{1,64},{2,67},{3,66},{4,69},{5,68},{6,71},{7,70},{8,73},{9,... | collective-permute-start | bytes 1572872 | tf_op jit(solution)/shard_map/ppermute | solution.py:130
  38.6 0.0 collective-permute-done.6
  38.6 3.1 %collective-permute-start.12 = (bf16[128,2048]{1,0:T(8,128)(2,1)S(1)}, bf16[128,2048]{1,0:T(8,128)(2,1)S(1)}, u32[]{:S(2)}, u32[]{:S(2)}) collective-permute-start(bf16[128,2048]{1,0:T(8,128)(2,1)S(1)} %get-tuple-element.77), channel_id=1, source_target_pairs={{0,64},{1,65},{2,66},{3,67},{4,68},{5,69},{6,70},{7,71},{8,72},{9,... | collective-permute-start | bytes 1572872 | tf_op jit(solution)/shard_map/ppermute | solution.py:130
  41.8 1.0 %pad_maximum_fusion.1.refs_0_ = bf16[2,144,512]{2,1,0:T(8,128)(2,1)S(1)} fusion(bf16[1,144,512]{2,1,0:T(8,128)(2,1)} %bitcast.7, bf16[1,144,512]{2,1,0:T(8,128)(2,1)} %bitcast.13), kind=kLoop, calls=%fused_computation.5 | loop fusion | flops 147456 | bytes 589824 | tf_op jit(solution)/shard_map/stack | solution.py:158
  42.8 0.0 collective-permute-done.2.refs_2_
  42.8 0.0 collective-permute-done.3.refs_3_
  42.8 0.0 collective-permute-done.4.refs_4_
  42.9 2.2 %collective-permute-start.7 = (bf16[2,144,512]{2,1,0:T(8,128)(2,1)S(1)}, bf16[2,144,512]{2,1,0:T(8,128)(2,1)S(1)}, u32[]{:S(2)}, u32[]{:S(2)}) collective-permute-start(bf16[2,144,512]{2,1,0:T(8,128)(2,1)S(1)} %get-tuple-element.80), channel_id=1, source_target_pairs={{0,2},{1,3},{2,0},{3,1},{4,6},{5,7},{6,4},{7,5},{8,10},{9,11},{10,... | collective-permute-start | bytes 884744 | tf_op jit(solution)/shard_map/ppermute | solution.py:136
  45.1 2.5 %collective-permute-start.8 = (bf16[2,144,512]{2,1,0:T(8,128)(2,1)S(1)}, bf16[2,144,512]{2,1,0:T(8,128)(2,1)S(1)}, u32[]{:S(2)}, u32[]{:S(2)}) collective-permute-start(bf16[2,144,512]{2,1,0:T(8,128)(2,1)S(1)} %get-tuple-element.79), channel_id=1, source_target_pairs={{0,6},{1,7},{2,4},{3,5},{4,2},{5,3},{6,0},{7,1},{8,14},{9,15},{10,... | collective-permute-start | bytes 884744 | tf_op jit(solution)/shard_map/ppermute | solution.py:139
  47.6 3.6 %collective-permute-done.9.q_ref = bf16[128,2048]{1,0:T(8,128)(2,1)S(1)} collective-permute-done((bf16[128,2048]{1,0:T(8,128)(2,1)}, bf16[128,2048]{1,0:T(8,128)(2,1)S(1)}, u32[]{:S(2)}, u32[]{:S(2)}) %collective-permute-start.9) | collective-permute-done | bytes 524320 | tf_op jit(solution)/shard_map/ppermute | solution.py:130
  51.1 3.8 %shard_map.46 = (f32[2048,128]{1,0:T(8,128)S(1)}, f32[2048,128]{1,0:T(8,128)S(1)}, f32[2048,128]{1,0:T(8,128)S(1)}) custom-call(s32[1]{0:T(128)} %bitcast.core_ref, bf16[128,2048]{1,0:T(8,128)(2,1)S(1)} %collective-permute-done.9.q_ref, bf16[2,144,512]{2,1,0:T(8,128)(2,1)S(1)} %pad_maximum_fusion.1.refs_0_, ...), custom_call_target="tpu_custom_call" | custom-call | flops 2684354560 | bytes 4194304 | tf_op jit(solution)/shard_map/pallas_call | solution.py:110
  54.9 0.0 collective-permute-done.7.refs_5_.refs_1_
  54.9 2.3 %collective-permute-done.8.refs_6_.refs_2_ = bf16[2,144,512]{2,1,0:T(8,128)(2,1)S(1)} collective-permute-done((bf16[2,144,512]{2,1,0:T(8,128)(2,1)S(1)}, bf16[2,144,512]{2,1,0:T(8,128)(2,1)S(1)}, u32[]{:S(2)}, u32[]{:S(2)}) %collective-permute-start.8) | collective-permute-done | bytes 294944 | tf_op jit(solution)/shard_map/ppermute | solution.py:139
  57.2 1.9 %collective-permute-start.10 = (bf16[2,144,512]{2,1,0:T(8,128)(2,1)S(1)}, bf16[2,144,512]{2,1,0:T(8,128)(2,1)S(1)}, u32[]{:S(2)}, u32[]{:S(2)}) collective-permute-start(bf16[2,144,512]{2,1,0:T(8,128)(2,1)S(1)} %collective-permute-done.8.refs_6_.refs_2_), channel_id=1, source_target_pairs={{0,2},{1,3},{2,0},{3,1},{4,6},{5,7},{6,4},{7,5},{8,10},{9,11},{10,... | collective-permute-start | bytes 884744 | tf_op jit(solution)/shard_map/ppermute | solution.py:136
  59.1 2.7 %collective-permute-start.11 = (bf16[2,144,512]{2,1,0:T(8,128)(2,1)S(1)}, bf16[2,144,512]{2,1,0:T(8,128)(2,1)S(1)}, u32[]{:S(2)}, u32[]{:S(2)}) collective-permute-start(bf16[2,144,512]{2,1,0:T(8,128)(2,1)S(1)} %collective-permute-done.3.refs_3_), channel_id=1, source_target_pairs={{0,6},{1,7},{2,4},{3,5},{4,2},{5,3},{6,0},{7,1},{8,14},{9,15},{10,... | collective-permute-start | bytes 884744 | tf_op jit(solution)/shard_map/ppermute | solution.py:139
  61.8 1.1 %collective-permute-done.12.q_ref = bf16[128,2048]{1,0:T(8,128)(2,1)S(1)} collective-permute-done((bf16[128,2048]{1,0:T(8,128)(2,1)S(1)}, bf16[128,2048]{1,0:T(8,128)(2,1)S(1)}, u32[]{:S(2)}, u32[]{:S(2)}) %collective-permute-start.12) | collective-permute-done | bytes 524320 | tf_op jit(solution)/shard_map/ppermute | solution.py:130
  62.8 5.3 %shard_map.47 = (f32[2048,128]{1,0:T(8,128)S(1)}, f32[2048,128]{1,0:T(8,128)S(1)}, f32[2048,128]{1,0:T(8,128)S(1)}) custom-call(s32[1]{0:T(128)} %bitcast.core_ref, bf16[128,2048]{1,0:T(8,128)(2,1)S(1)} %collective-permute-done.12.q_ref, bf16[2,144,512]{2,1,0:T(8,128)(2,1)S(1)} %pad_maximum_fusion.1.refs_0_, ...), custom_call_target="tpu_custom_call" | custom-call | flops 3758096384 | bytes 4194304 | tf_op jit(solution)/shard_map/pallas_call | solution.py:110
  68.2 0.0 collective-permute-done.10.refs_1_.refs_3_
  68.2 2.0 %collective-permute-done.11.refs_2_.refs_4_ = bf16[2,144,512]{2,1,0:T(8,128)(2,1)S(1)} collective-permute-done((bf16[2,144,512]{2,1,0:T(8,128)(2,1)S(1)}, bf16[2,144,512]{2,1,0:T(8,128)(2,1)S(1)}, u32[]{:S(2)}, u32[]{:S(2)}) %collective-permute-start.11) | collective-permute-done | bytes 294944 | tf_op jit(solution)/shard_map/ppermute | solution.py:139
  70.2 3.2 %shard_map.49 = bf16[128,2048]{1,0:T(8,128)(2,1)S(1)} custom-call(s32[1]{0:T(128)} %bitcast.core_ref, bf16[128,2048]{1,0:T(8,128)(2,1)S(1)} %collective-permute-done.9.q_ref, bf16[2,144,512]{2,1,0:T(8,128)(2,1)S(1)} %pad_maximum_fusion.1.refs_0_, bf16[2,144,512]{2,1,0:T(8,128)(2,1)S(1)} %collective-permute-done.7.refs_5_.refs_1_, ...), custom_call_target="tpu_custom_call" | custom-call | flops 2147483648 | bytes 4194304 | tf_op jit(solution)/shard_map/pallas_call | solution.py:110
  73.4 3.4 %collective-permute-start.13 = (bf16[128,2048]{1,0:T(8,128)(2,1)S(1)}, bf16[128,2048]{1,0:T(8,128)(2,1)S(1)}, u32[]{:S(2)}, u32[]{:S(2)}) collective-permute-start(bf16[128,2048]{1,0:T(8,128)(2,1)S(1)} %shard_map.49), channel_id=1, source_target_pairs={{0,1},{1,0},{2,3},{3,2},{4,5},{5,4},{6,7},{7,6},{8,9},{9,8},{10,11... | collective-permute-start | bytes 1572872 | tf_op jit(solution)/shard_map/ppermute | solution.py:142
  76.8 1.9 %shard_map.48 = bf16[128,2048]{1,0:T(8,128)(2,1)S(1)} custom-call(s32[1]{0:T(128)} %bitcast.core_ref, bf16[128,2048]{1,0:T(8,128)(2,1)S(1)} %collective-permute-done.12.q_ref, bf16[2,144,512]{2,1,0:T(8,128)(2,1)S(1)} %pad_maximum_fusion.1.refs_0_, bf16[2,144,512]{2,1,0:T(8,128)(2,1)S(1)} %collective-permute-done.10.refs_1_.refs_3_, ...), custom_call_target="tpu_custom_call" | custom-call | flops 1073741824 | bytes 4194304 | tf_op jit(solution)/shard_map/pallas_call | solution.py:110
  78.7 0.0 collective-permute-done.13
  78.7 1.2 %maximum_select_fusion = bf16[1,128,4096]{2,1,0:T(8,128)(2,1)} fusion(bf16[1,128,2048]{2,1,0:T(8,128)(2,1)S(1)} %bitcast.12, bf16[1,128,2048]{2,1,0:T(8,128)(2,1)S(1)} %bitcast.10, pred[]{:T(512)S(6)} %eq.10), kind=kLoop, calls=%fused_computation | loop fusion | flops 4718592 | bytes 2097153 | tf_op jit(solution)/shard_map/jit(_where)/select_n | solution.py:174
  (3 shorter events, 0.1 us)
Async XLA Ops:
  0.0 32.6 %copy-start = (bf16[1,128,4096]{2,1,0:T(8,128)(2,1)S(1)}, bf16[1,128,4096]{2,1,0:T(8,128)(2,1)}, u32[]{:S(2)}) copy-start(bf16[1,128,4096]{2,1,0:T(8,128)(2,1)} %param.4) | copy-start | bytes 3145732
  1.8 20.7 %collective-permute-start = (bf16[144,512]{1,0:T(8,128)(2,1)S(1)}, bf16[144,512]{1,0:T(8,128)(2,1)S(1)}, u32[]{:S(2)}, u32[]{:S(2)}) collective-permute-start(bf16[144,512]{1,0:T(8,128)(2,1)S(1)} %get-tuple-element.81), channel_id=1, source_target_pairs={{0,72},{1,73},{2,74},{3,75},{4,76},{5,77},{6,78},{7,79},{8,80},{9,... | collective-permute-start | bytes 442376 | tf_op jit(solution)/shard_map/ppermute | solution.py:130
  7.6 15.9 %collective-permute-start.1 = (bf16[144,512]{1,0:T(8,128)(2,1)S(1)}, bf16[144,512]{1,0:T(8,128)(2,1)S(1)}, u32[]{:S(2)}, u32[]{:S(2)}) collective-permute-start(bf16[144,512]{1,0:T(8,128)(2,1)S(1)} %get-tuple-element.82), channel_id=1, source_target_pairs={{0,73},{1,72},{2,75},{3,74},{4,77},{5,76},{6,79},{7,78},{8,81},{9,... | collective-permute-start | bytes 442376 | tf_op jit(solution)/shard_map/ppermute | solution.py:130
  13.5 20.0 %collective-permute-start.5 = (bf16[144,512]{1,0:T(8,128)(2,1)S(1)}, bf16[144,512]{1,0:T(8,128)(2,1)S(1)}, u32[]{:S(2)}, u32[]{:S(2)}) collective-permute-start(bf16[144,512]{1,0:T(8,128)(2,1)S(1)} %get-tuple-element.81), channel_id=1, source_target_pairs={{0,64},{1,65},{2,66},{3,67},{4,68},{5,69},{6,70},{7,71},{8,72},{9,... | collective-permute-start | bytes 442376 | tf_op jit(solution)/shard_map/ppermute | solution.py:130
  17.5 21.2 %collective-permute-start.6 = (bf16[144,512]{1,0:T(8,128)(2,1)S(1)}, bf16[144,512]{1,0:T(8,128)(2,1)}, u32[]{:S(2)}, u32[]{:S(2)}) collective-permute-start(bf16[144,512]{1,0:T(8,128)(2,1)S(1)} %get-tuple-element.82), channel_id=1, source_target_pairs={{0,65},{1,64},{2,67},{3,66},{4,69},{5,68},{6,71},{7,70},{8,73},{9,... | collective-permute-start | bytes 442376 | tf_op jit(solution)/shard_map/ppermute | solution.py:130
  23.6 19.2 %collective-permute-start.2 = (bf16[2,144,512]{2,1,0:T(8,128)(2,1)S(1)}, bf16[2,144,512]{2,1,0:T(8,128)(2,1)S(1)}, u32[]{:S(2)}, u32[]{:S(2)}) collective-permute-start(bf16[2,144,512]{2,1,0:T(8,128)(2,1)S(1)} %pad_maximum_fusion.refs_1_), channel_id=1, source_target_pairs={{0,8},{1,9},{2,10},{3,11},{4,12},{5,13},{6,14},{7,15},{8,16},{9,17... | collective-permute-start | bytes 884744 | tf_op jit(solution)/shard_map/ppermute | solution.py:133
  25.7 17.1 %collective-permute-start.3 = (bf16[2,144,512]{2,1,0:T(8,128)(2,1)S(1)}, bf16[2,144,512]{2,1,0:T(8,128)(2,1)S(1)}, u32[]{:S(2)}, u32[]{:S(2)}) collective-permute-start(bf16[2,144,512]{2,1,0:T(8,128)(2,1)S(1)} %pad_maximum_fusion.refs_1_), channel_id=1, source_target_pairs={{0,2},{1,3},{2,0},{3,1},{4,6},{5,7},{6,4},{7,5},{8,10},{9,11},{10,... | collective-permute-start | bytes 884744 | tf_op jit(solution)/shard_map/ppermute | solution.py:136
  28.8 14.0 %collective-permute-start.4 = (bf16[2,144,512]{2,1,0:T(8,128)(2,1)S(1)}, bf16[2,144,512]{2,1,0:T(8,128)(2,1)S(1)}, u32[]{:S(2)}, u32[]{:S(2)}) collective-permute-start(bf16[2,144,512]{2,1,0:T(8,128)(2,1)S(1)} %pad_maximum_fusion.refs_1_), channel_id=1, source_target_pairs={{0,6},{1,7},{2,4},{3,5},{4,2},{5,3},{6,0},{7,1},{8,14},{9,15},{10,... | collective-permute-start | bytes 884744 | tf_op jit(solution)/shard_map/ppermute | solution.py:139
  33.4 0.7 copy-start.1
  34.1 17.0 %collective-permute-start.9 = (bf16[128,2048]{1,0:T(8,128)(2,1)}, bf16[128,2048]{1,0:T(8,128)(2,1)S(1)}, u32[]{:S(2)}, u32[]{:S(2)}) collective-permute-start(bf16[128,2048]{1,0:T(8,128)(2,1)} %get-tuple-element.78), channel_id=1, source_target_pairs={{0,65},{1,64},{2,67},{3,66},{4,69},{5,68},{6,71},{7,70},{8,73},{9,... | collective-permute-start | bytes 1572872 | tf_op jit(solution)/shard_map/ppermute | solution.py:130
  38.6 24.2 %collective-permute-start.12 = (bf16[128,2048]{1,0:T(8,128)(2,1)S(1)}, bf16[128,2048]{1,0:T(8,128)(2,1)S(1)}, u32[]{:S(2)}, u32[]{:S(2)}) collective-permute-start(bf16[128,2048]{1,0:T(8,128)(2,1)S(1)} %get-tuple-element.77), channel_id=1, source_target_pairs={{0,64},{1,65},{2,66},{3,67},{4,68},{5,69},{6,70},{7,71},{8,72},{9,... | collective-permute-start | bytes 1572872 | tf_op jit(solution)/shard_map/ppermute | solution.py:130
  42.9 12.1 %collective-permute-start.7 = (bf16[2,144,512]{2,1,0:T(8,128)(2,1)S(1)}, bf16[2,144,512]{2,1,0:T(8,128)(2,1)S(1)}, u32[]{:S(2)}, u32[]{:S(2)}) collective-permute-start(bf16[2,144,512]{2,1,0:T(8,128)(2,1)S(1)} %get-tuple-element.80), channel_id=1, source_target_pairs={{0,2},{1,3},{2,0},{3,1},{4,6},{5,7},{6,4},{7,5},{8,10},{9,11},{10,... | collective-permute-start | bytes 884744 | tf_op jit(solution)/shard_map/ppermute | solution.py:136
  45.1 12.1 %collective-permute-start.8 = (bf16[2,144,512]{2,1,0:T(8,128)(2,1)S(1)}, bf16[2,144,512]{2,1,0:T(8,128)(2,1)S(1)}, u32[]{:S(2)}, u32[]{:S(2)}) collective-permute-start(bf16[2,144,512]{2,1,0:T(8,128)(2,1)S(1)} %get-tuple-element.79), channel_id=1, source_target_pairs={{0,6},{1,7},{2,4},{3,5},{4,2},{5,3},{6,0},{7,1},{8,14},{9,15},{10,... | collective-permute-start | bytes 884744 | tf_op jit(solution)/shard_map/ppermute | solution.py:139
  57.2 11.0 %collective-permute-start.10 = (bf16[2,144,512]{2,1,0:T(8,128)(2,1)S(1)}, bf16[2,144,512]{2,1,0:T(8,128)(2,1)S(1)}, u32[]{:S(2)}, u32[]{:S(2)}) collective-permute-start(bf16[2,144,512]{2,1,0:T(8,128)(2,1)S(1)} %collective-permute-done.8.refs_6_.refs_2_), channel_id=1, source_target_pairs={{0,2},{1,3},{2,0},{3,1},{4,6},{5,7},{6,4},{7,5},{8,10},{9,11},{10,... | collective-permute-start | bytes 884744 | tf_op jit(solution)/shard_map/ppermute | solution.py:136
  59.1 11.0 %collective-permute-start.11 = (bf16[2,144,512]{2,1,0:T(8,128)(2,1)S(1)}, bf16[2,144,512]{2,1,0:T(8,128)(2,1)S(1)}, u32[]{:S(2)}, u32[]{:S(2)}) collective-permute-start(bf16[2,144,512]{2,1,0:T(8,128)(2,1)S(1)} %collective-permute-done.3.refs_3_), channel_id=1, source_target_pairs={{0,6},{1,7},{2,4},{3,5},{4,2},{5,3},{6,0},{7,1},{8,14},{9,15},{10,... | collective-permute-start | bytes 884744 | tf_op jit(solution)/shard_map/ppermute | solution.py:139
  73.4 5.3 %collective-permute-start.13 = (bf16[128,2048]{1,0:T(8,128)(2,1)S(1)}, bf16[128,2048]{1,0:T(8,128)(2,1)S(1)}, u32[]{:S(2)}, u32[]{:S(2)}) collective-permute-start(bf16[128,2048]{1,0:T(8,128)(2,1)S(1)} %shard_map.49), channel_id=1, source_target_pairs={{0,1},{1,0},{2,3},{3,2},{4,5},{5,4},{6,7},{7,6},{8,9},{9,8},{10,11... | collective-permute-start | bytes 1572872 | tf_op jit(solution)/shard_map/ppermute | solution.py:142

commit v5 on v4

--- a/solution.py
+++ b/solution.py
@@ -129,8 +129,8 @@
         pairs = [(p * 64 + s, (p + 1) % 8 * 64 + ((s + 8 * dy) % 64 ^ flip)) for p in range(8) for s in range(64)]
         return lax.ppermute(block, ("pp", "sp"), pairs)
 
-    def along_y(block):
-        return lax.ppermute(block, "sp", [(s, (s + 8) % 64) for s in range(64)])
+    def along_y(block, step0, step1):
+        return lax.ppermute(block, "sp", [(s, (s + 8 * (step1 if s % 2 else step0)) % 64) for s in range(64)])
 
     def even_pair(block):
         return lax.ppermute(block, "sp", [(s, s ^ 2) for s in range(64)])
@@ -151,26 +151,28 @@
     mine, other = jnp.where(first, half0, half1), jnp.where(first, half1, half0)
     q = queries[0]
     b4 = jnp.stack([section(mine, 0, 1), section(other, 1, 1)])
-    b4, q = lax.optimization_barrier((b4, q))
-    b8 = along_y(b4)
+    qf = section(jnp.where(first, q[:, 2048:], q[:, :2048]), 1)
+    qs = section(jnp.where(first, q[:, :2048], q[:, 2048:]), 0)
+    (b4,) = lax.optimization_barrier((b4,))
+    ya = along_y(b4, 1, -1)
+    yb = along_y(b4, -1, 1)
     e1 = even_pair(b4)
+    ya, yb, b4, qf = lax.optimization_barrier((ya, yb, b4, qf))
+    f2 = odd_pair(jnp.where((column < 2) == first, yb, ya))
+    e2 = even_pair(jnp.where((column % 2 == 0) == first, yb, ya))
     f1 = odd_pair(b4)
-    b0 = jnp.stack(lax.optimization_barrier((section(mine, 0), section(other, 1))))
-    qf = section(jnp.where(first, q[:, 2048:], q[:, :2048]), 1)
-    b8, e1, f1, b0, b4 = lax.optimization_barrier((b8, e1, f1, b0, b4))
-    qs = section(jnp.where(first, q[:, :2048], q[:, 2048:]), 0)
-    f2 = odd_pair(jnp.where(column < 2, b0, b8))
-    e2 = even_pair(jnp.where(column % 2 == 0, b0, b8))
+    b0, b8 = jnp.where(first, yb, ya), jnp.where(first, ya, yb)
     at = core[None].astype(jnp.int32)
-    state = attend(at, 1, qf, b0, [b4, b8, e1, f1], own=True)
-    e2, f2, qf, b0, b4, b8, e1, f1, *state = lax.optimization_barrier((e2, f2, qf, b0, b4, b8, e1, f1, *state))
+    state = attend(at, 1, qf, b0, [b4, b8, e1], own=True)
+    f2, e1, *state = lax.optimization_barrier((f2, e1, *state))
+    f3 = odd_pair(e1)
     e3 = even_pair(f2)
-    f3 = odd_pair(e1)
     state2 = attend(at, 0, qs, b0, [b4, b8, e1, f1, e2, f2], own=True)
-    e3, f3, qs, qf, b0, e2, f2, *state2 = lax.optimization_barrier((e3, f3, qs, qf, b0, e2, f2, *state2))
-    of_ = attend(at, 1, qf, b0, [e2, f2, e3, f3], state=state, last=True)
+    state = attend(at, 1, qf, b0, [f1, e2, f2], state=state)
+    e3, f3, qs, qf, b0, *both = lax.optimization_barrier((e3, f3, qs, qf, b0, *state, *state2))
+    of_ = attend(at, 1, qf, b0, [e3, f3], state=both[:3], last=True)
     got = swap(of_)
-    os_ = attend(at, 0, qs, b0, [e3, f3], state=state2, last=True)
+    os_ = attend(at, 0, qs, b0, [e3, f3], state=both[3:], last=True)
     out = jnp.where(first, jnp.concatenate([os_, got], axis=1), jnp.concatenate([got, os_], axis=1))
     return out[None]
 

time: 80.8 us -> 73.3 us (0.907)
  waiting for transfers between devices: 9.97 us -> 6.55 us
  starting transfers between devices: 49.8 us -> 47 us
  other arithmetic: 3.96 us -> 2.2 us
  Pallas kernels: 14.2 us -> 15.7 us
    ppermute x6 -> x4, starting transfers between devices: 28.2 us -> 17.1 us  [section(): return lax.ppermute(block, ('pp', 'sp'), pairs)]
    ppermute x1 -> x2, starting transfers between devices: 2.12 us -> 6.49 us  [along_y(): lax.ppermute(block, 'sp', [(s, (s + 8 * (step1 if s % 2 else step0)) % 64...]
    ppermute x3, waiting for transfers between devices: 4.23 us -> 0.01 us  [odd_pair(): lax.ppermute(block, 'sp', [(s, s // 8 * 8 + (s + (2 if s & 2 else -2)) %...]
    ppermute x3, starting transfers between devices: 8.85 us -> 10.6 us  [odd_pair(): lax.ppermute(block, 'sp', [(s, s // 8 * 8 + (s + (2 if s & 2 else -2)) %...]
    pallas_call x4 -> x5, Pallas kernels: 14.2 us -> 15.7 us  [attend(): pl.pallas_call(functools.partial(piece, half, own, bool(state), last, 1 +...]
    ppermute x1, starting transfers between devices: 3.4 us -> 4.86 us  [swap(): return lax.ppermute(block, 'sp', [(s, s ^ 1) for s in range(64)])]
    another operation x1 -> x0, other arithmetic: 1.01 us -> none  [shards(): jnp.stack(lax.optimization_barrier((section(mine, 0), section(other, 1))))]
    ppermute x6 -> x4, waiting for transfers between devices: 5.73 us -> 6.52 us  [section(): return lax.ppermute(block, ('pp', 'sp'), pairs)]
  transfers between devices with their start and end apart: 14 -> 13, of which waited for: 5 -> 2; matrix products, arithmetic and copies ran while one was open for 2% -> 0% of each run, Pallas kernels for 14% -> 19%
where the time goes in v5:
time: 73.3 us; the launch traced here: 72.8 us
  starting transfers between devices  47 us (64%)
  Pallas kernels  15.7 us (21%)
  waiting for transfers between devices  6.55 us (9%)
  other arithmetic  2.2 us (3%)
  local copies, waits for them, and re-layouts  0.96 us (1%)
    ppermute x4, starting transfers between devices, section(): return lax.ppermute(block, ('pp', 'sp'), pairs)  17.1 us
    pallas_call x5, Pallas kernels, attend(): pl.pallas_call(functools.partial(piece, half, own, bool(state), last, 1 +...  15.7 us
    ppermute x3, starting transfers between devices, odd_pair(): lax.ppermute(block, 'sp', [(s, s // 8 * 8 + (s + (2 if s & 2 else -2)) %...  10.6 us
    ppermute x3, starting transfers between devices, even_pair(): return lax.ppermute(block, 'sp', [(s, s ^ 2) for s in range(64)])  7.98 us
    ppermute x4, waiting for transfers between devices, section(): return lax.ppermute(block, ('pp', 'sp'), pairs)  6.52 us
    ppermute x2, starting transfers between devices, along_y(): lax.ppermute(block, 'sp', [(s, (s + 8 * (step1 if s % 2 else step0)) % 64...  6.49 us
    ppermute x1, starting transfers between devices, swap(): return lax.ppermute(block, 'sp', [(s, s ^ 1) for s in range(64)])  4.86 us
  transfers between devices with their start and end apart: 13, of which 2 were waited for; matrix products, arithmetic and copies ran while one was open for 0% of the time, Pallas kernels for 19%

profile of v5, /device:TPU:1, one launch (start us, length us, event | category | flops | bytes accessed | tf_op | source)
XLA Modules:
  0.0 72.8 jit_solution(1536284811591447723)
XLA Ops:
  0.0 0.0 copy-start
  0.0 0.7 %convert_element_type.6 = bf16[1,128]{1,0:T(2,128)(2,1)S(1)} convert(s32[1,128]{1,0:T(1,128)} %param.7) | non-fusion elementwise | flops 128 | bytes 768 | tf_op jit(solution)/shard_map/convert_element_type | solution.py:144
  0.8 1.0 %fusion.3 = (bf16[128,256]{1,0:T(8,128)(2,1)S(1)}, bf16[128,256]{1,0:T(8,128)(2,1)S(1)}, bf16[128,256]{1,0:T(8,128)(2,1)S(1)}, bf16[128,256]{1,0:T(8,128)(2,1)S(1)}) fusion(bf16[128,512]{1,0:T(8,128)(2,1)} %bitcast.13, bf16[128,512]{1,0:T(8,128)(2,1)} %bitcast.14), kind=kLoop, calls=%fused_computation.14 | loop fusion | bytes 524288 | tf_op jit(solution)/shard_map/slice | solution.py:148
  1.8 5.8 %collective-permute-start = (bf16[144,512]{1,0:T(8,128)(2,1)S(1)}, bf16[144,512]{1,0:T(8,128)(2,1)S(1)}, u32[]{:S(2)}, u32[]{:S(2)}) collective-permute-start(bf16[144,512]{1,0:T(8,128)(2,1)S(1)} %get-tuple-element.69), channel_id=1, source_target_pairs={{0,72},{1,73},{2,74},{3,75},{4,76},{5,77},{6,78},{7,79},{8,80},{9,... | collective-permute-start | bytes 442376 | tf_op jit(solution)/shard_map/ppermute | solution.py:130
  7.6 5.9 %collective-permute-start.1 = (bf16[144,512]{1,0:T(8,128)(2,1)S(1)}, bf16[144,512]{1,0:T(8,128)(2,1)S(1)}, u32[]{:S(2)}, u32[]{:S(2)}) collective-permute-start(bf16[144,512]{1,0:T(8,128)(2,1)S(1)} %get-tuple-element.70), channel_id=1, source_target_pairs={{0,73},{1,72},{2,75},{3,74},{4,77},{5,76},{6,79},{7,78},{8,81},{9,... | collective-permute-start | bytes 442376 | tf_op jit(solution)/shard_map/ppermute | solution.py:130
  13.5 0.0 copy-done
  13.5 0.1 broadcast_select_fusion
  13.6 3.4 %collective-permute-start.4 = (bf16[128,2048]{1,0:T(8,128)(2,1)S(1)}, bf16[128,2048]{1,0:T(8,128)(2,1)S(1)}, u32[]{:S(2)}, u32[]{:S(2)}) collective-permute-start(bf16[128,2048]{1,0:T(8,128)(2,1)S(1)} %get-tuple-element.64), channel_id=1, source_target_pairs={{0,65},{1,64},{2,67},{3,66},{4,69},{5,68},{6,71},{7,70},{8,73},{9,... | collective-permute-start | bytes 1572872 | tf_op jit(solution)/shard_map/ppermute | solution.py:130
  17.0 2.7 %collective-permute-done = bf16[144,512]{1,0:T(8,128)(2,1)S(1)} collective-permute-done((bf16[144,512]{1,0:T(8,128)(2,1)S(1)}, bf16[144,512]{1,0:T(8,128)(2,1)S(1)}, u32[]{:S(2)}, u32[]{:S(2)}) %collective-permute-start) | collective-permute-done | bytes 147488 | tf_op jit(solution)/shard_map/ppermute | solution.py:130
  19.7 3.8 %collective-permute-done.1 = bf16[144,512]{1,0:T(8,128)(2,1)S(1)} collective-permute-done((bf16[144,512]{1,0:T(8,128)(2,1)S(1)}, bf16[144,512]{1,0:T(8,128)(2,1)S(1)}, u32[]{:S(2)}, u32[]{:S(2)}) %collective-permute-start.1) | collective-permute-done | bytes 147488 | tf_op jit(solution)/shard_map/ppermute | solution.py:130
  23.6 1.9 %collective-permute-start.3 = (bf16[2,144,512]{2,1,0:T(8,128)(2,1)S(1)}, bf16[2,144,512]{2,1,0:T(8,128)(2,1)S(1)}, u32[]{:S(2)}, u32[]{:S(2)}) collective-permute-start(bf16[2,144,512]{2,1,0:T(8,128)(2,1)S(1)} %pad_maximum_fusion.refs_1_), channel_id=1, source_target_pairs={{0,56},{1,9},{2,58},{3,11},{4,60},{5,13},{6,62},{7,15},{8,0},{9,17... | collective-permute-start | bytes 884744 | tf_op jit(solution)/shard_map/ppermute | solution.py:133
  25.5 4.6 %collective-permute-start.2 = (bf16[2,144,512]{2,1,0:T(8,128)(2,1)S(1)}, bf16[2,144,512]{2,1,0:T(8,128)(2,1)S(1)}, u32[]{:S(2)}, u32[]{:S(2)}) collective-permute-start(bf16[2,144,512]{2,1,0:T(8,128)(2,1)S(1)} %pad_maximum_fusion.refs_1_), channel_id=1, source_target_pairs={{0,8},{1,57},{2,10},{3,59},{4,12},{5,61},{6,14},{7,63},{8,16},{9,1... | collective-permute-start | bytes 884744 | tf_op jit(solution)/shard_map/ppermute | solution.py:133
  30.1 1.9 %collective-permute-start.9 = (bf16[128,2048]{1,0:T(8,128)(2,1)S(1)}, bf16[128,2048]{1,0:T(8,128)(2,1)S(1)}, u32[]{:S(2)}, u32[]{:S(2)}) collective-permute-start(bf16[128,2048]{1,0:T(8,128)(2,1)S(1)} %get-tuple-element.63), channel_id=1, source_target_pairs={{0,64},{1,65},{2,66},{3,67},{4,68},{5,69},{6,70},{7,71},{8,72},{9,... | collective-permute-start | bytes 1572872 | tf_op jit(solution)/shard_map/ppermute | solution.py:130
  32.1 3.1 %collective-permute-start.6 = (bf16[2,144,512]{2,1,0:T(8,128)(2,1)S(1)}, bf16[2,144,512]{2,1,0:T(8,128)(2,1)S(1)}, u32[]{:S(2)}, u32[]{:S(2)}) collective-permute-start(bf16[2,144,512]{2,1,0:T(8,128)(2,1)S(1)} %pad_maximum_fusion.refs_1_), channel_id=1, source_target_pairs={{0,2},{1,3},{2,0},{3,1},{4,6},{5,7},{6,4},{7,5},{8,10},{9,11},{10,... | collective-permute-start | bytes 884744 | tf_op jit(solution)/shard_map/ppermute | solution.py:136
  35.2 0.0 collective-permute-done.3
  35.2 0.0 collective-permute-done.2
  35.2 0.0 collective-permute-done.4.q_ref
  35.2 0.1 broadcast_select_fusion.2
  35.3 4.1 %collective-permute-start.5 = (bf16[2,144,512]{2,1,0:T(8,128)(2,1)S(1)}, bf16[2,144,512]{2,1,0:T(8,128)(2,1)S(1)}, u32[]{:S(2)}, u32[]{:S(2)}) collective-permute-start(bf16[2,144,512]{2,1,0:T(8,128)(2,1)S(1)} %get-tuple-element.68), channel_id=1, source_target_pairs={{0,6},{1,7},{2,4},{3,5},{4,2},{5,3},{6,0},{7,1},{8,14},{9,15},{10,... | collective-permute-start | bytes 884744 | tf_op jit(solution)/shard_map/ppermute | solution.py:139
  39.4 2.4 %collective-permute-start.10 = (bf16[2,144,512]{2,1,0:T(8,128)(2,1)S(1)}, bf16[2,144,512]{2,1,0:T(8,128)(2,1)S(1)}, u32[]{:S(2)}, u32[]{:S(2)}) collective-permute-start(bf16[2,144,512]{2,1,0:T(8,128)(2,1)S(1)} %pad_maximum_fusion.refs_1_), channel_id=1, source_target_pairs={{0,6},{1,7},{2,4},{3,5},{4,2},{5,3},{6,0},{7,1},{8,14},{9,15},{10,... | collective-permute-start | bytes 884744 | tf_op jit(solution)/shard_map/ppermute | solution.py:139
  41.8 1.9 %collective-permute-start.11 = (bf16[2,144,512]{2,1,0:T(8,128)(2,1)S(1)}, bf16[2,144,512]{2,1,0:T(8,128)(2,1)S(1)}, u32[]{:S(2)}, u32[]{:S(2)}) collective-permute-start(bf16[2,144,512]{2,1,0:T(8,128)(2,1)S(1)} %get-tuple-element.65), channel_id=1, source_target_pairs={{0,2},{1,3},{2,0},{3,1},{4,6},{5,7},{6,4},{7,5},{8,10},{9,11},{10,... | collective-permute-start | bytes 884744 | tf_op jit(solution)/shard_map/ppermute | solution.py:136
  43.7 0.0 collective-permute-done.6.refs_3_
  43.8 3.3 %shard_map.46 = (f32[2048,128]{1,0:T(8,128)S(1)}, f32[2048,128]{1,0:T(8,128)S(1)}, f32[2048,128]{1,0:T(8,128)S(1)}) custom-call(s32[1]{0:T(128)} %bitcast.core_ref, bf16[128,2048]{1,0:T(8,128)(2,1)S(1)} %collective-permute-done.4.q_ref, bf16[2,144,512]{2,1,0:T(8,128)(2,1)S(1)} %get-tuple-element.53.refs_0_, ...), custom_call_target="tpu_custom_call" | custom-call | flops 2147483648 | bytes 4194304 | tf_op jit(solution)/shard_map/pallas_call | solution.py:110
  47.1 0.0 collective-permute-done.5.refs_3_.refs_6_
  47.1 4.1 %collective-permute-start.8 = (bf16[2,144,512]{2,1,0:T(8,128)(2,1)S(1)}, bf16[2,144,512]{2,1,0:T(8,128)(2,1)S(1)}, u32[]{:S(2)}, u32[]{:S(2)}) collective-permute-start(bf16[2,144,512]{2,1,0:T(8,128)(2,1)S(1)} %collective-permute-done.6.refs_3_), channel_id=1, source_target_pairs={{0,6},{1,7},{2,4},{3,5},{4,2},{5,3},{6,0},{7,1},{8,14},{9,15},{10,... | collective-permute-start | bytes 884744 | tf_op jit(solution)/shard_map/ppermute | solution.py:139
  51.2 2.9 %collective-permute-start.7 = (bf16[2,144,512]{2,1,0:T(8,128)(2,1)S(1)}, bf16[2,144,512]{2,1,0:T(8,128)(2,1)S(1)}, u32[]{:S(2)}, u32[]{:S(2)}) collective-permute-start(bf16[2,144,512]{2,1,0:T(8,128)(2,1)S(1)} %collective-permute-done.5.refs_3_.refs_6_), channel_id=1, source_target_pairs={{0,2},{1,3},{2,0},{3,1},{4,6},{5,7},{6,4},{7,5},{8,10},{9,11},{10,... | collective-permute-start | bytes 884744 | tf_op jit(solution)/shard_map/ppermute | solution.py:136
  54.2 0.0 collective-permute-done.10.refs_1_.refs_4_
  54.2 0.0 collective-permute-done.11.refs_2_.refs_5_
  54.2 2.7 %shard_map.47 = (f32[2048,128]{1,0:T(8,128)S(1)}, f32[2048,128]{1,0:T(8,128)S(1)}, f32[2048,128]{1,0:T(8,128)S(1)}) custom-call(s32[1]{0:T(128)} %bitcast.core_ref, bf16[128,2048]{1,0:T(8,128)(2,1)S(1)} %collective-permute-done.4.q_ref, bf16[2,144,512]{2,1,0:T(8,128)(2,1)S(1)} %get-tuple-element.53.refs_0_, ...), custom_call_target="tpu_custom_call" | custom-call | flops 1610612736 | bytes 4194304 | tf_op jit(solution)/shard_map/pallas_call | solution.py:110
  56.9 0.0 collective-permute-done.9.q_ref
  57.0 5.6 %shard_map.48 = (f32[2048,128]{1,0:T(8,128)S(1)}, f32[2048,128]{1,0:T(8,128)S(1)}, f32[2048,128]{1,0:T(8,128)S(1)}) custom-call(s32[1]{0:T(128)} %bitcast.core_ref, bf16[128,2048]{1,0:T(8,128)(2,1)S(1)} %collective-permute-done.9.q_ref, bf16[2,144,512]{2,1,0:T(8,128)(2,1)S(1)} %get-tuple-element.53.refs_0_, ...), custom_call_target="tpu_custom_call" | custom-call | flops 3758096384 | bytes 4194304 | tf_op jit(solution)/shard_map/pallas_call | solution.py:110
  62.6 0.0 collective-permute-done.8.refs_2_
  62.6 0.0 collective-permute-done.7.refs_1_
  62.6 2.0 %shard_map.50 = bf16[128,2048]{1,0:T(8,128)(2,1)S(1)} custom-call(s32[1]{0:T(128)} %bitcast.core_ref, bf16[128,2048]{1,0:T(8,128)(2,1)S(1)} %collective-permute-done.4.q_ref, bf16[2,144,512]{2,1,0:T(8,128)(2,1)S(1)} %get-tuple-element.53.refs_0_, bf16[2,144,512]{2,1,0:T(8,128)(2,1)S(1)} %collective-permute-done.7.refs_1_, ...), custom_call_target="tpu_custom_call" | custom-call | flops 1073741824 | bytes 4194304 | tf_op jit(solution)/shard_map/pallas_call | solution.py:110
  64.6 4.9 %collective-permute-start.12 = (bf16[128,2048]{1,0:T(8,128)(2,1)S(1)}, bf16[128,2048]{1,0:T(8,128)(2,1)S(1)}, u32[]{:S(2)}, u32[]{:S(2)}) collective-permute-start(bf16[128,2048]{1,0:T(8,128)(2,1)S(1)} %shard_map.50), channel_id=1, source_target_pairs={{0,1},{1,0},{2,3},{3,2},{4,5},{5,4},{6,7},{7,6},{8,9},{9,8},{10,11... | collective-permute-start | bytes 1572872 | tf_op jit(solution)/shard_map/ppermute | solution.py:142
  69.5 2.0 %shard_map.49 = bf16[128,2048]{1,0:T(8,128)(2,1)S(1)} custom-call(s32[1]{0:T(128)} %bitcast.core_ref, bf16[128,2048]{1,0:T(8,128)(2,1)S(1)} %collective-permute-done.9.q_ref, bf16[2,144,512]{2,1,0:T(8,128)(2,1)S(1)} %get-tuple-element.53.refs_0_, bf16[2,144,512]{2,1,0:T(8,128)(2,1)S(1)} %collective-permute-done.7.refs_1_, ...), custom_call_target="tpu_custom_call" | custom-call | flops 1073741824 | bytes 4194304 | tf_op jit(solution)/shard_map/pallas_call | solution.py:110
  71.5 0.0 collective-permute-done.12
  71.6 1.2 %maximum_select_fusion = bf16[1,128,4096]{2,1,0:T(8,128)(2,1)} fusion(bf16[1,128,2048]{2,1,0:T(8,128)(2,1)S(1)} %bitcast.10, bf16[1,128,2048]{2,1,0:T(8,128)(2,1)S(1)} %bitcast.8, pred[]{:T(512)S(6)} %eq.16), kind=kLoop, calls=%fused_computation | loop fusion | flops 4718592 | bytes 2097153 | tf_op jit(solution)/shard_map/jit(_where)/select_n | solution.py:176
  (2 shorter events, 0.1 us)
Async XLA Ops:
  0.0 13.5 %copy-start = (bf16[1,128,4096]{2,1,0:T(8,128)(2,1)S(1)}, bf16[1,128,4096]{2,1,0:T(8,128)(2,1)}, u32[]{:S(2)}) copy-start(bf16[1,128,4096]{2,1,0:T(8,128)(2,1)} %param.4) | copy-start | bytes 3145732
  1.8 18.0 %collective-permute-start = (bf16[144,512]{1,0:T(8,128)(2,1)S(1)}, bf16[144,512]{1,0:T(8,128)(2,1)S(1)}, u32[]{:S(2)}, u32[]{:S(2)}) collective-permute-start(bf16[144,512]{1,0:T(8,128)(2,1)S(1)} %get-tuple-element.69), channel_id=1, source_target_pairs={{0,72},{1,73},{2,74},{3,75},{4,76},{5,77},{6,78},{7,79},{8,80},{9,... | collective-permute-start | bytes 442376 | tf_op jit(solution)/shard_map/ppermute | solution.py:130
  7.6 15.9 %collective-permute-start.1 = (bf16[144,512]{1,0:T(8,128)(2,1)S(1)}, bf16[144,512]{1,0:T(8,128)(2,1)S(1)}, u32[]{:S(2)}, u32[]{:S(2)}) collective-permute-start(bf16[144,512]{1,0:T(8,128)(2,1)S(1)} %get-tuple-element.70), channel_id=1, source_target_pairs={{0,73},{1,72},{2,75},{3,74},{4,77},{5,76},{6,79},{7,78},{8,81},{9,... | collective-permute-start | bytes 442376 | tf_op jit(solution)/shard_map/ppermute | solution.py:130
  13.6 21.6 %collective-permute-start.4 = (bf16[128,2048]{1,0:T(8,128)(2,1)S(1)}, bf16[128,2048]{1,0:T(8,128)(2,1)S(1)}, u32[]{:S(2)}, u32[]{:S(2)}) collective-permute-start(bf16[128,2048]{1,0:T(8,128)(2,1)S(1)} %get-tuple-element.64), channel_id=1, source_target_pairs={{0,65},{1,64},{2,67},{3,66},{4,69},{5,68},{6,71},{7,70},{8,73},{9,... | collective-permute-start | bytes 1572872 | tf_op jit(solution)/shard_map/ppermute | solution.py:130
  23.6 11.6 %collective-permute-start.3 = (bf16[2,144,512]{2,1,0:T(8,128)(2,1)S(1)}, bf16[2,144,512]{2,1,0:T(8,128)(2,1)S(1)}, u32[]{:S(2)}, u32[]{:S(2)}) collective-permute-start(bf16[2,144,512]{2,1,0:T(8,128)(2,1)S(1)} %pad_maximum_fusion.refs_1_), channel_id=1, source_target_pairs={{0,56},{1,9},{2,58},{3,11},{4,60},{5,13},{6,62},{7,15},{8,0},{9,17... | collective-permute-start | bytes 884744 | tf_op jit(solution)/shard_map/ppermute | solution.py:133
  25.5 9.7 %collective-permute-start.2 = (bf16[2,144,512]{2,1,0:T(8,128)(2,1)S(1)}, bf16[2,144,512]{2,1,0:T(8,128)(2,1)S(1)}, u32[]{:S(2)}, u32[]{:S(2)}) collective-permute-start(bf16[2,144,512]{2,1,0:T(8,128)(2,1)S(1)} %pad_maximum_fusion.refs_1_), channel_id=1, source_target_pairs={{0,8},{1,57},{2,10},{3,59},{4,12},{5,61},{6,14},{7,63},{8,16},{9,1... | collective-permute-start | bytes 884744 | tf_op jit(solution)/shard_map/ppermute | solution.py:133
  30.1 26.9 %collective-permute-start.9 = (bf16[128,2048]{1,0:T(8,128)(2,1)S(1)}, bf16[128,2048]{1,0:T(8,128)(2,1)S(1)}, u32[]{:S(2)}, u32[]{:S(2)}) collective-permute-start(bf16[128,2048]{1,0:T(8,128)(2,1)S(1)} %get-tuple-element.63), channel_id=1, source_target_pairs={{0,64},{1,65},{2,66},{3,67},{4,68},{5,69},{6,70},{7,71},{8,72},{9,... | collective-permute-start | bytes 1572872 | tf_op jit(solution)/shard_map/ppermute | solution.py:130
  32.1 11.7 %collective-permute-start.6 = (bf16[2,144,512]{2,1,0:T(8,128)(2,1)S(1)}, bf16[2,144,512]{2,1,0:T(8,128)(2,1)S(1)}, u32[]{:S(2)}, u32[]{:S(2)}) collective-permute-start(bf16[2,144,512]{2,1,0:T(8,128)(2,1)S(1)} %pad_maximum_fusion.refs_1_), channel_id=1, source_target_pairs={{0,2},{1,3},{2,0},{3,1},{4,6},{5,7},{6,4},{7,5},{8,10},{9,11},{10,... | collective-permute-start | bytes 884744 | tf_op jit(solution)/shard_map/ppermute | solution.py:136
  35.3 11.8 %collective-permute-start.5 = (bf16[2,144,512]{2,1,0:T(8,128)(2,1)S(1)}, bf16[2,144,512]{2,1,0:T(8,128)(2,1)S(1)}, u32[]{:S(2)}, u32[]{:S(2)}) collective-permute-start(bf16[2,144,512]{2,1,0:T(8,128)(2,1)S(1)} %get-tuple-element.68), channel_id=1, source_target_pairs={{0,6},{1,7},{2,4},{3,5},{4,2},{5,3},{6,0},{7,1},{8,14},{9,15},{10,... | collective-permute-start | bytes 884744 | tf_op jit(solution)/shard_map/ppermute | solution.py:139
  39.4 14.7 %collective-permute-start.10 = (bf16[2,144,512]{2,1,0:T(8,128)(2,1)S(1)}, bf16[2,144,512]{2,1,0:T(8,128)(2,1)S(1)}, u32[]{:S(2)}, u32[]{:S(2)}) collective-permute-start(bf16[2,144,512]{2,1,0:T(8,128)(2,1)S(1)} %pad_maximum_fusion.refs_1_), channel_id=1, source_target_pairs={{0,6},{1,7},{2,4},{3,5},{4,2},{5,3},{6,0},{7,1},{8,14},{9,15},{10,... | collective-permute-start | bytes 884744 | tf_op jit(solution)/shard_map/ppermute | solution.py:139
  41.8 12.4 %collective-permute-start.11 = (bf16[2,144,512]{2,1,0:T(8,128)(2,1)S(1)}, bf16[2,144,512]{2,1,0:T(8,128)(2,1)S(1)}, u32[]{:S(2)}, u32[]{:S(2)}) collective-permute-start(bf16[2,144,512]{2,1,0:T(8,128)(2,1)S(1)} %get-tuple-element.65), channel_id=1, source_target_pairs={{0,2},{1,3},{2,0},{3,1},{4,6},{5,7},{6,4},{7,5},{8,10},{9,11},{10,... | collective-permute-start | bytes 884744 | tf_op jit(solution)/shard_map/ppermute | solution.py:136
  47.1 15.5 %collective-permute-start.8 = (bf16[2,144,512]{2,1,0:T(8,128)(2,1)S(1)}, bf16[2,144,512]{2,1,0:T(8,128)(2,1)S(1)}, u32[]{:S(2)}, u32[]{:S(2)}) collective-permute-start(bf16[2,144,512]{2,1,0:T(8,128)(2,1)S(1)} %collective-permute-done.6.refs_3_), channel_id=1, source_target_pairs={{0,6},{1,7},{2,4},{3,5},{4,2},{5,3},{6,0},{7,1},{8,14},{9,15},{10,... | collective-permute-start | bytes 884744 | tf_op jit(solution)/shard_map/ppermute | solution.py:139
  51.2 11.4 %collective-permute-start.7 = (bf16[2,144,512]{2,1,0:T(8,128)(2,1)S(1)}, bf16[2,144,512]{2,1,0:T(8,128)(2,1)S(1)}, u32[]{:S(2)}, u32[]{:S(2)}) collective-permute-start(bf16[2,144,512]{2,1,0:T(8,128)(2,1)S(1)} %collective-permute-done.5.refs_3_.refs_6_), channel_id=1, source_target_pairs={{0,2},{1,3},{2,0},{3,1},{4,6},{5,7},{6,4},{7,5},{8,10},{9,11},{10,... | collective-permute-start | bytes 884744 | tf_op jit(solution)/shard_map/ppermute | solution.py:136
  64.6 6.9 %collective-permute-start.12 = (bf16[128,2048]{1,0:T(8,128)(2,1)S(1)}, bf16[128,2048]{1,0:T(8,128)(2,1)S(1)}, u32[]{:S(2)}, u32[]{:S(2)}) collective-permute-start(bf16[128,2048]{1,0:T(8,128)(2,1)S(1)} %shard_map.50), channel_id=1, source_target_pairs={{0,1},{1,0},{2,3},{3,2},{4,5},{5,4},{6,7},{7,6},{8,9},{9,8},{10,11... | collective-permute-start | bytes 1572872 | tf_op jit(solution)/shard_map/ppermute | solution.py:142

commit v6 on v5

--- a/solution.py
+++ b/solution.py
@@ -65,37 +65,57 @@
         qat = (core ^ half) * BLOCK + (tall & (BLOCK - 1))
         kat = (core ^ (wide >> 7)) * BLOCK + (wide & (BLOCK - 1))
         future = kat > qat
-    for kv in range(2):
-        for pair in range(GROUP // 2):
-            head = kv * GROUP + 2 * pair
-            at = head * HEAD
-            rows = slice(head * BLOCK, (head + 2) * BLOCK)
-            q2 = jnp.concatenate([q_ref[:, at : at + HEAD], q_ref[:, at + HEAD : at + 2 * HEAD]], axis=0)
-            q2 = jnp.concatenate([q2, away], axis=1)
-            score = lax.dot_general(q2, kaug[kv], NT, preferred_element_type=jnp.float32)
-            if own:
-                mine = jnp.where(future, FAR, score[:, : 2 * BLOCK])
-                score = mine if len(blocks) == 1 else jnp.concatenate([mine, score[:, 2 * BLOCK :]], axis=1)
-            top = jnp.max(score, axis=1, keepdims=True)
-            if carried:
-                before = old[0][rows, :]
-                top = jnp.maximum(jnp.broadcast_to(top, before.shape), before)
-            wide = jnp.concatenate([top] * (2 * len(blocks)), axis=1) if carried else top
-            weight = jnp.exp2((score - wide) * SCALE).astype(jnp.bfloat16)
-            both = jnp.dot(weight, vaug[kv], preferred_element_type=jnp.float32)
-            total, accum = both[:, HEAD:], both[:, :HEAD]
-            if carried:
-                factor = jnp.exp2((before - top) * SCALE)
-                total = total + old[1][rows, :] * factor
-                accum = accum + old[2][rows, :] * factor
-            if last:
-                result = (accum / total).astype(jnp.bfloat16)
-                new[0][:, at : at + HEAD] = result[:BLOCK]
-                new[0][:, at + HEAD : at + 2 * HEAD] = result[BLOCK:]
-            else:
-                new[0][rows, :] = jnp.broadcast_to(top, (2 * BLOCK, HEAD))
-                new[1][rows, :] = total
-                new[2][rows, :] = accum
+    def scores(kv, pair):
+        at = (kv * GROUP + 2 * pair) * HEAD
+        q2 = jnp.concatenate([q_ref[:, at : at + HEAD], q_ref[:, at + HEAD : at + 2 * HEAD]], axis=0)
+        q2 = jnp.concatenate([q2, away], axis=1)
+        score = lax.dot_general(q2, kaug[kv], NT, preferred_element_type=jnp.float32)
+        if own:
+            mine = jnp.where(future, FAR, score[:, : 2 * BLOCK])
+            score = mine if len(blocks) == 1 else jnp.concatenate([mine, score[:, 2 * BLOCK :]], axis=1)
+        return score
+
+    def weights(score, kv, pair):
+        head = kv * GROUP + 2 * pair
+        rows = slice(head * BLOCK, (head + 2) * BLOCK)
+        top = jnp.max(score, axis=1, keepdims=True)
+        factor = None
+        if carried:
+            before = old[0][rows, :]
+            top = jnp.maximum(jnp.broadcast_to(top, before.shape), before)
+            factor = jnp.exp2((before - top) * SCALE)
+        wide = jnp.concatenate([top] * (2 * len(blocks)), axis=1) if carried else top
+        return jnp.exp2((score - wide) * SCALE).astype(jnp.bfloat16), top, factor
+
+    def finish(weight, top, factor, kv, pair):
+        head = kv * GROUP + 2 * pair
+        at = head * HEAD
+        rows = slice(head * BLOCK, (head + 2) * BLOCK)
+        both = jnp.dot(weight, vaug[kv], preferred_element_type=jnp.float32)
+        total, accum = both[:, HEAD:], both[:, :HEAD]
+        if carried:
+            total = total + old[1][rows, :] * factor
+            accum = accum + old[2][rows, :] * factor
+        if last:
+            result = (accum / total).astype(jnp.bfloat16)
+            new[0][:, at : at + HEAD] = result[:BLOCK]
+            new[0][:, at + HEAD : at + 2 * HEAD] = result[BLOCK:]
+        else:
+            new[0][rows, :] = jnp.broadcast_to(top, (2 * BLOCK, HEAD))
+            new[1][rows, :] = total
+            new[2][rows, :] = accum
+
+    tiles = [(kv, pair) for kv in range(2) for pair in range(GROUP // 2)]
+    ahead = scores(*tiles[0])
+    pending = None
+    for i, tile in enumerate(tiles):
+        score = ahead
+        if i + 1 < len(tiles):
+            ahead = scores(*tiles[i + 1])
+        if pending is not None:
+            finish(*pending)
+        pending = (*weights(score, *tile), *tile)
+    finish(*pending)
 
 
 def attend(core, half, q, b0, blocks, own=False, state=(), last=False):
@@ -154,25 +174,24 @@
     qf = section(jnp.where(first, q[:, 2048:], q[:, :2048]), 1)
     qs = section(jnp.where(first, q[:, :2048], q[:, 2048:]), 0)
     (b4,) = lax.optimization_barrier((b4,))
+    e1 = even_pair(b4)
     ya = along_y(b4, 1, -1)
     yb = along_y(b4, -1, 1)
-    e1 = even_pair(b4)
-    ya, yb, b4, qf = lax.optimization_barrier((ya, yb, b4, qf))
+    ya, yb, b4, qf, e1 = lax.optimization_barrier((ya, yb, b4, qf, e1))
     f2 = odd_pair(jnp.where((column < 2) == first, yb, ya))
     e2 = even_pair(jnp.where((column % 2 == 0) == first, yb, ya))
-    f1 = odd_pair(b4)
+    f13 = odd_pair(jnp.stack([b4, e1]))
     b0, b8 = jnp.where(first, yb, ya), jnp.where(first, ya, yb)
     at = core[None].astype(jnp.int32)
     state = attend(at, 1, qf, b0, [b4, b8, e1], own=True)
-    f2, e1, *state = lax.optimization_barrier((f2, e1, *state))
-    f3 = odd_pair(e1)
+    f2, *state = lax.optimization_barrier((f2, *state))
     e3 = even_pair(f2)
-    state2 = attend(at, 0, qs, b0, [b4, b8, e1, f1, e2, f2], own=True)
-    state = attend(at, 1, qf, b0, [f1, e2, f2], state=state)
-    e3, f3, qs, qf, b0, *both = lax.optimization_barrier((e3, f3, qs, qf, b0, *state, *state2))
-    of_ = attend(at, 1, qf, b0, [e3, f3], state=both[:3], last=True)
+    state2 = attend(at, 0, qs, b0, [b4, b8, e1, e2, f2], own=True)
+    state = attend(at, 1, qf, b0, [e2, f2], state=state)
+    e3, f13, qs, qf, b0, *both = lax.optimization_barrier((e3, f13, qs, qf, b0, *state, *state2))
+    of_ = attend(at, 1, qf, b0, [e3, f13], state=both[:3], last=True)
     got = swap(of_)
-    os_ = attend(at, 0, qs, b0, [e3, f3], state=both[3:], last=True)
+    os_ = attend(at, 0, qs, b0, [e3, f13], state=both[3:], last=True)
     out = jnp.where(first, jnp.concatenate([os_, got], axis=1), jnp.concatenate([got, os_], axis=1))
     return out[None]
 

time: 73.3 us -> 74.7 us (1.019)
  waiting for transfers between devices: 6.55 us -> 13.7 us
  starting transfers between devices: 47 us -> 41.5 us
    ppermute x3 -> x2, waiting for transfers between devices: 0.01 us -> 4.2 us  [odd_pair(): lax.ppermute(block, 'sp', [(s, s // 8 * 8 + (s + (2 if s & 2 else -2)) %...]
    ppermute x3 -> x2, starting transfers between devices: 10.6 us -> 6.49 us  [odd_pair(): lax.ppermute(block, 'sp', [(s, s // 8 * 8 + (s + (2 if s & 2 else -2)) %...]
    ppermute x2, waiting for transfers between devices: 0.01 us -> 3.01 us  [along_y(): lax.ppermute(block, 'sp', [(s, (s + 8 * (step1 if s % 2 else step0)) % 64...]
    ppermute x1, starting transfers between devices: 4.86 us -> 4.11 us  [swap(): return lax.ppermute(block, 'sp', [(s, s ^ 1) for s in range(64)])]
  transfers between devices with their start and end apart: 13 -> 12, of which waited for: 2 -> 5; matrix products, arithmetic and copies ran while one was open for 0% -> 0% of each run, Pallas kernels for 19% -> 17%
where the time goes in v6:
time: 74.7 us; the launch traced here: 74.2 us
  starting transfers between devices  41.5 us (56%)
  Pallas kernels  15.4 us (21%)
  waiting for transfers between devices  13.7 us (18%)
  other arithmetic  2.25 us (3%)
  local copies, waits for them, and re-layouts  0.96 us (1%)
    ppermute x4, starting transfers between devices, section(): return lax.ppermute(block, ('pp', 'sp'), pairs)  17.1 us
    pallas_call x5, Pallas kernels, attend(): pl.pallas_call(functools.partial(piece, half, own, bool(state), last, 1 +...  15.4 us
    ppermute x3, starting transfers between devices, even_pair(): return lax.ppermute(block, 'sp', [(s, s ^ 2) for s in range(64)])  7.38 us
    ppermute x4, waiting for transfers between devices, section(): return lax.ppermute(block, ('pp', 'sp'), pairs)  6.52 us
    ppermute x2, starting transfers between devices, odd_pair(): lax.ppermute(block, 'sp', [(s, s // 8 * 8 + (s + (2 if s & 2 else -2)) %...  6.49 us
    ppermute x2, starting transfers between devices, along_y(): lax.ppermute(block, 'sp', [(s, (s + 8 * (step1 if s % 2 else step0)) % 64...  6.49 us
    ppermute x2, waiting for transfers between devices, odd_pair(): lax.ppermute(block, 'sp', [(s, s // 8 * 8 + (s + (2 if s & 2 else -2)) %...  4.2 us
    ppermute x1, starting transfers between devices, swap(): return lax.ppermute(block, 'sp', [(s, s ^ 1) for s in range(64)])  4.11 us
  transfers between devices with their start and end apart: 12, of which 5 were waited for; matrix products, arithmetic and copies ran while one was open for 0% of the time, Pallas kernels for 17%

profile of v6, /device:TPU:1, one launch (start us, length us, event | category | flops | bytes accessed | tf_op | source)
XLA Modules:
  0.0 74.2 jit_solution(15458430629060761652)
XLA Ops:
  0.0 0.0 copy-start
  0.0 0.7 %convert_element_type.6 = bf16[1,128]{1,0:T(2,128)(2,1)S(1)} convert(s32[1,128]{1,0:T(1,128)} %param.7) | non-fusion elementwise | flops 128 | bytes 768 | tf_op jit(solution)/shard_map/convert_element_type | solution.py:164
  0.8 1.0 %fusion.3 = (bf16[128,256]{1,0:T(8,128)(2,1)S(1)}, bf16[128,256]{1,0:T(8,128)(2,1)S(1)}, bf16[128,256]{1,0:T(8,128)(2,1)S(1)}, bf16[128,256]{1,0:T(8,128)(2,1)S(1)}) fusion(bf16[128,512]{1,0:T(8,128)(2,1)} %bitcast.17, bf16[128,512]{1,0:T(8,128)(2,1)} %bitcast.18), kind=kLoop, calls=%fused_computation.15 | loop fusion | bytes 524288 | tf_op jit(solution)/shard_map/slice | solution.py:168
  1.8 5.8 %collective-permute-start = (bf16[144,512]{1,0:T(8,128)(2,1)S(1)}, bf16[144,512]{1,0:T(8,128)(2,1)S(1)}, u32[]{:S(2)}, u32[]{:S(2)}) collective-permute-start(bf16[144,512]{1,0:T(8,128)(2,1)S(1)} %get-tuple-element.69), channel_id=1, source_target_pairs={{0,72},{1,73},{2,74},{3,75},{4,76},{5,77},{6,78},{7,79},{8,80},{9,... | collective-permute-start | bytes 442376 | tf_op jit(solution)/shard_map/ppermute | solution.py:150
  7.6 5.9 %collective-permute-start.1 = (bf16[144,512]{1,0:T(8,128)(2,1)S(1)}, bf16[144,512]{1,0:T(8,128)(2,1)S(1)}, u32[]{:S(2)}, u32[]{:S(2)}) collective-permute-start(bf16[144,512]{1,0:T(8,128)(2,1)S(1)} %get-tuple-element.70), channel_id=1, source_target_pairs={{0,73},{1,72},{2,75},{3,74},{4,77},{5,76},{6,79},{7,78},{8,81},{9,... | collective-permute-start | bytes 442376 | tf_op jit(solution)/shard_map/ppermute | solution.py:150
  13.5 0.0 copy-done
  13.5 0.1 broadcast_select_fusion
  13.6 3.4 %collective-permute-start.4 = (bf16[128,2048]{1,0:T(8,128)(2,1)S(1)}, bf16[128,2048]{1,0:T(8,128)(2,1)S(1)}, u32[]{:S(2)}, u32[]{:S(2)}) collective-permute-start(bf16[128,2048]{1,0:T(8,128)(2,1)S(1)} %get-tuple-element.64), channel_id=1, source_target_pairs={{0,65},{1,64},{2,67},{3,66},{4,69},{5,68},{6,71},{7,70},{8,73},{9,... | collective-permute-start | bytes 1572872 | tf_op jit(solution)/shard_map/ppermute | solution.py:150
  17.0 2.7 %collective-permute-done = bf16[144,512]{1,0:T(8,128)(2,1)S(1)} collective-permute-done((bf16[144,512]{1,0:T(8,128)(2,1)S(1)}, bf16[144,512]{1,0:T(8,128)(2,1)S(1)}, u32[]{:S(2)}, u32[]{:S(2)}) %collective-permute-start) | collective-permute-done | bytes 147488 | tf_op jit(solution)/shard_map/ppermute | solution.py:150
  19.7 3.8 %collective-permute-done.1 = bf16[144,512]{1,0:T(8,128)(2,1)S(1)} collective-permute-done((bf16[144,512]{1,0:T(8,128)(2,1)S(1)}, bf16[144,512]{1,0:T(8,128)(2,1)S(1)}, u32[]{:S(2)}, u32[]{:S(2)}) %collective-permute-start.1) | collective-permute-done | bytes 147488 | tf_op jit(solution)/shard_map/ppermute | solution.py:150
  23.6 3.1 %collective-permute-start.5 = (bf16[2,144,512]{2,1,0:T(8,128)(2,1)S(1)}, bf16[2,144,512]{2,1,0:T(8,128)(2,1)S(1)}, u32[]{:S(2)}, u32[]{:S(2)}) collective-permute-start(bf16[2,144,512]{2,1,0:T(8,128)(2,1)S(1)} %pad_maximum_fusion.1.refs_1_), channel_id=1, source_target_pairs={{0,2},{1,3},{2,0},{3,1},{4,6},{5,7},{6,4},{7,5},{8,10},{9,11},{10,... | collective-permute-start | bytes 884744 | tf_op jit(solution)/shard_map/ppermute | solution.py:156
  26.7 1.9 %collective-permute-start.3 = (bf16[2,144,512]{2,1,0:T(8,128)(2,1)S(1)}, bf16[2,144,512]{2,1,0:T(8,128)(2,1)S(1)}, u32[]{:S(2)}, u32[]{:S(2)}) collective-permute-start(bf16[2,144,512]{2,1,0:T(8,128)(2,1)S(1)} %pad_maximum_fusion.1.refs_1_), channel_id=1, source_target_pairs={{0,56},{1,9},{2,58},{3,11},{4,60},{5,13},{6,62},{7,15},{8,0},{9,17... | collective-permute-start | bytes 884744 | tf_op jit(solution)/shard_map/ppermute | solution.py:153
  28.6 4.6 %collective-permute-start.2 = (bf16[2,144,512]{2,1,0:T(8,128)(2,1)S(1)}, bf16[2,144,512]{2,1,0:T(8,128)(2,1)S(1)}, u32[]{:S(2)}, u32[]{:S(2)}) collective-permute-start(bf16[2,144,512]{2,1,0:T(8,128)(2,1)S(1)} %pad_maximum_fusion.1.refs_1_), channel_id=1, source_target_pairs={{0,8},{1,57},{2,10},{3,59},{4,12},{5,61},{6,14},{7,63},{8,16},{9,1... | collective-permute-start | bytes 884744 | tf_op jit(solution)/shard_map/ppermute | solution.py:153
  33.2 1.9 %collective-permute-start.9 = (bf16[128,2048]{1,0:T(8,128)(2,1)S(1)}, bf16[128,2048]{1,0:T(8,128)(2,1)S(1)}, u32[]{:S(2)}, u32[]{:S(2)}) collective-permute-start(bf16[128,2048]{1,0:T(8,128)(2,1)S(1)} %get-tuple-element.63), channel_id=1, source_target_pairs={{0,64},{1,65},{2,66},{3,67},{4,68},{5,69},{6,70},{7,71},{8,72},{9,... | collective-permute-start | bytes 1572872 | tf_op jit(solution)/shard_map/ppermute | solution.py:150
  35.2 0.0 collective-permute-done.5.refs_3_
  35.2 0.2 collective-permute-done.3
  35.4 2.8 %collective-permute-done.2 = bf16[2,144,512]{2,1,0:T(8,128)(2,1)S(1)} collective-permute-done((bf16[2,144,512]{2,1,0:T(8,128)(2,1)S(1)}, bf16[2,144,512]{2,1,0:T(8,128)(2,1)S(1)}, u32[]{:S(2)}, u32[]{:S(2)}) %collective-permute-start.2) | collective-permute-done | bytes 294944 | tf_op jit(solution)/shard_map/ppermute | solution.py:153
  38.2 0.0 collective-permute-done.4.q_ref
  38.2 0.1 broadcast_select_fusion.2
  38.3 2.2 %collective-permute-start.10 = (bf16[2,144,512]{2,1,0:T(8,128)(2,1)S(1)}, bf16[2,144,512]{2,1,0:T(8,128)(2,1)S(1)}, u32[]{:S(2)}, u32[]{:S(2)}) collective-permute-start(bf16[2,144,512]{2,1,0:T(8,128)(2,1)S(1)} %get-tuple-element.65), channel_id=1, source_target_pairs={{0,2},{1,3},{2,0},{3,1},{4,6},{5,7},{6,4},{7,5},{8,10},{9,11},{10,... | collective-permute-start | bytes 884744 | tf_op jit(solution)/shard_map/ppermute | solution.py:156
  40.5 4.4 %collective-permute-start.6 = (bf16[2,144,512]{2,1,0:T(8,128)(2,1)S(1)}, bf16[2,144,512]{2,1,0:T(8,128)(2,1)S(1)}, u32[]{:S(2)}, u32[]{:S(2)}) collective-permute-start(bf16[2,144,512]{2,1,0:T(8,128)(2,1)S(1)} %get-tuple-element.68), channel_id=1, source_target_pairs={{0,6},{1,7},{2,4},{3,5},{4,2},{5,3},{6,0},{7,1},{8,14},{9,15},{10,... | collective-permute-start | bytes 884744 | tf_op jit(solution)/shard_map/ppermute | solution.py:159
  44.9 0.1 pad_maximum_fusion
  44.9 2.1 %collective-permute-start.8 = (bf16[2,2,144,512]{3,2,1,0:T(8,128)(2,1)S(1)}, bf16[2,2,144,512]{3,2,1,0:T(8,128)(2,1)S(1)}, u32[]{:S(2)}, u32[]{:S(2)}) collective-permute-start(bf16[2,2,144,512]{3,2,1,0:T(8,128)(2,1)S(1)} %pad_maximum_fusion), channel_id=1, source_target_pairs={{0,6},{1,7},{2,4},{3,5},{4,2},{5,3},{6,0},{7,1},{8,14},{9,15},{10,... | collective-permute-start | bytes 1769480 | tf_op jit(solution)/shard_map/ppermute | solution.py:159
  47.0 3.3 %shard_map.46 = (f32[2048,128]{1,0:T(8,128)S(1)}, f32[2048,128]{1,0:T(8,128)S(1)}, f32[2048,128]{1,0:T(8,128)S(1)}) custom-call(s32[1]{0:T(128)} %bitcast.core_ref, bf16[128,2048]{1,0:T(8,128)(2,1)S(1)} %collective-permute-done.4.q_ref, bf16[2,144,512]{2,1,0:T(8,128)(2,1)S(1)} %get-tuple-element.53.refs_0_, ...), custom_call_target="tpu_custom_call" | custom-call | flops 2147483648 | bytes 4194304 | tf_op jit(solution)/shard_map/pallas_call | solution.py:130
  50.4 0.0 collective-permute-done.6.refs_2_.refs_5_
  50.4 2.1 %collective-permute-start.7 = (bf16[2,144,512]{2,1,0:T(8,128)(2,1)S(1)}, bf16[2,144,512]{2,1,0:T(8,128)(2,1)S(1)}, u32[]{:S(2)}, u32[]{:S(2)}) collective-permute-start(bf16[2,144,512]{2,1,0:T(8,128)(2,1)S(1)} %collective-permute-done.6.refs_2_.refs_5_), channel_id=1, source_target_pairs={{0,2},{1,3},{2,0},{3,1},{4,6},{5,7},{6,4},{7,5},{8,10},{9,11},{10,... | collective-permute-start | bytes 884744 | tf_op jit(solution)/shard_map/ppermute | solution.py:156
  52.5 0.0 collective-permute-done.10.refs_1_.refs_4_
  52.5 2.1 %shard_map.47 = (f32[2048,128]{1,0:T(8,128)S(1)}, f32[2048,128]{1,0:T(8,128)S(1)}, f32[2048,128]{1,0:T(8,128)S(1)}) custom-call(s32[1]{0:T(128)} %bitcast.core_ref, bf16[128,2048]{1,0:T(8,128)(2,1)S(1)} %collective-permute-done.4.q_ref, bf16[2,144,512]{2,1,0:T(8,128)(2,1)S(1)} %get-tuple-element.53.refs_0_, ...), custom_call_target="tpu_custom_call" | custom-call | flops 1073741824 | bytes 4194304 | tf_op jit(solution)/shard_map/pallas_call | solution.py:130
  54.6 0.0 collective-permute-done.9.q_ref
  54.6 4.6 %shard_map.48 = (f32[2048,128]{1,0:T(8,128)S(1)}, f32[2048,128]{1,0:T(8,128)S(1)}, f32[2048,128]{1,0:T(8,128)S(1)}) custom-call(s32[1]{0:T(128)} %bitcast.core_ref, bf16[128,2048]{1,0:T(8,128)(2,1)S(1)} %collective-permute-done.9.q_ref, bf16[2,144,512]{2,1,0:T(8,128)(2,1)S(1)} %get-tuple-element.53.refs_0_, ...), custom_call_target="tpu_custom_call" | custom-call | flops 3221225472 | bytes 4194304 | tf_op jit(solution)/shard_map/pallas_call | solution.py:130
  59.2 4.2 %collective-permute-done.8.refs_2_ = bf16[2,2,144,512]{3,2,1,0:T(8,128)(2,1)S(1)} collective-permute-done((bf16[2,2,144,512]{3,2,1,0:T(8,128)(2,1)S(1)}, bf16[2,2,144,512]{3,2,1,0:T(8,128)(2,1)S(1)}, u32[]{:S(2)}, u32[]{:S(2)}) %collective-permute-start.8) | collective-permute-done | bytes 589856 | tf_op jit(solution)/shard_map/ppermute | solution.py:159
  63.4 0.0 collective-permute-done.7.refs_1_
  63.4 2.7 %shard_map.50 = bf16[128,2048]{1,0:T(8,128)(2,1)S(1)} custom-call(s32[1]{0:T(128)} %bitcast.core_ref, bf16[128,2048]{1,0:T(8,128)(2,1)S(1)} %collective-permute-done.4.q_ref, bf16[2,144,512]{2,1,0:T(8,128)(2,1)S(1)} %get-tuple-element.53.refs_0_, bf16[2,144,512]{2,1,0:T(8,128)(2,1)S(1)} %collective-permute-done.7.refs_1_, ...), custom_call_target="tpu_custom_call" | custom-call | flops 1610612736 | bytes 4194304 | tf_op jit(solution)/shard_map/pallas_call | solution.py:130
  66.1 4.1 %collective-permute-start.11 = (bf16[128,2048]{1,0:T(8,128)(2,1)S(1)}, bf16[128,2048]{1,0:T(8,128)(2,1)S(1)}, u32[]{:S(2)}, u32[]{:S(2)}) collective-permute-start(bf16[128,2048]{1,0:T(8,128)(2,1)S(1)} %shard_map.50), channel_id=1, source_target_pairs={{0,1},{1,0},{2,3},{3,2},{4,5},{5,4},{6,7},{7,6},{8,9},{9,8},{10,11... | collective-permute-start | bytes 1572872 | tf_op jit(solution)/shard_map/ppermute | solution.py:162
  70.3 2.7 %shard_map.49 = bf16[128,2048]{1,0:T(8,128)(2,1)S(1)} custom-call(s32[1]{0:T(128)} %bitcast.core_ref, bf16[128,2048]{1,0:T(8,128)(2,1)S(1)} %collective-permute-done.9.q_ref, bf16[2,144,512]{2,1,0:T(8,128)(2,1)S(1)} %get-tuple-element.53.refs_0_, bf16[2,144,512]{2,1,0:T(8,128)(2,1)S(1)} %collective-permute-done.7.refs_1_, ...), custom_call_target="tpu_custom_call" | custom-call | flops 1610612736 | bytes 4194304 | tf_op jit(solution)/shard_map/pallas_call | solution.py:130
  73.0 0.0 collective-permute-done.11
  73.0 1.2 %maximum_select_fusion = bf16[1,128,4096]{2,1,0:T(8,128)(2,1)} fusion(bf16[1,128,2048]{2,1,0:T(8,128)(2,1)S(1)} %bitcast.14, bf16[1,128,2048]{2,1,0:T(8,128)(2,1)S(1)} %bitcast.11, pred[]{:T(512)S(6)} %eq.16), kind=kLoop, calls=%fused_computation | loop fusion | flops 4718592 | bytes 2097153 | tf_op jit(solution)/shard_map/jit(_where)/select_n | solution.py:195
  (2 shorter events, 0.1 us)
Async XLA Ops:
  0.0 13.5 %copy-start = (bf16[1,128,4096]{2,1,0:T(8,128)(2,1)S(1)}, bf16[1,128,4096]{2,1,0:T(8,128)(2,1)}, u32[]{:S(2)}) copy-start(bf16[1,128,4096]{2,1,0:T(8,128)(2,1)} %param.4) | copy-start | bytes 3145732
  1.8 18.0 %collective-permute-start = (bf16[144,512]{1,0:T(8,128)(2,1)S(1)}, bf16[144,512]{1,0:T(8,128)(2,1)S(1)}, u32[]{:S(2)}, u32[]{:S(2)}) collective-permute-start(bf16[144,512]{1,0:T(8,128)(2,1)S(1)} %get-tuple-element.69), channel_id=1, source_target_pairs={{0,72},{1,73},{2,74},{3,75},{4,76},{5,77},{6,78},{7,79},{8,80},{9,... | collective-permute-start | bytes 442376 | tf_op jit(solution)/shard_map/ppermute | solution.py:150
  7.6 15.9 %collective-permute-start.1 = (bf16[144,512]{1,0:T(8,128)(2,1)S(1)}, bf16[144,512]{1,0:T(8,128)(2,1)S(1)}, u32[]{:S(2)}, u32[]{:S(2)}) collective-permute-start(bf16[144,512]{1,0:T(8,128)(2,1)S(1)} %get-tuple-element.70), channel_id=1, source_target_pairs={{0,73},{1,72},{2,75},{3,74},{4,77},{5,76},{6,79},{7,78},{8,81},{9,... | collective-permute-start | bytes 442376 | tf_op jit(solution)/shard_map/ppermute | solution.py:150
  13.6 24.6 %collective-permute-start.4 = (bf16[128,2048]{1,0:T(8,128)(2,1)S(1)}, bf16[128,2048]{1,0:T(8,128)(2,1)S(1)}, u32[]{:S(2)}, u32[]{:S(2)}) collective-permute-start(bf16[128,2048]{1,0:T(8,128)(2,1)S(1)} %get-tuple-element.64), channel_id=1, source_target_pairs={{0,65},{1,64},{2,67},{3,66},{4,69},{5,68},{6,71},{7,70},{8,73},{9,... | collective-permute-start | bytes 1572872 | tf_op jit(solution)/shard_map/ppermute | solution.py:150
  23.6 11.6 %collective-permute-start.5 = (bf16[2,144,512]{2,1,0:T(8,128)(2,1)S(1)}, bf16[2,144,512]{2,1,0:T(8,128)(2,1)S(1)}, u32[]{:S(2)}, u32[]{:S(2)}) collective-permute-start(bf16[2,144,512]{2,1,0:T(8,128)(2,1)S(1)} %pad_maximum_fusion.1.refs_1_), channel_id=1, source_target_pairs={{0,2},{1,3},{2,0},{3,1},{4,6},{5,7},{6,4},{7,5},{8,10},{9,11},{10,... | collective-permute-start | bytes 884744 | tf_op jit(solution)/shard_map/ppermute | solution.py:156
  26.7 8.7 %collective-permute-start.3 = (bf16[2,144,512]{2,1,0:T(8,128)(2,1)S(1)}, bf16[2,144,512]{2,1,0:T(8,128)(2,1)S(1)}, u32[]{:S(2)}, u32[]{:S(2)}) collective-permute-start(bf16[2,144,512]{2,1,0:T(8,128)(2,1)S(1)} %pad_maximum_fusion.1.refs_1_), channel_id=1, source_target_pairs={{0,56},{1,9},{2,58},{3,11},{4,60},{5,13},{6,62},{7,15},{8,0},{9,17... | collective-permute-start | bytes 884744 | tf_op jit(solution)/shard_map/ppermute | solution.py:153
  28.6 9.6 %collective-permute-start.2 = (bf16[2,144,512]{2,1,0:T(8,128)(2,1)S(1)}, bf16[2,144,512]{2,1,0:T(8,128)(2,1)S(1)}, u32[]{:S(2)}, u32[]{:S(2)}) collective-permute-start(bf16[2,144,512]{2,1,0:T(8,128)(2,1)S(1)} %pad_maximum_fusion.1.refs_1_), channel_id=1, source_target_pairs={{0,8},{1,57},{2,10},{3,59},{4,12},{5,61},{6,14},{7,63},{8,16},{9,1... | collective-permute-start | bytes 884744 | tf_op jit(solution)/shard_map/ppermute | solution.py:153
  33.2 21.4 %collective-permute-start.9 = (bf16[128,2048]{1,0:T(8,128)(2,1)S(1)}, bf16[128,2048]{1,0:T(8,128)(2,1)S(1)}, u32[]{:S(2)}, u32[]{:S(2)}) collective-permute-start(bf16[128,2048]{1,0:T(8,128)(2,1)S(1)} %get-tuple-element.63), channel_id=1, source_target_pairs={{0,64},{1,65},{2,66},{3,67},{4,68},{5,69},{6,70},{7,71},{8,72},{9,... | collective-permute-start | bytes 1572872 | tf_op jit(solution)/shard_map/ppermute | solution.py:150
  38.3 14.2 %collective-permute-start.10 = (bf16[2,144,512]{2,1,0:T(8,128)(2,1)S(1)}, bf16[2,144,512]{2,1,0:T(8,128)(2,1)S(1)}, u32[]{:S(2)}, u32[]{:S(2)}) collective-permute-start(bf16[2,144,512]{2,1,0:T(8,128)(2,1)S(1)} %get-tuple-element.65), channel_id=1, source_target_pairs={{0,2},{1,3},{2,0},{3,1},{4,6},{5,7},{6,4},{7,5},{8,10},{9,11},{10,... | collective-permute-start | bytes 884744 | tf_op jit(solution)/shard_map/ppermute | solution.py:156
  40.5 9.9 %collective-permute-start.6 = (bf16[2,144,512]{2,1,0:T(8,128)(2,1)S(1)}, bf16[2,144,512]{2,1,0:T(8,128)(2,1)S(1)}, u32[]{:S(2)}, u32[]{:S(2)}) collective-permute-start(bf16[2,144,512]{2,1,0:T(8,128)(2,1)S(1)} %get-tuple-element.68), channel_id=1, source_target_pairs={{0,6},{1,7},{2,4},{3,5},{4,2},{5,3},{6,0},{7,1},{8,14},{9,15},{10,... | collective-permute-start | bytes 884744 | tf_op jit(solution)/shard_map/ppermute | solution.py:159
  44.9 18.5 %collective-permute-start.8 = (bf16[2,2,144,512]{3,2,1,0:T(8,128)(2,1)S(1)}, bf16[2,2,144,512]{3,2,1,0:T(8,128)(2,1)S(1)}, u32[]{:S(2)}, u32[]{:S(2)}) collective-permute-start(bf16[2,2,144,512]{3,2,1,0:T(8,128)(2,1)S(1)} %pad_maximum_fusion), channel_id=1, source_target_pairs={{0,6},{1,7},{2,4},{3,5},{4,2},{5,3},{6,0},{7,1},{8,14},{9,15},{10,... | collective-permute-start | bytes 1769480 | tf_op jit(solution)/shard_map/ppermute | solution.py:159
  50.4 13.0 %collective-permute-start.7 = (bf16[2,144,512]{2,1,0:T(8,128)(2,1)S(1)}, bf16[2,144,512]{2,1,0:T(8,128)(2,1)S(1)}, u32[]{:S(2)}, u32[]{:S(2)}) collective-permute-start(bf16[2,144,512]{2,1,0:T(8,128)(2,1)S(1)} %collective-permute-done.6.refs_2_.refs_5_), channel_id=1, source_target_pairs={{0,2},{1,3},{2,0},{3,1},{4,6},{5,7},{6,4},{7,5},{8,10},{9,11},{10,... | collective-permute-start | bytes 884744 | tf_op jit(solution)/shard_map/ppermute | solution.py:156
  66.1 6.8 %collective-permute-start.11 = (bf16[128,2048]{1,0:T(8,128)(2,1)S(1)}, bf16[128,2048]{1,0:T(8,128)(2,1)S(1)}, u32[]{:S(2)}, u32[]{:S(2)}) collective-permute-start(bf16[128,2048]{1,0:T(8,128)(2,1)S(1)} %shard_map.50), channel_id=1, source_target_pairs={{0,1},{1,0},{2,3},{3,2},{4,5},{5,4},{6,7},{7,6},{8,9},{9,8},{10,11... | collective-permute-start | bytes 1572872 | tf_op jit(solution)/shard_map/ppermute | solution.py:162

commit v7 on v6

--- a/solution.py
+++ b/solution.py
@@ -177,7 +177,7 @@
     e1 = even_pair(b4)
     ya = along_y(b4, 1, -1)
     yb = along_y(b4, -1, 1)
-    ya, yb, b4, qf, e1 = lax.optimization_barrier((ya, yb, b4, qf, e1))
+    ya, yb, b4, qf = lax.optimization_barrier((ya, yb, b4, qf))
     f2 = odd_pair(jnp.where((column < 2) == first, yb, ya))
     e2 = even_pair(jnp.where((column % 2 == 0) == first, yb, ya))
     f13 = odd_pair(jnp.stack([b4, e1]))

time: 74.7 us -> 72.4 us (0.969)
  waiting for transfers between devices: 13.7 us -> 9.81 us
  starting transfers between devices: 41.5 us -> 43.1 us
    ppermute x2, waiting for transfers between devices: 3.01 us -> 0.01 us  [along_y(): lax.ppermute(block, 'sp', [(s, (s + 8 * (step1 if s % 2 else step0)) % 64...]
    ppermute x2, waiting for transfers between devices: 4.2 us -> 3.27 us  [odd_pair(): lax.ppermute(block, 'sp', [(s, s // 8 * 8 + (s + (2 if s & 2 else -2)) %...]
  transfers between devices with their start and end apart: 12 -> 12, of which waited for: 5 -> 3; matrix products, arithmetic and copies ran while one was open for 0% -> 0% of each run, Pallas kernels for 17% -> 18%
where the time goes in v7:
time: 72.4 us; the launch traced here: 71.9 us
  starting transfers between devices  43.1 us (60%)
  Pallas kernels  15.4 us (21%)
  waiting for transfers between devices  9.81 us (14%)
  other arithmetic  2.26 us (3%)
  local copies, waits for them, and re-layouts  0.96 us (1%)
    ppermute x4, starting transfers between devices, section(): return lax.ppermute(block, ('pp', 'sp'), pairs)  17.1 us
    pallas_call x5, Pallas kernels, attend(): pl.pallas_call(functools.partial(piece, half, own, bool(state), last, 1 +...  15.4 us
    ppermute x3, starting transfers between devices, even_pair(): return lax.ppermute(block, 'sp', [(s, s ^ 2) for s in range(64)])  8.08 us
    ppermute x2, starting transfers between devices, odd_pair(): lax.ppermute(block, 'sp', [(s, s // 8 * 8 + (s + (2 if s & 2 else -2)) %...  6.85 us
    ppermute x4, waiting for transfers between devices, section(): return lax.ppermute(block, ('pp', 'sp'), pairs)  6.52 us
    ppermute x2, starting transfers between devices, along_y(): lax.ppermute(block, 'sp', [(s, (s + 8 * (step1 if s % 2 else step0)) % 64...  6.49 us
    ppermute x1, starting transfers between devices, swap(): return lax.ppermute(block, 'sp', [(s, s ^ 1) for s in range(64)])  4.67 us
    ppermute x2, waiting for transfers between devices, odd_pair(): lax.ppermute(block, 'sp', [(s, s // 8 * 8 + (s + (2 if s & 2 else -2)) %...  3.27 us
  transfers between devices with their start and end apart: 12, of which 3 were waited for; matrix products, arithmetic and copies ran while one was open for 0% of the time, Pallas kernels for 18%

profile of v7, /device:TPU:1, one launch (start us, length us, event | category | flops | bytes accessed | tf_op | source)
XLA Modules:
  0.0 71.9 jit_solution(11499592062206478783)
XLA Ops:
  0.0 0.0 copy-start
  0.0 0.7 %convert_element_type.6 = bf16[1,128]{1,0:T(2,128)(2,1)S(1)} convert(s32[1,128]{1,0:T(1,128)} %param.7) | non-fusion elementwise | flops 128 | bytes 768 | tf_op jit(solution)/shard_map/convert_element_type | solution.py:164
  0.8 1.0 %fusion.3 = (bf16[128,256]{1,0:T(8,128)(2,1)S(1)}, bf16[128,256]{1,0:T(8,128)(2,1)S(1)}, bf16[128,256]{1,0:T(8,128)(2,1)S(1)}, bf16[128,256]{1,0:T(8,128)(2,1)S(1)}) fusion(bf16[128,512]{1,0:T(8,128)(2,1)} %bitcast.17, bf16[128,512]{1,0:T(8,128)(2,1)} %bitcast.18), kind=kLoop, calls=%fused_computation.15 | loop fusion | bytes 524288 | tf_op jit(solution)/shard_map/slice | solution.py:168
  1.8 5.8 %collective-permute-start = (bf16[144,512]{1,0:T(8,128)(2,1)S(1)}, bf16[144,512]{1,0:T(8,128)(2,1)S(1)}, u32[]{:S(2)}, u32[]{:S(2)}) collective-permute-start(bf16[144,512]{1,0:T(8,128)(2,1)S(1)} %get-tuple-element.67), channel_id=1, source_target_pairs={{0,72},{1,73},{2,74},{3,75},{4,76},{5,77},{6,78},{7,79},{8,80},{9,... | collective-permute-start | bytes 442376 | tf_op jit(solution)/shard_map/ppermute | solution.py:150
  7.6 5.9 %collective-permute-start.1 = (bf16[144,512]{1,0:T(8,128)(2,1)S(1)}, bf16[144,512]{1,0:T(8,128)(2,1)S(1)}, u32[]{:S(2)}, u32[]{:S(2)}) collective-permute-start(bf16[144,512]{1,0:T(8,128)(2,1)S(1)} %get-tuple-element.68), channel_id=1, source_target_pairs={{0,73},{1,72},{2,75},{3,74},{4,77},{5,76},{6,79},{7,78},{8,81},{9,... | collective-permute-start | bytes 442376 | tf_op jit(solution)/shard_map/ppermute | solution.py:150
  13.5 0.0 copy-done
  13.5 0.1 broadcast_select_fusion
  13.6 3.4 %collective-permute-start.4 = (bf16[128,2048]{1,0:T(8,128)(2,1)S(1)}, bf16[128,2048]{1,0:T(8,128)(2,1)S(1)}, u32[]{:S(2)}, u32[]{:S(2)}) collective-permute-start(bf16[128,2048]{1,0:T(8,128)(2,1)S(1)} %get-tuple-element.62), channel_id=1, source_target_pairs={{0,65},{1,64},{2,67},{3,66},{4,69},{5,68},{6,71},{7,70},{8,73},{9,... | collective-permute-start | bytes 1572872 | tf_op jit(solution)/shard_map/ppermute | solution.py:150
  17.0 2.7 %collective-permute-done = bf16[144,512]{1,0:T(8,128)(2,1)S(1)} collective-permute-done((bf16[144,512]{1,0:T(8,128)(2,1)S(1)}, bf16[144,512]{1,0:T(8,128)(2,1)S(1)}, u32[]{:S(2)}, u32[]{:S(2)}) %collective-permute-start) | collective-permute-done | bytes 147488 | tf_op jit(solution)/shard_map/ppermute | solution.py:150
  19.7 3.8 %collective-permute-done.1 = bf16[144,512]{1,0:T(8,128)(2,1)S(1)} collective-permute-done((bf16[144,512]{1,0:T(8,128)(2,1)S(1)}, bf16[144,512]{1,0:T(8,128)(2,1)S(1)}, u32[]{:S(2)}, u32[]{:S(2)}) %collective-permute-start.1) | collective-permute-done | bytes 147488 | tf_op jit(solution)/shard_map/ppermute | solution.py:150
  23.6 1.9 %collective-permute-start.3 = (bf16[2,144,512]{2,1,0:T(8,128)(2,1)S(1)}, bf16[2,144,512]{2,1,0:T(8,128)(2,1)S(1)}, u32[]{:S(2)}, u32[]{:S(2)}) collective-permute-start(bf16[2,144,512]{2,1,0:T(8,128)(2,1)S(1)} %pad_maximum_fusion.1.refs_1_), channel_id=1, source_target_pairs={{0,56},{1,9},{2,58},{3,11},{4,60},{5,13},{6,62},{7,15},{8,0},{9,17... | collective-permute-start | bytes 884744 | tf_op jit(solution)/shard_map/ppermute | solution.py:153
  25.5 4.6 %collective-permute-start.2 = (bf16[2,144,512]{2,1,0:T(8,128)(2,1)S(1)}, bf16[2,144,512]{2,1,0:T(8,128)(2,1)S(1)}, u32[]{:S(2)}, u32[]{:S(2)}) collective-permute-start(bf16[2,144,512]{2,1,0:T(8,128)(2,1)S(1)} %pad_maximum_fusion.1.refs_1_), channel_id=1, source_target_pairs={{0,8},{1,57},{2,10},{3,59},{4,12},{5,61},{6,14},{7,63},{8,16},{9,1... | collective-permute-start | bytes 884744 | tf_op jit(solution)/shard_map/ppermute | solution.py:153
  30.1 3.1 %collective-permute-start.6 = (bf16[2,144,512]{2,1,0:T(8,128)(2,1)S(1)}, bf16[2,144,512]{2,1,0:T(8,128)(2,1)S(1)}, u32[]{:S(2)}, u32[]{:S(2)}) collective-permute-start(bf16[2,144,512]{2,1,0:T(8,128)(2,1)S(1)} %pad_maximum_fusion.1.refs_1_), channel_id=1, source_target_pairs={{0,2},{1,3},{2,0},{3,1},{4,6},{5,7},{6,4},{7,5},{8,10},{9,11},{10,... | collective-permute-start | bytes 884744 | tf_op jit(solution)/shard_map/ppermute | solution.py:156
  33.2 1.9 %collective-permute-start.9 = (bf16[128,2048]{1,0:T(8,128)(2,1)S(1)}, bf16[128,2048]{1,0:T(8,128)(2,1)S(1)}, u32[]{:S(2)}, u32[]{:S(2)}) collective-permute-start(bf16[128,2048]{1,0:T(8,128)(2,1)S(1)} %get-tuple-element.61), channel_id=1, source_target_pairs={{0,64},{1,65},{2,66},{3,67},{4,68},{5,69},{6,70},{7,71},{8,72},{9,... | collective-permute-start | bytes 1572872 | tf_op jit(solution)/shard_map/ppermute | solution.py:150
  35.2 0.0 collective-permute-done.3
  35.2 0.0 collective-permute-done.2
  35.2 0.0 collective-permute-done.4.q_ref
  35.2 0.1 broadcast_select_fusion.2
  35.3 2.9 %collective-permute-start.10 = (bf16[2,144,512]{2,1,0:T(8,128)(2,1)S(1)}, bf16[2,144,512]{2,1,0:T(8,128)(2,1)S(1)}, u32[]{:S(2)}, u32[]{:S(2)}) collective-permute-start(bf16[2,144,512]{2,1,0:T(8,128)(2,1)S(1)} %get-tuple-element.63), channel_id=1, source_target_pairs={{0,2},{1,3},{2,0},{3,1},{4,6},{5,7},{6,4},{7,5},{8,10},{9,11},{10,... | collective-permute-start | bytes 884744 | tf_op jit(solution)/shard_map/ppermute | solution.py:156
  38.2 3.7 %collective-permute-start.5 = (bf16[2,144,512]{2,1,0:T(8,128)(2,1)S(1)}, bf16[2,144,512]{2,1,0:T(8,128)(2,1)S(1)}, u32[]{:S(2)}, u32[]{:S(2)}) collective-permute-start(bf16[2,144,512]{2,1,0:T(8,128)(2,1)S(1)} %get-tuple-element.66), channel_id=1, source_target_pairs={{0,6},{1,7},{2,4},{3,5},{4,2},{5,3},{6,0},{7,1},{8,14},{9,15},{10,... | collective-permute-start | bytes 884744 | tf_op jit(solution)/shard_map/ppermute | solution.py:159
  41.9 0.0 collective-permute-done.6.refs_3_
  41.9 0.1 pad_maximum_fusion
  42.0 3.1 %collective-permute-start.8 = (bf16[2,2,144,512]{3,2,1,0:T(8,128)(2,1)S(1)}, bf16[2,2,144,512]{3,2,1,0:T(8,128)(2,1)S(1)}, u32[]{:S(2)}, u32[]{:S(2)}) collective-permute-start(bf16[2,2,144,512]{3,2,1,0:T(8,128)(2,1)S(1)} %pad_maximum_fusion), channel_id=1, source_target_pairs={{0,6},{1,7},{2,4},{3,5},{4,2},{5,3},{6,0},{7,1},{8,14},{9,15},{10,... | collective-permute-start | bytes 1769480 | tf_op jit(solution)/shard_map/ppermute | solution.py:159
  45.1 3.3 %shard_map.46 = (f32[2048,128]{1,0:T(8,128)S(1)}, f32[2048,128]{1,0:T(8,128)S(1)}, f32[2048,128]{1,0:T(8,128)S(1)}) custom-call(s32[1]{0:T(128)} %bitcast.core_ref, bf16[128,2048]{1,0:T(8,128)(2,1)S(1)} %collective-permute-done.4.q_ref, bf16[2,144,512]{2,1,0:T(8,128)(2,1)S(1)} %get-tuple-element.51.refs_0_, ...), custom_call_target="tpu_custom_call" | custom-call | flops 2147483648 | bytes 4194304 | tf_op jit(solution)/shard_map/pallas_call | solution.py:130
  48.5 0.0 collective-permute-done.5.refs_2_.refs_5_
  48.5 2.1 %collective-permute-start.7 = (bf16[2,144,512]{2,1,0:T(8,128)(2,1)S(1)}, bf16[2,144,512]{2,1,0:T(8,128)(2,1)S(1)}, u32[]{:S(2)}, u32[]{:S(2)}) collective-permute-start(bf16[2,144,512]{2,1,0:T(8,128)(2,1)S(1)} %collective-permute-done.5.refs_2_.refs_5_), channel_id=1, source_target_pairs={{0,2},{1,3},{2,0},{3,1},{4,6},{5,7},{6,4},{7,5},{8,10},{9,11},{10,... | collective-permute-start | bytes 884744 | tf_op jit(solution)/shard_map/ppermute | solution.py:156
  50.6 0.0 collective-permute-done.10.refs_1_.refs_4_
  50.6 2.1 %shard_map.47 = (f32[2048,128]{1,0:T(8,128)S(1)}, f32[2048,128]{1,0:T(8,128)S(1)}, f32[2048,128]{1,0:T(8,128)S(1)}) custom-call(s32[1]{0:T(128)} %bitcast.core_ref, bf16[128,2048]{1,0:T(8,128)(2,1)S(1)} %collective-permute-done.4.q_ref, bf16[2,144,512]{2,1,0:T(8,128)(2,1)S(1)} %get-tuple-element.51.refs_0_, ...), custom_call_target="tpu_custom_call" | custom-call | flops 1073741824 | bytes 4194304 | tf_op jit(solution)/shard_map/pallas_call | solution.py:130
  52.7 0.0 collective-permute-done.9.q_ref
  52.7 4.6 %shard_map.48 = (f32[2048,128]{1,0:T(8,128)S(1)}, f32[2048,128]{1,0:T(8,128)S(1)}, f32[2048,128]{1,0:T(8,128)S(1)}) custom-call(s32[1]{0:T(128)} %bitcast.core_ref, bf16[128,2048]{1,0:T(8,128)(2,1)S(1)} %collective-permute-done.9.q_ref, bf16[2,144,512]{2,1,0:T(8,128)(2,1)S(1)} %get-tuple-element.51.refs_0_, ...), custom_call_target="tpu_custom_call" | custom-call | flops 3221225472 | bytes 4194304 | tf_op jit(solution)/shard_map/pallas_call | solution.py:130
  57.3 3.3 %collective-permute-done.8.refs_2_ = bf16[2,2,144,512]{3,2,1,0:T(8,128)(2,1)S(1)} collective-permute-done((bf16[2,2,144,512]{3,2,1,0:T(8,128)(2,1)S(1)}, bf16[2,2,144,512]{3,2,1,0:T(8,128)(2,1)S(1)}, u32[]{:S(2)}, u32[]{:S(2)}) %collective-permute-start.8) | collective-permute-done | bytes 589856 | tf_op jit(solution)/shard_map/ppermute | solution.py:159
  60.6 0.0 collective-permute-done.7.refs_1_
  60.6 2.7 %shard_map.50 = bf16[128,2048]{1,0:T(8,128)(2,1)S(1)} custom-call(s32[1]{0:T(128)} %bitcast.core_ref, bf16[128,2048]{1,0:T(8,128)(2,1)S(1)} %collective-permute-done.4.q_ref, bf16[2,144,512]{2,1,0:T(8,128)(2,1)S(1)} %get-tuple-element.51.refs_0_, bf16[2,144,512]{2,1,0:T(8,128)(2,1)S(1)} %collective-permute-done.7.refs_1_, ...), custom_call_target="tpu_custom_call" | custom-call | flops 1610612736 | bytes 4194304 | tf_op jit(solution)/shard_map/pallas_call | solution.py:130
  63.3 4.7 %collective-permute-start.11 = (bf16[128,2048]{1,0:T(8,128)(2,1)S(1)}, bf16[128,2048]{1,0:T(8,128)(2,1)S(1)}, u32[]{:S(2)}, u32[]{:S(2)}) collective-permute-start(bf16[128,2048]{1,0:T(8,128)(2,1)S(1)} %shard_map.50), channel_id=1, source_target_pairs={{0,1},{1,0},{2,3},{3,2},{4,5},{5,4},{6,7},{7,6},{8,9},{9,8},{10,11... | collective-permute-start | bytes 1572872 | tf_op jit(solution)/shard_map/ppermute | solution.py:162
  68.0 2.7 %shard_map.49 = bf16[128,2048]{1,0:T(8,128)(2,1)S(1)} custom-call(s32[1]{0:T(128)} %bitcast.core_ref, bf16[128,2048]{1,0:T(8,128)(2,1)S(1)} %collective-permute-done.9.q_ref, bf16[2,144,512]{2,1,0:T(8,128)(2,1)S(1)} %get-tuple-element.51.refs_0_, bf16[2,144,512]{2,1,0:T(8,128)(2,1)S(1)} %collective-permute-done.7.refs_1_, ...), custom_call_target="tpu_custom_call" | custom-call | flops 1610612736 | bytes 4194304 | tf_op jit(solution)/shard_map/pallas_call | solution.py:130
  70.7 0.0 collective-permute-done.11
  70.7 1.2 %maximum_select_fusion = bf16[1,128,4096]{2,1,0:T(8,128)(2,1)} fusion(bf16[1,128,2048]{2,1,0:T(8,128)(2,1)S(1)} %bitcast.14, bf16[1,128,2048]{2,1,0:T(8,128)(2,1)S(1)} %bitcast.11, pred[]{:T(512)S(6)} %eq.16), kind=kLoop, calls=%fused_computation | loop fusion | flops 4718592 | bytes 2097153 | tf_op jit(solution)/shard_map/jit(_where)/select_n | solution.py:195
  (2 shorter events, 0.1 us)
Async XLA Ops:
  0.0 13.5 %copy-start = (bf16[1,128,4096]{2,1,0:T(8,128)(2,1)S(1)}, bf16[1,128,4096]{2,1,0:T(8,128)(2,1)}, u32[]{:S(2)}) copy-start(bf16[1,128,4096]{2,1,0:T(8,128)(2,1)} %param.4) | copy-start | bytes 3145732
  1.8 18.0 %collective-permute-start = (bf16[144,512]{1,0:T(8,128)(2,1)S(1)}, bf16[144,512]{1,0:T(8,128)(2,1)S(1)}, u32[]{:S(2)}, u32[]{:S(2)}) collective-permute-start(bf16[144,512]{1,0:T(8,128)(2,1)S(1)} %get-tuple-element.67), channel_id=1, source_target_pairs={{0,72},{1,73},{2,74},{3,75},{4,76},{5,77},{6,78},{7,79},{8,80},{9,... | collective-permute-start | bytes 442376 | tf_op jit(solution)/shard_map/ppermute | solution.py:150
  7.6 15.9 %collective-permute-start.1 = (bf16[144,512]{1,0:T(8,128)(2,1)S(1)}, bf16[144,512]{1,0:T(8,128)(2,1)S(1)}, u32[]{:S(2)}, u32[]{:S(2)}) collective-permute-start(bf16[144,512]{1,0:T(8,128)(2,1)S(1)} %get-tuple-element.68), channel_id=1, source_target_pairs={{0,73},{1,72},{2,75},{3,74},{4,77},{5,76},{6,79},{7,78},{8,81},{9,... | collective-permute-start | bytes 442376 | tf_op jit(solution)/shard_map/ppermute | solution.py:150
  13.6 21.6 %collective-permute-start.4 = (bf16[128,2048]{1,0:T(8,128)(2,1)S(1)}, bf16[128,2048]{1,0:T(8,128)(2,1)S(1)}, u32[]{:S(2)}, u32[]{:S(2)}) collective-permute-start(bf16[128,2048]{1,0:T(8,128)(2,1)S(1)} %get-tuple-element.62), channel_id=1, source_target_pairs={{0,65},{1,64},{2,67},{3,66},{4,69},{5,68},{6,71},{7,70},{8,73},{9,... | collective-permute-start | bytes 1572872 | tf_op jit(solution)/shard_map/ppermute | solution.py:150
  23.6 11.6 %collective-permute-start.3 = (bf16[2,144,512]{2,1,0:T(8,128)(2,1)S(1)}, bf16[2,144,512]{2,1,0:T(8,128)(2,1)S(1)}, u32[]{:S(2)}, u32[]{:S(2)}) collective-permute-start(bf16[2,144,512]{2,1,0:T(8,128)(2,1)S(1)} %pad_maximum_fusion.1.refs_1_), channel_id=1, source_target_pairs={{0,56},{1,9},{2,58},{3,11},{4,60},{5,13},{6,62},{7,15},{8,0},{9,17... | collective-permute-start | bytes 884744 | tf_op jit(solution)/shard_map/ppermute | solution.py:153
  25.5 9.7 %collective-permute-start.2 = (bf16[2,144,512]{2,1,0:T(8,128)(2,1)S(1)}, bf16[2,144,512]{2,1,0:T(8,128)(2,1)S(1)}, u32[]{:S(2)}, u32[]{:S(2)}) collective-permute-start(bf16[2,144,512]{2,1,0:T(8,128)(2,1)S(1)} %pad_maximum_fusion.1.refs_1_), channel_id=1, source_target_pairs={{0,8},{1,57},{2,10},{3,59},{4,12},{5,61},{6,14},{7,63},{8,16},{9,1... | collective-permute-start | bytes 884744 | tf_op jit(solution)/shard_map/ppermute | solution.py:153
  30.1 11.8 %collective-permute-start.6 = (bf16[2,144,512]{2,1,0:T(8,128)(2,1)S(1)}, bf16[2,144,512]{2,1,0:T(8,128)(2,1)S(1)}, u32[]{:S(2)}, u32[]{:S(2)}) collective-permute-start(bf16[2,144,512]{2,1,0:T(8,128)(2,1)S(1)} %pad_maximum_fusion.1.refs_1_), channel_id=1, source_target_pairs={{0,2},{1,3},{2,0},{3,1},{4,6},{5,7},{6,4},{7,5},{8,10},{9,11},{10,... | collective-permute-start | bytes 884744 | tf_op jit(solution)/shard_map/ppermute | solution.py:156
  33.2 19.5 %collective-permute-start.9 = (bf16[128,2048]{1,0:T(8,128)(2,1)S(1)}, bf16[128,2048]{1,0:T(8,128)(2,1)S(1)}, u32[]{:S(2)}, u32[]{:S(2)}) collective-permute-start(bf16[128,2048]{1,0:T(8,128)(2,1)S(1)} %get-tuple-element.61), channel_id=1, source_target_pairs={{0,64},{1,65},{2,66},{3,67},{4,68},{5,69},{6,70},{7,71},{8,72},{9,... | collective-permute-start | bytes 1572872 | tf_op jit(solution)/shard_map/ppermute | solution.py:150
  35.3 15.3 %collective-permute-start.10 = (bf16[2,144,512]{2,1,0:T(8,128)(2,1)S(1)}, bf16[2,144,512]{2,1,0:T(8,128)(2,1)S(1)}, u32[]{:S(2)}, u32[]{:S(2)}) collective-permute-start(bf16[2,144,512]{2,1,0:T(8,128)(2,1)S(1)} %get-tuple-element.63), channel_id=1, source_target_pairs={{0,2},{1,3},{2,0},{3,1},{4,6},{5,7},{6,4},{7,5},{8,10},{9,11},{10,... | collective-permute-start | bytes 884744 | tf_op jit(solution)/shard_map/ppermute | solution.py:156
  38.2 10.3 %collective-permute-start.5 = (bf16[2,144,512]{2,1,0:T(8,128)(2,1)S(1)}, bf16[2,144,512]{2,1,0:T(8,128)(2,1)S(1)}, u32[]{:S(2)}, u32[]{:S(2)}) collective-permute-start(bf16[2,144,512]{2,1,0:T(8,128)(2,1)S(1)} %get-tuple-element.66), channel_id=1, source_target_pairs={{0,6},{1,7},{2,4},{3,5},{4,2},{5,3},{6,0},{7,1},{8,14},{9,15},{10,... | collective-permute-start | bytes 884744 | tf_op jit(solution)/shard_map/ppermute | solution.py:159
  42.0 18.6 %collective-permute-start.8 = (bf16[2,2,144,512]{3,2,1,0:T(8,128)(2,1)S(1)}, bf16[2,2,144,512]{3,2,1,0:T(8,128)(2,1)S(1)}, u32[]{:S(2)}, u32[]{:S(2)}) collective-permute-start(bf16[2,2,144,512]{3,2,1,0:T(8,128)(2,1)S(1)} %pad_maximum_fusion), channel_id=1, source_target_pairs={{0,6},{1,7},{2,4},{3,5},{4,2},{5,3},{6,0},{7,1},{8,14},{9,15},{10,... | collective-permute-start | bytes 1769480 | tf_op jit(solution)/shard_map/ppermute | solution.py:159
  48.5 12.1 %collective-permute-start.7 = (bf16[2,144,512]{2,1,0:T(8,128)(2,1)S(1)}, bf16[2,144,512]{2,1,0:T(8,128)(2,1)S(1)}, u32[]{:S(2)}, u32[]{:S(2)}) collective-permute-start(bf16[2,144,512]{2,1,0:T(8,128)(2,1)S(1)} %collective-permute-done.5.refs_2_.refs_5_), channel_id=1, source_target_pairs={{0,2},{1,3},{2,0},{3,1},{4,6},{5,7},{6,4},{7,5},{8,10},{9,11},{10,... | collective-permute-start | bytes 884744 | tf_op jit(solution)/shard_map/ppermute | solution.py:156
  63.3 7.4 %collective-permute-start.11 = (bf16[128,2048]{1,0:T(8,128)(2,1)S(1)}, bf16[128,2048]{1,0:T(8,128)(2,1)S(1)}, u32[]{:S(2)}, u32[]{:S(2)}) collective-permute-start(bf16[128,2048]{1,0:T(8,128)(2,1)S(1)} %shard_map.50), channel_id=1, source_target_pairs={{0,1},{1,0},{2,3},{3,2},{4,5},{5,4},{6,7},{7,6},{8,9},{9,8},{10,11... | collective-permute-start | bytes 1572872 | tf_op jit(solution)/shard_map/ppermute | solution.py:162

commit v8 on v7

--- a/solution.py
+++ b/solution.py
@@ -184,7 +184,7 @@
     b0, b8 = jnp.where(first, yb, ya), jnp.where(first, ya, yb)
     at = core[None].astype(jnp.int32)
     state = attend(at, 1, qf, b0, [b4, b8, e1], own=True)
-    f2, *state = lax.optimization_barrier((f2, *state))
+    (f2,) = lax.optimization_barrier((f2,))
     e3 = even_pair(f2)
     state2 = attend(at, 0, qs, b0, [b4, b8, e1, e2, f2], own=True)
     state = attend(at, 1, qf, b0, [e2, f2], state=state)

time: 72.4 us -> 70.9 us (0.979)
  starting transfers between devices: 43.1 us -> 40.7 us
  waiting for transfers between devices: 9.81 us -> 10.9 us
    ppermute x2, waiting for transfers between devices: 0.01 us -> 3.17 us  [along_y(): lax.ppermute(block, 'sp', [(s, (s + 8 * (step1 if s % 2 else step0)) % 64...]
    ppermute x2, waiting for transfers between devices: 3.27 us -> 1.32 us  [odd_pair(): lax.ppermute(block, 'sp', [(s, s // 8 * 8 + (s + (2 if s & 2 else -2)) %...]
    ppermute x1, starting transfers between devices: 4.67 us -> 3.14 us  [swap(): return lax.ppermute(block, 'sp', [(s, s ^ 1) for s in range(64)])]
    ppermute x2, starting transfers between devices: 6.49 us -> 5.28 us  [along_y(): lax.ppermute(block, 'sp', [(s, (s + 8 * (step1 if s % 2 else step0)) % 64...]
    ppermute x4, waiting for transfers between devices: 6.52 us -> 5.64 us  [section(): return lax.ppermute(block, ('pp', 'sp'), pairs)]
    ppermute x3, waiting for transfers between devices: 0.01 us -> 0.74 us  [even_pair(): return lax.ppermute(block, 'sp', [(s, s ^ 2) for s in range(64)])]
  transfers between devices with their start and end apart: 12 -> 12, of which waited for: 3 -> 5; matrix products, arithmetic and copies ran while one was open for 0% -> 0% of each run, Pallas kernels for 18% -> 18%
where the time goes in v8:
time: 70.9 us; the launch traced here: 70.4 us
  starting transfers between devices  40.7 us (57%)
  Pallas kernels  15.4 us (22%)
  waiting for transfers between devices  10.9 us (15%)
  other arithmetic  2.25 us (3%)
  local copies, waits for them, and re-layouts  0.96 us (1%)
    ppermute x4, starting transfers between devices, section(): return lax.ppermute(block, ('pp', 'sp'), pairs)  17.3 us
    pallas_call x5, Pallas kernels, attend(): pl.pallas_call(functools.partial(piece, half, own, bool(state), last, 1 +...  15.4 us
    ppermute x3, starting transfers between devices, even_pair(): return lax.ppermute(block, 'sp', [(s, s ^ 2) for s in range(64)])  7.81 us
    ppermute x2, starting transfers between devices, odd_pair(): lax.ppermute(block, 'sp', [(s, s // 8 * 8 + (s + (2 if s & 2 else -2)) %...  7.09 us
    ppermute x4, waiting for transfers between devices, section(): return lax.ppermute(block, ('pp', 'sp'), pairs)  5.64 us
    ppermute x2, starting transfers between devices, along_y(): lax.ppermute(block, 'sp', [(s, (s + 8 * (step1 if s % 2 else step0)) % 64...  5.28 us
    ppermute x2, waiting for transfers between devices, along_y(): lax.ppermute(block, 'sp', [(s, (s + 8 * (step1 if s % 2 else step0)) % 64...  3.17 us
    ppermute x1, starting transfers between devices, swap(): return lax.ppermute(block, 'sp', [(s, s ^ 1) for s in range(64)])  3.14 us
  transfers between devices with their start and end apart: 12, of which 5 were waited for; matrix products, arithmetic and copies ran while one was open for 0% of the time, Pallas kernels for 18%

profile of v8, /device:TPU:1, one launch (start us, length us, event | category | flops | bytes accessed | tf_op | source)
XLA Modules:
  0.0 70.4 jit_solution(14591313117455937835)
XLA Ops:
  0.0 0.0 copy-start
  0.0 0.7 %convert_element_type.6 = bf16[1,128]{1,0:T(2,128)(2,1)S(1)} convert(s32[1,128]{1,0:T(1,128)} %param.7) | non-fusion elementwise | flops 128 | bytes 768 | tf_op jit(solution)/shard_map/convert_element_type | solution.py:164
  0.8 1.0 %fusion.3 = (bf16[128,256]{1,0:T(8,128)(2,1)S(1)}, bf16[128,256]{1,0:T(8,128)(2,1)S(1)}, bf16[128,256]{1,0:T(8,128)(2,1)S(1)}, bf16[128,256]{1,0:T(8,128)(2,1)S(1)}) fusion(bf16[128,512]{1,0:T(8,128)(2,1)} %bitcast.17, bf16[128,512]{1,0:T(8,128)(2,1)} %bitcast.18), kind=kLoop, calls=%fused_computation.15 | loop fusion | bytes 524288 | tf_op jit(solution)/shard_map/slice | solution.py:168
  1.8 6.4 %collective-permute-start.1 = (bf16[144,512]{1,0:T(8,128)(2,1)S(1)}, bf16[144,512]{1,0:T(8,128)(2,1)S(1)}, u32[]{:S(2)}, u32[]{:S(2)}) collective-permute-start(bf16[144,512]{1,0:T(8,128)(2,1)S(1)} %get-tuple-element.60), channel_id=1, source_target_pairs={{0,73},{1,72},{2,75},{3,74},{4,77},{5,76},{6,79},{7,78},{8,81},{9,... | collective-permute-start | bytes 442376 | tf_op jit(solution)/shard_map/ppermute | solution.py:150
  8.2 5.0 %collective-permute-start = (bf16[144,512]{1,0:T(8,128)(2,1)S(1)}, bf16[144,512]{1,0:T(8,128)(2,1)S(1)}, u32[]{:S(2)}, u32[]{:S(2)}) collective-permute-start(bf16[144,512]{1,0:T(8,128)(2,1)S(1)} %get-tuple-element.59), channel_id=1, source_target_pairs={{0,72},{1,73},{2,74},{3,75},{4,76},{5,77},{6,78},{7,79},{8,80},{9,... | collective-permute-start | bytes 442376 | tf_op jit(solution)/shard_map/ppermute | solution.py:150
  13.2 0.0 copy-done
  13.2 0.1 broadcast_select_fusion
  13.3 4.0 %collective-permute-start.4 = (bf16[128,2048]{1,0:T(8,128)(2,1)S(1)}, bf16[128,2048]{1,0:T(8,128)(2,1)S(1)}, u32[]{:S(2)}, u32[]{:S(2)}) collective-permute-start(bf16[128,2048]{1,0:T(8,128)(2,1)S(1)} %get-tuple-element.54), channel_id=1, source_target_pairs={{0,65},{1,64},{2,67},{3,66},{4,69},{5,68},{6,71},{7,70},{8,73},{9,... | collective-permute-start | bytes 1572872 | tf_op jit(solution)/shard_map/ppermute | solution.py:150
  17.3 3.9 %collective-permute-done.1 = bf16[144,512]{1,0:T(8,128)(2,1)S(1)} collective-permute-done((bf16[144,512]{1,0:T(8,128)(2,1)S(1)}, bf16[144,512]{1,0:T(8,128)(2,1)S(1)}, u32[]{:S(2)}, u32[]{:S(2)}) %collective-permute-start.1) | collective-permute-done | bytes 147488 | tf_op jit(solution)/shard_map/ppermute | solution.py:150
  21.2 1.7 %collective-permute-done = bf16[144,512]{1,0:T(8,128)(2,1)S(1)} collective-permute-done((bf16[144,512]{1,0:T(8,128)(2,1)S(1)}, bf16[144,512]{1,0:T(8,128)(2,1)S(1)}, u32[]{:S(2)}, u32[]{:S(2)}) %collective-permute-start) | collective-permute-done | bytes 147488 | tf_op jit(solution)/shard_map/ppermute | solution.py:150
  23.0 3.0 %collective-permute-start.2 = (bf16[2,144,512]{2,1,0:T(8,128)(2,1)S(1)}, bf16[2,144,512]{2,1,0:T(8,128)(2,1)S(1)}, u32[]{:S(2)}, u32[]{:S(2)}) collective-permute-start(bf16[2,144,512]{2,1,0:T(8,128)(2,1)S(1)} %pad_maximum_fusion.1.refs_1_), channel_id=1, source_target_pairs={{0,8},{1,57},{2,10},{3,59},{4,12},{5,61},{6,14},{7,63},{8,16},{9,1... | collective-permute-start | bytes 884744 | tf_op jit(solution)/shard_map/ppermute | solution.py:153
  26.0 2.3 %collective-permute-start.3 = (bf16[2,144,512]{2,1,0:T(8,128)(2,1)S(1)}, bf16[2,144,512]{2,1,0:T(8,128)(2,1)S(1)}, u32[]{:S(2)}, u32[]{:S(2)}) collective-permute-start(bf16[2,144,512]{2,1,0:T(8,128)(2,1)S(1)} %pad_maximum_fusion.1.refs_1_), channel_id=1, source_target_pairs={{0,56},{1,9},{2,58},{3,11},{4,60},{5,13},{6,62},{7,15},{8,0},{9,17... | collective-permute-start | bytes 884744 | tf_op jit(solution)/shard_map/ppermute | solution.py:153
  28.3 3.1 %collective-permute-start.7 = (bf16[2,144,512]{2,1,0:T(8,128)(2,1)S(1)}, bf16[2,144,512]{2,1,0:T(8,128)(2,1)S(1)}, u32[]{:S(2)}, u32[]{:S(2)}) collective-permute-start(bf16[2,144,512]{2,1,0:T(8,128)(2,1)S(1)} %pad_maximum_fusion.1.refs_1_), channel_id=1, source_target_pairs={{0,2},{1,3},{2,0},{3,1},{4,6},{5,7},{6,4},{7,5},{8,10},{9,11},{10,... | collective-permute-start | bytes 884744 | tf_op jit(solution)/shard_map/ppermute | solution.py:156
  31.4 1.9 %collective-permute-start.9 = (bf16[128,2048]{1,0:T(8,128)(2,1)S(1)}, bf16[128,2048]{1,0:T(8,128)(2,1)S(1)}, u32[]{:S(2)}, u32[]{:S(2)}) collective-permute-start(bf16[128,2048]{1,0:T(8,128)(2,1)S(1)} %get-tuple-element.53), channel_id=1, source_target_pairs={{0,64},{1,65},{2,66},{3,67},{4,68},{5,69},{6,70},{7,71},{8,72},{9,... | collective-permute-start | bytes 1572872 | tf_op jit(solution)/shard_map/ppermute | solution.py:150
  33.4 0.0 collective-permute-done.2
  33.4 3.2 %collective-permute-done.3 = bf16[2,144,512]{2,1,0:T(8,128)(2,1)S(1)} collective-permute-done((bf16[2,144,512]{2,1,0:T(8,128)(2,1)S(1)}, bf16[2,144,512]{2,1,0:T(8,128)(2,1)S(1)}, u32[]{:S(2)}, u32[]{:S(2)}) %collective-permute-start.3) | collective-permute-done | bytes 294944 | tf_op jit(solution)/shard_map/ppermute | solution.py:153
  36.6 0.0 collective-permute-done.4.q_ref
  36.6 0.1 broadcast_select_fusion.3
  36.6 4.4 %collective-permute-start.5 = (bf16[2,144,512]{2,1,0:T(8,128)(2,1)S(1)}, bf16[2,144,512]{2,1,0:T(8,128)(2,1)S(1)}, u32[]{:S(2)}, u32[]{:S(2)}) collective-permute-start(bf16[2,144,512]{2,1,0:T(8,128)(2,1)S(1)} %get-tuple-element.58), channel_id=1, source_target_pairs={{0,6},{1,7},{2,4},{3,5},{4,2},{5,3},{6,0},{7,1},{8,14},{9,15},{10,... | collective-permute-start | bytes 884744 | tf_op jit(solution)/shard_map/ppermute | solution.py:159
  41.0 1.9 %collective-permute-start.10 = (bf16[2,144,512]{2,1,0:T(8,128)(2,1)S(1)}, bf16[2,144,512]{2,1,0:T(8,128)(2,1)S(1)}, u32[]{:S(2)}, u32[]{:S(2)}) collective-permute-start(bf16[2,144,512]{2,1,0:T(8,128)(2,1)S(1)} %get-tuple-element.56), channel_id=1, source_target_pairs={{0,2},{1,3},{2,0},{3,1},{4,6},{5,7},{6,4},{7,5},{8,10},{9,11},{10,... | collective-permute-start | bytes 884744 | tf_op jit(solution)/shard_map/ppermute | solution.py:156
  43.0 0.0 collective-permute-done.7.refs_3_
  43.0 0.1 pad_maximum_fusion
  43.0 2.7 %collective-permute-start.8 = (bf16[2,2,144,512]{3,2,1,0:T(8,128)(2,1)S(1)}, bf16[2,2,144,512]{3,2,1,0:T(8,128)(2,1)S(1)}, u32[]{:S(2)}, u32[]{:S(2)}) collective-permute-start(bf16[2,2,144,512]{3,2,1,0:T(8,128)(2,1)S(1)} %pad_maximum_fusion), channel_id=1, source_target_pairs={{0,6},{1,7},{2,4},{3,5},{4,2},{5,3},{6,0},{7,1},{8,14},{9,15},{10,... | collective-permute-start | bytes 1769480 | tf_op jit(solution)/shard_map/ppermute | solution.py:159
  45.8 3.3 %shard_map.46 = (f32[2048,128]{1,0:T(8,128)S(1)}, f32[2048,128]{1,0:T(8,128)S(1)}, f32[2048,128]{1,0:T(8,128)S(1)}) custom-call(s32[1]{0:T(128)} %bitcast.core_ref, bf16[128,2048]{1,0:T(8,128)(2,1)S(1)} %collective-permute-done.4.q_ref, bf16[2,144,512]{2,1,0:T(8,128)(2,1)S(1)} %get-tuple-element.43.refs_0_, ...), custom_call_target="tpu_custom_call" | custom-call | flops 2147483648 | bytes 4194304 | tf_op jit(solution)/shard_map/pallas_call | solution.py:130
  49.1 0.0 collective-permute-done.5.refs_2_.refs_5_
  49.1 2.8 %collective-permute-start.6 = (bf16[2,144,512]{2,1,0:T(8,128)(2,1)S(1)}, bf16[2,144,512]{2,1,0:T(8,128)(2,1)S(1)}, u32[]{:S(2)}, u32[]{:S(2)}) collective-permute-start(bf16[2,144,512]{2,1,0:T(8,128)(2,1)S(1)} %collective-permute-done.5.refs_2_.refs_5_), channel_id=1, source_target_pairs={{0,2},{1,3},{2,0},{3,1},{4,6},{5,7},{6,4},{7,5},{8,10},{9,11},{10,... | collective-permute-start | bytes 884744 | tf_op jit(solution)/shard_map/ppermute | solution.py:156
  51.9 0.0 collective-permute-done.10.refs_1_.refs_4_
  51.9 2.1 %shard_map.47 = (f32[2048,128]{1,0:T(8,128)S(1)}, f32[2048,128]{1,0:T(8,128)S(1)}, f32[2048,128]{1,0:T(8,128)S(1)}) custom-call(s32[1]{0:T(128)} %bitcast.core_ref, bf16[128,2048]{1,0:T(8,128)(2,1)S(1)} %collective-permute-done.4.q_ref, bf16[2,144,512]{2,1,0:T(8,128)(2,1)S(1)} %get-tuple-element.43.refs_0_, ...), custom_call_target="tpu_custom_call" | custom-call | flops 1073741824 | bytes 4194304 | tf_op jit(solution)/shard_map/pallas_call | solution.py:130
  54.0 0.0 collective-permute-done.9.q_ref
  54.0 4.6 %shard_map.48 = (f32[2048,128]{1,0:T(8,128)S(1)}, f32[2048,128]{1,0:T(8,128)S(1)}, f32[2048,128]{1,0:T(8,128)S(1)}) custom-call(s32[1]{0:T(128)} %bitcast.core_ref, bf16[128,2048]{1,0:T(8,128)(2,1)S(1)} %collective-permute-done.9.q_ref, bf16[2,144,512]{2,1,0:T(8,128)(2,1)S(1)} %get-tuple-element.43.refs_0_, ...), custom_call_target="tpu_custom_call" | custom-call | flops 3221225472 | bytes 4194304 | tf_op jit(solution)/shard_map/pallas_call | solution.py:130
  58.6 0.7 %collective-permute-done.6.refs_1_ = bf16[2,144,512]{2,1,0:T(8,128)(2,1)S(1)} collective-permute-done((bf16[2,144,512]{2,1,0:T(8,128)(2,1)S(1)}, bf16[2,144,512]{2,1,0:T(8,128)(2,1)S(1)}, u32[]{:S(2)}, u32[]{:S(2)}) %collective-permute-start.6) | collective-permute-done | bytes 294944 | tf_op jit(solution)/shard_map/ppermute | solution.py:156
  59.3 1.3 %collective-permute-done.8.refs_2_ = bf16[2,2,144,512]{3,2,1,0:T(8,128)(2,1)S(1)} collective-permute-done((bf16[2,2,144,512]{3,2,1,0:T(8,128)(2,1)S(1)}, bf16[2,2,144,512]{3,2,1,0:T(8,128)(2,1)S(1)}, u32[]{:S(2)}, u32[]{:S(2)}) %collective-permute-start.8) | collective-permute-done | bytes 589856 | tf_op jit(solution)/shard_map/ppermute | solution.py:159
  60.7 2.7 %shard_map.50 = bf16[128,2048]{1,0:T(8,128)(2,1)S(1)} custom-call(s32[1]{0:T(128)} %bitcast.core_ref, bf16[128,2048]{1,0:T(8,128)(2,1)S(1)} %collective-permute-done.4.q_ref, bf16[2,144,512]{2,1,0:T(8,128)(2,1)S(1)} %get-tuple-element.43.refs_0_, bf16[2,144,512]{2,1,0:T(8,128)(2,1)S(1)} %collective-permute-done.6.refs_1_, ...), custom_call_target="tpu_custom_call" | custom-call | flops 1610612736 | bytes 4194304 | tf_op jit(solution)/shard_map/pallas_call | solution.py:130
  63.4 3.1 %collective-permute-start.11 = (bf16[128,2048]{1,0:T(8,128)(2,1)S(1)}, bf16[128,2048]{1,0:T(8,128)(2,1)S(1)}, u32[]{:S(2)}, u32[]{:S(2)}) collective-permute-start(bf16[128,2048]{1,0:T(8,128)(2,1)S(1)} %shard_map.50), channel_id=1, source_target_pairs={{0,1},{1,0},{2,3},{3,2},{4,5},{5,4},{6,7},{7,6},{8,9},{9,8},{10,11... | collective-permute-start | bytes 1572872 | tf_op jit(solution)/shard_map/ppermute | solution.py:162
  66.5 2.7 %shard_map.49 = bf16[128,2048]{1,0:T(8,128)(2,1)S(1)} custom-call(s32[1]{0:T(128)} %bitcast.core_ref, bf16[128,2048]{1,0:T(8,128)(2,1)S(1)} %collective-permute-done.9.q_ref, bf16[2,144,512]{2,1,0:T(8,128)(2,1)S(1)} %get-tuple-element.43.refs_0_, bf16[2,144,512]{2,1,0:T(8,128)(2,1)S(1)} %collective-permute-done.6.refs_1_, ...), custom_call_target="tpu_custom_call" | custom-call | flops 1610612736 | bytes 4194304 | tf_op jit(solution)/shard_map/pallas_call | solution.py:130
  69.2 0.0 collective-permute-done.11
  69.2 1.2 %maximum_select_fusion = bf16[1,128,4096]{2,1,0:T(8,128)(2,1)} fusion(bf16[1,128,2048]{2,1,0:T(8,128)(2,1)S(1)} %bitcast.14, bf16[1,128,2048]{2,1,0:T(8,128)(2,1)S(1)} %bitcast.11, pred[]{:T(512)S(6)} %eq.16), kind=kLoop, calls=%fused_computation | loop fusion | flops 4718592 | bytes 2097153 | tf_op jit(solution)/shard_map/jit(_where)/select_n | solution.py:195
  (2 shorter events, 0.1 us)
Async XLA Ops:
  0.0 13.2 %copy-start = (bf16[1,128,4096]{2,1,0:T(8,128)(2,1)S(1)}, bf16[1,128,4096]{2,1,0:T(8,128)(2,1)}, u32[]{:S(2)}) copy-start(bf16[1,128,4096]{2,1,0:T(8,128)(2,1)} %param.4) | copy-start | bytes 3145732
  1.8 19.4 %collective-permute-start.1 = (bf16[144,512]{1,0:T(8,128)(2,1)S(1)}, bf16[144,512]{1,0:T(8,128)(2,1)S(1)}, u32[]{:S(2)}, u32[]{:S(2)}) collective-permute-start(bf16[144,512]{1,0:T(8,128)(2,1)S(1)} %get-tuple-element.60), channel_id=1, source_target_pairs={{0,73},{1,72},{2,75},{3,74},{4,77},{5,76},{6,79},{7,78},{8,81},{9,... | collective-permute-start | bytes 442376 | tf_op jit(solution)/shard_map/ppermute | solution.py:150
  8.2 14.8 %collective-permute-start = (bf16[144,512]{1,0:T(8,128)(2,1)S(1)}, bf16[144,512]{1,0:T(8,128)(2,1)S(1)}, u32[]{:S(2)}, u32[]{:S(2)}) collective-permute-start(bf16[144,512]{1,0:T(8,128)(2,1)S(1)} %get-tuple-element.59), channel_id=1, source_target_pairs={{0,72},{1,73},{2,74},{3,75},{4,76},{5,77},{6,78},{7,79},{8,80},{9,... | collective-permute-start | bytes 442376 | tf_op jit(solution)/shard_map/ppermute | solution.py:150
  13.3 23.3 %collective-permute-start.4 = (bf16[128,2048]{1,0:T(8,128)(2,1)S(1)}, bf16[128,2048]{1,0:T(8,128)(2,1)S(1)}, u32[]{:S(2)}, u32[]{:S(2)}) collective-permute-start(bf16[128,2048]{1,0:T(8,128)(2,1)S(1)} %get-tuple-element.54), channel_id=1, source_target_pairs={{0,65},{1,64},{2,67},{3,66},{4,69},{5,68},{6,71},{7,70},{8,73},{9,... | collective-permute-start | bytes 1572872 | tf_op jit(solution)/shard_map/ppermute | solution.py:150
  23.0 10.4 %collective-permute-start.2 = (bf16[2,144,512]{2,1,0:T(8,128)(2,1)S(1)}, bf16[2,144,512]{2,1,0:T(8,128)(2,1)S(1)}, u32[]{:S(2)}, u32[]{:S(2)}) collective-permute-start(bf16[2,144,512]{2,1,0:T(8,128)(2,1)S(1)} %pad_maximum_fusion.1.refs_1_), channel_id=1, source_target_pairs={{0,8},{1,57},{2,10},{3,59},{4,12},{5,61},{6,14},{7,63},{8,16},{9,1... | collective-permute-start | bytes 884744 | tf_op jit(solution)/shard_map/ppermute | solution.py:153
  26.0 10.6 %collective-permute-start.3 = (bf16[2,144,512]{2,1,0:T(8,128)(2,1)S(1)}, bf16[2,144,512]{2,1,0:T(8,128)(2,1)S(1)}, u32[]{:S(2)}, u32[]{:S(2)}) collective-permute-start(bf16[2,144,512]{2,1,0:T(8,128)(2,1)S(1)} %pad_maximum_fusion.1.refs_1_), channel_id=1, source_target_pairs={{0,56},{1,9},{2,58},{3,11},{4,60},{5,13},{6,62},{7,15},{8,0},{9,17... | collective-permute-start | bytes 884744 | tf_op jit(solution)/shard_map/ppermute | solution.py:153
  28.3 14.7 %collective-permute-start.7 = (bf16[2,144,512]{2,1,0:T(8,128)(2,1)S(1)}, bf16[2,144,512]{2,1,0:T(8,128)(2,1)S(1)}, u32[]{:S(2)}, u32[]{:S(2)}) collective-permute-start(bf16[2,144,512]{2,1,0:T(8,128)(2,1)S(1)} %pad_maximum_fusion.1.refs_1_), channel_id=1, source_target_pairs={{0,2},{1,3},{2,0},{3,1},{4,6},{5,7},{6,4},{7,5},{8,10},{9,11},{10,... | collective-permute-start | bytes 884744 | tf_op jit(solution)/shard_map/ppermute | solution.py:156
  31.4 22.6 %collective-permute-start.9 = (bf16[128,2048]{1,0:T(8,128)(2,1)S(1)}, bf16[128,2048]{1,0:T(8,128)(2,1)S(1)}, u32[]{:S(2)}, u32[]{:S(2)}) collective-permute-start(bf16[128,2048]{1,0:T(8,128)(2,1)S(1)} %get-tuple-element.53), channel_id=1, source_target_pairs={{0,64},{1,65},{2,66},{3,67},{4,68},{5,69},{6,70},{7,71},{8,72},{9,... | collective-permute-start | bytes 1572872 | tf_op jit(solution)/shard_map/ppermute | solution.py:150
  36.6 12.5 %collective-permute-start.5 = (bf16[2,144,512]{2,1,0:T(8,128)(2,1)S(1)}, bf16[2,144,512]{2,1,0:T(8,128)(2,1)S(1)}, u32[]{:S(2)}, u32[]{:S(2)}) collective-permute-start(bf16[2,144,512]{2,1,0:T(8,128)(2,1)S(1)} %get-tuple-element.58), channel_id=1, source_target_pairs={{0,6},{1,7},{2,4},{3,5},{4,2},{5,3},{6,0},{7,1},{8,14},{9,15},{10,... | collective-permute-start | bytes 884744 | tf_op jit(solution)/shard_map/ppermute | solution.py:159
  41.0 10.8 %collective-permute-start.10 = (bf16[2,144,512]{2,1,0:T(8,128)(2,1)S(1)}, bf16[2,144,512]{2,1,0:T(8,128)(2,1)S(1)}, u32[]{:S(2)}, u32[]{:S(2)}) collective-permute-start(bf16[2,144,512]{2,1,0:T(8,128)(2,1)S(1)} %get-tuple-element.56), channel_id=1, source_target_pairs={{0,2},{1,3},{2,0},{3,1},{4,6},{5,7},{6,4},{7,5},{8,10},{9,11},{10,... | collective-permute-start | bytes 884744 | tf_op jit(solution)/shard_map/ppermute | solution.py:156
  43.0 17.6 %collective-permute-start.8 = (bf16[2,2,144,512]{3,2,1,0:T(8,128)(2,1)S(1)}, bf16[2,2,144,512]{3,2,1,0:T(8,128)(2,1)S(1)}, u32[]{:S(2)}, u32[]{:S(2)}) collective-permute-start(bf16[2,2,144,512]{3,2,1,0:T(8,128)(2,1)S(1)} %pad_maximum_fusion), channel_id=1, source_target_pairs={{0,6},{1,7},{2,4},{3,5},{4,2},{5,3},{6,0},{7,1},{8,14},{9,15},{10,... | collective-permute-start | bytes 1769480 | tf_op jit(solution)/shard_map/ppermute | solution.py:159
  49.1 10.2 %collective-permute-start.6 = (bf16[2,144,512]{2,1,0:T(8,128)(2,1)S(1)}, bf16[2,144,512]{2,1,0:T(8,128)(2,1)S(1)}, u32[]{:S(2)}, u32[]{:S(2)}) collective-permute-start(bf16[2,144,512]{2,1,0:T(8,128)(2,1)S(1)} %collective-permute-done.5.refs_2_.refs_5_), channel_id=1, source_target_pairs={{0,2},{1,3},{2,0},{3,1},{4,6},{5,7},{6,4},{7,5},{8,10},{9,11},{10,... | collective-permute-start | bytes 884744 | tf_op jit(solution)/shard_map/ppermute | solution.py:156
  63.4 5.9 %collective-permute-start.11 = (bf16[128,2048]{1,0:T(8,128)(2,1)S(1)}, bf16[128,2048]{1,0:T(8,128)(2,1)S(1)}, u32[]{:S(2)}, u32[]{:S(2)}) collective-permute-start(bf16[128,2048]{1,0:T(8,128)(2,1)S(1)} %shard_map.50), channel_id=1, source_target_pairs={{0,1},{1,0},{2,3},{3,2},{4,5},{5,4},{6,7},{7,6},{8,9},{9,8},{10,11... | collective-permute-start | bytes 1572872 | tf_op jit(solution)/shard_map/ppermute | solution.py:162

commit v9 on v8

--- a/solution.py
+++ b/solution.py
@@ -16,6 +16,39 @@
 SCALE = 1.4426950408889634 / HEAD**0.5
 FAR = -131072.0
 NT = (((1,), (1,)), ((), ()))
+
+
+def pack(core_ref, k_ref, v_ref, ids_ref, mine_ref, other_ref, ids_vmem, sems):
+    half = 2 * HEAD
+    copies = [pltpu.make_async_copy(ids_ref, ids_vmem, sems.at[4])]
+    for i, ref in enumerate((mine_ref, other_ref)):
+        cols = pl.ds(pl.multiple_of((core_ref[0] ^ i) * half, half), half)
+        for j, source in enumerate((k_ref, v_ref)):
+            target = ref.at[:BLOCK, j * half : (j + 1) * half]
+            copies.append(pltpu.make_async_copy(source.at[:, cols], target, sems.at[2 * i + j]))
+    for copy in copies:
+        copy.start()
+    copies[0].wait()
+    row = lax.broadcasted_iota(jnp.int32, (16, HEAD), 0)
+    ids = jnp.where(row == 0, ids_vmem[...].astype(jnp.float32), 0.0).astype(jnp.bfloat16)
+    for ref in (mine_ref, other_ref):
+        ref[BLOCK:, :HEAD] = ids
+        ref[BLOCK:, HEAD:] = jnp.zeros((16, 3 * HEAD), jnp.bfloat16)
+    for copy in copies[1:]:
+        copy.wait()
+
+
+def packed(core, keys, values, ids):
+    vmem = pl.BlockSpec(memory_space=pltpu.VMEM)
+    hbm = pl.BlockSpec(memory_space=pltpu.HBM)
+    return pl.pallas_call(
+        pack,
+        out_shape=[jax.ShapeDtypeStruct((ROWS, 4 * HEAD), jnp.bfloat16)] * 2,
+        in_specs=[pl.BlockSpec(memory_space=pltpu.SMEM)] + [hbm] * 3,
+        out_specs=[vmem] * 2,
+        scratch_shapes=[pltpu.VMEM(ids.shape, jnp.int32), pltpu.SemaphoreType.DMA((5,))],
+        compiler_params=pltpu.CompilerParams(vmem_limit_bytes=8 * 1024 * 1024),
+    )(core, keys, values, ids)
 
 
 def marks(refs):
@@ -32,6 +65,11 @@
     return first, last
 
 
+def place(core, half, part, parts):
+    width = HQ * HEAD // 2 // parts
+    return pl.ds(pl.multiple_of((core ^ half) * (HQ * HEAD // 2) + part * width, width), width)
+
+
 def piece(half, own, carried, last, n_blocks, core_ref, q_ref, *refs):
     b0 = refs[0]
     blocks = []
@@ -39,8 +77,20 @@
         blocks.extend([ref] if len(ref.shape) == 3 else [ref.at[0], ref.at[1]])
     refs = refs[n_blocks:]
     old, refs = (refs[:3], refs[3:]) if carried else (None, refs)
-    new, (kaug, vaug) = refs[:-2], refs[-2:]
     core = core_ref[0]
+    ends = last and half == 0
+    if ends:
+        out, *new, kaug, vaug, sems = refs
+        copies = [
+            pltpu.make_async_copy(
+                new[0].at[:, part * (GROUP * HEAD) : (part + 1) * (GROUP * HEAD)],
+                out.at[:, place(core, 0, part, 2)],
+                sems.at[part],
+            )
+            for part in range(2)
+        ]
+    else:
+        *new, kaug, vaug = refs
     row = lax.broadcasted_iota(jnp.int32, (BLOCK, HEAD), 0)
     lane = lax.broadcasted_iota(jnp.int32, (BLOCK, HEAD), 1)
     first, end = marks([b0] + blocks)
@@ -114,8 +164,33 @@
             ahead = scores(*tiles[i + 1])
         if pending is not None:
             finish(*pending)
+        if ends and i == len(tiles) // 2:
+            copies[0].start()
         pending = (*weights(score, *tile), *tile)
     finish(*pending)
+    if ends:
+        copies[1].start()
+        copies[0].wait()
+        copies[1].wait()
+
+
+def fill(core_ref, got, old, out, sem):
+    copy = pltpu.make_async_copy(got, out.at[:, place(core_ref[0], 1, 0, 1)], sem)
+    copy.start()
+    copy.wait()
+
+
+def filled(core, got, out):
+    hbm = pl.BlockSpec(memory_space=pl.ANY)
+    return pl.pallas_call(
+        fill,
+        out_shape=jax.ShapeDtypeStruct(out.shape, out.dtype),
+        in_specs=[pl.BlockSpec(memory_space=pltpu.SMEM), pl.BlockSpec(memory_space=pltpu.VMEM), hbm],
+        out_specs=hbm,
+        scratch_shapes=[pltpu.SemaphoreType.DMA],
+        input_output_aliases={2: 0},
+        compiler_params=pltpu.CompilerParams(vmem_limit_bytes=8 * 1024 * 1024),
+    )(core, got, out)
 
 
 def attend(core, half, q, b0, blocks, own=False, state=(), last=False):
@@ -123,7 +198,14 @@
     count = own + sum(1 if block.ndim == 3 else 2 for block in blocks)
     keys = 2 * BLOCK * count
     rows = BLOCK * HQ // 2
-    if last:
+    ends = last and half == 0
+    out_spec = vmem
+    scratch = [pltpu.VMEM((2, keys, 2 * HEAD), jnp.bfloat16)] * 2
+    if ends:
+        out_shape = jax.ShapeDtypeStruct((BLOCK, HQ * HEAD), jnp.bfloat16)
+        out_spec = pl.BlockSpec(memory_space=pl.ANY)
+        scratch = [pltpu.VMEM(q.shape, jnp.bfloat16)] + scratch + [pltpu.SemaphoreType.DMA((2,))]
+    elif last:
         out_shape = jax.ShapeDtypeStruct(q.shape, jnp.bfloat16)
     else:
         out_shape = [jax.ShapeDtypeStruct((rows, HEAD), jnp.float32)] * 3
@@ -131,8 +213,8 @@
         functools.partial(piece, half, own, bool(state), last, 1 + len(blocks)),
         out_shape=out_shape,
         in_specs=[pl.BlockSpec(memory_space=pltpu.SMEM)] + [vmem] * (2 + len(blocks) + len(state)),
-        out_specs=vmem if last else [vmem] * 3,
-        scratch_shapes=[pltpu.VMEM((2, keys, 2 * HEAD), jnp.bfloat16)] * 2,
+        out_specs=out_spec if last else [vmem] * 3,
+        scratch_shapes=scratch,
         compiler_params=pltpu.CompilerParams(vmem_limit_bytes=32 * 1024 * 1024),
         cost_estimate=pl.CostEstimate(
             flops=8 * rows * keys * HEAD, bytes_accessed=4 << 20, transcendentals=rows * keys
@@ -161,14 +243,8 @@
     def swap(block):
         return lax.ppermute(block, "sp", [(s, s ^ 1) for s in range(64)])
 
-    ids = jnp.pad(doc_ids[0].astype(jnp.bfloat16)[None], ((0, 15), (0, 384)))
-
-    def part(j):
-        cols = slice(j * 256, (j + 1) * 256)
-        return jnp.concatenate([jnp.concatenate([keys[0][:, cols], values[0][:, cols]], axis=1), ids], axis=0)
-
-    half0, half1 = part(0), part(1)
-    mine, other = jnp.where(first, half0, half1), jnp.where(first, half1, half0)
+    at = core[None].astype(jnp.int32)
+    mine, other = packed(at, keys[0], values[0], doc_ids)
     q = queries[0]
     b4 = jnp.stack([section(mine, 0, 1), section(other, 1, 1)])
     qf = section(jnp.where(first, q[:, 2048:], q[:, :2048]), 1)
@@ -182,17 +258,19 @@
     e2 = even_pair(jnp.where((column % 2 == 0) == first, yb, ya))
     f13 = odd_pair(jnp.stack([b4, e1]))
     b0, b8 = jnp.where(first, yb, ya), jnp.where(first, ya, yb)
-    at = core[None].astype(jnp.int32)
     state = attend(at, 1, qf, b0, [b4, b8, e1], own=True)
     (f2,) = lax.optimization_barrier((f2,))
     e3 = even_pair(f2)
     state2 = attend(at, 0, qs, b0, [b4, b8, e1, e2, f2], own=True)
     state = attend(at, 1, qf, b0, [e2, f2], state=state)
+    e3, *state = lax.optimization_barrier((e3, *state, *state2))
+    state, state2 = state[:3], state[3:]
+    state = attend(at, 1, qf, b0, [e3], state=state)
     e3, f13, qs, qf, b0, *both = lax.optimization_barrier((e3, f13, qs, qf, b0, *state, *state2))
-    of_ = attend(at, 1, qf, b0, [e3, f13], state=both[:3], last=True)
+    of_ = attend(at, 1, qf, b0, [f13], state=both[:3], last=True)
     got = swap(of_)
     os_ = attend(at, 0, qs, b0, [e3, f13], state=both[3:], last=True)
-    out = jnp.where(first, jnp.concatenate([os_, got], axis=1), jnp.concatenate([got, os_], axis=1))
+    out = filled(at, got, os_)
     return out[None]
 
 

time: 70.9 us -> 71.6 us (level)
  waiting for transfers between devices: 10.9 us -> 8.36 us
  Pallas kernels: 15.4 us -> 17.7 us
  local copies, waits for them, and re-layouts: 0.96 us -> 2.46 us
  other arithmetic: 2.25 us -> 1.44 us
    unnamed x2 -> x6, local copies, waits for them, and re-layouts: 0.01 us -> 2.46 us
    pallas_call x5 -> x6, Pallas kernels: 15.4 us -> 16.8 us  [attend(): pl.pallas_call(functools.partial(piece, half, own, bool(state), last, 1 +...]
    select_n x2 -> x0, other arithmetic: 1.26 us -> none  [the longest x1 1.22 us: shards(): jnp.where(first, jnp.concatenate([os_, got], axis=1), jnp.concatenate([go...]
    ppermute x2, waiting for transfers between devices: 1.32 us -> 0.05 us  [odd_pair(): lax.ppermute(block, 'sp', [(s, s // 8 * 8 + (s + (2 if s & 2 else -2)) %...]
    ppermute x4, waiting for transfers between devices: 5.64 us -> 4.41 us  [section(): return lax.ppermute(block, ('pp', 'sp'), pairs)]
    select_n x1, other arithmetic: 0.07 us -> 1.27 us  [shards(): qs = section(jnp.where(first, q[:, :2048], q[:, 2048:]), 0)]
    slice x1 -> x0, local copies, waits for them, and re-layouts: 0.95 us -> none  [part(): keys[0][:, cols]]
    pallas_call x0 -> x2, Pallas kernels: none -> 0.89 us  [the longest x1 0.81 us: filled(): pl.pallas_call(fill, out_shape=jax.ShapeDtypeStruct(out.shape, out.dtype)...]
  transfers between devices with their start and end apart: 12 -> 12, of which waited for: 5 -> 4; matrix products, arithmetic and copies ran while one was open for 0% -> 2% of each run, Pallas kernels for 18% -> 21%
where the time goes in v9:
time: 71.6 us; the launch traced here: 71.1 us
  starting transfers between devices  40.7 us (57%)
  Pallas kernels  17.7 us (25%)
  waiting for transfers between devices  8.36 us (12%)
  local copies, waits for them, and re-layouts  2.46 us (3%)
  other arithmetic  1.44 us (2%)
    ppermute x4, starting transfers between devices, section(): return lax.ppermute(block, ('pp', 'sp'), pairs)  17.3 us
    pallas_call x6, Pallas kernels, attend(): pl.pallas_call(functools.partial(piece, half, own, bool(state), last, 1 +...  16.8 us
    ppermute x3, starting transfers between devices, even_pair(): return lax.ppermute(block, 'sp', [(s, s ^ 2) for s in range(64)])  7.81 us
    ppermute x2, starting transfers between devices, odd_pair(): lax.ppermute(block, 'sp', [(s, s // 8 * 8 + (s + (2 if s & 2 else -2)) %...  7.09 us
    ppermute x2, starting transfers between devices, along_y(): lax.ppermute(block, 'sp', [(s, (s + 8 * (step1 if s % 2 else step0)) % 64...  5.28 us
    ppermute x4, waiting for transfers between devices, section(): return lax.ppermute(block, ('pp', 'sp'), pairs)  4.41 us
    ppermute x2, waiting for transfers between devices, along_y(): lax.ppermute(block, 'sp', [(s, (s + 8 * (step1 if s % 2 else step0)) % 64...  3.21 us
    ppermute x1, starting transfers between devices, swap(): return lax.ppermute(block, 'sp', [(s, s ^ 1) for s in range(64)])  3.14 us
  transfers between devices with their start and end apart: 12, of which 4 were waited for; matrix products, arithmetic and copies ran while one was open for 2% of the time, Pallas kernels for 21%

profile of v9, /device:TPU:1, one launch (start us, length us, event | category | flops | bytes accessed | tf_op | source)
XLA Modules:
  0.0 71.1 jit_solution(3334836414649879257)
XLA Ops:
  0.0 0.0 copy-start.2
  0.0 0.7 copy-done.2
  0.7 0.0 copy-start
  0.7 0.9 %copy-done = bf16[1,128,512]{2,1,0:T(8,128)(2,1)S(1)} copy-done((bf16[1,128,512]{2,1,0:T(8,128)(2,1)S(1)}, bf16[1,128,512]{2,1,0:T(8,128)(2,1)}, u32[]{:S(2)}) %copy-start) | copy-done | bytes 131096
  1.6 0.0 copy-start.1
  1.6 0.9 %copy-done.1 = bf16[1,128,512]{2,1,0:T(8,128)(2,1)S(1)} copy-done((bf16[1,128,512]{2,1,0:T(8,128)(2,1)S(1)}, bf16[1,128,512]{2,1,0:T(8,128)(2,1)}, u32[]{:S(2)}) %copy-start.1) | copy-done | bytes 131096
  2.5 0.1 shard_map.46
  2.6 6.4 %collective-permute-start.1 = (bf16[144,512]{1,0:T(8,128)(2,1)S(1)}, bf16[144,512]{1,0:T(8,128)(2,1)S(1)}, u32[]{:S(2)}, u32[]{:S(2)}) collective-permute-start(bf16[144,512]{1,0:T(8,128)(2,1)S(1)} %get-tuple-element.42), channel_id=1, source_target_pairs={{0,73},{1,72},{2,75},{3,74},{4,77},{5,76},{6,79},{7,78},{8,81},{9,... | collective-permute-start | bytes 442376 | tf_op jit(solution)/shard_map/ppermute | solution.py:232
  9.0 5.0 %collective-permute-start = (bf16[144,512]{1,0:T(8,128)(2,1)S(1)}, bf16[144,512]{1,0:T(8,128)(2,1)S(1)}, u32[]{:S(2)}, u32[]{:S(2)}) collective-permute-start(bf16[144,512]{1,0:T(8,128)(2,1)S(1)} %get-tuple-element.41), channel_id=1, source_target_pairs={{0,72},{1,73},{2,74},{3,75},{4,76},{5,77},{6,78},{7,79},{8,80},{9,... | collective-permute-start | bytes 442376 | tf_op jit(solution)/shard_map/ppermute | solution.py:232
  14.0 1.3 %broadcast_select_fusion = (bf16[128,2048]{1,0:T(8,128)(2,1)S(1)}, bf16[128,2048]{1,0:T(8,128)(2,1)S(1)}) fusion(pred[]{:T(512)S(6)} %eq.16, bf16[128,4096]{1,0:T(8,128)(2,1)} %bitcast.13), kind=kLoop, calls=%fused_computation.1 | loop fusion | flops 524288 | bytes 2097153 | tf_op jit(solution)/shard_map/jit(_where)/select_n | solution.py:251
  15.3 4.0 %collective-permute-start.4 = (bf16[128,2048]{1,0:T(8,128)(2,1)S(1)}, bf16[128,2048]{1,0:T(8,128)(2,1)S(1)}, u32[]{:S(2)}, u32[]{:S(2)}) collective-permute-start(bf16[128,2048]{1,0:T(8,128)(2,1)S(1)} %get-tuple-element.78), channel_id=1, source_target_pairs={{0,65},{1,64},{2,67},{3,66},{4,69},{5,68},{6,71},{7,70},{8,73},{9,... | collective-permute-start | bytes 1572872 | tf_op jit(solution)/shard_map/ppermute | solution.py:232
  19.3 2.7 %collective-permute-done.1 = bf16[144,512]{1,0:T(8,128)(2,1)S(1)} collective-permute-done((bf16[144,512]{1,0:T(8,128)(2,1)S(1)}, bf16[144,512]{1,0:T(8,128)(2,1)S(1)}, u32[]{:S(2)}, u32[]{:S(2)}) %collective-permute-start.1) | collective-permute-done | bytes 147488 | tf_op jit(solution)/shard_map/ppermute | solution.py:232
  22.0 1.7 %collective-permute-done = bf16[144,512]{1,0:T(8,128)(2,1)S(1)} collective-permute-done((bf16[144,512]{1,0:T(8,128)(2,1)S(1)}, bf16[144,512]{1,0:T(8,128)(2,1)S(1)}, u32[]{:S(2)}, u32[]{:S(2)}) %collective-permute-start) | collective-permute-done | bytes 147488 | tf_op jit(solution)/shard_map/ppermute | solution.py:232
  23.7 3.0 %collective-permute-start.2 = (bf16[2,144,512]{2,1,0:T(8,128)(2,1)S(1)}, bf16[2,144,512]{2,1,0:T(8,128)(2,1)S(1)}, u32[]{:S(2)}, u32[]{:S(2)}) collective-permute-start(bf16[2,144,512]{2,1,0:T(8,128)(2,1)S(1)} %pad_maximum_fusion.1.refs_1_), channel_id=1, source_target_pairs={{0,8},{1,57},{2,10},{3,59},{4,12},{5,61},{6,14},{7,63},{8,16},{9,1... | collective-permute-start | bytes 884744 | tf_op jit(solution)/shard_map/ppermute | solution.py:235
  26.7 2.3 %collective-permute-start.3 = (bf16[2,144,512]{2,1,0:T(8,128)(2,1)S(1)}, bf16[2,144,512]{2,1,0:T(8,128)(2,1)S(1)}, u32[]{:S(2)}, u32[]{:S(2)}) collective-permute-start(bf16[2,144,512]{2,1,0:T(8,128)(2,1)S(1)} %pad_maximum_fusion.1.refs_1_), channel_id=1, source_target_pairs={{0,56},{1,9},{2,58},{3,11},{4,60},{5,13},{6,62},{7,15},{8,0},{9,17... | collective-permute-start | bytes 884744 | tf_op jit(solution)/shard_map/ppermute | solution.py:235
  29.0 3.1 %collective-permute-start.8 = (bf16[2,144,512]{2,1,0:T(8,128)(2,1)S(1)}, bf16[2,144,512]{2,1,0:T(8,128)(2,1)S(1)}, u32[]{:S(2)}, u32[]{:S(2)}) collective-permute-start(bf16[2,144,512]{2,1,0:T(8,128)(2,1)S(1)} %pad_maximum_fusion.1.refs_1_), channel_id=1, source_target_pairs={{0,2},{1,3},{2,0},{3,1},{4,6},{5,7},{6,4},{7,5},{8,10},{9,11},{10,... | collective-permute-start | bytes 884744 | tf_op jit(solution)/shard_map/ppermute | solution.py:238
  32.1 1.9 %collective-permute-start.9 = (bf16[128,2048]{1,0:T(8,128)(2,1)S(1)}, bf16[128,2048]{1,0:T(8,128)(2,1)S(1)}, u32[]{:S(2)}, u32[]{:S(2)}) collective-permute-start(bf16[128,2048]{1,0:T(8,128)(2,1)S(1)} %get-tuple-element.77), channel_id=1, source_target_pairs={{0,64},{1,65},{2,66},{3,67},{4,68},{5,69},{6,70},{7,71},{8,72},{9,... | collective-permute-start | bytes 1572872 | tf_op jit(solution)/shard_map/ppermute | solution.py:232
  34.1 0.0 collective-permute-done.2
  34.1 3.2 %collective-permute-done.3 = bf16[2,144,512]{2,1,0:T(8,128)(2,1)S(1)} collective-permute-done((bf16[2,144,512]{2,1,0:T(8,128)(2,1)S(1)}, bf16[2,144,512]{2,1,0:T(8,128)(2,1)S(1)}, u32[]{:S(2)}, u32[]{:S(2)}) %collective-permute-start.3) | collective-permute-done | bytes 294944 | tf_op jit(solution)/shard_map/ppermute | solution.py:235
  37.3 0.0 collective-permute-done.4.q_ref
  37.3 0.1 broadcast_select_fusion.3
  37.4 4.4 %collective-permute-start.5 = (bf16[2,144,512]{2,1,0:T(8,128)(2,1)S(1)}, bf16[2,144,512]{2,1,0:T(8,128)(2,1)S(1)}, u32[]{:S(2)}, u32[]{:S(2)}) collective-permute-start(bf16[2,144,512]{2,1,0:T(8,128)(2,1)S(1)} %get-tuple-element.82), channel_id=1, source_target_pairs={{0,6},{1,7},{2,4},{3,5},{4,2},{5,3},{6,0},{7,1},{8,14},{9,15},{10,... | collective-permute-start | bytes 884744 | tf_op jit(solution)/shard_map/ppermute | solution.py:241
  41.8 1.9 %collective-permute-start.7 = (bf16[2,144,512]{2,1,0:T(8,128)(2,1)S(1)}, bf16[2,144,512]{2,1,0:T(8,128)(2,1)S(1)}, u32[]{:S(2)}, u32[]{:S(2)}) collective-permute-start(bf16[2,144,512]{2,1,0:T(8,128)(2,1)S(1)} %get-tuple-element.80), channel_id=1, source_target_pairs={{0,2},{1,3},{2,0},{3,1},{4,6},{5,7},{6,4},{7,5},{8,10},{9,11},{10,... | collective-permute-start | bytes 884744 | tf_op jit(solution)/shard_map/ppermute | solution.py:238
  43.8 0.0 collective-permute-done.8.refs_3_
  43.8 0.1 pad_maximum_fusion
  43.8 2.7 %collective-permute-start.10 = (bf16[2,2,144,512]{3,2,1,0:T(8,128)(2,1)S(1)}, bf16[2,2,144,512]{3,2,1,0:T(8,128)(2,1)S(1)}, u32[]{:S(2)}, u32[]{:S(2)}) collective-permute-start(bf16[2,2,144,512]{3,2,1,0:T(8,128)(2,1)S(1)} %pad_maximum_fusion), channel_id=1, source_target_pairs={{0,6},{1,7},{2,4},{3,5},{4,2},{5,3},{6,0},{7,1},{8,14},{9,15},{10,... | collective-permute-start | bytes 1769480 | tf_op jit(solution)/shard_map/ppermute | solution.py:241
  46.5 3.3 %shard_map.47 = (f32[2048,128]{1,0:T(8,128)S(1)}, f32[2048,128]{1,0:T(8,128)S(1)}, f32[2048,128]{1,0:T(8,128)S(1)}) custom-call(s32[1]{0:T(128)} %bitcast.core_ref, bf16[128,2048]{1,0:T(8,128)(2,1)S(1)} %collective-permute-done.4.q_ref, bf16[2,144,512]{2,1,0:T(8,128)(2,1)S(1)} %get-tuple-element.67.refs_0_, ...), custom_call_target="tpu_custom_call" | custom-call | flops 2147483648 | bytes 4194304 | tf_op jit(solution)/shard_map/pallas_call | solution.py:212
  49.9 0.0 collective-permute-done.5.refs_2_.refs_5_
  49.9 2.8 %collective-permute-start.6 = (bf16[2,144,512]{2,1,0:T(8,128)(2,1)S(1)}, bf16[2,144,512]{2,1,0:T(8,128)(2,1)S(1)}, u32[]{:S(2)}, u32[]{:S(2)}) collective-permute-start(bf16[2,144,512]{2,1,0:T(8,128)(2,1)S(1)} %collective-permute-done.5.refs_2_.refs_5_), channel_id=1, source_target_pairs={{0,2},{1,3},{2,0},{3,1},{4,6},{5,7},{6,4},{7,5},{8,10},{9,11},{10,... | collective-permute-start | bytes 884744 | tf_op jit(solution)/shard_map/ppermute | solution.py:238
  52.7 0.0 collective-permute-done.7.refs_1_.refs_4_
  52.7 2.1 %shard_map.48 = (f32[2048,128]{1,0:T(8,128)S(1)}, f32[2048,128]{1,0:T(8,128)S(1)}, f32[2048,128]{1,0:T(8,128)S(1)}) custom-call(s32[1]{0:T(128)} %bitcast.core_ref, bf16[128,2048]{1,0:T(8,128)(2,1)S(1)} %collective-permute-done.4.q_ref, bf16[2,144,512]{2,1,0:T(8,128)(2,1)S(1)} %get-tuple-element.67.refs_0_, ...), custom_call_target="tpu_custom_call" | custom-call | flops 1073741824 | bytes 4194304 | tf_op jit(solution)/shard_map/pallas_call | solution.py:212
  54.7 0.0 collective-permute-done.9.q_ref
  54.8 4.6 %shard_map.49 = (f32[2048,128]{1,0:T(8,128)S(1)}, f32[2048,128]{1,0:T(8,128)S(1)}, f32[2048,128]{1,0:T(8,128)S(1)}) custom-call(s32[1]{0:T(128)} %bitcast.core_ref, bf16[128,2048]{1,0:T(8,128)(2,1)S(1)} %collective-permute-done.9.q_ref, bf16[2,144,512]{2,1,0:T(8,128)(2,1)S(1)} %get-tuple-element.67.refs_0_, ...), custom_call_target="tpu_custom_call" | custom-call | flops 3221225472 | bytes 4194304 | tf_op jit(solution)/shard_map/pallas_call | solution.py:212
  59.4 0.7 collective-permute-done.6.refs_1_
  60.1 1.3 %shard_map.50 = (f32[2048,128]{1,0:T(8,128)S(1)}, f32[2048,128]{1,0:T(8,128)S(1)}, f32[2048,128]{1,0:T(8,128)S(1)}) custom-call(s32[1]{0:T(128)} %bitcast.core_ref, bf16[128,2048]{1,0:T(8,128)(2,1)S(1)} %collective-permute-done.4.q_ref, bf16[2,144,512]{2,1,0:T(8,128)(2,1)S(1)} %get-tuple-element.67.refs_0_, ...), custom_call_target="tpu_custom_call" | custom-call | flops 536870912 | bytes 4194304 | tf_op jit(solution)/shard_map/pallas_call | solution.py:212
  61.4 0.1 collective-permute-done.10.refs_1_.refs_2_
  61.5 2.1 %shard_map.51 = bf16[128,2048]{1,0:T(8,128)(2,1)S(1)} custom-call(s32[1]{0:T(128)} %bitcast.core_ref, bf16[128,2048]{1,0:T(8,128)(2,1)S(1)} %collective-permute-done.4.q_ref, bf16[2,144,512]{2,1,0:T(8,128)(2,1)S(1)} %get-tuple-element.67.refs_0_, bf16[2,2,144,512]{3,2,1,0:T(8,128)(2,1)S(1)} %collective-permute-done.10.refs_1_.refs_2_, ...), custom_call_target="tpu_custom_call" | custom-call | flops 1073741824 | bytes 4194304 | tf_op jit(solution)/shard_map/pallas_call | solution.py:212
  63.5 3.1 %collective-permute-start.11 = (bf16[128,2048]{1,0:T(8,128)(2,1)S(1)}, bf16[128,2048]{1,0:T(8,128)(2,1)S(1)}, u32[]{:S(2)}, u32[]{:S(2)}) collective-permute-start(bf16[128,2048]{1,0:T(8,128)(2,1)S(1)} %shard_map.51), channel_id=1, source_target_pairs={{0,1},{1,0},{2,3},{3,2},{4,5},{5,4},{6,7},{7,6},{8,9},{9,8},{10,11... | collective-permute-start | bytes 1572872 | tf_op jit(solution)/shard_map/ppermute | solution.py:244
  66.7 3.4 %shard_map.52.old = bf16[128,4096]{1,0:T(8,128)(2,1)} custom-call(s32[1]{0:T(128)} %bitcast.core_ref, bf16[128,2048]{1,0:T(8,128)(2,1)S(1)} %collective-permute-done.9.q_ref, bf16[2,144,512]{2,1,0:T(8,128)(2,1)S(1)} %get-tuple-element.67.refs_0_, bf16[2,144,512]{2,1,0:T(8,128)(2,1)S(1)} %collective-permute-done.6.refs_1_, ...), custom_call_target="tpu_custom_call" | custom-call | flops 1610612736 | bytes 4194304 | tf_op jit(solution)/shard_map/pallas_call | solution.py:212
  70.1 0.0 collective-permute-done.11.got
  70.1 0.8 %shard_map.53 = bf16[128,4096]{1,0:T(8,128)(2,1)} custom-call(s32[1]{0:T(128)} %bitcast.core_ref, bf16[128,2048]{1,0:T(8,128)(2,1)S(1)} %collective-permute-done.11.got, bf16[128,4096]{1,0:T(8,128)(2,1)} %shard_map.52.old), custom_call_target="tpu_custom_call", output_to_operand_aliasing={{}: (2, {})} | custom-call | tf_op jit(solution)/shard_map/pallas_call | solution.py:185
  (1 shorter events, 0.0 us)
Async XLA Ops:
  0.0 0.7 copy-start.2
  0.7 0.9 %copy-start = (bf16[1,128,512]{2,1,0:T(8,128)(2,1)S(1)}, bf16[1,128,512]{2,1,0:T(8,128)(2,1)}, u32[]{:S(2)}) copy-start(bf16[1,128,512]{2,1,0:T(8,128)(2,1)} %param.5) | copy-start | bytes 393220
  1.6 0.9 %copy-start.1 = (bf16[1,128,512]{2,1,0:T(8,128)(2,1)S(1)}, bf16[1,128,512]{2,1,0:T(8,128)(2,1)}, u32[]{:S(2)}) copy-start(bf16[1,128,512]{2,1,0:T(8,128)(2,1)} %param.6) | copy-start | bytes 393220
  2.6 19.4 %collective-permute-start.1 = (bf16[144,512]{1,0:T(8,128)(2,1)S(1)}, bf16[144,512]{1,0:T(8,128)(2,1)S(1)}, u32[]{:S(2)}, u32[]{:S(2)}) collective-permute-start(bf16[144,512]{1,0:T(8,128)(2,1)S(1)} %get-tuple-element.42), channel_id=1, source_target_pairs={{0,73},{1,72},{2,75},{3,74},{4,77},{5,76},{6,79},{7,78},{8,81},{9,... | collective-permute-start | bytes 442376 | tf_op jit(solution)/shard_map/ppermute | solution.py:232
  9.0 14.7 %collective-permute-start = (bf16[144,512]{1,0:T(8,128)(2,1)S(1)}, bf16[144,512]{1,0:T(8,128)(2,1)S(1)}, u32[]{:S(2)}, u32[]{:S(2)}) collective-permute-start(bf16[144,512]{1,0:T(8,128)(2,1)S(1)} %get-tuple-element.41), channel_id=1, source_target_pairs={{0,72},{1,73},{2,74},{3,75},{4,76},{5,77},{6,78},{7,79},{8,80},{9,... | collective-permute-start | bytes 442376 | tf_op jit(solution)/shard_map/ppermute | solution.py:232
  15.3 22.1 %collective-permute-start.4 = (bf16[128,2048]{1,0:T(8,128)(2,1)S(1)}, bf16[128,2048]{1,0:T(8,128)(2,1)S(1)}, u32[]{:S(2)}, u32[]{:S(2)}) collective-permute-start(bf16[128,2048]{1,0:T(8,128)(2,1)S(1)} %get-tuple-element.78), channel_id=1, source_target_pairs={{0,65},{1,64},{2,67},{3,66},{4,69},{5,68},{6,71},{7,70},{8,73},{9,... | collective-permute-start | bytes 1572872 | tf_op jit(solution)/shard_map/ppermute | solution.py:232
  23.7 10.4 %collective-permute-start.2 = (bf16[2,144,512]{2,1,0:T(8,128)(2,1)S(1)}, bf16[2,144,512]{2,1,0:T(8,128)(2,1)S(1)}, u32[]{:S(2)}, u32[]{:S(2)}) collective-permute-start(bf16[2,144,512]{2,1,0:T(8,128)(2,1)S(1)} %pad_maximum_fusion.1.refs_1_), channel_id=1, source_target_pairs={{0,8},{1,57},{2,10},{3,59},{4,12},{5,61},{6,14},{7,63},{8,16},{9,1... | collective-permute-start | bytes 884744 | tf_op jit(solution)/shard_map/ppermute | solution.py:235
  26.7 10.6 %collective-permute-start.3 = (bf16[2,144,512]{2,1,0:T(8,128)(2,1)S(1)}, bf16[2,144,512]{2,1,0:T(8,128)(2,1)S(1)}, u32[]{:S(2)}, u32[]{:S(2)}) collective-permute-start(bf16[2,144,512]{2,1,0:T(8,128)(2,1)S(1)} %pad_maximum_fusion.1.refs_1_), channel_id=1, source_target_pairs={{0,56},{1,9},{2,58},{3,11},{4,60},{5,13},{6,62},{7,15},{8,0},{9,17... | collective-permute-start | bytes 884744 | tf_op jit(solution)/shard_map/ppermute | solution.py:235
  29.0 14.7 %collective-permute-start.8 = (bf16[2,144,512]{2,1,0:T(8,128)(2,1)S(1)}, bf16[2,144,512]{2,1,0:T(8,128)(2,1)S(1)}, u32[]{:S(2)}, u32[]{:S(2)}) collective-permute-start(bf16[2,144,512]{2,1,0:T(8,128)(2,1)S(1)} %pad_maximum_fusion.1.refs_1_), channel_id=1, source_target_pairs={{0,2},{1,3},{2,0},{3,1},{4,6},{5,7},{6,4},{7,5},{8,10},{9,11},{10,... | collective-permute-start | bytes 884744 | tf_op jit(solution)/shard_map/ppermute | solution.py:238
  32.1 22.6 %collective-permute-start.9 = (bf16[128,2048]{1,0:T(8,128)(2,1)S(1)}, bf16[128,2048]{1,0:T(8,128)(2,1)S(1)}, u32[]{:S(2)}, u32[]{:S(2)}) collective-permute-start(bf16[128,2048]{1,0:T(8,128)(2,1)S(1)} %get-tuple-element.77), channel_id=1, source_target_pairs={{0,64},{1,65},{2,66},{3,67},{4,68},{5,69},{6,70},{7,71},{8,72},{9,... | collective-permute-start | bytes 1572872 | tf_op jit(solution)/shard_map/ppermute | solution.py:232
  37.4 12.5 %collective-permute-start.5 = (bf16[2,144,512]{2,1,0:T(8,128)(2,1)S(1)}, bf16[2,144,512]{2,1,0:T(8,128)(2,1)S(1)}, u32[]{:S(2)}, u32[]{:S(2)}) collective-permute-start(bf16[2,144,512]{2,1,0:T(8,128)(2,1)S(1)} %get-tuple-element.82), channel_id=1, source_target_pairs={{0,6},{1,7},{2,4},{3,5},{4,2},{5,3},{6,0},{7,1},{8,14},{9,15},{10,... | collective-permute-start | bytes 884744 | tf_op jit(solution)/shard_map/ppermute | solution.py:241
  41.8 10.8 %collective-permute-start.7 = (bf16[2,144,512]{2,1,0:T(8,128)(2,1)S(1)}, bf16[2,144,512]{2,1,0:T(8,128)(2,1)S(1)}, u32[]{:S(2)}, u32[]{:S(2)}) collective-permute-start(bf16[2,144,512]{2,1,0:T(8,128)(2,1)S(1)} %get-tuple-element.80), channel_id=1, source_target_pairs={{0,2},{1,3},{2,0},{3,1},{4,6},{5,7},{6,4},{7,5},{8,10},{9,11},{10,... | collective-permute-start | bytes 884744 | tf_op jit(solution)/shard_map/ppermute | solution.py:238
  43.8 17.6 %collective-permute-start.10 = (bf16[2,2,144,512]{3,2,1,0:T(8,128)(2,1)S(1)}, bf16[2,2,144,512]{3,2,1,0:T(8,128)(2,1)S(1)}, u32[]{:S(2)}, u32[]{:S(2)}) collective-permute-start(bf16[2,2,144,512]{3,2,1,0:T(8,128)(2,1)S(1)} %pad_maximum_fusion), channel_id=1, source_target_pairs={{0,6},{1,7},{2,4},{3,5},{4,2},{5,3},{6,0},{7,1},{8,14},{9,15},{10,... | collective-permute-start | bytes 1769480 | tf_op jit(solution)/shard_map/ppermute | solution.py:241
  49.9 10.2 %collective-permute-start.6 = (bf16[2,144,512]{2,1,0:T(8,128)(2,1)S(1)}, bf16[2,144,512]{2,1,0:T(8,128)(2,1)S(1)}, u32[]{:S(2)}, u32[]{:S(2)}) collective-permute-start(bf16[2,144,512]{2,1,0:T(8,128)(2,1)S(1)} %collective-permute-done.5.refs_2_.refs_5_), channel_id=1, source_target_pairs={{0,2},{1,3},{2,0},{3,1},{4,6},{5,7},{6,4},{7,5},{8,10},{9,11},{10,... | collective-permute-start | bytes 884744 | tf_op jit(solution)/shard_map/ppermute | solution.py:238
  63.5 6.6 %collective-permute-start.11 = (bf16[128,2048]{1,0:T(8,128)(2,1)S(1)}, bf16[128,2048]{1,0:T(8,128)(2,1)S(1)}, u32[]{:S(2)}, u32[]{:S(2)}) collective-permute-start(bf16[128,2048]{1,0:T(8,128)(2,1)S(1)} %shard_map.51), channel_id=1, source_target_pairs={{0,1},{1,0},{2,3},{3,2},{4,5},{5,4},{6,7},{7,6},{8,9},{9,8},{10,11... | collective-permute-start | bytes 1572872 | tf_op jit(solution)/shard_map/ppermute | solution.py:244

commit v10 on v8

--- a/solution.py
+++ b/solution.py
@@ -18,8 +18,9 @@
 NT = (((1,), (1,)), ((), ()))
 
 
-def marks(refs):
-    ids = [ref[half, BLOCK : BLOCK + 16, :HEAD][0:1].astype(jnp.float32) for ref in refs for half in range(2)]
+def marks(q_ref, refs):
+    ids = [q_ref[0:16, HQ // 2 * HEAD :][0:1].astype(jnp.float32)]
+    ids += [ref[half, BLOCK : BLOCK + 16, :HEAD][0:1].astype(jnp.float32) for ref in refs for half in range(2)]
     ids = jnp.concatenate(ids, axis=0)
     lane = lax.broadcasted_iota(jnp.int32, ids.shape, 1)
     first = jnp.zeros(ids.shape, jnp.int32)
@@ -33,9 +34,8 @@
 
 
 def piece(half, own, carried, last, n_blocks, core_ref, q_ref, *refs):
-    b0 = refs[0]
     blocks = []
-    for ref in refs[1 - own : n_blocks]:
+    for ref in refs[:n_blocks]:
         blocks.extend([ref] if len(ref.shape) == 3 else [ref.at[0], ref.at[1]])
     refs = refs[n_blocks:]
     old, refs = (refs[:3], refs[3:]) if carried else (None, refs)
@@ -43,12 +43,12 @@
     core = core_ref[0]
     row = lax.broadcasted_iota(jnp.int32, (BLOCK, HEAD), 0)
     lane = lax.broadcasted_iota(jnp.int32, (BLOCK, HEAD), 1)
-    first, end = marks([b0] + blocks)
+    first, end = marks(q_ref, blocks)
     one = jnp.ones((BLOCK, HEAD), jnp.bfloat16)
     for slot, ref in enumerate(blocks):
         for part in range(2):
             at = (2 * slot + part) * BLOCK
-            mark = 2 * slot + part + 2
+            mark = 2 * slot + part + 1
             inside = (row >= first[mark : mark + 1]) & (row < end[mark : mark + 1])
             hot = jnp.where(inside, 1.0, 0.0).astype(jnp.bfloat16)
             for kv in range(2):
@@ -56,7 +56,7 @@
                 kaug[kv, at : at + BLOCK, HEAD:] = hot
                 vaug[kv, at : at + BLOCK, :HEAD] = ref[part, :BLOCK, (2 + kv) * HEAD : (3 + kv) * HEAD]
                 vaug[kv, at : at + BLOCK, HEAD:] = one
-    inside = (row >= first[half : half + 1]) & (row < end[half : half + 1])
+    inside = (row >= first[0:1]) & (row < end[0:1])
     away = jnp.where(inside | (lane > 7), 0.0, FAR).astype(jnp.bfloat16)
     away = jnp.concatenate([away, away], axis=0)
     if own:
@@ -64,15 +64,18 @@
         wide = lax.broadcasted_iota(jnp.int32, (2 * BLOCK, 2 * BLOCK), 1)
         qat = (core ^ half) * BLOCK + (tall & (BLOCK - 1))
         kat = (core ^ (wide >> 7)) * BLOCK + (wide & (BLOCK - 1))
-        future = kat > qat
+        future = [kat - (1 - core_ref[flag]) * 2 * BLOCK > qat for flag in own]
     def scores(kv, pair):
         at = (kv * GROUP + 2 * pair) * HEAD
         q2 = jnp.concatenate([q_ref[:, at : at + HEAD], q_ref[:, at + HEAD : at + 2 * HEAD]], axis=0)
         q2 = jnp.concatenate([q2, away], axis=1)
         score = lax.dot_general(q2, kaug[kv], NT, preferred_element_type=jnp.float32)
         if own:
-            mine = jnp.where(future, FAR, score[:, : 2 * BLOCK])
-            score = mine if len(blocks) == 1 else jnp.concatenate([mine, score[:, 2 * BLOCK :]], axis=1)
+            wide = 2 * BLOCK
+            parts = [jnp.where(late, FAR, score[:, i * wide : (i + 1) * wide]) for i, late in enumerate(future)]
+            if len(own) < len(blocks):
+                parts.append(score[:, len(own) * wide :])
+            score = parts[0] if len(parts) == 1 else jnp.concatenate(parts, axis=1)
         return score
 
     def weights(score, kv, pair):
@@ -118,26 +121,26 @@
     finish(*pending)
 
 
-def attend(core, half, q, b0, blocks, own=False, state=(), last=False):
+def attend(core, half, q, blocks, own=(), state=(), last=False):
     vmem = pl.BlockSpec(memory_space=pltpu.VMEM)
-    count = own + sum(1 if block.ndim == 3 else 2 for block in blocks)
+    count = sum(1 if block.ndim == 3 else 2 for block in blocks)
     keys = 2 * BLOCK * count
     rows = BLOCK * HQ // 2
     if last:
-        out_shape = jax.ShapeDtypeStruct(q.shape, jnp.bfloat16)
+        out_shape = jax.ShapeDtypeStruct((BLOCK, HQ // 2 * HEAD), jnp.bfloat16)
     else:
         out_shape = [jax.ShapeDtypeStruct((rows, HEAD), jnp.float32)] * 3
     return pl.pallas_call(
-        functools.partial(piece, half, own, bool(state), last, 1 + len(blocks)),
+        functools.partial(piece, half, own, bool(state), last, len(blocks)),
         out_shape=out_shape,
-        in_specs=[pl.BlockSpec(memory_space=pltpu.SMEM)] + [vmem] * (2 + len(blocks) + len(state)),
+        in_specs=[pl.BlockSpec(memory_space=pltpu.SMEM)] + [vmem] * (1 + len(blocks) + len(state)),
         out_specs=vmem if last else [vmem] * 3,
         scratch_shapes=[pltpu.VMEM((2, keys, 2 * HEAD), jnp.bfloat16)] * 2,
         compiler_params=pltpu.CompilerParams(vmem_limit_bytes=32 * 1024 * 1024),
         cost_estimate=pl.CostEstimate(
             flops=8 * rows * keys * HEAD, bytes_accessed=4 << 20, transcendentals=rows * keys
         ),
-    )(core, q, b0, *blocks, *state)
+    )(core, q, *blocks, *state)
 
 
 def shards(queries, keys, values, doc_ids):
@@ -149,8 +152,8 @@
         pairs = [(p * 64 + s, (p + 1) % 8 * 64 + ((s + 8 * dy) % 64 ^ flip)) for p in range(8) for s in range(64)]
         return lax.ppermute(block, ("pp", "sp"), pairs)
 
-    def along_y(block, step0, step1):
-        return lax.ppermute(block, "sp", [(s, (s + 8 * (step1 if s % 2 else step0)) % 64) for s in range(64)])
+    def along_y(block, steps):
+        return lax.ppermute(block, "sp", [(s, (s + 8 * steps[s // 2 % 4]) % 64) for s in range(64)])
 
     def even_pair(block):
         return lax.ppermute(block, "sp", [(s, s ^ 2) for s in range(64)])
@@ -171,27 +174,31 @@
     mine, other = jnp.where(first, half0, half1), jnp.where(first, half1, half0)
     q = queries[0]
     b4 = jnp.stack([section(mine, 0, 1), section(other, 1, 1)])
-    qf = section(jnp.where(first, q[:, 2048:], q[:, :2048]), 1)
-    qs = section(jnp.where(first, q[:, :2048], q[:, 2048:]), 0)
+    rider = jnp.pad(doc_ids[0].astype(jnp.bfloat16)[None], ((0, BLOCK - 1), (0, 0)))
+    qf = section(jnp.concatenate([jnp.where(first, q[:, 2048:], q[:, :2048]), rider], axis=1), 1)
+    qs = section(jnp.concatenate([jnp.where(first, q[:, :2048], q[:, 2048:]), rider], axis=1), 0)
     (b4,) = lax.optimization_barrier((b4,))
+    ya = along_y(b4, (-1, -1, 1, 1))
     e1 = even_pair(b4)
-    ya = along_y(b4, 1, -1)
-    yb = along_y(b4, -1, 1)
-    ya, yb, b4, qf = lax.optimization_barrier((ya, yb, b4, qf))
-    f2 = odd_pair(jnp.where((column < 2) == first, yb, ya))
-    e2 = even_pair(jnp.where((column % 2 == 0) == first, yb, ya))
+    ya, b4, qf = lax.optimization_barrier((ya, b4, qf))
+    f2 = odd_pair(ya)
+    e1, ya = lax.optimization_barrier((e1, ya))
+    e2 = along_y(e1, (1, -1, 1, -1))
     f13 = odd_pair(jnp.stack([b4, e1]))
-    b0, b8 = jnp.where(first, yb, ya), jnp.where(first, ya, yb)
-    at = core[None].astype(jnp.int32)
-    state = attend(at, 1, qf, b0, [b4, b8, e1], own=True)
-    (f2,) = lax.optimization_barrier((f2,))
+    left = (column < 2).astype(jnp.int32)
+    at = jnp.stack([core.astype(jnp.int32), left, 1 - left])
+    state = attend(at, 1, qf, [ya, b4, e1], own=(1,))
+    f2, b5 = lax.optimization_barrier((f2, b4))
     e3 = even_pair(f2)
-    state2 = attend(at, 0, qs, b0, [b4, b8, e1, e2, f2], own=True)
-    state = attend(at, 1, qf, b0, [e2, f2], state=state)
-    e3, f13, qs, qf, b0, *both = lax.optimization_barrier((e3, f13, qs, qf, b0, *state, *state2))
-    of_ = attend(at, 1, qf, b0, [e3, f13], state=both[:3], last=True)
+    yb = along_y(b5, (1, 1, -1, -1))
+    state2 = attend(at, 0, qs, [ya, b4, e1, f2, e2], own=(1,))
+    state = attend(at, 1, qf, [f2, e2], state=state)
+    yb, f13, *both = lax.optimization_barrier((yb, f13, *state, *state2))
+    state = attend(at, 1, qf, [yb, f13], own=(2,), state=both[:3])
+    e3, yb, f13, qs, qf, *both = lax.optimization_barrier((e3, yb, f13, qs, qf, *state, *both[3:]))
+    of_ = attend(at, 1, qf, [e3], state=both[:3], last=True)
     got = swap(of_)
-    os_ = attend(at, 0, qs, b0, [e3, f13], state=both[3:], last=True)
+    os_ = attend(at, 0, qs, [yb, e3, f13], own=(2,), state=both[3:], last=True)
     out = jnp.where(first, jnp.concatenate([os_, got], axis=1), jnp.concatenate([got, os_], axis=1))
     return out[None]
 

time: 70.9 us -> 76.1 us (1.073)
  the two profiles are of different devices: /device:TPU:1 before, /device:TPU:5 now
where the time goes in v10:
time: 76.1 us; the launch traced here: 75.7 us
  starting transfers between devices  40.9 us (54%)
  Pallas kernels  19.3 us (25%)
  waiting for transfers between devices  11.9 us (16%)
  other arithmetic  2.35 us (3%)
  local copies, waits for them, and re-layouts  0.96 us (1%)
    pallas_call x6, Pallas kernels, attend(): pl.pallas_call(functools.partial(piece, half, own, bool(state), last, len...  19.3 us
    ppermute x4, starting transfers between devices, section(): return lax.ppermute(block, ('pp', 'sp'), pairs)  16.2 us
    ppermute x2, starting transfers between devices, even_pair(): return lax.ppermute(block, 'sp', [(s, s ^ 2) for s in range(64)])  7.7 us
    ppermute x3, starting transfers between devices, along_y(): lax.ppermute(block, 'sp', [(s, (s + 8 * steps[s // 2 % 4]) % 64) for s in...  6.82 us
    ppermute x4, waiting for transfers between devices, section(): return lax.ppermute(block, ('pp', 'sp'), pairs)  6.74 us
    ppermute x2, starting transfers between devices, odd_pair(): lax.ppermute(block, 'sp', [(s, s // 8 * 8 + (s + (2 if s & 2 else -2)) %...  6.21 us
    ppermute x3, waiting for transfers between devices, along_y(): lax.ppermute(block, 'sp', [(s, (s + 8 * steps[s // 2 % 4]) % 64) for s in...  5.1 us
    ppermute x1, starting transfers between devices, swap(): return lax.ppermute(block, 'sp', [(s, s ^ 1) for s in range(64)])  3.93 us
  transfers between devices with their start and end apart: 12, of which 4 were waited for; matrix products, arithmetic and copies ran while one was open for 0% of the time, Pallas kernels for 23%

profile of v10, /device:TPU:5, one launch (start us, length us, event | category | flops | bytes accessed | tf_op | source)
XLA Modules:
  0.0 75.7 jit_solution(9775136869292154893)
XLA Ops:
  0.0 0.0 copy-start
  0.0 0.7 convert_element_type.13
  0.8 1.0 %fusion.6 = (bf16[128,256]{1,0:T(8,128)(2,1)S(1)}, bf16[128,256]{1,0:T(8,128)(2,1)S(1)}, bf16[128,256]{1,0:T(8,128)(2,1)S(1)}, bf16[128,256]{1,0:T(8,128)(2,1)S(1)}) fusion(bf16[128,512]{1,0:T(8,128)(2,1)} %bitcast.19, bf16[128,512]{1,0:T(8,128)(2,1)} %bitcast.20), kind=kLoop, calls=%fused_computation.16 | loop fusion | bytes 524288 | tf_op jit(solution)/shard_map/slice | solution.py:171
  1.8 5.0 %collective-permute-start = (bf16[144,512]{1,0:T(8,128)(2,1)S(1)}, bf16[144,512]{1,0:T(8,128)(2,1)S(1)}, u32[]{:S(2)}, u32[]{:S(2)}) collective-permute-start(bf16[144,512]{1,0:T(8,128)(2,1)S(1)} %get-tuple-element.83), channel_id=1, source_target_pairs={{0,72},{1,73},{2,74},{3,75},{4,76},{5,77},{6,78},{7,79},{8,80},{9,... | collective-permute-start | bytes 442376 | tf_op jit(solution)/shard_map/ppermute | solution.py:153
  6.8 5.9 %collective-permute-start.1 = (bf16[144,512]{1,0:T(8,128)(2,1)S(1)}, bf16[144,512]{1,0:T(8,128)(2,1)S(1)}, u32[]{:S(2)}, u32[]{:S(2)}) collective-permute-start(bf16[144,512]{1,0:T(8,128)(2,1)S(1)} %get-tuple-element.84), channel_id=1, source_target_pairs={{0,73},{1,72},{2,75},{3,74},{4,77},{5,76},{6,79},{7,78},{8,81},{9,... | collective-permute-start | bytes 442376 | tf_op jit(solution)/shard_map/ppermute | solution.py:153
  12.6 0.0 copy-done
  12.7 0.1 broadcast_select_fusion
  12.7 0.1 fusion.2
  12.8 3.4 %collective-permute-start.3 = (bf16[128,2176]{1,0:T(8,128)(2,1)S(1)}, bf16[128,2176]{1,0:T(8,128)(2,1)S(1)}, u32[]{:S(2)}, u32[]{:S(2)}) collective-permute-start(bf16[128,2176]{1,0:T(8,128)(2,1)S(1)} %get-tuple-element.90), channel_id=1, source_target_pairs={{0,65},{1,64},{2,67},{3,66},{4,69},{5,68},{6,71},{7,70},{8,73},{9,... | collective-permute-start | bytes 1671176 | tf_op jit(solution)/shard_map/ppermute | solution.py:153
  16.3 2.6 %collective-permute-done = bf16[144,512]{1,0:T(8,128)(2,1)S(1)} collective-permute-done((bf16[144,512]{1,0:T(8,128)(2,1)S(1)}, bf16[144,512]{1,0:T(8,128)(2,1)S(1)}, u32[]{:S(2)}, u32[]{:S(2)}) %collective-permute-start) | collective-permute-done | bytes 147488 | tf_op jit(solution)/shard_map/ppermute | solution.py:153
  18.9 3.8 %collective-permute-done.1 = bf16[144,512]{1,0:T(8,128)(2,1)S(1)} collective-permute-done((bf16[144,512]{1,0:T(8,128)(2,1)S(1)}, bf16[144,512]{1,0:T(8,128)(2,1)S(1)}, u32[]{:S(2)}, u32[]{:S(2)}) %collective-permute-start.1) | collective-permute-done | bytes 147488 | tf_op jit(solution)/shard_map/ppermute | solution.py:153
  22.7 1.9 %collective-permute-start.2 = (bf16[2,144,512]{2,1,0:T(8,128)(2,1)S(1)}, bf16[2,144,512]{2,1,0:T(8,128)(2,1)S(1)}, u32[]{:S(2)}, u32[]{:S(2)}) collective-permute-start(bf16[2,144,512]{2,1,0:T(8,128)(2,1)S(1)} %pad_maximum_fusion.1.refs_1_), channel_id=1, source_target_pairs={{0,56},{1,57},{2,58},{3,59},{4,12},{5,13},{6,14},{7,15},{8,0},{9,1... | collective-permute-start | bytes 884744 | tf_op jit(solution)/shard_map/ppermute | solution.py:156
  24.7 2.8 %collective-permute-start.7 = (bf16[2,144,512]{2,1,0:T(8,128)(2,1)S(1)}, bf16[2,144,512]{2,1,0:T(8,128)(2,1)S(1)}, u32[]{:S(2)}, u32[]{:S(2)}) collective-permute-start(bf16[2,144,512]{2,1,0:T(8,128)(2,1)S(1)} %pad_maximum_fusion.1.refs_1_), channel_id=1, source_target_pairs={{0,2},{1,3},{2,0},{3,1},{4,6},{5,7},{6,4},{7,5},{8,10},{9,11},{10,... | collective-permute-start | bytes 884744 | tf_op jit(solution)/shard_map/ppermute | solution.py:159
  27.5 1.9 %collective-permute-start.10 = (bf16[128,2176]{1,0:T(8,128)(2,1)S(1)}, bf16[128,2176]{1,0:T(8,128)(2,1)S(1)}, u32[]{:S(2)}, u32[]{:S(2)}) collective-permute-start(bf16[128,2176]{1,0:T(8,128)(2,1)S(1)} %get-tuple-element.89), channel_id=1, source_target_pairs={{0,64},{1,65},{2,66},{3,67},{4,68},{5,69},{6,70},{7,71},{8,72},{9,... | collective-permute-start | bytes 1671176 | tf_op jit(solution)/shard_map/ppermute | solution.py:153
  29.5 5.1 %collective-permute-done.2.refs_0_ = bf16[2,144,512]{2,1,0:T(8,128)(2,1)S(1)} collective-permute-done((bf16[2,144,512]{2,1,0:T(8,128)(2,1)S(1)}, bf16[2,144,512]{2,1,0:T(8,128)(2,1)S(1)}, u32[]{:S(2)}, u32[]{:S(2)}) %collective-permute-start.2) | collective-permute-done | bytes 294944 | tf_op jit(solution)/shard_map/ppermute | solution.py:156
  34.6 0.3 collective-permute-done.3.q_ref
  34.9 2.0 %collective-permute-start.4 = (bf16[2,144,512]{2,1,0:T(8,128)(2,1)S(1)}, bf16[2,144,512]{2,1,0:T(8,128)(2,1)S(1)}, u32[]{:S(2)}, u32[]{:S(2)}) collective-permute-start(bf16[2,144,512]{2,1,0:T(8,128)(2,1)S(1)} %collective-permute-done.2.refs_0_), channel_id=1, source_target_pairs={{0,6},{1,7},{2,4},{3,5},{4,2},{5,3},{6,0},{7,1},{8,14},{9,15},{10,... | collective-permute-start | bytes 884744 | tf_op jit(solution)/shard_map/ppermute | solution.py:162
  36.9 0.0 collective-permute-done.7.refs_2_
  36.9 1.9 %collective-permute-start.9 = (bf16[2,144,512]{2,1,0:T(8,128)(2,1)S(1)}, bf16[2,144,512]{2,1,0:T(8,128)(2,1)S(1)}, u32[]{:S(2)}, u32[]{:S(2)}) collective-permute-start(bf16[2,144,512]{2,1,0:T(8,128)(2,1)S(1)} %collective-permute-done.7.refs_2_), channel_id=1, source_target_pairs={{0,8},{1,9},{2,58},{3,59},{4,12},{5,13},{6,62},{7,63},{8,16},{9,17... | collective-permute-start | bytes 884744 | tf_op jit(solution)/shard_map/ppermute | solution.py:156
  38.8 0.1 pad_maximum_fusion
  38.9 4.2 %collective-permute-start.8 = (bf16[2,2,144,512]{3,2,1,0:T(8,128)(2,1)S(1)}, bf16[2,2,144,512]{3,2,1,0:T(8,128)(2,1)S(1)}, u32[]{:S(2)}, u32[]{:S(2)}) collective-permute-start(bf16[2,2,144,512]{3,2,1,0:T(8,128)(2,1)S(1)} %pad_maximum_fusion), channel_id=1, source_target_pairs={{0,6},{1,7},{2,4},{3,5},{4,2},{5,3},{6,0},{7,1},{8,14},{9,15},{10,... | collective-permute-start | bytes 1769480 | tf_op jit(solution)/shard_map/ppermute | solution.py:162
  43.1 0.1 pad_add_fusion.core_ref
  43.2 3.1 %shard_map.46 = (f32[2048,128]{1,0:T(8,128)S(1)}, f32[2048,128]{1,0:T(8,128)S(1)}, f32[2048,128]{1,0:T(8,128)S(1)}) custom-call(s32[3]{0:T(128)S(1)} %pad_add_fusion.core_ref, bf16[128,2176]{1,0:T(8,128)(2,1)S(1)} %collective-permute-done.3.q_ref, bf16[2,144,512]{2,1,0:T(8,128)(2,1)S(1)} %collective-permute-done.2.refs_0_, ...), custom_call_target="tpu_custom_call" | custom-call | flops 1610612736 | bytes 4194304 | tf_op jit(solution)/shard_map/pallas_call | solution.py:133
  46.3 0.0 collective-permute-done.4.refs_0_.refs_3_
  46.3 3.0 %collective-permute-start.6 = (bf16[2,144,512]{2,1,0:T(8,128)(2,1)S(1)}, bf16[2,144,512]{2,1,0:T(8,128)(2,1)S(1)}, u32[]{:S(2)}, u32[]{:S(2)}) collective-permute-start(bf16[2,144,512]{2,1,0:T(8,128)(2,1)S(1)} %pad_maximum_fusion.1.refs_1_), channel_id=1, source_target_pairs={{0,8},{1,9},{2,10},{3,11},{4,60},{5,61},{6,62},{7,63},{8,16},{9,17... | collective-permute-start | bytes 884744 | tf_op jit(solution)/shard_map/ppermute | solution.py:156
  49.3 4.9 %collective-permute-start.5 = (bf16[2,144,512]{2,1,0:T(8,128)(2,1)S(1)}, bf16[2,144,512]{2,1,0:T(8,128)(2,1)S(1)}, u32[]{:S(2)}, u32[]{:S(2)}) collective-permute-start(bf16[2,144,512]{2,1,0:T(8,128)(2,1)S(1)} %collective-permute-done.4.refs_0_.refs_3_), channel_id=1, source_target_pairs={{0,2},{1,3},{2,0},{3,1},{4,6},{5,7},{6,4},{7,5},{8,10},{9,11},{10,... | collective-permute-start | bytes 884744 | tf_op jit(solution)/shard_map/ppermute | solution.py:159
  54.2 0.0 collective-permute-done.10.q_ref
  54.2 0.0 collective-permute-done.9.refs_1_.refs_4_
  54.2 4.6 %shard_map.48 = (f32[2048,128]{1,0:T(8,128)S(1)}, f32[2048,128]{1,0:T(8,128)S(1)}, f32[2048,128]{1,0:T(8,128)S(1)}) custom-call(s32[3]{0:T(128)S(1)} %pad_add_fusion.core_ref, bf16[128,2176]{1,0:T(8,128)(2,1)S(1)} %collective-permute-done.10.q_ref, bf16[2,144,512]{2,1,0:T(8,128)(2,1)S(1)} %collective-permute-done.2.refs_0_, ...), custom_call_target="tpu_custom_call" | custom-call | flops 2684354560 | bytes 4194304 | tf_op jit(solution)/shard_map/pallas_call | solution.py:133
  58.8 2.5 %shard_map.47 = (f32[2048,128]{1,0:T(8,128)S(1)}, f32[2048,128]{1,0:T(8,128)S(1)}, f32[2048,128]{1,0:T(8,128)S(1)}) custom-call(s32[3]{0:T(128)S(1)} %pad_add_fusion.core_ref, bf16[128,2176]{1,0:T(8,128)(2,1)S(1)} %collective-permute-done.3.q_ref, bf16[2,144,512]{2,1,0:T(8,128)(2,1)S(1)} %collective-permute-done.4.refs_0_.refs_3_, ...), custom_call_target="tpu_custom_call" | custom-call | flops 1073741824 | bytes 4194304 | tf_op jit(solution)/shard_map/pallas_call | solution.py:133
  61.3 0.0 collective-permute-done.8.refs_1_.refs_2_
  61.3 0.0 collective-permute-done.6.refs_0_
  61.3 3.3 %shard_map.49 = (f32[2048,128]{1,0:T(8,128)S(1)}, f32[2048,128]{1,0:T(8,128)S(1)}, f32[2048,128]{1,0:T(8,128)S(1)}) custom-call(s32[3]{0:T(128)S(1)} %pad_add_fusion.core_ref, bf16[128,2176]{1,0:T(8,128)(2,1)S(1)} %collective-permute-done.3.q_ref, bf16[2,144,512]{2,1,0:T(8,128)(2,1)S(1)} %collective-permute-done.6.refs_0_, ...), custom_call_target="tpu_custom_call" | custom-call | flops 1610612736 | bytes 4194304 | tf_op jit(solution)/shard_map/pallas_call | solution.py:133
  64.6 0.0 collective-permute-done.5.refs_1_.refs_0_
  64.6 1.9 %shard_map.51 = bf16[128,2048]{1,0:T(8,128)(2,1)S(1)} custom-call(s32[3]{0:T(128)S(1)} %pad_add_fusion.core_ref, bf16[128,2176]{1,0:T(8,128)(2,1)S(1)} %collective-permute-done.3.q_ref, bf16[2,144,512]{2,1,0:T(8,128)(2,1)S(1)} %collective-permute-done.5.refs_1_.refs_0_, f32[2048,128]{1,0:T(8,128)S(1)} %get-tuple-element.78.refs_1_, ...), custom_call_target="tpu_custom_call" | custom-call | flops 536870912 | bytes 4194304 | tf_op jit(solution)/shard_map/pallas_call | solution.py:133
  66.5 3.9 %collective-permute-start.11 = (bf16[128,2048]{1,0:T(8,128)(2,1)S(1)}, bf16[128,2048]{1,0:T(8,128)(2,1)S(1)}, u32[]{:S(2)}, u32[]{:S(2)}) collective-permute-start(bf16[128,2048]{1,0:T(8,128)(2,1)S(1)} %shard_map.51), channel_id=1, source_target_pairs={{0,1},{1,0},{2,3},{3,2},{4,5},{5,4},{6,7},{7,6},{8,9},{9,8},{10,11... | collective-permute-start | bytes 1572872 | tf_op jit(solution)/shard_map/ppermute | solution.py:165
  70.5 4.0 %shard_map.50 = bf16[128,2048]{1,0:T(8,128)(2,1)S(1)} custom-call(s32[3]{0:T(128)S(1)} %pad_add_fusion.core_ref, bf16[128,2176]{1,0:T(8,128)(2,1)S(1)} %collective-permute-done.10.q_ref, bf16[2,144,512]{2,1,0:T(8,128)(2,1)S(1)} %collective-permute-done.6.refs_0_, bf16[2,144,512]{2,1,0:T(8,128)(2,1)S(1)} %collective-permute-done.5.refs_1_.refs_0_, ...), custom_call_target="tpu_custom_call" | custom-call | flops 2147483648 | bytes 4194304 | tf_op jit(solution)/shard_map/pallas_call | solution.py:133
  74.4 0.0 collective-permute-done.11
  74.4 1.2 %maximum_select_fusion = bf16[1,128,4096]{2,1,0:T(8,128)(2,1)} fusion(bf16[1,128,2048]{2,1,0:T(8,128)(2,1)S(1)} %bitcast.16, bf16[1,128,2048]{2,1,0:T(8,128)(2,1)S(1)} %bitcast.13, pred[]{:T(512)S(6)} %eq.6), kind=kLoop, calls=%fused_computation.2 | loop fusion | flops 4718592 | bytes 2097153 | tf_op jit(solution)/shard_map/jit(_where)/select_n | solution.py:202
  (2 shorter events, 0.1 us)
Async XLA Ops:
  0.0 12.6 %copy-start = (bf16[1,128,4096]{2,1,0:T(8,128)(2,1)S(1)}, bf16[1,128,4096]{2,1,0:T(8,128)(2,1)}, u32[]{:S(2)}) copy-start(bf16[1,128,4096]{2,1,0:T(8,128)(2,1)} %param.4) | copy-start | bytes 3145732
  1.8 17.1 %collective-permute-start = (bf16[144,512]{1,0:T(8,128)(2,1)S(1)}, bf16[144,512]{1,0:T(8,128)(2,1)S(1)}, u32[]{:S(2)}, u32[]{:S(2)}) collective-permute-start(bf16[144,512]{1,0:T(8,128)(2,1)S(1)} %get-tuple-element.83), channel_id=1, source_target_pairs={{0,72},{1,73},{2,74},{3,75},{4,76},{5,77},{6,78},{7,79},{8,80},{9,... | collective-permute-start | bytes 442376 | tf_op jit(solution)/shard_map/ppermute | solution.py:153
  6.8 15.9 %collective-permute-start.1 = (bf16[144,512]{1,0:T(8,128)(2,1)S(1)}, bf16[144,512]{1,0:T(8,128)(2,1)S(1)}, u32[]{:S(2)}, u32[]{:S(2)}) collective-permute-start(bf16[144,512]{1,0:T(8,128)(2,1)S(1)} %get-tuple-element.84), channel_id=1, source_target_pairs={{0,73},{1,72},{2,75},{3,74},{4,77},{5,76},{6,79},{7,78},{8,81},{9,... | collective-permute-start | bytes 442376 | tf_op jit(solution)/shard_map/ppermute | solution.py:153
  12.8 22.0 %collective-permute-start.3 = (bf16[128,2176]{1,0:T(8,128)(2,1)S(1)}, bf16[128,2176]{1,0:T(8,128)(2,1)S(1)}, u32[]{:S(2)}, u32[]{:S(2)}) collective-permute-start(bf16[128,2176]{1,0:T(8,128)(2,1)S(1)} %get-tuple-element.90), channel_id=1, source_target_pairs={{0,65},{1,64},{2,67},{3,66},{4,69},{5,68},{6,71},{7,70},{8,73},{9,... | collective-permute-start | bytes 1671176 | tf_op jit(solution)/shard_map/ppermute | solution.py:153
  22.7 11.8 %collective-permute-start.2 = (bf16[2,144,512]{2,1,0:T(8,128)(2,1)S(1)}, bf16[2,144,512]{2,1,0:T(8,128)(2,1)S(1)}, u32[]{:S(2)}, u32[]{:S(2)}) collective-permute-start(bf16[2,144,512]{2,1,0:T(8,128)(2,1)S(1)} %pad_maximum_fusion.1.refs_1_), channel_id=1, source_target_pairs={{0,56},{1,57},{2,58},{3,59},{4,12},{5,13},{6,14},{7,15},{8,0},{9,1... | collective-permute-start | bytes 884744 | tf_op jit(solution)/shard_map/ppermute | solution.py:156
  24.7 12.2 %collective-permute-start.7 = (bf16[2,144,512]{2,1,0:T(8,128)(2,1)S(1)}, bf16[2,144,512]{2,1,0:T(8,128)(2,1)S(1)}, u32[]{:S(2)}, u32[]{:S(2)}) collective-permute-start(bf16[2,144,512]{2,1,0:T(8,128)(2,1)S(1)} %pad_maximum_fusion.1.refs_1_), channel_id=1, source_target_pairs={{0,2},{1,3},{2,0},{3,1},{4,6},{5,7},{6,4},{7,5},{8,10},{9,11},{10,... | collective-permute-start | bytes 884744 | tf_op jit(solution)/shard_map/ppermute | solution.py:159
  27.5 26.7 %collective-permute-start.10 = (bf16[128,2176]{1,0:T(8,128)(2,1)S(1)}, bf16[128,2176]{1,0:T(8,128)(2,1)S(1)}, u32[]{:S(2)}, u32[]{:S(2)}) collective-permute-start(bf16[128,2176]{1,0:T(8,128)(2,1)S(1)} %get-tuple-element.89), channel_id=1, source_target_pairs={{0,64},{1,65},{2,66},{3,67},{4,68},{5,69},{6,70},{7,71},{8,72},{9,... | collective-permute-start | bytes 1671176 | tf_op jit(solution)/shard_map/ppermute | solution.py:153
  34.9 11.4 %collective-permute-start.4 = (bf16[2,144,512]{2,1,0:T(8,128)(2,1)S(1)}, bf16[2,144,512]{2,1,0:T(8,128)(2,1)S(1)}, u32[]{:S(2)}, u32[]{:S(2)}) collective-permute-start(bf16[2,144,512]{2,1,0:T(8,128)(2,1)S(1)} %collective-permute-done.2.refs_0_), channel_id=1, source_target_pairs={{0,6},{1,7},{2,4},{3,5},{4,2},{5,3},{6,0},{7,1},{8,14},{9,15},{10,... | collective-permute-start | bytes 884744 | tf_op jit(solution)/shard_map/ppermute | solution.py:162
  36.9 17.3 %collective-permute-start.9 = (bf16[2,144,512]{2,1,0:T(8,128)(2,1)S(1)}, bf16[2,144,512]{2,1,0:T(8,128)(2,1)S(1)}, u32[]{:S(2)}, u32[]{:S(2)}) collective-permute-start(bf16[2,144,512]{2,1,0:T(8,128)(2,1)S(1)} %collective-permute-done.7.refs_2_), channel_id=1, source_target_pairs={{0,8},{1,9},{2,58},{3,59},{4,12},{5,13},{6,62},{7,63},{8,16},{9,17... | collective-permute-start | bytes 884744 | tf_op jit(solution)/shard_map/ppermute | solution.py:156
  38.9 22.4 %collective-permute-start.8 = (bf16[2,2,144,512]{3,2,1,0:T(8,128)(2,1)S(1)}, bf16[2,2,144,512]{3,2,1,0:T(8,128)(2,1)S(1)}, u32[]{:S(2)}, u32[]{:S(2)}) collective-permute-start(bf16[2,2,144,512]{3,2,1,0:T(8,128)(2,1)S(1)} %pad_maximum_fusion), channel_id=1, source_target_pairs={{0,6},{1,7},{2,4},{3,5},{4,2},{5,3},{6,0},{7,1},{8,14},{9,15},{10,... | collective-permute-start | bytes 1769480 | tf_op jit(solution)/shard_map/ppermute | solution.py:162
  46.3 15.0 %collective-permute-start.6 = (bf16[2,144,512]{2,1,0:T(8,128)(2,1)S(1)}, bf16[2,144,512]{2,1,0:T(8,128)(2,1)S(1)}, u32[]{:S(2)}, u32[]{:S(2)}) collective-permute-start(bf16[2,144,512]{2,1,0:T(8,128)(2,1)S(1)} %pad_maximum_fusion.1.refs_1_), channel_id=1, source_target_pairs={{0,8},{1,9},{2,10},{3,11},{4,60},{5,61},{6,62},{7,63},{8,16},{9,17... | collective-permute-start | bytes 884744 | tf_op jit(solution)/shard_map/ppermute | solution.py:156
  49.3 15.3 %collective-permute-start.5 = (bf16[2,144,512]{2,1,0:T(8,128)(2,1)S(1)}, bf16[2,144,512]{2,1,0:T(8,128)(2,1)S(1)}, u32[]{:S(2)}, u32[]{:S(2)}) collective-permute-start(bf16[2,144,512]{2,1,0:T(8,128)(2,1)S(1)} %collective-permute-done.4.refs_0_.refs_3_), channel_id=1, source_target_pairs={{0,2},{1,3},{2,0},{3,1},{4,6},{5,7},{6,4},{7,5},{8,10},{9,11},{10,... | collective-permute-start | bytes 884744 | tf_op jit(solution)/shard_map/ppermute | solution.py:159
  66.5 7.9 %collective-permute-start.11 = (bf16[128,2048]{1,0:T(8,128)(2,1)S(1)}, bf16[128,2048]{1,0:T(8,128)(2,1)S(1)}, u32[]{:S(2)}, u32[]{:S(2)}) collective-permute-start(bf16[128,2048]{1,0:T(8,128)(2,1)S(1)} %shard_map.51), channel_id=1, source_target_pairs={{0,1},{1,0},{2,3},{3,2},{4,5},{5,4},{6,7},{7,6},{8,9},{9,8},{10,11... | collective-permute-start | bytes 1572872 | tf_op jit(solution)/shard_map/ppermute | solution.py:165

commit v11 on v8

--- a/solution.py
+++ b/solution.py
@@ -188,8 +188,11 @@
     e3 = even_pair(f2)
     state2 = attend(at, 0, qs, b0, [b4, b8, e1, e2, f2], own=True)
     state = attend(at, 1, qf, b0, [e2, f2], state=state)
+    e3, *state = lax.optimization_barrier((e3, *state, *state2))
+    state, state2 = state[:3], state[3:]
+    state = attend(at, 1, qf, b0, [e3], state=state)
     e3, f13, qs, qf, b0, *both = lax.optimization_barrier((e3, f13, qs, qf, b0, *state, *state2))
-    of_ = attend(at, 1, qf, b0, [e3, f13], state=both[:3], last=True)
+    of_ = attend(at, 1, qf, b0, [f13], state=both[:3], last=True)
     got = swap(of_)
     os_ = attend(at, 0, qs, b0, [e3, f13], state=both[3:], last=True)
     out = jnp.where(first, jnp.concatenate([os_, got], axis=1), jnp.concatenate([got, os_], axis=1))

time: 70.9 us -> 70.3 us (level)
  waiting for transfers between devices: 10.9 us -> 9.56 us
    ppermute x2, waiting for transfers between devices: 1.32 us -> 0.01 us  [odd_pair(): lax.ppermute(block, 'sp', [(s, s // 8 * 8 + (s + (2 if s & 2 else -2)) %...]
    pallas_call x5 -> x6, Pallas kernels: 15.4 us -> 16.1 us  [attend(): pl.pallas_call(functools.partial(piece, half, own, bool(state), last, 1 +...]
  transfers between devices with their start and end apart: 12 -> 12, of which waited for: 5 -> 4; matrix products, arithmetic and copies ran while one was open for 0% -> 0% of each run, Pallas kernels for 18% -> 20%
where the time goes in v11:
time: 70.3 us; the launch traced here: 69.8 us
  starting transfers between devices  40.6 us (58%)
  Pallas kernels  16.1 us (23%)
  waiting for transfers between devices  9.56 us (14%)
  other arithmetic  2.25 us (3%)
  local copies, waits for them, and re-layouts  0.96 us (1%)
    ppermute x4, starting transfers between devices, section(): return lax.ppermute(block, ('pp', 'sp'), pairs)  17.3 us
    pallas_call x6, Pallas kernels, attend(): pl.pallas_call(functools.partial(piece, half, own, bool(state), last, 1 +...  16.1 us
    ppermute x3, starting transfers between devices, even_pair(): return lax.ppermute(block, 'sp', [(s, s ^ 2) for s in range(64)])  7.81 us
    ppermute x2, starting transfers between devices, odd_pair(): lax.ppermute(block, 'sp', [(s, s // 8 * 8 + (s + (2 if s & 2 else -2)) %...  7.09 us
    ppermute x4, waiting for transfers between devices, section(): return lax.ppermute(block, ('pp', 'sp'), pairs)  5.64 us
    ppermute x2, starting transfers between devices, along_y(): lax.ppermute(block, 'sp', [(s, (s + 8 * (step1 if s % 2 else step0)) % 64...  5.28 us
    ppermute x2, waiting for transfers between devices, along_y(): lax.ppermute(block, 'sp', [(s, (s + 8 * (step1 if s % 2 else step0)) % 64...  3.17 us
    ppermute x1, starting transfers between devices, swap(): return lax.ppermute(block, 'sp', [(s, s ^ 1) for s in range(64)])  3.12 us
  transfers between devices with their start and end apart: 12, of which 4 were waited for; matrix products, arithmetic and copies ran while one was open for 0% of the time, Pallas kernels for 20%

profile of v11, /device:TPU:1, one launch (start us, length us, event | category | flops | bytes accessed | tf_op | source)
XLA Modules:
  0.0 69.8 jit_solution(9177663840899858251)
XLA Ops:
  0.0 0.0 copy-start
  0.0 0.7 %convert_element_type.6 = bf16[1,128]{1,0:T(2,128)(2,1)S(1)} convert(s32[1,128]{1,0:T(1,128)} %param.7) | non-fusion elementwise | flops 128 | bytes 768 | tf_op jit(solution)/shard_map/convert_element_type | solution.py:164
  0.8 1.0 %fusion.3 = (bf16[128,256]{1,0:T(8,128)(2,1)S(1)}, bf16[128,256]{1,0:T(8,128)(2,1)S(1)}, bf16[128,256]{1,0:T(8,128)(2,1)S(1)}, bf16[128,256]{1,0:T(8,128)(2,1)S(1)}) fusion(bf16[128,512]{1,0:T(8,128)(2,1)} %bitcast.17, bf16[128,512]{1,0:T(8,128)(2,1)} %bitcast.18), kind=kLoop, calls=%fused_computation.15 | loop fusion | bytes 524288 | tf_op jit(solution)/shard_map/slice | solution.py:168
  1.8 6.4 %collective-permute-start.1 = (bf16[144,512]{1,0:T(8,128)(2,1)S(1)}, bf16[144,512]{1,0:T(8,128)(2,1)S(1)}, u32[]{:S(2)}, u32[]{:S(2)}) collective-permute-start(bf16[144,512]{1,0:T(8,128)(2,1)S(1)} %get-tuple-element.80), channel_id=1, source_target_pairs={{0,73},{1,72},{2,75},{3,74},{4,77},{5,76},{6,79},{7,78},{8,81},{9,... | collective-permute-start | bytes 442376 | tf_op jit(solution)/shard_map/ppermute | solution.py:150
  8.2 5.0 %collective-permute-start = (bf16[144,512]{1,0:T(8,128)(2,1)S(1)}, bf16[144,512]{1,0:T(8,128)(2,1)S(1)}, u32[]{:S(2)}, u32[]{:S(2)}) collective-permute-start(bf16[144,512]{1,0:T(8,128)(2,1)S(1)} %get-tuple-element.79), channel_id=1, source_target_pairs={{0,72},{1,73},{2,74},{3,75},{4,76},{5,77},{6,78},{7,79},{8,80},{9,... | collective-permute-start | bytes 442376 | tf_op jit(solution)/shard_map/ppermute | solution.py:150
  13.2 0.0 copy-done
  13.2 0.1 broadcast_select_fusion
  13.3 4.0 %collective-permute-start.4 = (bf16[128,2048]{1,0:T(8,128)(2,1)S(1)}, bf16[128,2048]{1,0:T(8,128)(2,1)S(1)}, u32[]{:S(2)}, u32[]{:S(2)}) collective-permute-start(bf16[128,2048]{1,0:T(8,128)(2,1)S(1)} %get-tuple-element.74), channel_id=1, source_target_pairs={{0,65},{1,64},{2,67},{3,66},{4,69},{5,68},{6,71},{7,70},{8,73},{9,... | collective-permute-start | bytes 1572872 | tf_op jit(solution)/shard_map/ppermute | solution.py:150
  17.3 3.9 %collective-permute-done.1 = bf16[144,512]{1,0:T(8,128)(2,1)S(1)} collective-permute-done((bf16[144,512]{1,0:T(8,128)(2,1)S(1)}, bf16[144,512]{1,0:T(8,128)(2,1)S(1)}, u32[]{:S(2)}, u32[]{:S(2)}) %collective-permute-start.1) | collective-permute-done | bytes 147488 | tf_op jit(solution)/shard_map/ppermute | solution.py:150
  21.2 1.7 %collective-permute-done = bf16[144,512]{1,0:T(8,128)(2,1)S(1)} collective-permute-done((bf16[144,512]{1,0:T(8,128)(2,1)S(1)}, bf16[144,512]{1,0:T(8,128)(2,1)S(1)}, u32[]{:S(2)}, u32[]{:S(2)}) %collective-permute-start) | collective-permute-done | bytes 147488 | tf_op jit(solution)/shard_map/ppermute | solution.py:150
  23.0 3.0 %collective-permute-start.2 = (bf16[2,144,512]{2,1,0:T(8,128)(2,1)S(1)}, bf16[2,144,512]{2,1,0:T(8,128)(2,1)S(1)}, u32[]{:S(2)}, u32[]{:S(2)}) collective-permute-start(bf16[2,144,512]{2,1,0:T(8,128)(2,1)S(1)} %pad_maximum_fusion.1.refs_1_), channel_id=1, source_target_pairs={{0,8},{1,57},{2,10},{3,59},{4,12},{5,61},{6,14},{7,63},{8,16},{9,1... | collective-permute-start | bytes 884744 | tf_op jit(solution)/shard_map/ppermute | solution.py:153
  26.0 2.3 %collective-permute-start.3 = (bf16[2,144,512]{2,1,0:T(8,128)(2,1)S(1)}, bf16[2,144,512]{2,1,0:T(8,128)(2,1)S(1)}, u32[]{:S(2)}, u32[]{:S(2)}) collective-permute-start(bf16[2,144,512]{2,1,0:T(8,128)(2,1)S(1)} %pad_maximum_fusion.1.refs_1_), channel_id=1, source_target_pairs={{0,56},{1,9},{2,58},{3,11},{4,60},{5,13},{6,62},{7,15},{8,0},{9,17... | collective-permute-start | bytes 884744 | tf_op jit(solution)/shard_map/ppermute | solution.py:153
  28.3 3.1 %collective-permute-start.8 = (bf16[2,144,512]{2,1,0:T(8,128)(2,1)S(1)}, bf16[2,144,512]{2,1,0:T(8,128)(2,1)S(1)}, u32[]{:S(2)}, u32[]{:S(2)}) collective-permute-start(bf16[2,144,512]{2,1,0:T(8,128)(2,1)S(1)} %pad_maximum_fusion.1.refs_1_), channel_id=1, source_target_pairs={{0,2},{1,3},{2,0},{3,1},{4,6},{5,7},{6,4},{7,5},{8,10},{9,11},{10,... | collective-permute-start | bytes 884744 | tf_op jit(solution)/shard_map/ppermute | solution.py:156
  31.4 1.9 %collective-permute-start.9 = (bf16[128,2048]{1,0:T(8,128)(2,1)S(1)}, bf16[128,2048]{1,0:T(8,128)(2,1)S(1)}, u32[]{:S(2)}, u32[]{:S(2)}) collective-permute-start(bf16[128,2048]{1,0:T(8,128)(2,1)S(1)} %get-tuple-element.73), channel_id=1, source_target_pairs={{0,64},{1,65},{2,66},{3,67},{4,68},{5,69},{6,70},{7,71},{8,72},{9,... | collective-permute-start | bytes 1572872 | tf_op jit(solution)/shard_map/ppermute | solution.py:150
  33.4 0.0 collective-permute-done.2
  33.4 3.2 %collective-permute-done.3 = bf16[2,144,512]{2,1,0:T(8,128)(2,1)S(1)} collective-permute-done((bf16[2,144,512]{2,1,0:T(8,128)(2,1)S(1)}, bf16[2,144,512]{2,1,0:T(8,128)(2,1)S(1)}, u32[]{:S(2)}, u32[]{:S(2)}) %collective-permute-start.3) | collective-permute-done | bytes 294944 | tf_op jit(solution)/shard_map/ppermute | solution.py:153
  36.6 0.0 collective-permute-done.4.q_ref
  36.6 0.1 broadcast_select_fusion.3
  36.6 4.4 %collective-permute-start.5 = (bf16[2,144,512]{2,1,0:T(8,128)(2,1)S(1)}, bf16[2,144,512]{2,1,0:T(8,128)(2,1)S(1)}, u32[]{:S(2)}, u32[]{:S(2)}) collective-permute-start(bf16[2,144,512]{2,1,0:T(8,128)(2,1)S(1)} %get-tuple-element.78), channel_id=1, source_target_pairs={{0,6},{1,7},{2,4},{3,5},{4,2},{5,3},{6,0},{7,1},{8,14},{9,15},{10,... | collective-permute-start | bytes 884744 | tf_op jit(solution)/shard_map/ppermute | solution.py:159
  41.0 1.9 %collective-permute-start.7 = (bf16[2,144,512]{2,1,0:T(8,128)(2,1)S(1)}, bf16[2,144,512]{2,1,0:T(8,128)(2,1)S(1)}, u32[]{:S(2)}, u32[]{:S(2)}) collective-permute-start(bf16[2,144,512]{2,1,0:T(8,128)(2,1)S(1)} %get-tuple-element.76), channel_id=1, source_target_pairs={{0,2},{1,3},{2,0},{3,1},{4,6},{5,7},{6,4},{7,5},{8,10},{9,11},{10,... | collective-permute-start | bytes 884744 | tf_op jit(solution)/shard_map/ppermute | solution.py:156
  43.0 0.0 collective-permute-done.8.refs_3_
  43.0 0.1 pad_maximum_fusion
  43.0 2.7 %collective-permute-start.10 = (bf16[2,2,144,512]{3,2,1,0:T(8,128)(2,1)S(1)}, bf16[2,2,144,512]{3,2,1,0:T(8,128)(2,1)S(1)}, u32[]{:S(2)}, u32[]{:S(2)}) collective-permute-start(bf16[2,2,144,512]{3,2,1,0:T(8,128)(2,1)S(1)} %pad_maximum_fusion), channel_id=1, source_target_pairs={{0,6},{1,7},{2,4},{3,5},{4,2},{5,3},{6,0},{7,1},{8,14},{9,15},{10,... | collective-permute-start | bytes 1769480 | tf_op jit(solution)/shard_map/ppermute | solution.py:159
  45.8 3.3 %shard_map.46 = (f32[2048,128]{1,0:T(8,128)S(1)}, f32[2048,128]{1,0:T(8,128)S(1)}, f32[2048,128]{1,0:T(8,128)S(1)}) custom-call(s32[1]{0:T(128)} %bitcast.core_ref, bf16[128,2048]{1,0:T(8,128)(2,1)S(1)} %collective-permute-done.4.q_ref, bf16[2,144,512]{2,1,0:T(8,128)(2,1)S(1)} %get-tuple-element.63.refs_0_, ...), custom_call_target="tpu_custom_call" | custom-call | flops 2147483648 | bytes 4194304 | tf_op jit(solution)/shard_map/pallas_call | solution.py:130
  49.1 0.0 collective-permute-done.5.refs_2_.refs_5_
  49.1 2.8 %collective-permute-start.6 = (bf16[2,144,512]{2,1,0:T(8,128)(2,1)S(1)}, bf16[2,144,512]{2,1,0:T(8,128)(2,1)S(1)}, u32[]{:S(2)}, u32[]{:S(2)}) collective-permute-start(bf16[2,144,512]{2,1,0:T(8,128)(2,1)S(1)} %collective-permute-done.5.refs_2_.refs_5_), channel_id=1, source_target_pairs={{0,2},{1,3},{2,0},{3,1},{4,6},{5,7},{6,4},{7,5},{8,10},{9,11},{10,... | collective-permute-start | bytes 884744 | tf_op jit(solution)/shard_map/ppermute | solution.py:156
  51.9 0.0 collective-permute-done.7.refs_1_.refs_4_
  51.9 2.1 %shard_map.47 = (f32[2048,128]{1,0:T(8,128)S(1)}, f32[2048,128]{1,0:T(8,128)S(1)}, f32[2048,128]{1,0:T(8,128)S(1)}) custom-call(s32[1]{0:T(128)} %bitcast.core_ref, bf16[128,2048]{1,0:T(8,128)(2,1)S(1)} %collective-permute-done.4.q_ref, bf16[2,144,512]{2,1,0:T(8,128)(2,1)S(1)} %get-tuple-element.63.refs_0_, ...), custom_call_target="tpu_custom_call" | custom-call | flops 1073741824 | bytes 4194304 | tf_op jit(solution)/shard_map/pallas_call | solution.py:130
  54.0 0.0 collective-permute-done.9.q_ref
  54.0 4.6 %shard_map.48 = (f32[2048,128]{1,0:T(8,128)S(1)}, f32[2048,128]{1,0:T(8,128)S(1)}, f32[2048,128]{1,0:T(8,128)S(1)}) custom-call(s32[1]{0:T(128)} %bitcast.core_ref, bf16[128,2048]{1,0:T(8,128)(2,1)S(1)} %collective-permute-done.9.q_ref, bf16[2,144,512]{2,1,0:T(8,128)(2,1)S(1)} %get-tuple-element.63.refs_0_, ...), custom_call_target="tpu_custom_call" | custom-call | flops 3221225472 | bytes 4194304 | tf_op jit(solution)/shard_map/pallas_call | solution.py:130
  58.6 0.7 %collective-permute-done.6.refs_1_ = bf16[2,144,512]{2,1,0:T(8,128)(2,1)S(1)} collective-permute-done((bf16[2,144,512]{2,1,0:T(8,128)(2,1)S(1)}, bf16[2,144,512]{2,1,0:T(8,128)(2,1)S(1)}, u32[]{:S(2)}, u32[]{:S(2)}) %collective-permute-start.6) | collective-permute-done | bytes 294944 | tf_op jit(solution)/shard_map/ppermute | solution.py:156
  59.3 1.3 %shard_map.49 = (f32[2048,128]{1,0:T(8,128)S(1)}, f32[2048,128]{1,0:T(8,128)S(1)}, f32[2048,128]{1,0:T(8,128)S(1)}) custom-call(s32[1]{0:T(128)} %bitcast.core_ref, bf16[128,2048]{1,0:T(8,128)(2,1)S(1)} %collective-permute-done.4.q_ref, bf16[2,144,512]{2,1,0:T(8,128)(2,1)S(1)} %get-tuple-element.63.refs_0_, ...), custom_call_target="tpu_custom_call" | custom-call | flops 536870912 | bytes 4194304 | tf_op jit(solution)/shard_map/pallas_call | solution.py:130
  60.7 0.0 collective-permute-done.10.refs_2_.refs_1_
  60.7 2.1 %shard_map.51 = bf16[128,2048]{1,0:T(8,128)(2,1)S(1)} custom-call(s32[1]{0:T(128)} %bitcast.core_ref, bf16[128,2048]{1,0:T(8,128)(2,1)S(1)} %collective-permute-done.4.q_ref, bf16[2,144,512]{2,1,0:T(8,128)(2,1)S(1)} %get-tuple-element.63.refs_0_, bf16[2,2,144,512]{3,2,1,0:T(8,128)(2,1)S(1)} %collective-permute-done.10.refs_2_.refs_1_, ...), custom_call_target="tpu_custom_call" | custom-call | flops 1073741824 | bytes 4194304 | tf_op jit(solution)/shard_map/pallas_call | solution.py:130
  62.8 3.1 %collective-permute-start.11 = (bf16[128,2048]{1,0:T(8,128)(2,1)S(1)}, bf16[128,2048]{1,0:T(8,128)(2,1)S(1)}, u32[]{:S(2)}, u32[]{:S(2)}) collective-permute-start(bf16[128,2048]{1,0:T(8,128)(2,1)S(1)} %shard_map.51), channel_id=1, source_target_pairs={{0,1},{1,0},{2,3},{3,2},{4,5},{5,4},{6,7},{7,6},{8,9},{9,8},{10,11... | collective-permute-start | bytes 1572872 | tf_op jit(solution)/shard_map/ppermute | solution.py:162
  65.9 2.7 %shard_map.50 = bf16[128,2048]{1,0:T(8,128)(2,1)S(1)} custom-call(s32[1]{0:T(128)} %bitcast.core_ref, bf16[128,2048]{1,0:T(8,128)(2,1)S(1)} %collective-permute-done.9.q_ref, bf16[2,144,512]{2,1,0:T(8,128)(2,1)S(1)} %get-tuple-element.63.refs_0_, bf16[2,144,512]{2,1,0:T(8,128)(2,1)S(1)} %collective-permute-done.6.refs_1_, ...), custom_call_target="tpu_custom_call" | custom-call | flops 1610612736 | bytes 4194304 | tf_op jit(solution)/shard_map/pallas_call | solution.py:130
  68.6 0.0 collective-permute-done.11
  68.6 1.2 %maximum_select_fusion = bf16[1,128,4096]{2,1,0:T(8,128)(2,1)} fusion(bf16[1,128,2048]{2,1,0:T(8,128)(2,1)S(1)} %bitcast.14, bf16[1,128,2048]{2,1,0:T(8,128)(2,1)S(1)} %bitcast.11, pred[]{:T(512)S(6)} %eq.16), kind=kLoop, calls=%fused_computation | loop fusion | flops 4718592 | bytes 2097153 | tf_op jit(solution)/shard_map/jit(_where)/select_n | solution.py:198
  (2 shorter events, 0.1 us)
Async XLA Ops:
  0.0 13.2 %copy-start = (bf16[1,128,4096]{2,1,0:T(8,128)(2,1)S(1)}, bf16[1,128,4096]{2,1,0:T(8,128)(2,1)}, u32[]{:S(2)}) copy-start(bf16[1,128,4096]{2,1,0:T(8,128)(2,1)} %param.4) | copy-start | bytes 3145732
  1.8 19.4 %collective-permute-start.1 = (bf16[144,512]{1,0:T(8,128)(2,1)S(1)}, bf16[144,512]{1,0:T(8,128)(2,1)S(1)}, u32[]{:S(2)}, u32[]{:S(2)}) collective-permute-start(bf16[144,512]{1,0:T(8,128)(2,1)S(1)} %get-tuple-element.80), channel_id=1, source_target_pairs={{0,73},{1,72},{2,75},{3,74},{4,77},{5,76},{6,79},{7,78},{8,81},{9,... | collective-permute-start | bytes 442376 | tf_op jit(solution)/shard_map/ppermute | solution.py:150
  8.2 14.8 %collective-permute-start = (bf16[144,512]{1,0:T(8,128)(2,1)S(1)}, bf16[144,512]{1,0:T(8,128)(2,1)S(1)}, u32[]{:S(2)}, u32[]{:S(2)}) collective-permute-start(bf16[144,512]{1,0:T(8,128)(2,1)S(1)} %get-tuple-element.79), channel_id=1, source_target_pairs={{0,72},{1,73},{2,74},{3,75},{4,76},{5,77},{6,78},{7,79},{8,80},{9,... | collective-permute-start | bytes 442376 | tf_op jit(solution)/shard_map/ppermute | solution.py:150
  13.3 23.3 %collective-permute-start.4 = (bf16[128,2048]{1,0:T(8,128)(2,1)S(1)}, bf16[128,2048]{1,0:T(8,128)(2,1)S(1)}, u32[]{:S(2)}, u32[]{:S(2)}) collective-permute-start(bf16[128,2048]{1,0:T(8,128)(2,1)S(1)} %get-tuple-element.74), channel_id=1, source_target_pairs={{0,65},{1,64},{2,67},{3,66},{4,69},{5,68},{6,71},{7,70},{8,73},{9,... | collective-permute-start | bytes 1572872 | tf_op jit(solution)/shard_map/ppermute | solution.py:150
  23.0 10.4 %collective-permute-start.2 = (bf16[2,144,512]{2,1,0:T(8,128)(2,1)S(1)}, bf16[2,144,512]{2,1,0:T(8,128)(2,1)S(1)}, u32[]{:S(2)}, u32[]{:S(2)}) collective-permute-start(bf16[2,144,512]{2,1,0:T(8,128)(2,1)S(1)} %pad_maximum_fusion.1.refs_1_), channel_id=1, source_target_pairs={{0,8},{1,57},{2,10},{3,59},{4,12},{5,61},{6,14},{7,63},{8,16},{9,1... | collective-permute-start | bytes 884744 | tf_op jit(solution)/shard_map/ppermute | solution.py:153
  26.0 10.6 %collective-permute-start.3 = (bf16[2,144,512]{2,1,0:T(8,128)(2,1)S(1)}, bf16[2,144,512]{2,1,0:T(8,128)(2,1)S(1)}, u32[]{:S(2)}, u32[]{:S(2)}) collective-permute-start(bf16[2,144,512]{2,1,0:T(8,128)(2,1)S(1)} %pad_maximum_fusion.1.refs_1_), channel_id=1, source_target_pairs={{0,56},{1,9},{2,58},{3,11},{4,60},{5,13},{6,62},{7,15},{8,0},{9,17... | collective-permute-start | bytes 884744 | tf_op jit(solution)/shard_map/ppermute | solution.py:153
  28.3 14.7 %collective-permute-start.8 = (bf16[2,144,512]{2,1,0:T(8,128)(2,1)S(1)}, bf16[2,144,512]{2,1,0:T(8,128)(2,1)S(1)}, u32[]{:S(2)}, u32[]{:S(2)}) collective-permute-start(bf16[2,144,512]{2,1,0:T(8,128)(2,1)S(1)} %pad_maximum_fusion.1.refs_1_), channel_id=1, source_target_pairs={{0,2},{1,3},{2,0},{3,1},{4,6},{5,7},{6,4},{7,5},{8,10},{9,11},{10,... | collective-permute-start | bytes 884744 | tf_op jit(solution)/shard_map/ppermute | solution.py:156
  31.4 22.6 %collective-permute-start.9 = (bf16[128,2048]{1,0:T(8,128)(2,1)S(1)}, bf16[128,2048]{1,0:T(8,128)(2,1)S(1)}, u32[]{:S(2)}, u32[]{:S(2)}) collective-permute-start(bf16[128,2048]{1,0:T(8,128)(2,1)S(1)} %get-tuple-element.73), channel_id=1, source_target_pairs={{0,64},{1,65},{2,66},{3,67},{4,68},{5,69},{6,70},{7,71},{8,72},{9,... | collective-permute-start | bytes 1572872 | tf_op jit(solution)/shard_map/ppermute | solution.py:150
  36.6 12.5 %collective-permute-start.5 = (bf16[2,144,512]{2,1,0:T(8,128)(2,1)S(1)}, bf16[2,144,512]{2,1,0:T(8,128)(2,1)S(1)}, u32[]{:S(2)}, u32[]{:S(2)}) collective-permute-start(bf16[2,144,512]{2,1,0:T(8,128)(2,1)S(1)} %get-tuple-element.78), channel_id=1, source_target_pairs={{0,6},{1,7},{2,4},{3,5},{4,2},{5,3},{6,0},{7,1},{8,14},{9,15},{10,... | collective-permute-start | bytes 884744 | tf_op jit(solution)/shard_map/ppermute | solution.py:159
  41.0 10.8 %collective-permute-start.7 = (bf16[2,144,512]{2,1,0:T(8,128)(2,1)S(1)}, bf16[2,144,512]{2,1,0:T(8,128)(2,1)S(1)}, u32[]{:S(2)}, u32[]{:S(2)}) collective-permute-start(bf16[2,144,512]{2,1,0:T(8,128)(2,1)S(1)} %get-tuple-element.76), channel_id=1, source_target_pairs={{0,2},{1,3},{2,0},{3,1},{4,6},{5,7},{6,4},{7,5},{8,10},{9,11},{10,... | collective-permute-start | bytes 884744 | tf_op jit(solution)/shard_map/ppermute | solution.py:156
  43.0 17.6 %collective-permute-start.10 = (bf16[2,2,144,512]{3,2,1,0:T(8,128)(2,1)S(1)}, bf16[2,2,144,512]{3,2,1,0:T(8,128)(2,1)S(1)}, u32[]{:S(2)}, u32[]{:S(2)}) collective-permute-start(bf16[2,2,144,512]{3,2,1,0:T(8,128)(2,1)S(1)} %pad_maximum_fusion), channel_id=1, source_target_pairs={{0,6},{1,7},{2,4},{3,5},{4,2},{5,3},{6,0},{7,1},{8,14},{9,15},{10,... | collective-permute-start | bytes 1769480 | tf_op jit(solution)/shard_map/ppermute | solution.py:159
  49.1 10.2 %collective-permute-start.6 = (bf16[2,144,512]{2,1,0:T(8,128)(2,1)S(1)}, bf16[2,144,512]{2,1,0:T(8,128)(2,1)S(1)}, u32[]{:S(2)}, u32[]{:S(2)}) collective-permute-start(bf16[2,144,512]{2,1,0:T(8,128)(2,1)S(1)} %collective-permute-done.5.refs_2_.refs_5_), channel_id=1, source_target_pairs={{0,2},{1,3},{2,0},{3,1},{4,6},{5,7},{6,4},{7,5},{8,10},{9,11},{10,... | collective-permute-start | bytes 884744 | tf_op jit(solution)/shard_map/ppermute | solution.py:156
  62.8 5.8 %collective-permute-start.11 = (bf16[128,2048]{1,0:T(8,128)(2,1)S(1)}, bf16[128,2048]{1,0:T(8,128)(2,1)S(1)}, u32[]{:S(2)}, u32[]{:S(2)}) collective-permute-start(bf16[128,2048]{1,0:T(8,128)(2,1)S(1)} %shard_map.51), channel_id=1, source_target_pairs={{0,1},{1,0},{2,3},{3,2},{4,5},{5,4},{6,7},{7,6},{8,9},{9,8},{10,11... | collective-permute-start | bytes 1572872 | tf_op jit(solution)/shard_map/ppermute | solution.py:162
